TPU v7x, 32 devices: a whole 2x2x4 slice. The times are simulated.
32 devices in a mesh: seq: 8 (over y, x, core), head: 4 (over z).
Axes of the slice: x: 2, y: 2, z: 4, core: 2. Of those that a mesh axis runs over, the one named last changes fastest.
Arguments:
- prompt_k: bfloat16 [1280, 1024], P(('seq', 'head')), may hold values from -6 to 6
- prompt_v: bfloat16 [1280, 1024], P(('seq', 'head')), may hold values from -6 to 6
- resp_q: bfloat16 [2048, 8192], P('seq', 'head'), may hold values from -7 to 7
- resp_k: bfloat16 [2048, 1024], P('seq', 'head'), may hold values from -6 to 6
- resp_v: bfloat16 [2048, 1024], P('seq', 'head'), may hold values from -6 to 6
- grad_out: bfloat16 [2048, 8192], P('seq', 'head'), may hold values from -6 to 6
- resp_lengths: int32 [8], replicated, may hold values from 1 to 1024, 2048 in all
Outputs:
- resp_out: bfloat16 [2048, 8192], P('seq', 'head')
- grad_q: bfloat16 [2048, 8192], P('seq', 'head')
- grad_k_resp: bfloat16 [2048, 1024], P('seq', 'head')
- grad_v_resp: bfloat16 [2048, 1024], P('seq', 'head')
- grad_k_prompt: bfloat16 [1280, 1024], P(('seq', 'head'))
- grad_v_prompt: bfloat16 [1280, 1024], P(('seq', 'head'))
Inputs may be any that keep to these rules, and one draw needn't show every extreme that they name: `resp_lengths`: the 8 lengths add up to 2048, and the largest is exactly 1024.
All inputs are finite; a program needn't handle non-finite values.
Results may differ from a plain program's by a relative error of at most 0.02.
Values may be sent and summed in bfloat16 or wider, within the bound.
No kernel may reach another device: no remote copies, remote signals or barrier semaphores. Data moves between devices by JAX's collectives and lax.ppermute only.
A program may use at most 128 MiB of HBM per device.

v0:
```python
import functools
import math

import jax
import jax.numpy as jnp
from jax import lax
from jax.experimental import pallas as pl
from jax.experimental.pallas import tpu as pltpu
from jax.sharding import PartitionSpec as P

HD = 128
SPAN = 4
NEG = -1e30
NT = (((1,), (1,)), ((), ()))


def dot(a, b):
    return jnp.dot(a, b, preferred_element_type=jnp.float32)


def dot_nt(a, b):
    return lax.dot_general(a, b, NT, preferred_element_type=jnp.float32)


def attention_kernel(
    prompt_chunks, chunk, meta, q_ref, do_ref, prompt_ref, *refs
):
    resp_refs = refs[: SPAN + 1]
    o_ref, dq_ref, dprompt_ref = refs[SPAN + 1 : SPAN + 4]
    dresp_refs = refs[SPAN + 4 : 2 * SPAN + 5]
    bias, s_buf, p_buf, dk_t, dv_t = refs[2 * SPAN + 5 :]
    rows = q_ref.shape[0]
    step = pl.program_id(1)
    last = pl.num_programs(1) - 1
    score_scale = 1.0 / math.sqrt(HD)
    exp_scale = score_scale * math.log2(math.e)
    count = prompt_chunks + SPAN + 1

    def keys_of(c):
        if c < prompt_chunks:
            return prompt_ref[c * chunk : (c + 1) * chunk, :HD]
        return resp_refs[c - prompt_chunks][:, :HD]

    def values_of(c):
        if c < prompt_chunks:
            return prompt_ref[c * chunk : (c + 1) * chunk, HD:]
        return resp_refs[c - prompt_chunks][:, HD:]

    @pl.when((step == 0) & (pl.program_id(0) == 0))
    def _():
        first_row = meta[0]
        row_pos = first_row + lax.broadcasted_iota(jnp.int32, (rows, rows), 0)
        seg_start = jnp.zeros((rows, rows), jnp.int32)
        end = jnp.int32(0)
        for i in range(1, meta.shape[0]):
            end = end + meta[i]
            seg_start = jnp.where(row_pos >= end, end, seg_start)
        for distance in range(SPAN + 1):
            key_pos = (first_row - distance * rows) + lax.broadcasted_iota(
                jnp.int32, (rows, rows), 1
            )
            allowed = (key_pos >= seg_start) & (key_pos <= row_pos)
            bias[distance] = jnp.where(allowed, 0.0, NEG)

    @pl.when(step == 0)
    def _():
        dk_t[...] = jnp.zeros_like(dk_t)
        dv_t[...] = jnp.zeros_like(dv_t)

    q = q_ref[...]
    top = None
    for c in range(count):
        s = dot_nt(q, keys_of(c))
        if c >= prompt_chunks:
            s = s + bias[c - prompt_chunks]
        s_buf[c, :, : s.shape[1]] = s
        for at in range(0, s.shape[1], HD):
            part = s[:, at : at + HD]
            top = part if top is None else jnp.maximum(top, part)
    top = jnp.max(top, axis=1, keepdims=True) * exp_scale

    def width_of(c):
        return chunk if c < prompt_chunks else rows

    total = jnp.zeros((rows, HD), jnp.float32)
    out = jnp.zeros((rows, HD), jnp.float32)
    for c in range(count):
        w = width_of(c)
        p = jnp.exp2(s_buf[c, :, :w] * exp_scale - top)
        for at in range(0, w, HD):
            total = total + p[:, at : at + HD]
        p = p.astype(jnp.bfloat16)
        p_buf[c, :, :w] = p
        out = out + dot(p, values_of(c))
    inverse = 1.0 / jnp.sum(total, axis=1, keepdims=True)
    out = (out * inverse).astype(jnp.bfloat16)
    o_ref[...] = out
    cot = (do_ref[...].astype(jnp.float32) * inverse).astype(jnp.bfloat16)
    delta = jnp.sum(
        cot.astype(jnp.float32) * out.astype(jnp.float32), axis=1, keepdims=True
    )
    cot_t = cot.T
    q_t = q.T
    dq = jnp.zeros((rows, HD), jnp.float32)
    for c in range(count):
        w = width_of(c)
        p = p_buf[c, :, :w]
        dp = dot_nt(cot, values_of(c))
        ds = (p.astype(jnp.float32) * (dp - delta)).astype(jnp.bfloat16)
        dq = dq + dot(ds, keys_of(c))
        dv_t[c, :, :w] += dot(cot_t, p)
        dk_t[c, :, :w] += dot(q_t, ds)
    dq_ref[...] = (dq * score_scale).astype(jnp.bfloat16)

    @pl.when(step == last)
    def _():
        for c in range(count):
            w = width_of(c)
            grad_k = (dk_t[c, :, :w] * score_scale).T
            grad_v = dv_t[c, :, :w].T
            if c < prompt_chunks:
                target = dprompt_ref.at[c * chunk : (c + 1) * chunk]
            else:
                target = dresp_refs[c - prompt_chunks]
            target[:, :HD] = grad_k.astype(target.dtype)
            target[:, HD:] = grad_v.astype(target.dtype)


def attention(meta, resp_q, grad_out, prompt_kv, resp_kvs):
    rows = resp_q.shape[0]
    prompt_len = prompt_kv.shape[0]
    kv_heads = prompt_kv.shape[1] // (2 * HD)
    group = resp_q.shape[1] // HD // kv_heads
    chunk = 256
    prompt_chunks = prompt_len // chunk
    count = prompt_chunks + SPAN + 1
    wide = max(chunk, rows)
    head_spec = pl.BlockSpec((rows, HD), lambda n, g: (0, n * group + g))
    prompt_spec = pl.BlockSpec((prompt_len, 2 * HD), lambda n, g: (0, n))
    resp_spec = pl.BlockSpec((rows, 2 * HD), lambda n, g: (0, n))
    resp_shape = (rows, kv_heads * 2 * HD)
    pairs = rows * kv_heads * group * (prompt_len + (SPAN + 1) * rows)
    return pl.pallas_call(
        functools.partial(attention_kernel, prompt_chunks, chunk),
        grid=(kv_heads, group),
        in_specs=[pl.BlockSpec(memory_space=pltpu.SMEM), head_spec, head_spec, prompt_spec]
        + [resp_spec] * (SPAN + 1),
        out_specs=[head_spec, head_spec, prompt_spec] + [resp_spec] * (SPAN + 1),
        out_shape=[
            jax.ShapeDtypeStruct(resp_q.shape, jnp.bfloat16),
            jax.ShapeDtypeStruct(resp_q.shape, jnp.bfloat16),
            jax.ShapeDtypeStruct(prompt_kv.shape, jnp.bfloat16),
            jax.ShapeDtypeStruct(resp_shape, jnp.float32),
        ]
        + [jax.ShapeDtypeStruct(resp_shape, jnp.bfloat16)] * SPAN,
        scratch_shapes=[
            pltpu.VMEM((SPAN + 1, rows, rows), jnp.float32),
            pltpu.VMEM((count, rows, wide), jnp.float32),
            pltpu.VMEM((count, rows, wide), jnp.bfloat16),
            pltpu.VMEM((count, HD, wide), jnp.float32),
            pltpu.VMEM((count, HD, wide), jnp.float32),
        ],
        compiler_params=pltpu.CompilerParams(vmem_limit_bytes=56 * 1024 * 1024),
        cost_estimate=pl.CostEstimate(
            flops=12 * HD * pairs, bytes_accessed=4 * resp_q.size * 2, transcendentals=pairs
        ),
        name="attention",
    )(meta, resp_q, grad_out, prompt_kv, *resp_kvs)


def passed_along(array, axis, by):
    devices = lax.axis_size(axis)
    pairs = [(i, i + by) for i in range(devices) if 0 <= i + by < devices]
    return lax.ppermute(array, axis, pairs)


def paired(keys, values, blocks):
    rows = keys.shape[0]
    stacked = jnp.stack(
        [keys.reshape(rows, blocks, HD), values.reshape(rows, blocks, HD)], axis=2
    )
    return stacked.reshape(rows, blocks * 2 * HD)


def unpaired(both):
    rows = both.shape[0]
    split = both.reshape(rows, -1, 2, HD)
    return split[:, :, 0].reshape(rows, -1), split[:, :, 1].reshape(rows, -1)


def shards(prompt_k, prompt_v, resp_q, resp_k, resp_v, grad_out, resp_lengths):
    kv_heads = resp_k.shape[1] // HD
    row_count = resp_q.shape[0]
    all_heads = prompt_k.shape[1] // HD
    first_row = (lax.axis_index("seq") * row_count).astype(jnp.int32)
    meta = jnp.concatenate([first_row[None], resp_lengths])

    prompt_kv = paired(prompt_k, prompt_v, all_heads)
    prompt_kv = lax.all_to_all(prompt_kv, "head", split_axis=1, concat_axis=0, tiled=True)
    prompt_kv = lax.all_gather(prompt_kv, "seq", axis=0, tiled=True)

    resp_kv = paired(resp_k, resp_v, kv_heads)
    resp_kvs = [resp_kv] + [
        passed_along(resp_kv, "seq", distance) for distance in range(1, SPAN + 1)
    ]

    resp_out, grad_q, grad_prompt, own, *others = attention(
        meta, resp_q, grad_out, prompt_kv, resp_kvs
    )

    grad_prompt = lax.psum_scatter(grad_prompt, "seq", scatter_dimension=0, tiled=True)
    grad_prompt = lax.all_to_all(grad_prompt, "head", split_axis=0, concat_axis=1, tiled=True)
    for distance, part in enumerate(others, start=1):
        own = own + passed_along(part, "seq", -distance).astype(jnp.float32)
    grad_k_resp, grad_v_resp = unpaired(own.astype(jnp.bfloat16))
    grad_k_prompt, grad_v_prompt = unpaired(grad_prompt)
    return (resp_out, grad_q, grad_k_resp, grad_v_resp, grad_k_prompt, grad_v_prompt)


def solution(mesh):
    placed = (
        P(("seq", "head"), None),
        P(("seq", "head"), None),
        P("seq", "head"),
        P("seq", "head"),
        P("seq", "head"),
        P("seq", "head"),
        P(),
    )
    return jax.shard_map(
        shards,
        mesh=mesh,
        in_specs=placed,
        out_specs=(
            P("seq", "head"),
            P("seq", "head"),
            P("seq", "head"),
            P("seq", "head"),
            P(("seq", "head"), None),
            P(("seq", "head"), None),
        ),
        check_vma=False,
    )
```

profile of v0, /device:TPU:6, one launch (start us, length us, event | category | flops | bytes accessed | tf_op | source)
XLA Modules:
  0.0 160.3 jit_solution(7167403915157740784)
XLA Ops:
  7.2 1.0 stack_reshape.16
  8.2 1.0 stack_reshape.17
  9.2 0.4 pad_maximum_fusion.1
  9.7 11.7 %all_to_all.35 = bf16[40,4,512]{2,0,1:T(8,128)(2,1)} all-to-all(bf16[40,4,512]{2,0,1:T(8,128)(2,1)S(1)} %copy.37), channel_id=1, replica_groups=mesh['seq'=8,'head'=4] {'head'}, dimensions={1} | all-to-all | bytes 327680 | tf_op jit(solution)/shard_map/all_to_all | solution.py:199
  21.6 0.6 pad_maximum_fusion
  22.3 0.1 reshape.30.refs_0_
  22.4 1.3 collective-permute-start.3
  23.7 1.3 collective-permute-start.2
  25.0 1.3 collective-permute-start.1
  26.3 1.9 %collective-permute-start = (bf16[256,512]{1,0:T(8,128)(2,1)S(1)}, bf16[256,512]{1,0:T(8,128)(2,1)S(1)}, u32[]{:S(2)}, u32[]{:S(2)}) collective-permute-start(bf16[256,512]{1,0:T(8,128)(2,1)S(1)} %reshape.30.refs_0_), channel_id=1, source_target_pairs={{0,4},{4,8},{8,12},{12,16},{16,20},{20,24},{24,28},{1,5},{5,9},{9,... | collective-permute-start | bytes 786440 | tf_op jit(solution)/shard_map/ppermute | solution.py:174
  28.2 0.6 pad_add_fusion.meta
  28.8 5.9 %collective-permute-done.3.refs_4_ = bf16[256,512]{1,0:T(8,128)(2,1)S(1)} collective-permute-done((bf16[256,512]{1,0:T(8,128)(2,1)S(1)}, bf16[256,512]{1,0:T(8,128)(2,1)S(1)}, u32[]{:S(2)}, u32[]{:S(2)}) %collective-permute-start.3) | collective-permute-done | bytes 262176 | tf_op jit(solution)/shard_map/ppermute | solution.py:174
  34.7 0.6 collective-permute-done.2.refs_3_
  35.3 5.2 %collective-permute-done.1.refs_2_ = bf16[256,512]{1,0:T(8,128)(2,1)S(1)} collective-permute-done((bf16[256,512]{1,0:T(8,128)(2,1)S(1)}, bf16[256,512]{1,0:T(8,128)(2,1)S(1)}, u32[]{:S(2)}, u32[]{:S(2)}) %collective-permute-start.1) | collective-permute-done | bytes 262176 | tf_op jit(solution)/shard_map/ppermute | solution.py:174
  40.6 14.1 %all-gather.2.cloned.1.call-done.prompt_ref = bf16[1280,512]{1,0:T(8,128)(2,1)} async-done(((bf16[160,512]{1,0:T(8,128)(2,1)}), bf16[1280,512]{1,0:T(8,128)(2,1)}) %all-gather.2.cloned.1.call-update) | async-done | bytes 1310736 | tf_op jit(solution)/shard_map/all_gather | solution.py:200
  54.8 46.2 %attention.1 = (bf16[256,2048]{1,0:T(8,128)(2,1)}, bf16[256,2048]{1,0:T(8,128)(2,1)}, bf16[1280,512]{1,0:T(8,128)(2,1)}, f32[256,512]{1,0:T(8,128)}, bf16[256,51...) custom-call(s32[9]{0:T(128)} %pad_add_fusion.meta, ...), custom_call_target="tpu_custom_call" | custom-call | flops 16106127360 | bytes 4194304 | tf_op jit(solution)/shard_map/attention/pallas_call | solution.py:143
  101.0 3.3 %collective-permute-start.4 = (bf16[256,512]{1,0:T(8,128)(2,1)}, bf16[256,512]{1,0:T(8,128)(2,1)S(1)}, u32[]{:S(2)}, u32[]{:S(2)}) collective-permute-start(bf16[256,512]{1,0:T(8,128)(2,1)} %get-tuple-element.17), channel_id=1, source_target_pairs={{4,0},{8,4},{12,8},{16,12},{20,16},{24,20},{28,24},{5,1},{9,5},{13... | collective-permute-start | bytes 786440 | tf_op jit(solution)/shard_map/ppermute | solution.py:174
  104.3 3.5 %collective-permute-start.5 = (bf16[256,512]{1,0:T(8,128)(2,1)S(1)}, bf16[256,512]{1,0:T(8,128)(2,1)S(1)}, u32[]{:S(2)}, u32[]{:S(2)}) collective-permute-start(bf16[256,512]{1,0:T(8,128)(2,1)S(1)} %copy-done.8), channel_id=1, source_target_pairs={{8,0},{12,4},{16,8},{20,12},{24,16},{28,20},{9,1},{13,5},{17,9},{2... | collective-permute-start | bytes 786440 | tf_op jit(solution)/shard_map/ppermute | solution.py:174
  107.8 1.3 collective-permute-start.6
  109.1 1.3 collective-permute-start.7
  110.5 30.2 %reduce-scatter.2.cloned.1.call-done = bf16[160,512]{1,0:T(8,128)(2,1)} async-done(((bf16[1280,512]{1,0:T(8,128)(2,1)}), bf16[160,512]{1,0:T(8,128)(2,1)}) %reduce-scatter.2.cloned.1.call-update) | async-done | bytes 163856 | tf_op jit(solution)/shard_map/reduce_scatter | solution.py:211
  140.7 4.6 %all-to-all-start.1 = ((bf16[4,40,512]{2,1,0:T(8,128)(2,1)}), bf16[4,40,512]{2,1,0:T(8,128)(2,1)S(1)}, u32[]{:S(2)}, u32[]{:S(2)}) async-start(bf16[4,40,512]{2,1,0:T(8,128)(2,1)} %bitcast.20), calls=%async_computation.2 | async-start | bytes 327680 | tf_op jit(solution)/shard_map/all_to_all | solution.py:212
  145.3 0.2 add_convert_fusion
  145.6 0.4 fusion
  146.0 0.1 copy.46
  146.1 0.8 copy.44
  146.9 0.1 copy.45
  147.0 0.8 copy.43
  147.8 4.0 %all-to-all-done.1 = bf16[4,40,512]{2,1,0:T(8,128)(2,1)S(1)} async-done(((bf16[4,40,512]{2,1,0:T(8,128)(2,1)}), bf16[4,40,512]{2,1,0:T(8,128)(2,1)S(1)}, u32[]{:S(2)}, u32[]{:S(2)}) %all-to-all-start.1) | async-done | bytes 163872 | tf_op jit(solution)/shard_map/all_to_all | solution.py:212
  151.7 0.1 copy.42
  151.9 0.9 slice_reduce_fusion
  152.8 0.7 copy_bitcast_fusion
  (39 shorter events, 0.6 us)
Async XLA Ops:
  7.2 14.3 %copy-start.2 = (bf16[256,256]{1,0:T(8,128)(2,1)S(1)}, bf16[256,256]{1,0:T(8,128)(2,1)}, u32[]{:S(2)}) copy-start(bf16[256,256]{1,0:T(8,128)(2,1)} %param.10) | copy-start | bytes 393220
  7.2 14.4 %copy-start.3 = (bf16[256,256]{1,0:T(8,128)(2,1)S(1)}, bf16[256,256]{1,0:T(8,128)(2,1)}, u32[]{:S(2)}) copy-start(bf16[256,256]{1,0:T(8,128)(2,1)} %param.11) | copy-start | bytes 393220
  7.2 47.6 %all-gather.2.cloned.1.call-start = ((), (), s32[]{:S(2)}) async-start(), calls=%async_computation.3 | async-start | bytes 1474560 | tf_op jit(solution)/shard_map/all_gather | solution.py:200
  9.7 18.5 %copy-start.11 = (s32[8]{0:T(128)S(1)}, s32[8]{0:T(128)}, u32[]{:S(2)}) copy-start(s32[8]{0:T(128)} %param.13) | copy-start | bytes 100
  21.5 119.2 %reduce-scatter.2.cloned.1.call-start = ((), (), s32[]{:S(2)}) async-start(), calls=%async_computation.4 | async-start | bytes 1474560 | tf_op jit(solution)/shard_map/reduce_scatter | solution.py:211
  22.4 32.4 %copy-start.1 = (bf16[256,512]{1,0:T(8,128)(2,1)}, bf16[256,512]{1,0:T(8,128)(2,1)S(1)}, u32[]{:S(2)}) copy-start(bf16[256,512]{1,0:T(8,128)(2,1)S(1)} %reshape.30.refs_0_) | copy-start | bytes 786436
  22.4 12.4 %collective-permute-start.3 = (bf16[256,512]{1,0:T(8,128)(2,1)S(1)}, bf16[256,512]{1,0:T(8,128)(2,1)S(1)}, u32[]{:S(2)}, u32[]{:S(2)}) collective-permute-start(bf16[256,512]{1,0:T(8,128)(2,1)S(1)} %reshape.30.refs_0_), channel_id=1, source_target_pairs={{0,16},{4,20},{8,24},{12,28},{1,17},{5,21},{9,25},{13,29},{2,18},{... | collective-permute-start | bytes 786440 | tf_op jit(solution)/shard_map/ppermute | solution.py:174
  23.7 11.6 %collective-permute-start.2 = (bf16[256,512]{1,0:T(8,128)(2,1)S(1)}, bf16[256,512]{1,0:T(8,128)(2,1)S(1)}, u32[]{:S(2)}, u32[]{:S(2)}) collective-permute-start(bf16[256,512]{1,0:T(8,128)(2,1)S(1)} %reshape.30.refs_0_), channel_id=1, source_target_pairs={{0,12},{4,16},{8,20},{12,24},{16,28},{1,13},{5,17},{9,21},{13,25},... | collective-permute-start | bytes 786440 | tf_op jit(solution)/shard_map/ppermute | solution.py:174
  25.0 15.6 %collective-permute-start.1 = (bf16[256,512]{1,0:T(8,128)(2,1)S(1)}, bf16[256,512]{1,0:T(8,128)(2,1)S(1)}, u32[]{:S(2)}, u32[]{:S(2)}) collective-permute-start(bf16[256,512]{1,0:T(8,128)(2,1)S(1)} %reshape.30.refs_0_), channel_id=1, source_target_pairs={{0,8},{4,12},{8,16},{12,20},{16,24},{20,28},{1,9},{5,13},{9,17},{1... | collective-permute-start | bytes 786440 | tf_op jit(solution)/shard_map/ppermute | solution.py:174
  26.3 14.4 %collective-permute-start = (bf16[256,512]{1,0:T(8,128)(2,1)S(1)}, bf16[256,512]{1,0:T(8,128)(2,1)S(1)}, u32[]{:S(2)}, u32[]{:S(2)}) collective-permute-start(bf16[256,512]{1,0:T(8,128)(2,1)S(1)} %reshape.30.refs_0_), channel_id=1, source_target_pairs={{0,4},{4,8},{8,12},{12,16},{16,20},{20,24},{24,28},{1,5},{5,9},{9,... | collective-permute-start | bytes 786440 | tf_op jit(solution)/shard_map/ppermute | solution.py:174
  34.7 20.0 %copy-start.5 = (bf16[256,512]{1,0:T(8,128)(2,1)}, bf16[256,512]{1,0:T(8,128)(2,1)S(1)}, u32[]{:S(2)}) copy-start(bf16[256,512]{1,0:T(8,128)(2,1)S(1)} %collective-permute-done.3.refs_4_) | copy-start | bytes 786436
  35.3 19.5 %copy-start.7 = (bf16[256,512]{1,0:T(8,128)(2,1)}, bf16[256,512]{1,0:T(8,128)(2,1)S(1)}, u32[]{:S(2)}) copy-start(bf16[256,512]{1,0:T(8,128)(2,1)S(1)} %collective-permute-done.2.refs_3_) | copy-start | bytes 786436
  40.6 14.2 %copy-start.9 = (bf16[256,512]{1,0:T(8,128)(2,1)}, bf16[256,512]{1,0:T(8,128)(2,1)S(1)}, u32[]{:S(2)}) copy-start(bf16[256,512]{1,0:T(8,128)(2,1)S(1)} %collective-permute-done.1.refs_2_) | copy-start | bytes 786436
  40.6 14.1 %copy-start.10 = (bf16[256,512]{1,0:T(8,128)(2,1)}, bf16[256,512]{1,0:T(8,128)(2,1)S(1)}, u32[]{:S(2)}) copy-start(bf16[256,512]{1,0:T(8,128)(2,1)S(1)} %collective-permute-done.refs_1_) | copy-start | bytes 786436
  101.0 3.4 %copy-start.8 = (bf16[256,512]{1,0:T(8,128)(2,1)S(1)}, bf16[256,512]{1,0:T(8,128)(2,1)}, u32[]{:S(2)}) copy-start(bf16[256,512]{1,0:T(8,128)(2,1)} %get-tuple-element.18) | copy-start | bytes 786436
  101.0 6.9 %copy-start.6 = (bf16[256,512]{1,0:T(8,128)(2,1)S(1)}, bf16[256,512]{1,0:T(8,128)(2,1)}, u32[]{:S(2)}) copy-start(bf16[256,512]{1,0:T(8,128)(2,1)} %get-tuple-element.19) | copy-start | bytes 786436
  101.0 8.2 %copy-start.4 = (bf16[256,512]{1,0:T(8,128)(2,1)S(1)}, bf16[256,512]{1,0:T(8,128)(2,1)}, u32[]{:S(2)}) copy-start(bf16[256,512]{1,0:T(8,128)(2,1)} %get-tuple-element.20) | copy-start | bytes 786436
  101.0 44.4 %copy-start = (f32[256,512]{1,0:T(8,128)S(1)}, f32[256,512]{1,0:T(8,128)}, u32[]{:S(2)}) copy-start(f32[256,512]{1,0:T(8,128)} %get-tuple-element.16) | copy-start | bytes 1572868
  101.0 44.3 %collective-permute-start.4 = (bf16[256,512]{1,0:T(8,128)(2,1)}, bf16[256,512]{1,0:T(8,128)(2,1)S(1)}, u32[]{:S(2)}, u32[]{:S(2)}) collective-permute-start(bf16[256,512]{1,0:T(8,128)(2,1)} %get-tuple-element.17), channel_id=1, source_target_pairs={{4,0},{8,4},{12,8},{16,12},{20,16},{24,20},{28,24},{5,1},{9,5},{13... | collective-permute-start | bytes 786440 | tf_op jit(solution)/shard_map/ppermute | solution.py:174
  104.3 41.0 %collective-permute-start.5 = (bf16[256,512]{1,0:T(8,128)(2,1)S(1)}, bf16[256,512]{1,0:T(8,128)(2,1)S(1)}, u32[]{:S(2)}, u32[]{:S(2)}) collective-permute-start(bf16[256,512]{1,0:T(8,128)(2,1)S(1)} %copy-done.8), channel_id=1, source_target_pairs={{8,0},{12,4},{16,8},{20,12},{24,16},{28,20},{9,1},{13,5},{17,9},{2... | collective-permute-start | bytes 786440 | tf_op jit(solution)/shard_map/ppermute | solution.py:174
  107.8 37.5 %collective-permute-start.6 = (bf16[256,512]{1,0:T(8,128)(2,1)S(1)}, bf16[256,512]{1,0:T(8,128)(2,1)S(1)}, u32[]{:S(2)}, u32[]{:S(2)}) collective-permute-start(bf16[256,512]{1,0:T(8,128)(2,1)S(1)} %copy-done.6), channel_id=1, source_target_pairs={{12,0},{16,4},{20,8},{24,12},{28,16},{13,1},{17,5},{21,9},{25,13},... | collective-permute-start | bytes 786440 | tf_op jit(solution)/shard_map/ppermute | solution.py:174
  109.1 36.2 %collective-permute-start.7 = (bf16[256,512]{1,0:T(8,128)(2,1)S(1)}, bf16[256,512]{1,0:T(8,128)(2,1)S(1)}, u32[]{:S(2)}, u32[]{:S(2)}) collective-permute-start(bf16[256,512]{1,0:T(8,128)(2,1)S(1)} %copy-done.4), channel_id=1, source_target_pairs={{16,0},{20,4},{24,8},{28,12},{17,1},{21,5},{25,9},{29,13},{18,2},{... | collective-permute-start | bytes 786440 | tf_op jit(solution)/shard_map/ppermute | solution.py:174
  140.7 11.0 %all-to-all-start.1 = ((bf16[4,40,512]{2,1,0:T(8,128)(2,1)}), bf16[4,40,512]{2,1,0:T(8,128)(2,1)S(1)}, u32[]{:S(2)}, u32[]{:S(2)}) async-start(bf16[4,40,512]{2,1,0:T(8,128)(2,1)} %bitcast.20), calls=%async_computation.2 | async-start | bytes 327680 | tf_op jit(solution)/shard_map/all_to_all | solution.py:212
Sparse Core Ops, SparseCore 0:
  21.6 33.1 all-gather.1
  101.1 39.5 reduce-scatter.1
where the time goes:
time: 163 us; the launch traced here: 160 us
  waiting for transfers between devices  60.2 us (37%)
  Pallas kernels  46.2 us (28%)
  starting transfers between devices  19.9 us (12%)
  between operations  14.4 us (9%)
  blocking collectives  11.7 us (7%)
  local copies, waits for them, and re-layouts  6.21 us (4%)
  other arithmetic  1.74 us (1%)
    pallas_call x1, Pallas kernels, attention(): pl.pallas_call(functools.partial(attention_kernel, prompt_chunks, chunk),...  46.2 us
    reduce_scatter x1, waiting for transfers between devices, shards(): lax.psum_scatter(grad_prompt, 'seq', scatter_dimension=0, tiled=True)  30.2 us
    ppermute x8, starting transfers between devices, passed_along(): return lax.ppermute(array, axis, pairs)  15.2 us
    all_gather x1, waiting for transfers between devices, shards(): prompt_kv = lax.all_gather(prompt_kv, 'seq', axis=0, tiled=True)  14.1 us
    ppermute x8, waiting for transfers between devices, passed_along(): return lax.ppermute(array, axis, pairs)  11.8 us
    all_to_all x1, blocking collectives, shards(): lax.all_to_all(prompt_kv, 'head', split_axis=1, concat_axis=0, tiled=True)  11.7 us
    all_to_all x1, starting transfers between devices, shards(): lax.all_to_all(grad_prompt, 'head', split_axis=0, concat_axis=1, tiled=True)  4.59 us
    all_to_all x1, waiting for transfers between devices, shards(): lax.all_to_all(grad_prompt, 'head', split_axis=0, concat_axis=1, tiled=True)  3.97 us
  transfers between devices with their start and end apart: 11, of which 7 were waited for; matrix products, arithmetic and copies ran while one was open for 2% of the time, Pallas kernels for 0%

commit v1 on v0

v1 whole, which is shorter than its diff:
```python
import functools
import math

import jax
import jax.numpy as jnp
from jax import lax
from jax.experimental import pallas as pl
from jax.experimental.pallas import tpu as pltpu
from jax.sharding import PartitionSpec as P

HD = 128
CORES = 2
FAR = 4
HEADS_PER_STEP = 2
CHUNK = 256
NEG = -1e30
NT = (((1,), (1,)), ((), ()))
BF16 = jnp.bfloat16
F32 = jnp.float32


def dot(a, b):
    return jnp.dot(a, b, preferred_element_type=F32)


def dot_nt(a, b):
    return lax.dot_general(a, b, NT, preferred_element_type=F32)


def whole(count):
    return [pl.BlockSpec(memory_space=pltpu.VMEM)] * count


def local_call(kernel, name, inputs, outputs, scratch=()):
    return pl.pallas_call(
        kernel,
        in_specs=whole(len(inputs)),
        out_specs=whole(len(outputs)),
        out_shape=[jax.ShapeDtypeStruct(shape, kind) for shape, kind in outputs],
        scratch_shapes=list(scratch),
        compiler_params=pltpu.CompilerParams(vmem_limit_bytes=40 * 1024 * 1024),
        name=name,
    )(*inputs)


def pack_kernel(pk_ref, pv_ref, rk_ref, rv_ref, *outs):
    pieces, resp = outs[:-1], outs[-1]
    head = lax.axis_index("head")
    width = pieces[0].shape[1]
    for k, piece in enumerate(pieces):
        start = pl.multiple_of((head ^ k) * (width // 2), HD)
        for n in range(width // (2 * HD)):
            at = pl.multiple_of(start + n * HD, HD)
            piece[:, 2 * n * HD : (2 * n + 1) * HD] = pk_ref[:, pl.ds(at, HD)]
            piece[:, (2 * n + 1) * HD : (2 * n + 2) * HD] = pv_ref[:, pl.ds(at, HD)]
    for n in range(width // (2 * HD)):
        resp[:, 2 * n * HD : (2 * n + 1) * HD] = rk_ref[:, n * HD : (n + 1) * HD]
        resp[:, (2 * n + 1) * HD : (2 * n + 2) * HD] = rv_ref[:, n * HD : (n + 1) * HD]


def merge_kernel(parts, rows, kept_ref, got_ref, *outs):
    pieces, back1, back2, own = outs[:parts], outs[parts], outs[parts + 1], outs[parts + 2]
    core = lax.rem(lax.axis_index("seq"), CORES)
    to_own = jnp.where(core == 0, 1.0, 0.0)
    half = kept_ref.shape[0] - 3 * rows
    share = half // parts
    for k, piece in enumerate(pieces):
        at = slice(k * share, (k + 1) * share)
        piece[...] = (kept_ref[at] + got_ref[at].astype(F32)).astype(BF16)
    one, two, three = half + rows, half + 2 * rows, half + 3 * rows
    back1[...] = (kept_ref[half:one] + got_ref[half:one].astype(F32)).astype(BF16)
    chosen = got_ref[one:two].astype(F32)
    back2[...] = (kept_ref[one:two] + chosen * (1.0 - to_own)).astype(BF16)
    own[...] = kept_ref[two:three] + chosen * to_own


def sum_kernel(parts, *refs):
    ins, outs, total = refs[:parts], refs[parts:-1], refs[-1]
    acc = ins[0][...].astype(F32)
    for ref in ins[1:]:
        acc = acc + ref[...].astype(F32)
    total[...] = acc
    share = total.shape[0] // len(outs)
    for k, out in enumerate(outs):
        out[...] = total[k * share : (k + 1) * share].astype(BF16)


def finish_prompt_kernel(*refs):
    pieces, (gk_ref, gv_ref) = refs[:-2], refs[-2:]
    head = lax.axis_index("head")
    width = pieces[0].shape[1]
    for k, piece in enumerate(pieces):
        start = pl.multiple_of((head ^ k) * (width // 2), HD)
        for n in range(width // (2 * HD)):
            at = pl.multiple_of(start + n * HD, HD)
            gk_ref[:, pl.ds(at, HD)] = piece[:, 2 * n * HD : (2 * n + 1) * HD]
            gv_ref[:, pl.ds(at, HD)] = piece[:, (2 * n + 1) * HD : (2 * n + 2) * HD]


def finish_resp_kernel(own_ref, one_ref, two_ref, gk_ref, gv_ref):
    total = (own_ref[...] + one_ref[...].astype(F32) + two_ref[...].astype(F32)).astype(BF16)
    for n in range(own_ref.shape[1] // (2 * HD)):
        gk_ref[:, n * HD : (n + 1) * HD] = total[:, 2 * n * HD : (2 * n + 1) * HD]
        gv_ref[:, n * HD : (n + 1) * HD] = total[:, (2 * n + 1) * HD : (2 * n + 2) * HD]


def attention_kernel(
    tokens, lengths, q_ref, do_ref, sent_ref, got_ref, own_ref, far_ref,
    o_ref, dq_ref, kept_ref, back_ref,
    bias, keys, values, q_all, do_all, s_buf, p_buf, o_all, dq_all, dk_t, dv_t,
):
    heads = q_ref.shape[1] // HD
    rows = heads * tokens
    total_keys = keys.shape[0]
    prompt_len = total_keys - 5 * tokens
    half = prompt_len // 2
    step = pl.program_id(1)
    last = pl.num_programs(1) - 1
    score_scale = 1.0 / math.sqrt(HD)
    exp_scale = score_scale * math.log2(math.e)
    resp_at = [prompt_len + i * tokens for i in range(6)]
    pieces = [
        (sent_ref, 0, half, 0),
        (got_ref, 0, half, half),
        (own_ref, 0, tokens, resp_at[0]),
        (sent_ref, half, tokens, resp_at[1]),
        (far_ref, 0, tokens, resp_at[2]),
        (got_ref, half, tokens, resp_at[3]),
        (got_ref, half + tokens, tokens, resp_at[4]),
    ]

    @pl.when((step == 0) & (pl.program_id(0) == 0))
    def _():
        place = lax.axis_index("seq")
        core = lax.rem(place, CORES)
        first_row = place * tokens
        row_pos = first_row + lax.broadcasted_iota(jnp.int32, (tokens, tokens), 0)
        seg_start = jnp.zeros((tokens, tokens), jnp.int32)
        end = jnp.int32(0)
        for i in range(lengths.shape[0]):
            end = end + lengths[i]
            seg_start = jnp.where(row_pos >= end, end, seg_start)
        near = 1 + 2 * core
        for i, distance in enumerate((0, 2, FAR, near, 4 - near)):
            key_pos = (first_row - distance * tokens) + lax.broadcasted_iota(
                jnp.int32, (tokens, tokens), 1
            )
            allowed = (key_pos >= seg_start) & (key_pos <= row_pos)
            bias[i] = jnp.where(allowed, 0.0, NEG)

    @pl.when(step == 0)
    def _():
        dk_t[...] = jnp.zeros_like(dk_t)
        dv_t[...] = jnp.zeros_like(dv_t)
        for ref, start, size, at in pieces:
            keys[at : at + size] = ref[start : start + size, :HD]
            values[at : at + size] = ref[start : start + size, HD:]

    for g in range(heads):
        q_all[g * tokens : (g + 1) * tokens] = q_ref[:, g * HD : (g + 1) * HD]
        do_all[g * tokens : (g + 1) * tokens] = do_ref[:, g * HD : (g + 1) * HD]

    q = q_all[...]
    top = None
    chunks = [slice(at, at + CHUNK) for at in range(0, total_keys, CHUNK)]
    for at in chunks:
        s = dot_nt(q, keys[at])
        if at.start >= prompt_len:
            which = (at.start - prompt_len) // tokens
            s = jnp.concatenate(
                [s[g * tokens : (g + 1) * tokens] + bias[which] for g in range(heads)], axis=0
            )
        s_buf[:, at] = s
        for col in range(0, CHUNK, HD):
            part = s[:, col : col + HD]
            top = part if top is None else jnp.maximum(top, part)
    top = jnp.max(top, axis=1, keepdims=True) * exp_scale

    total = jnp.zeros((rows, HD), F32)
    out = jnp.zeros((rows, HD), F32)
    for at in chunks:
        p = jnp.exp2(s_buf[:, at] * exp_scale - top)
        for col in range(0, CHUNK, HD):
            total = total + p[:, col : col + HD]
        p = p.astype(BF16)
        p_buf[:, at] = p
        out = out + dot(p, values[at])
    inverse = 1.0 / jnp.sum(total, axis=1, keepdims=True)
    out = (out * inverse).astype(BF16)
    o_all[...] = out
    cot = (do_all[...].astype(F32) * inverse).astype(BF16)
    delta = jnp.sum(cot.astype(F32) * out.astype(F32), axis=1, keepdims=True)
    cot_t = cot.T
    q_t = q.T
    dq = jnp.zeros((rows, HD), F32)
    for at in chunks:
        p = p_buf[:, at]
        dp = dot_nt(cot, values[at])
        ds = (p.astype(F32) * (dp - delta)).astype(BF16)
        dq = dq + dot(ds, keys[at])
        dv_t[:, at] += dot(cot_t, p)
        dk_t[:, at] += dot(q_t, ds)
    dq_all[...] = (dq * score_scale).astype(BF16)
    for g in range(heads):
        o_ref[:, g * HD : (g + 1) * HD] = o_all[g * tokens : (g + 1) * tokens]
        dq_ref[:, g * HD : (g + 1) * HD] = dq_all[g * tokens : (g + 1) * tokens]

    targets = [
        (kept_ref, 0, half, 0),
        (back_ref, 0, half, half),
        (kept_ref, half + 2 * tokens, tokens, resp_at[0]),
        (kept_ref, half, tokens, resp_at[1]),
        (kept_ref, half + tokens, tokens, resp_at[2]),
        (back_ref, half, tokens, resp_at[3]),
        (back_ref, half + tokens, tokens, resp_at[4]),
    ]

    @pl.when(step == last)
    def _():
        for ref, start, size, at in targets:
            grad_k = (dk_t[:, at : at + size] * score_scale).T
            grad_v = dv_t[:, at : at + size].T
            ref[start : start + size, :HD] = grad_k.astype(ref.dtype)
            ref[start : start + size, HD:] = grad_v.astype(ref.dtype)


def attention(lengths, resp_q, grad_out, sent, got, own, far):
    tokens = resp_q.shape[0]
    half = sent.shape[0] - 2 * tokens
    total_keys = 2 * half + 5 * tokens
    kv_heads = sent.shape[1] // (2 * HD)
    heads = HEADS_PER_STEP
    steps = resp_q.shape[1] // HD // kv_heads // heads
    rows = heads * tokens
    head_spec = pl.BlockSpec((tokens, heads * HD), lambda n, g: (0, n * steps + g))

    def kv_spec(size):
        return pl.BlockSpec((size, 2 * HD), lambda n, g: (0, n))

    pairs = rows * kv_heads * steps * total_keys
    return pl.pallas_call(
        functools.partial(attention_kernel, tokens),
        grid=(kv_heads, steps),
        in_specs=[
            pl.BlockSpec(memory_space=pltpu.SMEM),
            head_spec,
            head_spec,
            kv_spec(sent.shape[0]),
            kv_spec(got.shape[0]),
            kv_spec(tokens),
            kv_spec(tokens),
        ],
        out_specs=[head_spec, head_spec, kv_spec(half + 3 * tokens), kv_spec(half + 2 * tokens)],
        out_shape=[
            jax.ShapeDtypeStruct(resp_q.shape, BF16),
            jax.ShapeDtypeStruct(resp_q.shape, BF16),
            jax.ShapeDtypeStruct((half + 3 * tokens, sent.shape[1]), F32),
            jax.ShapeDtypeStruct((half + 2 * tokens, sent.shape[1]), BF16),
        ],
        scratch_shapes=[
            pltpu.VMEM((5, tokens, tokens), F32),
            pltpu.VMEM((total_keys, HD), BF16),
            pltpu.VMEM((total_keys, HD), BF16),
            pltpu.VMEM((rows, HD), BF16),
            pltpu.VMEM((rows, HD), BF16),
            pltpu.VMEM((rows, total_keys), F32),
            pltpu.VMEM((rows, total_keys), BF16),
            pltpu.VMEM((rows, HD), BF16),
            pltpu.VMEM((rows, HD), BF16),
            pltpu.VMEM((HD, total_keys), F32),
            pltpu.VMEM((HD, total_keys), F32),
        ],
        compiler_params=pltpu.CompilerParams(vmem_limit_bytes=56 * 1024 * 1024),
        cost_estimate=pl.CostEstimate(
            flops=12 * HD * pairs, bytes_accessed=8 * resp_q.size, transcendentals=pairs
        ),
        name="attention",
    )(lengths, resp_q, grad_out, sent, got, own, far)


def swap_heads(array, by):
    devices = lax.axis_size("head")
    return lax.ppermute(array, "head", [(i, i ^ by) for i in range(devices)])


def swap_chips(array, by):
    devices = lax.axis_size("seq")
    return lax.ppermute(array, "seq", [(i, i ^ (by * CORES)) for i in range(devices)])


def swap_cores(array):
    devices = lax.axis_size("seq")
    return lax.ppermute(array, "seq", [(i, i ^ 1) for i in range(devices)])


def shift_chips(array, by):
    devices = lax.axis_size("seq")
    by = by * CORES
    return lax.ppermute(array, "seq", [(i, i + by) for i in range(devices) if 0 <= i + by < devices])


def shards(prompt_k, prompt_v, resp_q, resp_k, resp_v, grad_out, resp_lengths):
    tokens, kv_cols = resp_k.shape
    wide = 2 * kv_cols
    groups = lax.axis_size("head")
    chips = lax.axis_size("seq") // CORES
    block = prompt_k.shape[0]
    core = lax.rem(lax.axis_index("seq"), CORES)

    *pieces, own = local_call(
        pack_kernel,
        "pack",
        [prompt_k, prompt_v, resp_k, resp_v],
        [((block, wide), BF16)] * groups + [((tokens, wide), BF16)],
    )
    pieces = [pieces[0]] + [swap_heads(pieces[k], k) for k in range(1, groups)]
    near = shift_chips(own, 1)
    far = shift_chips(own, 2)
    mine = jnp.concatenate(pieces, axis=0)
    parts = [mine] + [swap_chips(mine, k) for k in range(1, chips)]
    chosen = jnp.where(core == 1, far, own)
    sent = jnp.concatenate(parts + [near, chosen], axis=0)
    got = swap_cores(sent)

    resp_out, grad_q, kept, back = attention(
        resp_lengths, resp_q, grad_out, sent, got, own, far
    )

    back = swap_cores(back)
    share = groups * block
    *parts, near, far, own = local_call(
        functools.partial(merge_kernel, chips, tokens),
        "merge",
        [kept, back],
        [((share, wide), BF16)] * chips
        + [((tokens, wide), BF16)] * 2
        + [((tokens, wide), F32)],
    )
    parts = [parts[0]] + [swap_chips(parts[k], k) for k in range(1, chips)]
    near = shift_chips(near, -1)
    far = shift_chips(far, -2)
    pieces = local_call(
        functools.partial(sum_kernel, chips),
        "sum_chips",
        parts,
        [((block, wide), BF16)] * groups,
        [pltpu.VMEM((share, wide), F32)],
    )
    pieces = [pieces[0]] + [swap_heads(pieces[k], k) for k in range(1, groups)]
    grad_k_resp, grad_v_resp = local_call(
        finish_resp_kernel, "finish_resp", [own, near, far], [((tokens, kv_cols), BF16)] * 2
    )
    grad_k_prompt, grad_v_prompt = local_call(
        finish_prompt_kernel, "finish_prompt", pieces, [(prompt_k.shape, BF16)] * 2
    )
    return (resp_out, grad_q, grad_k_resp, grad_v_resp, grad_k_prompt, grad_v_prompt)


def solution(mesh):
    placed = (
        P(("seq", "head"), None),
        P(("seq", "head"), None),
        P("seq", "head"),
        P("seq", "head"),
        P("seq", "head"),
        P("seq", "head"),
        P(),
    )
    return jax.shard_map(
        shards,
        mesh=mesh,
        in_specs=placed,
        out_specs=(
            P("seq", "head"),
            P("seq", "head"),
            P("seq", "head"),
            P("seq", "head"),
            P(("seq", "head"), None),
            P(("seq", "head"), None),
        ),
        check_vma=False,
    )
```

time: 163 us -> 129 us (0.79)
  waiting for transfers between devices: 60.2 us -> 34.1 us
  between operations: 14.4 us -> 0.84 us
  blocking collectives: 11.7 us -> 0 us
  starting transfers between devices: 19.9 us -> 30.2 us
  Pallas kernels: 46.2 us -> 54.6 us
  other arithmetic: 1.74 us -> 0.07 us
    reduce_scatter x1 -> x0, waiting for transfers between devices: 30.2 us -> none  [shards(): lax.psum_scatter(grad_prompt, 'seq', scatter_dimension=0, tiled=True)]
    ppermute x8 -> x18, waiting for transfers between devices: 11.8 us -> 34.1 us  [the longest x6 20.1 us: swap_chips(): lax.ppermute(array, 'seq', [(i, i ^ by * CORES) for i in range(devices)])]
    ppermute x8 -> x18, starting transfers between devices: 15.2 us -> 30.2 us  [the longest x4 11.6 us: shift_chips(): lax.ppermute(array, 'seq', [(i, i + by) for i in range(devices) if 0 <= i...]
    all_gather x1 -> x0, waiting for transfers between devices: 14.1 us -> none  [shards(): prompt_kv = lax.all_gather(prompt_kv, 'seq', axis=0, tiled=True)]
    all_to_all x1 -> x0, blocking collectives: 11.7 us -> none  [shards(): lax.all_to_all(prompt_kv, 'head', split_axis=1, concat_axis=0, tiled=True)]
    pallas_call x1 -> x6, Pallas kernels: 46.2 us -> 54.6 us  [the longest x1 52.7 us: attention(): pl.pallas_call(functools.partial(attention_kernel, tokens), grid=(kv_head...]
    unnamed x28 -> x25, local copies, waits for them, and re-layouts: 1.82 us -> 6.55 us
    all_to_all x1 -> x0, starting transfers between devices: 4.59 us -> none  [shards(): lax.all_to_all(grad_prompt, 'head', split_axis=0, concat_axis=1, tiled=True)]
  transfers between devices with their start and end apart: 11 -> 18, of which waited for: 7 -> 10; matrix products, arithmetic and copies ran while one was open for 2% -> 0% of each run, Pallas kernels for 0% -> 1%
where the time goes in v1:
time: 129 us; the launch traced here: 126 us
  Pallas kernels  54.6 us (42%)
  waiting for transfers between devices  34.1 us (26%)
  starting transfers between devices  30.2 us (23%)
  local copies, waits for them, and re-layouts  6.55 us (5%)
    pallas_call x1, Pallas kernels, attention(): pl.pallas_call(functools.partial(attention_kernel, tokens), grid=(kv_head...  52.7 us
    ppermute x6, waiting for transfers between devices, swap_chips(): lax.ppermute(array, 'seq', [(i, i ^ by * CORES) for i in range(devices)])  20.1 us
    ppermute x4, starting transfers between devices, shift_chips(): lax.ppermute(array, 'seq', [(i, i + by) for i in range(devices) if 0 <= i...  11.6 us
    ppermute x6, starting transfers between devices, swap_chips(): lax.ppermute(array, 'seq', [(i, i ^ by * CORES) for i in range(devices)])  9.39 us
    ppermute x6, starting transfers between devices, swap_heads(): return lax.ppermute(array, 'head', [(i, i ^ by) for i in range(devices)])  8.9 us
    ppermute x6, waiting for transfers between devices, swap_heads(): return lax.ppermute(array, 'head', [(i, i ^ by) for i in range(devices)])  8.23 us
    unnamed x25, local copies, waits for them, and re-layouts  6.55 us
    ppermute x2, waiting for transfers between devices, swap_cores(): return lax.ppermute(array, 'seq', [(i, i ^ 1) for i in range(devices)])  5.75 us
  transfers between devices with their start and end apart: 18, of which 10 were waited for; matrix products, arithmetic and copies ran while one was open for 0% of the time, Pallas kernels for 1%

profile of v1, /device:TPU:6, one launch (start us, length us, event | category | flops | bytes accessed | tf_op | source)
XLA Modules:
  0.0 126.3 jit_solution(6547106209185423305)
XLA Ops:
  0.6 0.9 copy-done.2
  1.5 0.9 copy-done.3
  2.4 0.9 copy-done.4
  3.3 0.9 copy-done.5
  4.3 1.6 %collective-permute-start = (bf16[40,512]{1,0:T(8,128)(2,1)S(1)}, bf16[40,512]{1,0:T(8,128)(2,1)S(1)}, u32[]{:S(2)}, u32[]{:S(2)}) collective-permute-start(bf16[40,512]{1,0:T(8,128)(2,1)S(1)} %get-tuple-element.31), channel_id=1, source_target_pairs={{0,1},{1,0},{2,3},{3,2},{4,5},{5,4},{6,7},{7,6},{8,9},{9,8},{10,11... | collective-permute-start | bytes 122888 | tf_op jit(solution)/shard_map/ppermute | solution.py:283
  6.0 2.6 %collective-permute-start.1 = (bf16[40,512]{1,0:T(8,128)(2,1)S(1)}, bf16[40,512]{1,0:T(8,128)(2,1)S(1)}, u32[]{:S(2)}, u32[]{:S(2)}) collective-permute-start(bf16[40,512]{1,0:T(8,128)(2,1)S(1)} %get-tuple-element.32), channel_id=1, source_target_pairs={{0,2},{1,3},{2,0},{3,1},{4,6},{5,7},{6,4},{7,5},{8,10},{9,11},{10,... | collective-permute-start | bytes 122888 | tf_op jit(solution)/shard_map/ppermute | solution.py:283
  8.5 0.2 collective-permute-start.2
  8.8 2.8 %collective-permute-done.1 = bf16[40,512]{1,0:T(8,128)(2,1)S(1)} collective-permute-done((bf16[40,512]{1,0:T(8,128)(2,1)S(1)}, bf16[40,512]{1,0:T(8,128)(2,1)S(1)}, u32[]{:S(2)}, u32[]{:S(2)}) %collective-permute-start.1) | collective-permute-done | bytes 40992 | tf_op jit(solution)/shard_map/ppermute | solution.py:283
  11.6 2.7 %collective-permute-done.2 = bf16[40,512]{1,0:T(8,128)(2,1)S(1)} collective-permute-done((bf16[40,512]{1,0:T(8,128)(2,1)S(1)}, bf16[40,512]{1,0:T(8,128)(2,1)S(1)}, u32[]{:S(2)}, u32[]{:S(2)}) %collective-permute-start.2) | collective-permute-done | bytes 40992 | tf_op jit(solution)/shard_map/ppermute | solution.py:283
  14.3 0.5 collective-permute-start.3
  14.9 0.5 collective-permute-start.4
  15.4 1.3 %collective-permute-start.7 = (bf16[256,512]{1,0:T(8,128)(2,1)S(1)}, bf16[256,512]{1,0:T(8,128)(2,1)S(1)}, u32[]{:S(2)}, u32[]{:S(2)}) collective-permute-start(bf16[256,512]{1,0:T(8,128)(2,1)S(1)} %get-tuple-element.34.own_ref), channel_id=1, source_target_pairs={{0,16},{4,20},{8,24},{12,28},{1,17},{5,21},{9,25},{13,29},{2,18},{... | collective-permute-start | bytes 786440 | tf_op jit(solution)/shard_map/ppermute | solution.py:299
  16.7 1.3 %collective-permute-start.6 = (bf16[256,512]{1,0:T(8,128)(2,1)S(1)}, bf16[256,512]{1,0:T(8,128)(2,1)S(1)}, u32[]{:S(2)}, u32[]{:S(2)}) collective-permute-start(bf16[256,512]{1,0:T(8,128)(2,1)S(1)} %get-tuple-element.34.own_ref), channel_id=1, source_target_pairs={{0,8},{4,12},{8,16},{12,20},{16,24},{20,28},{1,9},{5,13},{9,17},{1... | collective-permute-start | bytes 786440 | tf_op jit(solution)/shard_map/ppermute | solution.py:299
  18.0 4.8 %collective-permute-start.5 = (bf16[160,512]{1,0:T(8,128)(2,1)S(1)}, bf16[160,512]{1,0:T(8,128)(2,1)S(1)}, u32[]{:S(2)}, u32[]{:S(2)}) collective-permute-start(bf16[160,512]{1,0:T(8,128)(2,1)S(1)} %get-tuple-element.54), channel_id=1, source_target_pairs={{0,24},{4,28},{8,16},{12,20},{16,8},{20,12},{24,0},{28,4},{1,25},{... | collective-permute-start | bytes 491528 | tf_op jit(solution)/shard_map/ppermute | solution.py:288
  22.8 6.9 %collective-permute-done.5 = bf16[160,512]{1,0:T(8,128)(2,1)S(1)} collective-permute-done((bf16[160,512]{1,0:T(8,128)(2,1)S(1)}, bf16[160,512]{1,0:T(8,128)(2,1)S(1)}, u32[]{:S(2)}, u32[]{:S(2)}) %collective-permute-start.5) | collective-permute-done | bytes 163872 | tf_op jit(solution)/shard_map/ppermute | solution.py:288
  30.0 2.8 %collective-permute-done.8.got_ref = bf16[1152,512]{1,0:T(8,128)(2,1)S(1)} collective-permute-done((bf16[1152,512]{1,0:T(8,128)(2,1)S(1)}, bf16[1152,512]{1,0:T(8,128)(2,1)S(1)}, u32[]{:S(2)}, u32[]{:S(2)}) %collective-permute-start.8) | collective-permute-done | bytes 1179680 | tf_op jit(solution)/shard_map/ppermute | solution.py:293
  32.9 1.1 copy-done.8
  33.9 52.7 %attention.1 = (bf16[256,2048]{1,0:T(8,128)(2,1)}, bf16[256,2048]{1,0:T(8,128)(2,1)}, f32[1408,512]{1,0:T(8,128)}, bf16[1152,512]{1,0:T(8,128)(2,1)}) custom-call(s32[8]{0:T(128)} %lengths.1, bf16[256,2048]{1,0:T(8,128)(2,1)} %q_ref.1, bf16[256,2048]{1,0:T(8,128)(2,1)} %do_ref.1, bf16[1152,512]{1,0:T(8,128)(2,1)} %copy-done.7, bf16[1152,512]{1,0:T(8,128)(2,1)} %copy-done.8, ...), custom_call_target="tpu_custom_call" | custom-call | flops 16106127360 | bytes 4194304 | tf_op jit(solution)/shard_map/attention/pallas_call | solution.py:241
  86.8 2.9 %collective-permute-done.9.got_ref = bf16[1152,512]{1,0:T(8,128)(2,1)S(1)} collective-permute-done((bf16[1152,512]{1,0:T(8,128)(2,1)}, bf16[1152,512]{1,0:T(8,128)(2,1)S(1)}, u32[]{:S(2)}, u32[]{:S(2)}) %collective-permute-start.9) | collective-permute-done | bytes 1179680 | tf_op jit(solution)/shard_map/ppermute | solution.py:293
  89.7 1.8 %copy-done = f32[1408,512]{1,0:T(8,128)S(1)} copy-done((f32[1408,512]{1,0:T(8,128)S(1)}, f32[1408,512]{1,0:T(8,128)}, u32[]{:S(2)}) %copy-start) | copy-done | bytes 2883608
  91.5 0.3 merge.1
  91.8 7.6 %collective-permute-start.10 = (bf16[256,512]{1,0:T(8,128)(2,1)S(1)}, bf16[256,512]{1,0:T(8,128)(2,1)S(1)}, u32[]{:S(2)}, u32[]{:S(2)}) collective-permute-start(bf16[256,512]{1,0:T(8,128)(2,1)S(1)} %get-tuple-element.40), channel_id=1, source_target_pairs={{8,0},{12,4},{16,8},{20,12},{24,16},{28,20},{9,1},{13,5},{17,9},{2... | collective-permute-start | bytes 786440 | tf_op jit(solution)/shard_map/ppermute | solution.py:299
  99.4 1.4 %collective-permute-start.11 = (bf16[256,512]{1,0:T(8,128)(2,1)S(1)}, bf16[256,512]{1,0:T(8,128)(2,1)S(1)}, u32[]{:S(2)}, u32[]{:S(2)}) collective-permute-start(bf16[256,512]{1,0:T(8,128)(2,1)S(1)} %get-tuple-element.41), channel_id=1, source_target_pairs={{16,0},{20,4},{24,8},{28,12},{17,1},{21,5},{25,9},{29,13},{18,2},{... | collective-permute-start | bytes 786440 | tf_op jit(solution)/shard_map/ppermute | solution.py:299
  101.0 3.4 %collective-permute-start.14 = (bf16[160,512]{1,0:T(8,128)(2,1)S(1)}, bf16[160,512]{1,0:T(8,128)(2,1)S(1)}, u32[]{:S(2)}, u32[]{:S(2)}) collective-permute-start(bf16[160,512]{1,0:T(8,128)(2,1)S(1)} %get-tuple-element.47), channel_id=1, source_target_pairs={{0,24},{4,28},{8,16},{12,20},{16,8},{20,12},{24,0},{28,4},{1,25},{... | collective-permute-start | bytes 491528 | tf_op jit(solution)/shard_map/ppermute | solution.py:288
  104.4 5.6 %collective-permute-done.12.refs_1_ = bf16[160,512]{1,0:T(8,128)(2,1)S(1)} collective-permute-done((bf16[160,512]{1,0:T(8,128)(2,1)S(1)}, bf16[160,512]{1,0:T(8,128)(2,1)S(1)}, u32[]{:S(2)}, u32[]{:S(2)}) %collective-permute-start.12) | collective-permute-done | bytes 163872 | tf_op jit(solution)/shard_map/ppermute | solution.py:288
  110.0 7.6 %collective-permute-done.13.refs_2_ = bf16[160,512]{1,0:T(8,128)(2,1)S(1)} collective-permute-done((bf16[160,512]{1,0:T(8,128)(2,1)S(1)}, bf16[160,512]{1,0:T(8,128)(2,1)S(1)}, u32[]{:S(2)}, u32[]{:S(2)}) %collective-permute-start.13) | collective-permute-done | bytes 163872 | tf_op jit(solution)/shard_map/ppermute | solution.py:288
  117.7 1.2 collective-permute-start.16
  119.0 3.2 %collective-permute-start.17 = (bf16[40,512]{1,0:T(8,128)(2,1)S(1)}, bf16[40,512]{1,0:T(8,128)(2,1)S(1)}, u32[]{:S(2)}, u32[]{:S(2)}) collective-permute-start(bf16[40,512]{1,0:T(8,128)(2,1)S(1)} %get-tuple-element.51), channel_id=1, source_target_pairs={{0,3},{1,2},{2,1},{3,0},{4,7},{5,6},{6,5},{7,4},{8,11},{9,10},{10,... | collective-permute-start | bytes 122888 | tf_op jit(solution)/shard_map/ppermute | solution.py:283
  122.2 1.4 %collective-permute-done.16.refs_2_ = bf16[40,512]{1,0:T(8,128)(2,1)S(1)} collective-permute-done((bf16[40,512]{1,0:T(8,128)(2,1)S(1)}, bf16[40,512]{1,0:T(8,128)(2,1)S(1)}, u32[]{:S(2)}, u32[]{:S(2)}) %collective-permute-start.16) | collective-permute-done | bytes 40992 | tf_op jit(solution)/shard_map/ppermute | solution.py:283
  123.6 1.2 collective-permute-done.17.refs_3_
  124.8 0.7 finish_prompt.1
  125.5 0.8 finish_resp.1
  (37 shorter events, 0.9 us)
Async XLA Ops:
  0.6 0.9 copy-start.2
  1.5 0.9 copy-start.3
  2.4 0.9 copy-start.4
  3.3 0.9 copy-start.5
  4.3 25.6 %copy-start.1 = (bf16[256,512]{1,0:T(8,128)(2,1)}, bf16[256,512]{1,0:T(8,128)(2,1)S(1)}, u32[]{:S(2)}) copy-start(bf16[256,512]{1,0:T(8,128)(2,1)S(1)} %get-tuple-element.34.own_ref) | copy-start | bytes 786436
  4.3 4.5 %collective-permute-start = (bf16[40,512]{1,0:T(8,128)(2,1)S(1)}, bf16[40,512]{1,0:T(8,128)(2,1)S(1)}, u32[]{:S(2)}, u32[]{:S(2)}) collective-permute-start(bf16[40,512]{1,0:T(8,128)(2,1)S(1)} %get-tuple-element.31), channel_id=1, source_target_pairs={{0,1},{1,0},{2,3},{3,2},{4,5},{5,4},{6,7},{7,6},{8,9},{9,8},{10,11... | collective-permute-start | bytes 122888 | tf_op jit(solution)/shard_map/ppermute | solution.py:283
  6.0 5.7 %collective-permute-start.1 = (bf16[40,512]{1,0:T(8,128)(2,1)S(1)}, bf16[40,512]{1,0:T(8,128)(2,1)S(1)}, u32[]{:S(2)}, u32[]{:S(2)}) collective-permute-start(bf16[40,512]{1,0:T(8,128)(2,1)S(1)} %get-tuple-element.32), channel_id=1, source_target_pairs={{0,2},{1,3},{2,0},{3,1},{4,6},{5,7},{6,4},{7,5},{8,10},{9,11},{10,... | collective-permute-start | bytes 122888 | tf_op jit(solution)/shard_map/ppermute | solution.py:283
  8.5 5.8 %collective-permute-start.2 = (bf16[40,512]{1,0:T(8,128)(2,1)S(1)}, bf16[40,512]{1,0:T(8,128)(2,1)S(1)}, u32[]{:S(2)}, u32[]{:S(2)}) collective-permute-start(bf16[40,512]{1,0:T(8,128)(2,1)S(1)} %get-tuple-element.33), channel_id=1, source_target_pairs={{0,3},{1,2},{2,1},{3,0},{4,7},{5,6},{6,5},{7,4},{8,11},{9,10},{10,... | collective-permute-start | bytes 122888 | tf_op jit(solution)/shard_map/ppermute | solution.py:283
  14.3 8.4 %collective-permute-start.3 = (bf16[160,512]{1,0:T(8,128)(2,1)S(1)}, bf16[160,512]{1,0:T(8,128)(2,1)S(1)}, u32[]{:S(2)}, u32[]{:S(2)}) collective-permute-start(bf16[160,512]{1,0:T(8,128)(2,1)S(1)} %get-tuple-element.54), channel_id=1, source_target_pairs={{0,8},{4,12},{8,0},{12,4},{16,24},{20,28},{24,16},{28,20},{1,9},{5... | collective-permute-start | bytes 491528 | tf_op jit(solution)/shard_map/ppermute | solution.py:288
  14.9 7.9 %collective-permute-start.4 = (bf16[160,512]{1,0:T(8,128)(2,1)S(1)}, bf16[160,512]{1,0:T(8,128)(2,1)S(1)}, u32[]{:S(2)}, u32[]{:S(2)}) collective-permute-start(bf16[160,512]{1,0:T(8,128)(2,1)S(1)} %get-tuple-element.54), channel_id=1, source_target_pairs={{0,16},{4,20},{8,24},{12,28},{16,0},{20,4},{24,8},{28,12},{1,17},{... | collective-permute-start | bytes 491528 | tf_op jit(solution)/shard_map/ppermute | solution.py:288
  15.4 14.4 %collective-permute-start.7 = (bf16[256,512]{1,0:T(8,128)(2,1)S(1)}, bf16[256,512]{1,0:T(8,128)(2,1)S(1)}, u32[]{:S(2)}, u32[]{:S(2)}) collective-permute-start(bf16[256,512]{1,0:T(8,128)(2,1)S(1)} %get-tuple-element.34.own_ref), channel_id=1, source_target_pairs={{0,16},{4,20},{8,24},{12,28},{1,17},{5,21},{9,25},{13,29},{2,18},{... | collective-permute-start | bytes 786440 | tf_op jit(solution)/shard_map/ppermute | solution.py:299
  16.7 13.1 %collective-permute-start.6 = (bf16[256,512]{1,0:T(8,128)(2,1)S(1)}, bf16[256,512]{1,0:T(8,128)(2,1)S(1)}, u32[]{:S(2)}, u32[]{:S(2)}) collective-permute-start(bf16[256,512]{1,0:T(8,128)(2,1)S(1)} %get-tuple-element.34.own_ref), channel_id=1, source_target_pairs={{0,8},{4,12},{8,16},{12,20},{16,24},{20,28},{1,9},{5,13},{9,17},{1... | collective-permute-start | bytes 786440 | tf_op jit(solution)/shard_map/ppermute | solution.py:299
  18.0 11.8 %collective-permute-start.5 = (bf16[160,512]{1,0:T(8,128)(2,1)S(1)}, bf16[160,512]{1,0:T(8,128)(2,1)S(1)}, u32[]{:S(2)}, u32[]{:S(2)}) collective-permute-start(bf16[160,512]{1,0:T(8,128)(2,1)S(1)} %get-tuple-element.54), channel_id=1, source_target_pairs={{0,24},{4,28},{8,16},{12,20},{16,8},{20,12},{24,0},{28,4},{1,25},{... | collective-permute-start | bytes 491528 | tf_op jit(solution)/shard_map/ppermute | solution.py:288
  29.8 3.0 %copy-start.6 = (bf16[256,512]{1,0:T(8,128)(2,1)}, bf16[256,512]{1,0:T(8,128)(2,1)S(1)}, u32[]{:S(2)}) copy-start(bf16[256,512]{1,0:T(8,128)(2,1)S(1)} %collective-permute-done.7.far_ref) | copy-start | bytes 786436
  29.9 2.9 %copy-start.7 = (bf16[1152,512]{1,0:T(8,128)(2,1)}, bf16[1152,512]{1,0:T(8,128)(2,1)S(1)}, u32[]{:S(2)}) copy-start(bf16[1152,512]{1,0:T(8,128)(2,1)S(1)} %select_dynamic-update-slice_fusion.sent_ref) | copy-start | bytes 3538948
  29.9 2.9 %collective-permute-start.8 = (bf16[1152,512]{1,0:T(8,128)(2,1)S(1)}, bf16[1152,512]{1,0:T(8,128)(2,1)S(1)}, u32[]{:S(2)}, u32[]{:S(2)}) collective-permute-start(bf16[1152,512]{1,0:T(8,128)(2,1)S(1)} %select_dynamic-update-slice_fusion.sent_ref), channel_id=1, source_target_pairs={{0,4},{4,0},{8,12},{12,8},{16,20},{20,16},{24,28},{28,24},{1,5},{5... | collective-permute-start | bytes 3538952 | tf_op jit(solution)/shard_map/ppermute | solution.py:293
  32.9 1.1 copy-start.8
  86.6 3.1 %collective-permute-start.9 = (bf16[1152,512]{1,0:T(8,128)(2,1)}, bf16[1152,512]{1,0:T(8,128)(2,1)S(1)}, u32[]{:S(2)}, u32[]{:S(2)}) collective-permute-start(bf16[1152,512]{1,0:T(8,128)(2,1)} %get-tuple-element.38), channel_id=1, source_target_pairs={{0,4},{4,0},{8,12},{12,8},{16,20},{20,16},{24,28},{28,24},{1,5},{5... | collective-permute-start | bytes 3538952 | tf_op jit(solution)/shard_map/ppermute | solution.py:293
  89.7 1.8 %copy-start = (f32[1408,512]{1,0:T(8,128)S(1)}, f32[1408,512]{1,0:T(8,128)}, u32[]{:S(2)}) copy-start(f32[1408,512]{1,0:T(8,128)} %get-tuple-element.37.kept_ref) | copy-start | bytes 8650756
  91.8 33.7 %collective-permute-start.10 = (bf16[256,512]{1,0:T(8,128)(2,1)S(1)}, bf16[256,512]{1,0:T(8,128)(2,1)S(1)}, u32[]{:S(2)}, u32[]{:S(2)}) collective-permute-start(bf16[256,512]{1,0:T(8,128)(2,1)S(1)} %get-tuple-element.40), channel_id=1, source_target_pairs={{8,0},{12,4},{16,8},{20,12},{24,16},{28,20},{9,1},{13,5},{17,9},{2... | collective-permute-start | bytes 786440 | tf_op jit(solution)/shard_map/ppermute | solution.py:299
  99.4 26.1 %collective-permute-start.11 = (bf16[256,512]{1,0:T(8,128)(2,1)S(1)}, bf16[256,512]{1,0:T(8,128)(2,1)S(1)}, u32[]{:S(2)}, u32[]{:S(2)}) collective-permute-start(bf16[256,512]{1,0:T(8,128)(2,1)S(1)} %get-tuple-element.41), channel_id=1, source_target_pairs={{16,0},{20,4},{24,8},{28,12},{17,1},{21,5},{25,9},{29,13},{18,2},{... | collective-permute-start | bytes 786440 | tf_op jit(solution)/shard_map/ppermute | solution.py:299
  100.8 9.2 %collective-permute-start.12 = (bf16[160,512]{1,0:T(8,128)(2,1)S(1)}, bf16[160,512]{1,0:T(8,128)(2,1)S(1)}, u32[]{:S(2)}, u32[]{:S(2)}) collective-permute-start(bf16[160,512]{1,0:T(8,128)(2,1)S(1)} %get-tuple-element.45), channel_id=1, source_target_pairs={{0,8},{4,12},{8,0},{12,4},{16,24},{20,28},{24,16},{28,20},{1,9},{5... | collective-permute-start | bytes 491528 | tf_op jit(solution)/shard_map/ppermute | solution.py:288
  100.9 16.7 %collective-permute-start.13 = (bf16[160,512]{1,0:T(8,128)(2,1)S(1)}, bf16[160,512]{1,0:T(8,128)(2,1)S(1)}, u32[]{:S(2)}, u32[]{:S(2)}) collective-permute-start(bf16[160,512]{1,0:T(8,128)(2,1)S(1)} %get-tuple-element.46), channel_id=1, source_target_pairs={{0,16},{4,20},{8,24},{12,28},{16,0},{20,4},{24,8},{28,12},{1,17},{... | collective-permute-start | bytes 491528 | tf_op jit(solution)/shard_map/ppermute | solution.py:288
  101.0 16.6 %collective-permute-start.14 = (bf16[160,512]{1,0:T(8,128)(2,1)S(1)}, bf16[160,512]{1,0:T(8,128)(2,1)S(1)}, u32[]{:S(2)}, u32[]{:S(2)}) collective-permute-start(bf16[160,512]{1,0:T(8,128)(2,1)S(1)} %get-tuple-element.47), channel_id=1, source_target_pairs={{0,24},{4,28},{8,16},{12,20},{16,8},{20,12},{24,0},{28,4},{1,25},{... | collective-permute-start | bytes 491528 | tf_op jit(solution)/shard_map/ppermute | solution.py:288
  117.7 4.5 %collective-permute-start.15 = (bf16[40,512]{1,0:T(8,128)(2,1)S(1)}, bf16[40,512]{1,0:T(8,128)(2,1)S(1)}, u32[]{:S(2)}, u32[]{:S(2)}) collective-permute-start(bf16[40,512]{1,0:T(8,128)(2,1)S(1)} %get-tuple-element.49), channel_id=1, source_target_pairs={{0,1},{1,0},{2,3},{3,2},{4,5},{5,4},{6,7},{7,6},{8,9},{9,8},{10,11... | collective-permute-start | bytes 122888 | tf_op jit(solution)/shard_map/ppermute | solution.py:283
  117.7 5.8 %collective-permute-start.16 = (bf16[40,512]{1,0:T(8,128)(2,1)S(1)}, bf16[40,512]{1,0:T(8,128)(2,1)S(1)}, u32[]{:S(2)}, u32[]{:S(2)}) collective-permute-start(bf16[40,512]{1,0:T(8,128)(2,1)S(1)} %get-tuple-element.50), channel_id=1, source_target_pairs={{0,2},{1,3},{2,0},{3,1},{4,6},{5,7},{6,4},{7,5},{8,10},{9,11},{10,... | collective-permute-start | bytes 122888 | tf_op jit(solution)/shard_map/ppermute | solution.py:283
  119.0 5.8 %collective-permute-start.17 = (bf16[40,512]{1,0:T(8,128)(2,1)S(1)}, bf16[40,512]{1,0:T(8,128)(2,1)S(1)}, u32[]{:S(2)}, u32[]{:S(2)}) collective-permute-start(bf16[40,512]{1,0:T(8,128)(2,1)S(1)} %get-tuple-element.51), channel_id=1, source_target_pairs={{0,3},{1,2},{2,1},{3,0},{4,7},{5,6},{6,5},{7,4},{8,11},{9,10},{10,... | collective-permute-start | bytes 122888 | tf_op jit(solution)/shard_map/ppermute | solution.py:283

commit v2 on v1

--- a/solution.py
+++ b/solution.py
@@ -11,20 +11,14 @@
 HD = 128
 CORES = 2
 FAR = 4
-HEADS_PER_STEP = 2
 CHUNK = 256
 NEG = -1e30
-NT = (((1,), (1,)), ((), ()))
 BF16 = jnp.bfloat16
 F32 = jnp.float32
 
 
 def dot(a, b):
     return jnp.dot(a, b, preferred_element_type=F32)
-
-
-def dot_nt(a, b):
-    return lax.dot_general(a, b, NT, preferred_element_type=F32)
 
 
 def whole(count):
@@ -56,6 +50,24 @@
     for n in range(width // (2 * HD)):
         resp[:, 2 * n * HD : (2 * n + 1) * HD] = rk_ref[:, n * HD : (n + 1) * HD]
         resp[:, (2 * n + 1) * HD : (2 * n + 2) * HD] = rv_ref[:, n * HD : (n + 1) * HD]
+
+
+def pack(inputs, groups):
+    def one(array):
+        return pl.BlockSpec(array.shape, lambda i: (0, 0))
+
+    block, tokens = inputs[0].shape[0], inputs[2].shape[0]
+    wide = 2 * inputs[2].shape[1]
+    shapes = [(block, wide)] * groups + [(tokens, wide)]
+    return pl.pallas_call(
+        pack_kernel,
+        grid=(1,),
+        in_specs=[one(array) for array in inputs],
+        out_specs=whole(groups + 1),
+        out_shape=[jax.ShapeDtypeStruct(shape, BF16) for shape in shapes],
+        compiler_params=pltpu.CompilerParams(vmem_limit_bytes=56 * 1024 * 1024),
+        name="pack",
+    )(*inputs)
 
 
 def merge_kernel(parts, rows, kept_ref, got_ref, *outs):
@@ -85,8 +97,8 @@
         out[...] = total[k * share : (k + 1) * share].astype(BF16)
 
 
-def finish_prompt_kernel(*refs):
-    pieces, (gk_ref, gv_ref) = refs[:-2], refs[-2:]
+def finish_kernel(own_ref, one_ref, two_ref, *refs):
+    pieces, (gk_ref, gv_ref, rk_ref, rv_ref) = refs[:-4], refs[-4:]
     head = lax.axis_index("head")
     width = pieces[0].shape[1]
     for k, piece in enumerate(pieces):
@@ -95,29 +107,27 @@
             at = pl.multiple_of(start + n * HD, HD)
             gk_ref[:, pl.ds(at, HD)] = piece[:, 2 * n * HD : (2 * n + 1) * HD]
             gv_ref[:, pl.ds(at, HD)] = piece[:, (2 * n + 1) * HD : (2 * n + 2) * HD]
-
-
-def finish_resp_kernel(own_ref, one_ref, two_ref, gk_ref, gv_ref):
     total = (own_ref[...] + one_ref[...].astype(F32) + two_ref[...].astype(F32)).astype(BF16)
-    for n in range(own_ref.shape[1] // (2 * HD)):
-        gk_ref[:, n * HD : (n + 1) * HD] = total[:, 2 * n * HD : (2 * n + 1) * HD]
-        gv_ref[:, n * HD : (n + 1) * HD] = total[:, (2 * n + 1) * HD : (2 * n + 2) * HD]
+    for n in range(width // (2 * HD)):
+        rk_ref[:, n * HD : (n + 1) * HD] = total[:, 2 * n * HD : (2 * n + 1) * HD]
+        rv_ref[:, n * HD : (n + 1) * HD] = total[:, (2 * n + 1) * HD : (2 * n + 2) * HD]
 
 
 def attention_kernel(
     tokens, lengths, q_ref, do_ref, sent_ref, got_ref, own_ref, far_ref,
     o_ref, dq_ref, kept_ref, back_ref,
-    bias, keys, values, q_all, do_all, s_buf, p_buf, o_all, dq_all, dk_t, dv_t,
+    bias, keys, values, keys_t, values_t, s_buf, p_buf, dk, dv,
 ):
-    heads = q_ref.shape[1] // HD
-    rows = heads * tokens
     total_keys = keys.shape[0]
     prompt_len = total_keys - 5 * tokens
     half = prompt_len // 2
+    head = pl.program_id(0)
     step = pl.program_id(1)
     last = pl.num_programs(1) - 1
     score_scale = 1.0 / math.sqrt(HD)
     exp_scale = score_scale * math.log2(math.e)
+    k_cols = pl.ds(pl.multiple_of(head * 2 * HD, HD), HD)
+    v_cols = pl.ds(pl.multiple_of(head * 2 * HD + HD, HD), HD)
     resp_at = [prompt_len + i * tokens for i in range(6)]
     pieces = [
         (sent_ref, 0, half, 0),
@@ -129,12 +139,12 @@
         (got_ref, half + tokens, tokens, resp_at[4]),
     ]
 
-    @pl.when((step == 0) & (pl.program_id(0) == 0))
+    @pl.when((step == 0) & (head == 0))
     def _():
         place = lax.axis_index("seq")
         core = lax.rem(place, CORES)
         first_row = place * tokens
-        row_pos = first_row + lax.broadcasted_iota(jnp.int32, (tokens, tokens), 0)
+        row_pos = first_row + lax.broadcasted_iota(jnp.int32, (tokens, tokens), 1)
         seg_start = jnp.zeros((tokens, tokens), jnp.int32)
         end = jnp.int32(0)
         for i in range(lengths.shape[0]):
@@ -143,67 +153,59 @@
         near = 1 + 2 * core
         for i, distance in enumerate((0, 2, FAR, near, 4 - near)):
             key_pos = (first_row - distance * tokens) + lax.broadcasted_iota(
-                jnp.int32, (tokens, tokens), 1
+                jnp.int32, (tokens, tokens), 0
             )
             allowed = (key_pos >= seg_start) & (key_pos <= row_pos)
             bias[i] = jnp.where(allowed, 0.0, NEG)
 
     @pl.when(step == 0)
     def _():
-        dk_t[...] = jnp.zeros_like(dk_t)
-        dv_t[...] = jnp.zeros_like(dv_t)
+        dk[...] = jnp.zeros_like(dk)
+        dv[...] = jnp.zeros_like(dv)
         for ref, start, size, at in pieces:
-            keys[at : at + size] = ref[start : start + size, :HD]
-            values[at : at + size] = ref[start : start + size, HD:]
-
-    for g in range(heads):
-        q_all[g * tokens : (g + 1) * tokens] = q_ref[:, g * HD : (g + 1) * HD]
-        do_all[g * tokens : (g + 1) * tokens] = do_ref[:, g * HD : (g + 1) * HD]
-
-    q = q_all[...]
+            k_rows = ref[start : start + size, k_cols]
+            v_rows = ref[start : start + size, v_cols]
+            keys[at : at + size] = k_rows
+            values[at : at + size] = v_rows
+            keys_t[:, at : at + size] = k_rows.T
+            values_t[:, at : at + size] = v_rows.T
+
+    q = q_ref[...]
+    q_t = q.T
+    chunks = [slice(at, at + CHUNK) for at in range(0, total_keys, CHUNK)]
     top = None
-    chunks = [slice(at, at + CHUNK) for at in range(0, total_keys, CHUNK)]
     for at in chunks:
-        s = dot_nt(q, keys[at])
+        s = dot(keys[at], q_t)
         if at.start >= prompt_len:
-            which = (at.start - prompt_len) // tokens
-            s = jnp.concatenate(
-                [s[g * tokens : (g + 1) * tokens] + bias[which] for g in range(heads)], axis=0
-            )
-        s_buf[:, at] = s
-        for col in range(0, CHUNK, HD):
-            part = s[:, col : col + HD]
-            top = part if top is None else jnp.maximum(top, part)
-    top = jnp.max(top, axis=1, keepdims=True) * exp_scale
-
-    total = jnp.zeros((rows, HD), F32)
-    out = jnp.zeros((rows, HD), F32)
+            s = s + bias[(at.start - prompt_len) // tokens]
+        s_buf[at] = s
+        part = jnp.max(s.reshape(CHUNK // 8, 8, tokens), axis=0)
+        top = part if top is None else jnp.maximum(top, part)
+    top = jnp.max(top, axis=0, keepdims=True) * exp_scale
+
+    total = jnp.zeros((8, tokens), F32)
+    out = jnp.zeros((HD, tokens), F32)
     for at in chunks:
-        p = jnp.exp2(s_buf[:, at] * exp_scale - top)
-        for col in range(0, CHUNK, HD):
-            total = total + p[:, col : col + HD]
+        p = jnp.exp2(s_buf[at] * exp_scale - top)
+        total = total + jnp.sum(p.reshape(CHUNK // 8, 8, tokens), axis=0)
         p = p.astype(BF16)
-        p_buf[:, at] = p
-        out = out + dot(p, values[at])
-    inverse = 1.0 / jnp.sum(total, axis=1, keepdims=True)
+        p_buf[at] = p
+        out = out + dot(values_t[:, at], p)
+    inverse = 1.0 / jnp.sum(total, axis=0, keepdims=True)
     out = (out * inverse).astype(BF16)
-    o_all[...] = out
-    cot = (do_all[...].astype(F32) * inverse).astype(BF16)
-    delta = jnp.sum(cot.astype(F32) * out.astype(F32), axis=1, keepdims=True)
-    cot_t = cot.T
-    q_t = q.T
-    dq = jnp.zeros((rows, HD), F32)
+    o_ref[...] = out.T
+    cot_t = (do_ref[...].T.astype(F32) * inverse).astype(BF16)
+    delta = jnp.sum(cot_t.astype(F32) * out.astype(F32), axis=0, keepdims=True)
+    cot = cot_t.T
+    dq = jnp.zeros((HD, tokens), F32)
     for at in chunks:
-        p = p_buf[:, at]
-        dp = dot_nt(cot, values[at])
+        p = p_buf[at]
+        dp = dot(values[at], cot_t)
         ds = (p.astype(F32) * (dp - delta)).astype(BF16)
-        dq = dq + dot(ds, keys[at])
-        dv_t[:, at] += dot(cot_t, p)
-        dk_t[:, at] += dot(q_t, ds)
-    dq_all[...] = (dq * score_scale).astype(BF16)
-    for g in range(heads):
-        o_ref[:, g * HD : (g + 1) * HD] = o_all[g * tokens : (g + 1) * tokens]
-        dq_ref[:, g * HD : (g + 1) * HD] = dq_all[g * tokens : (g + 1) * tokens]
+        dq = dq + dot(keys_t[:, at], ds)
+        dv[at] += dot(p, cot)
+        dk[at] += dot(ds, q)
+    dq_ref[...] = (dq * score_scale).T.astype(BF16)
 
     targets = [
         (kept_ref, 0, half, 0),
@@ -218,10 +220,8 @@
     @pl.when(step == last)
     def _():
         for ref, start, size, at in targets:
-            grad_k = (dk_t[:, at : at + size] * score_scale).T
-            grad_v = dv_t[:, at : at + size].T
-            ref[start : start + size, :HD] = grad_k.astype(ref.dtype)
-            ref[start : start + size, HD:] = grad_v.astype(ref.dtype)
+            ref[start : start + size, k_cols] = (dk[at : at + size] * score_scale).astype(ref.dtype)
+            ref[start : start + size, v_cols] = dv[at : at + size].astype(ref.dtype)
 
 
 def attention(lengths, resp_q, grad_out, sent, got, own, far):
@@ -229,28 +229,14 @@
     half = sent.shape[0] - 2 * tokens
     total_keys = 2 * half + 5 * tokens
     kv_heads = sent.shape[1] // (2 * HD)
-    heads = HEADS_PER_STEP
-    steps = resp_q.shape[1] // HD // kv_heads // heads
-    rows = heads * tokens
-    head_spec = pl.BlockSpec((tokens, heads * HD), lambda n, g: (0, n * steps + g))
-
-    def kv_spec(size):
-        return pl.BlockSpec((size, 2 * HD), lambda n, g: (0, n))
-
-    pairs = rows * kv_heads * steps * total_keys
+    steps = resp_q.shape[1] // HD // kv_heads
+    head_spec = pl.BlockSpec((tokens, HD), lambda n, g: (0, n * steps + g))
+    pairs = tokens * kv_heads * steps * total_keys
     return pl.pallas_call(
         functools.partial(attention_kernel, tokens),
         grid=(kv_heads, steps),
-        in_specs=[
-            pl.BlockSpec(memory_space=pltpu.SMEM),
-            head_spec,
-            head_spec,
-            kv_spec(sent.shape[0]),
-            kv_spec(got.shape[0]),
-            kv_spec(tokens),
-            kv_spec(tokens),
-        ],
-        out_specs=[head_spec, head_spec, kv_spec(half + 3 * tokens), kv_spec(half + 2 * tokens)],
+        in_specs=[pl.BlockSpec(memory_space=pltpu.SMEM), head_spec, head_spec] + whole(4),
+        out_specs=[head_spec, head_spec] + whole(2),
         out_shape=[
             jax.ShapeDtypeStruct(resp_q.shape, BF16),
             jax.ShapeDtypeStruct(resp_q.shape, BF16),
@@ -261,16 +247,14 @@
             pltpu.VMEM((5, tokens, tokens), F32),
             pltpu.VMEM((total_keys, HD), BF16),
             pltpu.VMEM((total_keys, HD), BF16),
-            pltpu.VMEM((rows, HD), BF16),
-            pltpu.VMEM((rows, HD), BF16),
-            pltpu.VMEM((rows, total_keys), F32),
-            pltpu.VMEM((rows, total_keys), BF16),
-            pltpu.VMEM((rows, HD), BF16),
-            pltpu.VMEM((rows, HD), BF16),
-            pltpu.VMEM((HD, total_keys), F32),
-            pltpu.VMEM((HD, total_keys), F32),
+            pltpu.VMEM((HD, total_keys), BF16),
+            pltpu.VMEM((HD, total_keys), BF16),
+            pltpu.VMEM((total_keys, tokens), F32),
+            pltpu.VMEM((total_keys, tokens), BF16),
+            pltpu.VMEM((total_keys, HD), F32),
+            pltpu.VMEM((total_keys, HD), F32),
         ],
-        compiler_params=pltpu.CompilerParams(vmem_limit_bytes=56 * 1024 * 1024),
+        compiler_params=pltpu.CompilerParams(vmem_limit_bytes=44 * 1024 * 1024),
         cost_estimate=pl.CostEstimate(
             flops=12 * HD * pairs, bytes_accessed=8 * resp_q.size, transcendentals=pairs
         ),
@@ -307,15 +291,11 @@
     block = prompt_k.shape[0]
     core = lax.rem(lax.axis_index("seq"), CORES)
 
-    *pieces, own = local_call(
-        pack_kernel,
-        "pack",
-        [prompt_k, prompt_v, resp_k, resp_v],
-        [((block, wide), BF16)] * groups + [((tokens, wide), BF16)],
-    )
+    *pieces, own = pack([prompt_k, prompt_v, resp_k, resp_v], groups)
     pieces = [pieces[0]] + [swap_heads(pieces[k], k) for k in range(1, groups)]
     near = shift_chips(own, 1)
     far = shift_chips(own, 2)
+    pieces, near, far = lax.optimization_barrier((pieces, near, far))
     mine = jnp.concatenate(pieces, axis=0)
     parts = [mine] + [swap_chips(mine, k) for k in range(1, chips)]
     chosen = jnp.where(core == 1, far, own)
@@ -337,6 +317,7 @@
         + [((tokens, wide), F32)],
     )
     parts = [parts[0]] + [swap_chips(parts[k], k) for k in range(1, chips)]
+    parts, near, far = lax.optimization_barrier((parts, near, far))
     near = shift_chips(near, -1)
     far = shift_chips(far, -2)
     pieces = local_call(
@@ -347,11 +328,11 @@
         [pltpu.VMEM((share, wide), F32)],
     )
     pieces = [pieces[0]] + [swap_heads(pieces[k], k) for k in range(1, groups)]
-    grad_k_resp, grad_v_resp = local_call(
-        finish_resp_kernel, "finish_resp", [own, near, far], [((tokens, kv_cols), BF16)] * 2
-    )
-    grad_k_prompt, grad_v_prompt = local_call(
-        finish_prompt_kernel, "finish_prompt", pieces, [(prompt_k.shape, BF16)] * 2
+    grad_k_prompt, grad_v_prompt, grad_k_resp, grad_v_resp = local_call(
+        finish_kernel,
+        "finish",
+        [own, near, far] + pieces,
+        [(prompt_k.shape, BF16)] * 2 + [((tokens, kv_cols), BF16)] * 2,
     )
     return (resp_out, grad_q, grad_k_resp, grad_v_resp, grad_k_prompt, grad_v_prompt)
 

time: 129 us -> 121 us (0.938)
  Pallas kernels: 54.6 us -> 61.3 us
  local copies, waits for them, and re-layouts: 6.55 us -> 0.89 us
  waiting for transfers between devices: 34.1 us -> 29.6 us
  starting transfers between devices: 30.2 us -> 26.9 us
    ppermute x6, waiting for transfers between devices: 20.1 us -> 13.8 us  [swap_chips(): lax.ppermute(array, 'seq', [(i, i ^ by * CORES) for i in range(devices)])]
    unnamed x25 -> x15, local copies, waits for them, and re-layouts: 6.55 us -> 0.88 us
    pallas_call x1, Pallas kernels: 52.7 us -> 58.2 us  [attention(): pl.pallas_call(functools.partial(attention_kernel, tokens), grid=(kv_head...]
    ppermute x4, starting transfers between devices: 11.6 us -> 8.83 us  [shift_chips(): lax.ppermute(array, 'seq', [(i, i + by) for i in range(devices) if 0 <= i...]
    ppermute x6, waiting for transfers between devices: 8.23 us -> 10.3 us  [swap_heads(): return lax.ppermute(array, 'head', [(i, i ^ by) for i in range(devices)])]
    pallas_call x0 -> x1, Pallas kernels: none -> 1.89 us  [pack(): pl.pallas_call(pack_kernel, grid=(1,), in_specs=[one(array) for array in...]
  transfers between devices with their start and end apart: 18 -> 18, of which waited for: 10 -> 10; matrix products, arithmetic and copies ran while one was open for 0% -> 0% of each run, Pallas kernels for 1% -> 0%
where the time goes in v2:
time: 121 us; the launch traced here: 119 us
  Pallas kernels  61.3 us (51%)
  waiting for transfers between devices  29.6 us (24%)
  starting transfers between devices  26.9 us (22%)
    pallas_call x1, Pallas kernels, attention(): pl.pallas_call(functools.partial(attention_kernel, tokens), grid=(kv_head...  58.2 us
    ppermute x6, waiting for transfers between devices, swap_chips(): lax.ppermute(array, 'seq', [(i, i ^ by * CORES) for i in range(devices)])  13.8 us
    ppermute x6, waiting for transfers between devices, swap_heads(): return lax.ppermute(array, 'head', [(i, i ^ by) for i in range(devices)])  10.3 us
    ppermute x6, starting transfers between devices, swap_chips(): lax.ppermute(array, 'seq', [(i, i ^ by * CORES) for i in range(devices)])  8.93 us
    ppermute x6, starting transfers between devices, swap_heads(): return lax.ppermute(array, 'head', [(i, i ^ by) for i in range(devices)])  8.9 us
    ppermute x4, starting transfers between devices, shift_chips(): lax.ppermute(array, 'seq', [(i, i + by) for i in range(devices) if 0 <= i...  8.83 us
    ppermute x2, waiting for transfers between devices, swap_cores(): return lax.ppermute(array, 'seq', [(i, i ^ 1) for i in range(devices)])  5.55 us
  transfers between devices with their start and end apart: 18, of which 10 were waited for; matrix products, arithmetic and copies ran while one was open for 0% of the time, Pallas kernels for 0%

profile of v2, /device:TPU:6, one launch (start us, length us, event | category | flops | bytes accessed | tf_op | source)
XLA Modules:
  0.0 119.5 jit_solution(14205495781059267027)
XLA Ops:
  0.6 1.9 %pack.1 = (bf16[40,512]{1,0:T(8,128)(2,1)}, bf16[40,512]{1,0:T(8,128)(2,1)}, bf16[40,512]{1,0:T(8,128)(2,1)}, bf16[40,512]{1,0:T(8,128)(2,1)}, bf16[256,512]{1,0:T(8,128)(2,1)}) custom-call(bf16[40,1024]{1,0:T(8,128)(2,1)} %pk_ref.1, bf16[40,1024]{1,0:T(8,128)(2,1)} %pv_ref.1, bf16[256,256]{1,0:T(8,128)(2,1)} %rk_ref.1, bf16[256,256]{1,0:T(8,128)(2,1)} %rv_ref.1), custom_call_target="tpu_custom_call" | custom-call | tf_op jit(solution)/shard_map/pack/pallas_call | solution.py:62
  2.5 1.4 %collective-permute-start.4 = (bf16[256,512]{1,0:T(8,128)(2,1)}, bf16[256,512]{1,0:T(8,128)(2,1)S(1)}, u32[]{:S(2)}, u32[]{:S(2)}) collective-permute-start(bf16[256,512]{1,0:T(8,128)(2,1)} %get-tuple-element.46.own_ref), channel_id=1, source_target_pairs={{0,16},{4,20},{8,24},{12,28},{1,17},{5,21},{9,25},{13,29},{2,18},{... | collective-permute-start | bytes 786440 | tf_op jit(solution)/shard_map/ppermute | solution.py:283
  3.9 1.3 %collective-permute-start.3 = (bf16[256,512]{1,0:T(8,128)(2,1)}, bf16[256,512]{1,0:T(8,128)(2,1)S(1)}, u32[]{:S(2)}, u32[]{:S(2)}) collective-permute-start(bf16[256,512]{1,0:T(8,128)(2,1)} %get-tuple-element.46.own_ref), channel_id=1, source_target_pairs={{0,8},{4,12},{8,16},{12,20},{16,24},{20,28},{1,9},{5,13},{9,17},{1... | collective-permute-start | bytes 786440 | tf_op jit(solution)/shard_map/ppermute | solution.py:283
  5.2 1.6 %collective-permute-start = (bf16[40,512]{1,0:T(8,128)(2,1)}, bf16[40,512]{1,0:T(8,128)(2,1)S(1)}, u32[]{:S(2)}, u32[]{:S(2)}) collective-permute-start(bf16[40,512]{1,0:T(8,128)(2,1)} %get-tuple-element.43), channel_id=1, source_target_pairs={{0,1},{1,0},{2,3},{3,2},{4,5},{5,4},{6,7},{7,6},{8,9},{9,8},{10,11... | collective-permute-start | bytes 122888 | tf_op jit(solution)/shard_map/ppermute | solution.py:267
  6.9 2.6 %collective-permute-start.1 = (bf16[40,512]{1,0:T(8,128)(2,1)}, bf16[40,512]{1,0:T(8,128)(2,1)S(1)}, u32[]{:S(2)}, u32[]{:S(2)}) collective-permute-start(bf16[40,512]{1,0:T(8,128)(2,1)} %get-tuple-element.44), channel_id=1, source_target_pairs={{0,2},{1,3},{2,0},{3,1},{4,6},{5,7},{6,4},{7,5},{8,10},{9,11},{10,... | collective-permute-start | bytes 122888 | tf_op jit(solution)/shard_map/ppermute | solution.py:267
  9.5 0.2 collective-permute-start.2
  9.7 3.1 %collective-permute-done.1 = bf16[40,512]{1,0:T(8,128)(2,1)S(1)} collective-permute-done((bf16[40,512]{1,0:T(8,128)(2,1)}, bf16[40,512]{1,0:T(8,128)(2,1)S(1)}, u32[]{:S(2)}, u32[]{:S(2)}) %collective-permute-start.1) | collective-permute-done | bytes 40992 | tf_op jit(solution)/shard_map/ppermute | solution.py:267
  12.8 2.7 %collective-permute-done.2 = bf16[40,512]{1,0:T(8,128)(2,1)S(1)} collective-permute-done((bf16[40,512]{1,0:T(8,128)(2,1)}, bf16[40,512]{1,0:T(8,128)(2,1)S(1)}, u32[]{:S(2)}, u32[]{:S(2)}) %collective-permute-start.2) | collective-permute-done | bytes 40992 | tf_op jit(solution)/shard_map/ppermute | solution.py:267
  15.5 0.8 constant_dynamic-update-slice_fusion.3
  16.3 3.5 %collective-permute-start.5 = (bf16[160,512]{1,0:T(8,128)(2,1)S(1)}, bf16[160,512]{1,0:T(8,128)(2,1)S(1)}, u32[]{:S(2)}, u32[]{:S(2)}) collective-permute-start(bf16[160,512]{1,0:T(8,128)(2,1)S(1)} %get-tuple-element.78), channel_id=1, source_target_pairs={{0,8},{4,12},{8,0},{12,4},{16,24},{20,28},{24,16},{28,20},{1,9},{5... | collective-permute-start | bytes 491528 | tf_op jit(solution)/shard_map/ppermute | solution.py:272
  19.9 1.9 %collective-permute-start.6 = (bf16[160,512]{1,0:T(8,128)(2,1)S(1)}, bf16[160,512]{1,0:T(8,128)(2,1)S(1)}, u32[]{:S(2)}, u32[]{:S(2)}) collective-permute-start(bf16[160,512]{1,0:T(8,128)(2,1)S(1)} %get-tuple-element.78), channel_id=1, source_target_pairs={{0,16},{4,20},{8,24},{12,28},{16,0},{20,4},{24,8},{28,12},{1,17},{... | collective-permute-start | bytes 491528 | tf_op jit(solution)/shard_map/ppermute | solution.py:272
  21.7 2.5 %collective-permute-done.5 = bf16[160,512]{1,0:T(8,128)(2,1)S(1)} collective-permute-done((bf16[160,512]{1,0:T(8,128)(2,1)S(1)}, bf16[160,512]{1,0:T(8,128)(2,1)S(1)}, u32[]{:S(2)}, u32[]{:S(2)}) %collective-permute-start.5) | collective-permute-done | bytes 163872 | tf_op jit(solution)/shard_map/ppermute | solution.py:272
  24.2 3.9 %collective-permute-done.6 = bf16[160,512]{1,0:T(8,128)(2,1)S(1)} collective-permute-done((bf16[160,512]{1,0:T(8,128)(2,1)S(1)}, bf16[160,512]{1,0:T(8,128)(2,1)S(1)}, u32[]{:S(2)}, u32[]{:S(2)}) %collective-permute-start.6) | collective-permute-done | bytes 163872 | tf_op jit(solution)/shard_map/ppermute | solution.py:272
  28.4 2.8 %collective-permute-done.8.got_ref = bf16[1152,512]{1,0:T(8,128)(2,1)S(1)} collective-permute-done((bf16[1152,512]{1,0:T(8,128)(2,1)S(1)}, bf16[1152,512]{1,0:T(8,128)(2,1)S(1)}, u32[]{:S(2)}, u32[]{:S(2)}) %collective-permute-start.8) | collective-permute-done | bytes 1179680 | tf_op jit(solution)/shard_map/ppermute | solution.py:277
  31.2 58.2 %attention.1 = (bf16[256,2048]{1,0:T(8,128)(2,1)}, bf16[256,2048]{1,0:T(8,128)(2,1)}, f32[1408,512]{1,0:T(8,128)S(1)}, bf16[1152,512]{1,0:T(8,128)(2,1)S(1)}) custom-call(s32[8]{0:T(128)S(1)} %copy-done.3, bf16[256,2048]{1,0:T(8,128)(2,1)S(1)} %copy-done.1, bf16[256,2048]{1,0:T(8,128)(2,1)S(1)} %copy-done.2, ...), custom_call_target="tpu_custom_call" | custom-call | flops 16106127360 | bytes 4194304 | tf_op jit(solution)/shard_map/attention/pallas_call | solution.py:235
  89.4 0.1 collective-permute-start.9
  89.5 2.7 %collective-permute-done.9.got_ref = bf16[1152,512]{1,0:T(8,128)(2,1)S(1)} collective-permute-done((bf16[1152,512]{1,0:T(8,128)(2,1)S(1)}, bf16[1152,512]{1,0:T(8,128)(2,1)S(1)}, u32[]{:S(2)}, u32[]{:S(2)}) %collective-permute-start.9) | collective-permute-done | bytes 1179680 | tf_op jit(solution)/shard_map/ppermute | solution.py:277
  92.3 0.3 merge.1
  92.6 0.4 collective-permute-start.10
  93.0 1.6 %collective-permute-start.11 = (bf16[160,512]{1,0:T(8,128)(2,1)S(1)}, bf16[160,512]{1,0:T(8,128)(2,1)S(1)}, u32[]{:S(2)}, u32[]{:S(2)}) collective-permute-start(bf16[160,512]{1,0:T(8,128)(2,1)S(1)} %get-tuple-element.60), channel_id=1, source_target_pairs={{0,16},{4,20},{8,24},{12,28},{16,0},{20,4},{24,8},{28,12},{1,17},{... | collective-permute-start | bytes 491528 | tf_op jit(solution)/shard_map/ppermute | solution.py:272
  94.6 1.5 %collective-permute-start.12 = (bf16[160,512]{1,0:T(8,128)(2,1)S(1)}, bf16[160,512]{1,0:T(8,128)(2,1)S(1)}, u32[]{:S(2)}, u32[]{:S(2)}) collective-permute-start(bf16[160,512]{1,0:T(8,128)(2,1)S(1)} %get-tuple-element.61), channel_id=1, source_target_pairs={{0,24},{4,28},{8,16},{12,20},{16,8},{20,12},{24,0},{28,4},{1,25},{... | collective-permute-start | bytes 491528 | tf_op jit(solution)/shard_map/ppermute | solution.py:272
  96.1 3.6 %collective-permute-done.10.refs_1_ = bf16[160,512]{1,0:T(8,128)(2,1)S(1)} collective-permute-done((bf16[160,512]{1,0:T(8,128)(2,1)S(1)}, bf16[160,512]{1,0:T(8,128)(2,1)S(1)}, u32[]{:S(2)}, u32[]{:S(2)}) %collective-permute-start.10) | collective-permute-done | bytes 163872 | tf_op jit(solution)/shard_map/ppermute | solution.py:272
  99.7 3.8 %collective-permute-done.12.refs_3_ = bf16[160,512]{1,0:T(8,128)(2,1)S(1)} collective-permute-done((bf16[160,512]{1,0:T(8,128)(2,1)S(1)}, bf16[160,512]{1,0:T(8,128)(2,1)S(1)}, u32[]{:S(2)}, u32[]{:S(2)}) %collective-permute-start.12) | collective-permute-done | bytes 163872 | tf_op jit(solution)/shard_map/ppermute | solution.py:272
  103.5 2.6 %collective-permute-start.13 = (bf16[256,512]{1,0:T(8,128)(2,1)S(1)}, bf16[256,512]{1,0:T(8,128)(2,1)S(1)}, u32[]{:S(2)}, u32[]{:S(2)}) collective-permute-start(bf16[256,512]{1,0:T(8,128)(2,1)S(1)} %get-tuple-element.64), channel_id=1, source_target_pairs={{8,0},{12,4},{16,8},{20,12},{24,16},{28,20},{9,1},{13,5},{17,9},{2... | collective-permute-start | bytes 786440 | tf_op jit(solution)/shard_map/ppermute | solution.py:283
  106.1 3.6 %collective-permute-start.14 = (bf16[256,512]{1,0:T(8,128)(2,1)S(1)}, bf16[256,512]{1,0:T(8,128)(2,1)S(1)}, u32[]{:S(2)}, u32[]{:S(2)}) collective-permute-start(bf16[256,512]{1,0:T(8,128)(2,1)S(1)} %get-tuple-element.65), channel_id=1, source_target_pairs={{16,0},{20,4},{24,8},{28,12},{17,1},{21,5},{25,9},{29,13},{18,2},{... | collective-permute-start | bytes 786440 | tf_op jit(solution)/shard_map/ppermute | solution.py:283
  109.6 0.1 sum_chips.1
  109.7 0.5 collective-permute-start.15
  110.2 2.6 %collective-permute-start.16 = (bf16[40,512]{1,0:T(8,128)(2,1)S(1)}, bf16[40,512]{1,0:T(8,128)(2,1)S(1)}, u32[]{:S(2)}, u32[]{:S(2)}) collective-permute-start(bf16[40,512]{1,0:T(8,128)(2,1)S(1)} %get-tuple-element.72), channel_id=1, source_target_pairs={{0,2},{1,3},{2,0},{3,1},{4,6},{5,7},{6,4},{7,5},{8,10},{9,11},{10,... | collective-permute-start | bytes 122888 | tf_op jit(solution)/shard_map/ppermute | solution.py:267
  112.8 1.3 %collective-permute-start.17 = (bf16[40,512]{1,0:T(8,128)(2,1)S(1)}, bf16[40,512]{1,0:T(8,128)(2,1)S(1)}, u32[]{:S(2)}, u32[]{:S(2)}) collective-permute-start(bf16[40,512]{1,0:T(8,128)(2,1)S(1)} %get-tuple-element.73), channel_id=1, source_target_pairs={{0,3},{1,2},{2,1},{3,0},{4,7},{5,6},{6,5},{7,4},{8,11},{9,10},{10,... | collective-permute-start | bytes 122888 | tf_op jit(solution)/shard_map/ppermute | solution.py:267
  114.2 1.4 %collective-permute-done.16.refs_2_ = bf16[40,512]{1,0:T(8,128)(2,1)S(1)} collective-permute-done((bf16[40,512]{1,0:T(8,128)(2,1)S(1)}, bf16[40,512]{1,0:T(8,128)(2,1)S(1)}, u32[]{:S(2)}, u32[]{:S(2)}) %collective-permute-start.16) | collective-permute-done | bytes 40992 | tf_op jit(solution)/shard_map/ppermute | solution.py:267
  115.6 3.0 %collective-permute-done.17.refs_3_ = bf16[40,512]{1,0:T(8,128)(2,1)S(1)} collective-permute-done((bf16[40,512]{1,0:T(8,128)(2,1)S(1)}, bf16[40,512]{1,0:T(8,128)(2,1)S(1)}, u32[]{:S(2)}, u32[]{:S(2)}) %collective-permute-start.17) | collective-permute-done | bytes 40992 | tf_op jit(solution)/shard_map/ppermute | solution.py:267
  118.6 0.8 finish.1
  (26 shorter events, 0.3 us)
Async XLA Ops:
  2.5 25.7 %copy-start = (bf16[256,512]{1,0:T(8,128)(2,1)S(1)}, bf16[256,512]{1,0:T(8,128)(2,1)}, u32[]{:S(2)}) copy-start(bf16[256,512]{1,0:T(8,128)(2,1)} %get-tuple-element.46.own_ref) | copy-start | bytes 786436
  2.5 13.0 %collective-permute-start.4 = (bf16[256,512]{1,0:T(8,128)(2,1)}, bf16[256,512]{1,0:T(8,128)(2,1)S(1)}, u32[]{:S(2)}, u32[]{:S(2)}) collective-permute-start(bf16[256,512]{1,0:T(8,128)(2,1)} %get-tuple-element.46.own_ref), channel_id=1, source_target_pairs={{0,16},{4,20},{8,24},{12,28},{1,17},{5,21},{9,25},{13,29},{2,18},{... | collective-permute-start | bytes 786440 | tf_op jit(solution)/shard_map/ppermute | solution.py:283
  3.9 11.5 %collective-permute-start.3 = (bf16[256,512]{1,0:T(8,128)(2,1)}, bf16[256,512]{1,0:T(8,128)(2,1)S(1)}, u32[]{:S(2)}, u32[]{:S(2)}) collective-permute-start(bf16[256,512]{1,0:T(8,128)(2,1)} %get-tuple-element.46.own_ref), channel_id=1, source_target_pairs={{0,8},{4,12},{8,16},{12,20},{16,24},{20,28},{1,9},{5,13},{9,17},{1... | collective-permute-start | bytes 786440 | tf_op jit(solution)/shard_map/ppermute | solution.py:283
  5.2 4.5 %collective-permute-start = (bf16[40,512]{1,0:T(8,128)(2,1)}, bf16[40,512]{1,0:T(8,128)(2,1)S(1)}, u32[]{:S(2)}, u32[]{:S(2)}) collective-permute-start(bf16[40,512]{1,0:T(8,128)(2,1)} %get-tuple-element.43), channel_id=1, source_target_pairs={{0,1},{1,0},{2,3},{3,2},{4,5},{5,4},{6,7},{7,6},{8,9},{9,8},{10,11... | collective-permute-start | bytes 122888 | tf_op jit(solution)/shard_map/ppermute | solution.py:267
  6.9 5.9 %collective-permute-start.1 = (bf16[40,512]{1,0:T(8,128)(2,1)}, bf16[40,512]{1,0:T(8,128)(2,1)S(1)}, u32[]{:S(2)}, u32[]{:S(2)}) collective-permute-start(bf16[40,512]{1,0:T(8,128)(2,1)} %get-tuple-element.44), channel_id=1, source_target_pairs={{0,2},{1,3},{2,0},{3,1},{4,6},{5,7},{6,4},{7,5},{8,10},{9,11},{10,... | collective-permute-start | bytes 122888 | tf_op jit(solution)/shard_map/ppermute | solution.py:267
  9.5 6.0 %collective-permute-start.2 = (bf16[40,512]{1,0:T(8,128)(2,1)}, bf16[40,512]{1,0:T(8,128)(2,1)S(1)}, u32[]{:S(2)}, u32[]{:S(2)}) collective-permute-start(bf16[40,512]{1,0:T(8,128)(2,1)} %get-tuple-element.45), channel_id=1, source_target_pairs={{0,3},{1,2},{2,1},{3,0},{4,7},{5,6},{6,5},{7,4},{8,11},{9,10},{10,... | collective-permute-start | bytes 122888 | tf_op jit(solution)/shard_map/ppermute | solution.py:267
  16.3 14.9 %copy-start.1 = (bf16[256,2048]{1,0:T(8,128)(2,1)S(1)}, bf16[256,2048]{1,0:T(8,128)(2,1)}, u32[]{:S(2)}) copy-start(bf16[256,2048]{1,0:T(8,128)(2,1)} %q_ref.1) | copy-start | bytes 3145732
  16.3 14.9 %copy-start.3 = (s32[8]{0:T(128)S(1)}, s32[8]{0:T(128)}, u32[]{:S(2)}) copy-start(s32[8]{0:T(128)} %lengths.1) | copy-start | bytes 100
  16.3 7.9 %collective-permute-start.5 = (bf16[160,512]{1,0:T(8,128)(2,1)S(1)}, bf16[160,512]{1,0:T(8,128)(2,1)S(1)}, u32[]{:S(2)}, u32[]{:S(2)}) collective-permute-start(bf16[160,512]{1,0:T(8,128)(2,1)S(1)} %get-tuple-element.78), channel_id=1, source_target_pairs={{0,8},{4,12},{8,0},{12,4},{16,24},{20,28},{24,16},{28,20},{1,9},{5... | collective-permute-start | bytes 491528 | tf_op jit(solution)/shard_map/ppermute | solution.py:272
  19.9 8.3 %collective-permute-start.6 = (bf16[160,512]{1,0:T(8,128)(2,1)S(1)}, bf16[160,512]{1,0:T(8,128)(2,1)S(1)}, u32[]{:S(2)}, u32[]{:S(2)}) collective-permute-start(bf16[160,512]{1,0:T(8,128)(2,1)S(1)} %get-tuple-element.78), channel_id=1, source_target_pairs={{0,16},{4,20},{8,24},{12,28},{16,0},{20,4},{24,8},{28,12},{1,17},{... | collective-permute-start | bytes 491528 | tf_op jit(solution)/shard_map/ppermute | solution.py:272
  21.7 9.5 %copy-start.2 = (bf16[256,2048]{1,0:T(8,128)(2,1)S(1)}, bf16[256,2048]{1,0:T(8,128)(2,1)}, u32[]{:S(2)}) copy-start(bf16[256,2048]{1,0:T(8,128)(2,1)} %do_ref.1) | copy-start | bytes 3145732
  21.7 6.5 %collective-permute-start.7 = (bf16[160,512]{1,0:T(8,128)(2,1)S(1)}, bf16[160,512]{1,0:T(8,128)(2,1)S(1)}, u32[]{:S(2)}, u32[]{:S(2)}) collective-permute-start(bf16[160,512]{1,0:T(8,128)(2,1)S(1)} %get-tuple-element.78), channel_id=1, source_target_pairs={{0,24},{4,28},{8,16},{12,20},{16,8},{20,12},{24,0},{28,4},{1,25},{... | collective-permute-start | bytes 491528 | tf_op jit(solution)/shard_map/ppermute | solution.py:272
  28.3 2.9 %collective-permute-start.8 = (bf16[1152,512]{1,0:T(8,128)(2,1)S(1)}, bf16[1152,512]{1,0:T(8,128)(2,1)S(1)}, u32[]{:S(2)}, u32[]{:S(2)}) collective-permute-start(bf16[1152,512]{1,0:T(8,128)(2,1)S(1)} %select_dynamic-update-slice_fusion.sent_ref), channel_id=1, source_target_pairs={{0,4},{4,0},{8,12},{12,8},{16,20},{20,16},{24,28},{28,24},{1,5},{5... | collective-permute-start | bytes 3538952 | tf_op jit(solution)/shard_map/ppermute | solution.py:277
  89.4 2.8 %collective-permute-start.9 = (bf16[1152,512]{1,0:T(8,128)(2,1)S(1)}, bf16[1152,512]{1,0:T(8,128)(2,1)S(1)}, u32[]{:S(2)}, u32[]{:S(2)}) collective-permute-start(bf16[1152,512]{1,0:T(8,128)(2,1)S(1)} %get-tuple-element.56), channel_id=1, source_target_pairs={{0,4},{4,0},{8,12},{12,8},{16,20},{20,16},{24,28},{28,24},{1,5},{5... | collective-permute-start | bytes 3538952 | tf_op jit(solution)/shard_map/ppermute | solution.py:277
  92.6 7.1 %collective-permute-start.10 = (bf16[160,512]{1,0:T(8,128)(2,1)S(1)}, bf16[160,512]{1,0:T(8,128)(2,1)S(1)}, u32[]{:S(2)}, u32[]{:S(2)}) collective-permute-start(bf16[160,512]{1,0:T(8,128)(2,1)S(1)} %get-tuple-element.59), channel_id=1, source_target_pairs={{0,8},{4,12},{8,0},{12,4},{16,24},{20,28},{24,16},{28,20},{1,9},{5... | collective-permute-start | bytes 491528 | tf_op jit(solution)/shard_map/ppermute | solution.py:272
  93.0 6.7 %collective-permute-start.11 = (bf16[160,512]{1,0:T(8,128)(2,1)S(1)}, bf16[160,512]{1,0:T(8,128)(2,1)S(1)}, u32[]{:S(2)}, u32[]{:S(2)}) collective-permute-start(bf16[160,512]{1,0:T(8,128)(2,1)S(1)} %get-tuple-element.60), channel_id=1, source_target_pairs={{0,16},{4,20},{8,24},{12,28},{16,0},{20,4},{24,8},{28,12},{1,17},{... | collective-permute-start | bytes 491528 | tf_op jit(solution)/shard_map/ppermute | solution.py:272
  94.6 8.9 %collective-permute-start.12 = (bf16[160,512]{1,0:T(8,128)(2,1)S(1)}, bf16[160,512]{1,0:T(8,128)(2,1)S(1)}, u32[]{:S(2)}, u32[]{:S(2)}) collective-permute-start(bf16[160,512]{1,0:T(8,128)(2,1)S(1)} %get-tuple-element.61), channel_id=1, source_target_pairs={{0,24},{4,28},{8,16},{12,20},{16,8},{20,12},{24,0},{28,4},{1,25},{... | collective-permute-start | bytes 491528 | tf_op jit(solution)/shard_map/ppermute | solution.py:272
  103.5 15.2 %collective-permute-start.13 = (bf16[256,512]{1,0:T(8,128)(2,1)S(1)}, bf16[256,512]{1,0:T(8,128)(2,1)S(1)}, u32[]{:S(2)}, u32[]{:S(2)}) collective-permute-start(bf16[256,512]{1,0:T(8,128)(2,1)S(1)} %get-tuple-element.64), channel_id=1, source_target_pairs={{8,0},{12,4},{16,8},{20,12},{24,16},{28,20},{9,1},{13,5},{17,9},{2... | collective-permute-start | bytes 786440 | tf_op jit(solution)/shard_map/ppermute | solution.py:283
  106.1 12.6 %collective-permute-start.14 = (bf16[256,512]{1,0:T(8,128)(2,1)S(1)}, bf16[256,512]{1,0:T(8,128)(2,1)S(1)}, u32[]{:S(2)}, u32[]{:S(2)}) collective-permute-start(bf16[256,512]{1,0:T(8,128)(2,1)S(1)} %get-tuple-element.65), channel_id=1, source_target_pairs={{16,0},{20,4},{24,8},{28,12},{17,1},{21,5},{25,9},{29,13},{18,2},{... | collective-permute-start | bytes 786440 | tf_op jit(solution)/shard_map/ppermute | solution.py:283
  109.7 4.5 %collective-permute-start.15 = (bf16[40,512]{1,0:T(8,128)(2,1)S(1)}, bf16[40,512]{1,0:T(8,128)(2,1)S(1)}, u32[]{:S(2)}, u32[]{:S(2)}) collective-permute-start(bf16[40,512]{1,0:T(8,128)(2,1)S(1)} %get-tuple-element.71), channel_id=1, source_target_pairs={{0,1},{1,0},{2,3},{3,2},{4,5},{5,4},{6,7},{7,6},{8,9},{9,8},{10,11... | collective-permute-start | bytes 122888 | tf_op jit(solution)/shard_map/ppermute | solution.py:267
  110.2 5.3 %collective-permute-start.16 = (bf16[40,512]{1,0:T(8,128)(2,1)S(1)}, bf16[40,512]{1,0:T(8,128)(2,1)S(1)}, u32[]{:S(2)}, u32[]{:S(2)}) collective-permute-start(bf16[40,512]{1,0:T(8,128)(2,1)S(1)} %get-tuple-element.72), channel_id=1, source_target_pairs={{0,2},{1,3},{2,0},{3,1},{4,6},{5,7},{6,4},{7,5},{8,10},{9,11},{10,... | collective-permute-start | bytes 122888 | tf_op jit(solution)/shard_map/ppermute | solution.py:267
  112.8 5.8 %collective-permute-start.17 = (bf16[40,512]{1,0:T(8,128)(2,1)S(1)}, bf16[40,512]{1,0:T(8,128)(2,1)S(1)}, u32[]{:S(2)}, u32[]{:S(2)}) collective-permute-start(bf16[40,512]{1,0:T(8,128)(2,1)S(1)} %get-tuple-element.73), channel_id=1, source_target_pairs={{0,3},{1,2},{2,1},{3,0},{4,7},{5,6},{6,5},{7,4},{8,11},{9,10},{10,... | collective-permute-start | bytes 122888 | tf_op jit(solution)/shard_map/ppermute | solution.py:267

commit v3 on v2

--- a/solution.py
+++ b/solution.py
@@ -13,12 +13,17 @@
 FAR = 4
 CHUNK = 256
 NEG = -1e30
+NT = (((1,), (1,)), ((), ()))
 BF16 = jnp.bfloat16
 F32 = jnp.float32
 
 
 def dot(a, b):
     return jnp.dot(a, b, preferred_element_type=F32)
+
+
+def dot_nt(a, b):
+    return lax.dot_general(a, b, NT, preferred_element_type=F32)
 
 
 def whole(count):
@@ -114,11 +119,11 @@
 
 
 def attention_kernel(
-    tokens, lengths, q_ref, do_ref, sent_ref, got_ref, own_ref, far_ref,
+    tokens, lengths, q_ref, next_ref, do_ref, sent_ref, got_ref, own_ref, far_ref,
     o_ref, dq_ref, kept_ref, back_ref,
-    bias, keys, values, keys_t, values_t, s_buf, p_buf, dk, dv,
+    bias, keys, values, s_even, s_odd, p_even, p_odd, top_even, dk_t, dv_t,
 ):
-    total_keys = keys.shape[0]
+    total_keys = keys.shape[1]
     prompt_len = total_keys - 5 * tokens
     half = prompt_len // 2
     head = pl.program_id(0)
@@ -126,25 +131,53 @@
     last = pl.num_programs(1) - 1
     score_scale = 1.0 / math.sqrt(HD)
     exp_scale = score_scale * math.log2(math.e)
-    k_cols = pl.ds(pl.multiple_of(head * 2 * HD, HD), HD)
-    v_cols = pl.ds(pl.multiple_of(head * 2 * HD + HD, HD), HD)
     resp_at = [prompt_len + i * tokens for i in range(6)]
-    pieces = [
-        (sent_ref, 0, half, 0),
-        (got_ref, 0, half, half),
-        (own_ref, 0, tokens, resp_at[0]),
-        (sent_ref, half, tokens, resp_at[1]),
-        (far_ref, 0, tokens, resp_at[2]),
-        (got_ref, half, tokens, resp_at[3]),
-        (got_ref, half + tokens, tokens, resp_at[4]),
-    ]
+    chunks = [slice(at, at + CHUNK) for at in range(0, total_keys, CHUNK)]
+
+    def front(q, at, which, s_buf, top):
+        s = dot_nt(q, keys[which, at])
+        if at.start >= prompt_len:
+            s = s + bias[(at.start - prompt_len) // tokens]
+        s_buf[:, at] = s
+        for col in range(0, CHUNK, HD):
+            part = s[:, col : col + HD]
+            top = part if top is None else jnp.maximum(top, part)
+        return top
+
+    def middle(at, s_buf, p_buf, top, total, out):
+        p = jnp.exp2(s_buf[:, at] * exp_scale - top)
+        for col in range(0, CHUNK, HD):
+            part = p[:, col : col + HD]
+            total = part if total is None else total + part
+        p = p.astype(BF16)
+        p_buf[:, at] = p
+        more = dot(p, values[head, at])
+        return total, more if out is None else out + more
+
+    def settle(q, cot, total, out):
+        inverse = 1.0 / jnp.sum(total, axis=1, keepdims=True)
+        out = (out * inverse).astype(BF16)
+        wide = cot.astype(F32)
+        delta = jnp.sum(wide * out.astype(F32), axis=1, keepdims=True)
+        cot_t = (wide * inverse).astype(BF16).T
+        q_t = (q.astype(F32) * inverse).astype(BF16).T
+        return inverse, out, delta, cot_t, q_t
+
+    def behind(at, p_buf, cot, delta, cot_t, q_t, dq):
+        p = p_buf[:, at]
+        dp = dot_nt(cot, values[head, at])
+        ds = (p.astype(F32) * (dp - delta)).astype(BF16)
+        dv_t[:, at] += dot(cot_t, p)
+        dk_t[:, at] += dot(q_t, ds)
+        more = dot(ds, keys[head, at])
+        return more if dq is None else dq + more
 
     @pl.when((step == 0) & (head == 0))
     def _():
         place = lax.axis_index("seq")
         core = lax.rem(place, CORES)
         first_row = place * tokens
-        row_pos = first_row + lax.broadcasted_iota(jnp.int32, (tokens, tokens), 1)
+        row_pos = first_row + lax.broadcasted_iota(jnp.int32, (tokens, tokens), 0)
         seg_start = jnp.zeros((tokens, tokens), jnp.int32)
         end = jnp.int32(0)
         for i in range(lengths.shape[0]):
@@ -153,75 +186,74 @@
         near = 1 + 2 * core
         for i, distance in enumerate((0, 2, FAR, near, 4 - near)):
             key_pos = (first_row - distance * tokens) + lax.broadcasted_iota(
-                jnp.int32, (tokens, tokens), 0
+                jnp.int32, (tokens, tokens), 1
             )
             allowed = (key_pos >= seg_start) & (key_pos <= row_pos)
             bias[i] = jnp.where(allowed, 0.0, NEG)
+        for n in range(keys.shape[0]):
+            k_at, v_at = 2 * n * HD, (2 * n + 1) * HD
+            for ref, start, size, at in (
+                (sent_ref, 0, half, 0),
+                (got_ref, 0, half, half),
+                (own_ref, 0, tokens, resp_at[0]),
+                (sent_ref, half, tokens, resp_at[1]),
+                (far_ref, 0, tokens, resp_at[2]),
+                (got_ref, half, tokens, resp_at[3]),
+                (got_ref, half + tokens, tokens, resp_at[4]),
+            ):
+                keys[n, at : at + size] = ref[start : start + size, k_at : k_at + HD]
+                values[n, at : at + size] = ref[start : start + size, v_at : v_at + HD]
+        top = None
+        for at in chunks:
+            top = front(q_ref[:, :HD], at, 0, s_even, top)
+        top_even[...] = top
 
     @pl.when(step == 0)
     def _():
-        dk[...] = jnp.zeros_like(dk)
-        dv[...] = jnp.zeros_like(dv)
-        for ref, start, size, at in pieces:
-            k_rows = ref[start : start + size, k_cols]
-            v_rows = ref[start : start + size, v_cols]
-            keys[at : at + size] = k_rows
-            values[at : at + size] = v_rows
-            keys_t[:, at : at + size] = k_rows.T
-            values_t[:, at : at + size] = v_rows.T
-
-    q = q_ref[...]
-    q_t = q.T
-    chunks = [slice(at, at + CHUNK) for at in range(0, total_keys, CHUNK)]
-    top = None
+        dk_t[...] = jnp.zeros_like(dk_t)
+        dv_t[...] = jnp.zeros_like(dv_t)
+
+    q_even, q_odd = q_ref[:, :HD], q_ref[:, HD:]
+    cot_even, cot_odd = do_ref[:, :HD], do_ref[:, HD:]
+    top = jnp.max(top_even[...], axis=1, keepdims=True) * exp_scale
+    total, out, other = None, None, None
     for at in chunks:
-        s = dot(keys[at], q_t)
-        if at.start >= prompt_len:
-            s = s + bias[(at.start - prompt_len) // tokens]
-        s_buf[at] = s
-        part = jnp.max(s.reshape(CHUNK // 8, 8, tokens), axis=0)
-        top = part if top is None else jnp.maximum(top, part)
-    top = jnp.max(top, axis=0, keepdims=True) * exp_scale
-
-    total = jnp.zeros((8, tokens), F32)
-    out = jnp.zeros((HD, tokens), F32)
+        total, out = middle(at, s_even, p_even, top, total, out)
+        other = front(q_odd, at, head, s_odd, other)
+    inverse, out, delta, cot_t, q_t = settle(q_even, cot_even, total, out)
+    o_ref[:, :HD] = out
+    top = jnp.max(other, axis=1, keepdims=True) * exp_scale
+    total, out, dq = None, None, None
     for at in chunks:
-        p = jnp.exp2(s_buf[at] * exp_scale - top)
-        total = total + jnp.sum(p.reshape(CHUNK // 8, 8, tokens), axis=0)
-        p = p.astype(BF16)
-        p_buf[at] = p
-        out = out + dot(values_t[:, at], p)
-    inverse = 1.0 / jnp.sum(total, axis=0, keepdims=True)
-    out = (out * inverse).astype(BF16)
-    o_ref[...] = out.T
-    cot_t = (do_ref[...].T.astype(F32) * inverse).astype(BF16)
-    delta = jnp.sum(cot_t.astype(F32) * out.astype(F32), axis=0, keepdims=True)
-    cot = cot_t.T
-    dq = jnp.zeros((HD, tokens), F32)
+        dq = behind(at, p_even, cot_even, delta, cot_t, q_t, dq)
+        total, out = middle(at, s_odd, p_odd, top, total, out)
+    dq_ref[:, :HD] = (dq * (inverse * score_scale)).astype(BF16)
+    inverse, out, delta, cot_t, q_t = settle(q_odd, cot_odd, total, out)
+    o_ref[:, HD:] = out
+    upcoming = jnp.minimum(head + (step == last).astype(jnp.int32), pl.num_programs(0) - 1)
+    dq, other = None, None
     for at in chunks:
-        p = p_buf[at]
-        dp = dot(values[at], cot_t)
-        ds = (p.astype(F32) * (dp - delta)).astype(BF16)
-        dq = dq + dot(keys_t[:, at], ds)
-        dv[at] += dot(p, cot)
-        dk[at] += dot(ds, q)
-    dq_ref[...] = (dq * score_scale).T.astype(BF16)
-
-    targets = [
-        (kept_ref, 0, half, 0),
-        (back_ref, 0, half, half),
-        (kept_ref, half + 2 * tokens, tokens, resp_at[0]),
-        (kept_ref, half, tokens, resp_at[1]),
-        (kept_ref, half + tokens, tokens, resp_at[2]),
-        (back_ref, half, tokens, resp_at[3]),
-        (back_ref, half + tokens, tokens, resp_at[4]),
-    ]
+        dq = behind(at, p_odd, cot_odd, delta, cot_t, q_t, dq)
+        other = front(next_ref[...], at, upcoming, s_even, other)
+    dq_ref[:, HD:] = (dq * (inverse * score_scale)).astype(BF16)
+    top_even[...] = other
 
     @pl.when(step == last)
     def _():
-        for ref, start, size, at in targets:
-            ref[start : start + size, k_cols] = (dk[at : at + size] * score_scale).astype(ref.dtype)
-            ref[start : start + size, v_cols] = dv[at : at + size].astype(ref.dtype)
+        k_cols = pl.ds(pl.multiple_of(head * 2 * HD, HD), HD)
+        v_cols = pl.ds(pl.multiple_of(head * 2 * HD + HD, HD), HD)
+        for ref, start, size, at in (
+            (kept_ref, 0, half, 0),
+            (back_ref, 0, half, half),
+            (kept_ref, half + 2 * tokens, tokens, resp_at[0]),
+            (kept_ref, half, tokens, resp_at[1]),
+            (kept_ref, half + tokens, tokens, resp_at[2]),
+            (back_ref, half, tokens, resp_at[3]),
+            (back_ref, half + tokens, tokens, resp_at[4]),
+        ):
+            grad_k = (dk_t[:, at : at + size] * score_scale).T
+            ref[start : start + size, k_cols] = grad_k.astype(ref.dtype)
+            ref[start : start + size, v_cols] = dv_t[:, at : at + size].T.astype(ref.dtype)
 
 
 def attention(lengths, resp_q, grad_out, sent, got, own, far):
@@ -229,14 +261,19 @@
     half = sent.shape[0] - 2 * tokens
     total_keys = 2 * half + 5 * tokens
     kv_heads = sent.shape[1] // (2 * HD)
-    steps = resp_q.shape[1] // HD // kv_heads
-    head_spec = pl.BlockSpec((tokens, HD), lambda n, g: (0, n * steps + g))
-    pairs = tokens * kv_heads * steps * total_keys
+    q_heads = resp_q.shape[1] // HD
+    steps = q_heads // kv_heads // 2
+    pair_spec = pl.BlockSpec((tokens, 2 * HD), lambda n, g: (0, n * steps + g))
+    next_spec = pl.BlockSpec(
+        (tokens, HD), lambda n, g: (0, jnp.minimum((n * steps + g) * 2 + 2, q_heads - 2))
+    )
+    pairs = tokens * q_heads * total_keys
     return pl.pallas_call(
         functools.partial(attention_kernel, tokens),
         grid=(kv_heads, steps),
-        in_specs=[pl.BlockSpec(memory_space=pltpu.SMEM), head_spec, head_spec] + whole(4),
-        out_specs=[head_spec, head_spec] + whole(2),
+        in_specs=[pl.BlockSpec(memory_space=pltpu.SMEM), pair_spec, next_spec, pair_spec]
+        + whole(4),
+        out_specs=[pair_spec, pair_spec] + whole(2),
         out_shape=[
             jax.ShapeDtypeStruct(resp_q.shape, BF16),
             jax.ShapeDtypeStruct(resp_q.shape, BF16),
@@ -245,21 +282,22 @@
         ],
         scratch_shapes=[
             pltpu.VMEM((5, tokens, tokens), F32),
-            pltpu.VMEM((total_keys, HD), BF16),
-            pltpu.VMEM((total_keys, HD), BF16),
-            pltpu.VMEM((HD, total_keys), BF16),
-            pltpu.VMEM((HD, total_keys), BF16),
-            pltpu.VMEM((total_keys, tokens), F32),
-            pltpu.VMEM((total_keys, tokens), BF16),
-            pltpu.VMEM((total_keys, HD), F32),
-            pltpu.VMEM((total_keys, HD), F32),
+            pltpu.VMEM((kv_heads, total_keys, HD), BF16),
+            pltpu.VMEM((kv_heads, total_keys, HD), BF16),
+            pltpu.VMEM((tokens, total_keys), F32),
+            pltpu.VMEM((tokens, total_keys), F32),
+            pltpu.VMEM((tokens, total_keys), BF16),
+            pltpu.VMEM((tokens, total_keys), BF16),
+            pltpu.VMEM((tokens, HD), F32),
+            pltpu.VMEM((HD, total_keys), F32),
+            pltpu.VMEM((HD, total_keys), F32),
         ],
         compiler_params=pltpu.CompilerParams(vmem_limit_bytes=44 * 1024 * 1024),
         cost_estimate=pl.CostEstimate(
             flops=12 * HD * pairs, bytes_accessed=8 * resp_q.size, transcendentals=pairs
         ),
         name="attention",
-    )(lengths, resp_q, grad_out, sent, got, own, far)
+    )(lengths, resp_q, resp_q, grad_out, sent, got, own, far)
 
 
 def swap_heads(array, by):

time: 121 us -> 112 us (0.926)
  Pallas kernels: 61.3 us -> 52.9 us
    pallas_call x1, Pallas kernels: 58.2 us -> 49.8 us  [attention(): pl.pallas_call(functools.partial(attention_kernel, tokens), grid=(kv_head...]
where the time goes in v3:
time: 112 us; the launch traced here: 111 us
  Pallas kernels  52.9 us (47%)
  waiting for transfers between devices  29.6 us (26%)
  starting transfers between devices  26.9 us (24%)
    pallas_call x1, Pallas kernels, attention(): pl.pallas_call(functools.partial(attention_kernel, tokens), grid=(kv_head...  49.8 us
    ppermute x6, waiting for transfers between devices, swap_chips(): lax.ppermute(array, 'seq', [(i, i ^ by * CORES) for i in range(devices)])  13.8 us
    ppermute x6, waiting for transfers between devices, swap_heads(): return lax.ppermute(array, 'head', [(i, i ^ by) for i in range(devices)])  10.3 us
    ppermute x6, starting transfers between devices, swap_chips(): lax.ppermute(array, 'seq', [(i, i ^ by * CORES) for i in range(devices)])  8.93 us
    ppermute x6, starting transfers between devices, swap_heads(): return lax.ppermute(array, 'head', [(i, i ^ by) for i in range(devices)])  8.9 us
    ppermute x4, starting transfers between devices, shift_chips(): lax.ppermute(array, 'seq', [(i, i + by) for i in range(devices) if 0 <= i...  8.83 us
    ppermute x2, waiting for transfers between devices, swap_cores(): return lax.ppermute(array, 'seq', [(i, i ^ 1) for i in range(devices)])  5.56 us
  transfers between devices with their start and end apart: 18, of which 10 were waited for; matrix products, arithmetic and copies ran while one was open for 0% of the time, Pallas kernels for 0%

profile of v3, /device:TPU:6, one launch (start us, length us, event | category | flops | bytes accessed | tf_op | source)
XLA Modules:
  0.0 111.1 jit_solution(2922916794948492914)
XLA Ops:
  0.6 1.9 %pack.1 = (bf16[40,512]{1,0:T(8,128)(2,1)}, bf16[40,512]{1,0:T(8,128)(2,1)}, bf16[40,512]{1,0:T(8,128)(2,1)}, bf16[40,512]{1,0:T(8,128)(2,1)}, bf16[256,512]{1,0:T(8,128)(2,1)}) custom-call(bf16[40,1024]{1,0:T(8,128)(2,1)} %pk_ref.1, bf16[40,1024]{1,0:T(8,128)(2,1)} %pv_ref.1, bf16[256,256]{1,0:T(8,128)(2,1)} %rk_ref.1, bf16[256,256]{1,0:T(8,128)(2,1)} %rv_ref.1), custom_call_target="tpu_custom_call" | custom-call | tf_op jit(solution)/shard_map/pack/pallas_call | solution.py:67
  2.5 1.4 %collective-permute-start.4 = (bf16[256,512]{1,0:T(8,128)(2,1)}, bf16[256,512]{1,0:T(8,128)(2,1)S(1)}, u32[]{:S(2)}, u32[]{:S(2)}) collective-permute-start(bf16[256,512]{1,0:T(8,128)(2,1)} %get-tuple-element.46.own_ref), channel_id=1, source_target_pairs={{0,16},{4,20},{8,24},{12,28},{1,17},{5,21},{9,25},{13,29},{2,18},{... | collective-permute-start | bytes 786440 | tf_op jit(solution)/shard_map/ppermute | solution.py:321
  3.9 1.3 %collective-permute-start.3 = (bf16[256,512]{1,0:T(8,128)(2,1)}, bf16[256,512]{1,0:T(8,128)(2,1)S(1)}, u32[]{:S(2)}, u32[]{:S(2)}) collective-permute-start(bf16[256,512]{1,0:T(8,128)(2,1)} %get-tuple-element.46.own_ref), channel_id=1, source_target_pairs={{0,8},{4,12},{8,16},{12,20},{16,24},{20,28},{1,9},{5,13},{9,17},{1... | collective-permute-start | bytes 786440 | tf_op jit(solution)/shard_map/ppermute | solution.py:321
  5.2 1.6 %collective-permute-start = (bf16[40,512]{1,0:T(8,128)(2,1)}, bf16[40,512]{1,0:T(8,128)(2,1)S(1)}, u32[]{:S(2)}, u32[]{:S(2)}) collective-permute-start(bf16[40,512]{1,0:T(8,128)(2,1)} %get-tuple-element.43), channel_id=1, source_target_pairs={{0,1},{1,0},{2,3},{3,2},{4,5},{5,4},{6,7},{7,6},{8,9},{9,8},{10,11... | collective-permute-start | bytes 122888 | tf_op jit(solution)/shard_map/ppermute | solution.py:305
  6.9 2.6 %collective-permute-start.1 = (bf16[40,512]{1,0:T(8,128)(2,1)}, bf16[40,512]{1,0:T(8,128)(2,1)S(1)}, u32[]{:S(2)}, u32[]{:S(2)}) collective-permute-start(bf16[40,512]{1,0:T(8,128)(2,1)} %get-tuple-element.44), channel_id=1, source_target_pairs={{0,2},{1,3},{2,0},{3,1},{4,6},{5,7},{6,4},{7,5},{8,10},{9,11},{10,... | collective-permute-start | bytes 122888 | tf_op jit(solution)/shard_map/ppermute | solution.py:305
  9.5 0.2 collective-permute-start.2
  9.7 3.1 %collective-permute-done.1 = bf16[40,512]{1,0:T(8,128)(2,1)S(1)} collective-permute-done((bf16[40,512]{1,0:T(8,128)(2,1)}, bf16[40,512]{1,0:T(8,128)(2,1)S(1)}, u32[]{:S(2)}, u32[]{:S(2)}) %collective-permute-start.1) | collective-permute-done | bytes 40992 | tf_op jit(solution)/shard_map/ppermute | solution.py:305
  12.8 2.7 %collective-permute-done.2 = bf16[40,512]{1,0:T(8,128)(2,1)S(1)} collective-permute-done((bf16[40,512]{1,0:T(8,128)(2,1)}, bf16[40,512]{1,0:T(8,128)(2,1)S(1)}, u32[]{:S(2)}, u32[]{:S(2)}) %collective-permute-start.2) | collective-permute-done | bytes 40992 | tf_op jit(solution)/shard_map/ppermute | solution.py:305
  15.5 0.8 constant_dynamic-update-slice_fusion.3
  16.3 3.5 %collective-permute-start.5 = (bf16[160,512]{1,0:T(8,128)(2,1)S(1)}, bf16[160,512]{1,0:T(8,128)(2,1)S(1)}, u32[]{:S(2)}, u32[]{:S(2)}) collective-permute-start(bf16[160,512]{1,0:T(8,128)(2,1)S(1)} %get-tuple-element.78), channel_id=1, source_target_pairs={{0,8},{4,12},{8,0},{12,4},{16,24},{20,28},{24,16},{28,20},{1,9},{5... | collective-permute-start | bytes 491528 | tf_op jit(solution)/shard_map/ppermute | solution.py:310
  19.9 1.9 %collective-permute-start.6 = (bf16[160,512]{1,0:T(8,128)(2,1)S(1)}, bf16[160,512]{1,0:T(8,128)(2,1)S(1)}, u32[]{:S(2)}, u32[]{:S(2)}) collective-permute-start(bf16[160,512]{1,0:T(8,128)(2,1)S(1)} %get-tuple-element.78), channel_id=1, source_target_pairs={{0,16},{4,20},{8,24},{12,28},{16,0},{20,4},{24,8},{28,12},{1,17},{... | collective-permute-start | bytes 491528 | tf_op jit(solution)/shard_map/ppermute | solution.py:310
  21.7 2.5 %collective-permute-done.5 = bf16[160,512]{1,0:T(8,128)(2,1)S(1)} collective-permute-done((bf16[160,512]{1,0:T(8,128)(2,1)S(1)}, bf16[160,512]{1,0:T(8,128)(2,1)S(1)}, u32[]{:S(2)}, u32[]{:S(2)}) %collective-permute-start.5) | collective-permute-done | bytes 163872 | tf_op jit(solution)/shard_map/ppermute | solution.py:310
  24.2 3.9 %collective-permute-done.6 = bf16[160,512]{1,0:T(8,128)(2,1)S(1)} collective-permute-done((bf16[160,512]{1,0:T(8,128)(2,1)S(1)}, bf16[160,512]{1,0:T(8,128)(2,1)S(1)}, u32[]{:S(2)}, u32[]{:S(2)}) %collective-permute-start.6) | collective-permute-done | bytes 163872 | tf_op jit(solution)/shard_map/ppermute | solution.py:310
  28.4 2.8 %collective-permute-done.8.got_ref = bf16[1152,512]{1,0:T(8,128)(2,1)S(1)} collective-permute-done((bf16[1152,512]{1,0:T(8,128)(2,1)S(1)}, bf16[1152,512]{1,0:T(8,128)(2,1)S(1)}, u32[]{:S(2)}, u32[]{:S(2)}) %collective-permute-start.8) | collective-permute-done | bytes 1179680 | tf_op jit(solution)/shard_map/ppermute | solution.py:315
  31.2 49.8 %attention.1 = (bf16[256,2048]{1,0:T(8,128)(2,1)}, bf16[256,2048]{1,0:T(8,128)(2,1)}, f32[1408,512]{1,0:T(8,128)S(1)}, bf16[1152,512]{1,0:T(8,128)(2,1)S(1)}) custom-call(s32[8]{0:T(128)S(1)} %copy-done.3, bf16[256,2048]{1,0:T(8,128)(2,1)S(1)} %copy-done.1, bf16[256,2048]{1,0:T(8,128)(2,1)S(1)} %copy-done.1, bf16[256,2048]{1,0:T(8,128)(2,1)S(1)} %copy-done.2, ...), custom_call_target="tpu_custom_call" | custom-call | flops 16106127360 | bytes 4194304 | tf_op jit(solution)/shard_map/attention/pallas_call | solution.py:271
  81.1 0.1 collective-permute-start.9
  81.2 2.7 %collective-permute-done.9.got_ref = bf16[1152,512]{1,0:T(8,128)(2,1)S(1)} collective-permute-done((bf16[1152,512]{1,0:T(8,128)(2,1)S(1)}, bf16[1152,512]{1,0:T(8,128)(2,1)S(1)}, u32[]{:S(2)}, u32[]{:S(2)}) %collective-permute-start.9) | collective-permute-done | bytes 1179680 | tf_op jit(solution)/shard_map/ppermute | solution.py:315
  83.9 0.3 merge.1
  84.2 0.4 collective-permute-start.10
  84.7 1.6 %collective-permute-start.11 = (bf16[160,512]{1,0:T(8,128)(2,1)S(1)}, bf16[160,512]{1,0:T(8,128)(2,1)S(1)}, u32[]{:S(2)}, u32[]{:S(2)}) collective-permute-start(bf16[160,512]{1,0:T(8,128)(2,1)S(1)} %get-tuple-element.60), channel_id=1, source_target_pairs={{0,16},{4,20},{8,24},{12,28},{16,0},{20,4},{24,8},{28,12},{1,17},{... | collective-permute-start | bytes 491528 | tf_op jit(solution)/shard_map/ppermute | solution.py:310
  86.3 1.5 %collective-permute-start.12 = (bf16[160,512]{1,0:T(8,128)(2,1)S(1)}, bf16[160,512]{1,0:T(8,128)(2,1)S(1)}, u32[]{:S(2)}, u32[]{:S(2)}) collective-permute-start(bf16[160,512]{1,0:T(8,128)(2,1)S(1)} %get-tuple-element.61), channel_id=1, source_target_pairs={{0,24},{4,28},{8,16},{12,20},{16,8},{20,12},{24,0},{28,4},{1,25},{... | collective-permute-start | bytes 491528 | tf_op jit(solution)/shard_map/ppermute | solution.py:310
  87.8 3.6 %collective-permute-done.10.refs_1_ = bf16[160,512]{1,0:T(8,128)(2,1)S(1)} collective-permute-done((bf16[160,512]{1,0:T(8,128)(2,1)S(1)}, bf16[160,512]{1,0:T(8,128)(2,1)S(1)}, u32[]{:S(2)}, u32[]{:S(2)}) %collective-permute-start.10) | collective-permute-done | bytes 163872 | tf_op jit(solution)/shard_map/ppermute | solution.py:310
  91.4 3.8 %collective-permute-done.12.refs_3_ = bf16[160,512]{1,0:T(8,128)(2,1)S(1)} collective-permute-done((bf16[160,512]{1,0:T(8,128)(2,1)S(1)}, bf16[160,512]{1,0:T(8,128)(2,1)S(1)}, u32[]{:S(2)}, u32[]{:S(2)}) %collective-permute-start.12) | collective-permute-done | bytes 163872 | tf_op jit(solution)/shard_map/ppermute | solution.py:310
  95.1 2.6 %collective-permute-start.13 = (bf16[256,512]{1,0:T(8,128)(2,1)S(1)}, bf16[256,512]{1,0:T(8,128)(2,1)S(1)}, u32[]{:S(2)}, u32[]{:S(2)}) collective-permute-start(bf16[256,512]{1,0:T(8,128)(2,1)S(1)} %get-tuple-element.64), channel_id=1, source_target_pairs={{8,0},{12,4},{16,8},{20,12},{24,16},{28,20},{9,1},{13,5},{17,9},{2... | collective-permute-start | bytes 786440 | tf_op jit(solution)/shard_map/ppermute | solution.py:321
  97.7 3.5 %collective-permute-start.14 = (bf16[256,512]{1,0:T(8,128)(2,1)S(1)}, bf16[256,512]{1,0:T(8,128)(2,1)S(1)}, u32[]{:S(2)}, u32[]{:S(2)}) collective-permute-start(bf16[256,512]{1,0:T(8,128)(2,1)S(1)} %get-tuple-element.65), channel_id=1, source_target_pairs={{16,0},{20,4},{24,8},{28,12},{17,1},{21,5},{25,9},{29,13},{18,2},{... | collective-permute-start | bytes 786440 | tf_op jit(solution)/shard_map/ppermute | solution.py:321
  101.3 0.1 sum_chips.1
  101.4 0.5 collective-permute-start.15
  101.9 2.6 %collective-permute-start.16 = (bf16[40,512]{1,0:T(8,128)(2,1)S(1)}, bf16[40,512]{1,0:T(8,128)(2,1)S(1)}, u32[]{:S(2)}, u32[]{:S(2)}) collective-permute-start(bf16[40,512]{1,0:T(8,128)(2,1)S(1)} %get-tuple-element.72), channel_id=1, source_target_pairs={{0,2},{1,3},{2,0},{3,1},{4,6},{5,7},{6,4},{7,5},{8,10},{9,11},{10,... | collective-permute-start | bytes 122888 | tf_op jit(solution)/shard_map/ppermute | solution.py:305
  104.5 1.3 %collective-permute-start.17 = (bf16[40,512]{1,0:T(8,128)(2,1)S(1)}, bf16[40,512]{1,0:T(8,128)(2,1)S(1)}, u32[]{:S(2)}, u32[]{:S(2)}) collective-permute-start(bf16[40,512]{1,0:T(8,128)(2,1)S(1)} %get-tuple-element.73), channel_id=1, source_target_pairs={{0,3},{1,2},{2,1},{3,0},{4,7},{5,6},{6,5},{7,4},{8,11},{9,10},{10,... | collective-permute-start | bytes 122888 | tf_op jit(solution)/shard_map/ppermute | solution.py:305
  105.8 1.4 %collective-permute-done.16.refs_2_ = bf16[40,512]{1,0:T(8,128)(2,1)S(1)} collective-permute-done((bf16[40,512]{1,0:T(8,128)(2,1)S(1)}, bf16[40,512]{1,0:T(8,128)(2,1)S(1)}, u32[]{:S(2)}, u32[]{:S(2)}) %collective-permute-start.16) | collective-permute-done | bytes 40992 | tf_op jit(solution)/shard_map/ppermute | solution.py:305
  107.3 3.1 %collective-permute-done.17.refs_3_ = bf16[40,512]{1,0:T(8,128)(2,1)S(1)} collective-permute-done((bf16[40,512]{1,0:T(8,128)(2,1)S(1)}, bf16[40,512]{1,0:T(8,128)(2,1)S(1)}, u32[]{:S(2)}, u32[]{:S(2)}) %collective-permute-start.17) | collective-permute-done | bytes 40992 | tf_op jit(solution)/shard_map/ppermute | solution.py:305
  110.3 0.8 finish.1
  (26 shorter events, 0.3 us)
Async XLA Ops:
  2.5 25.7 %copy-start = (bf16[256,512]{1,0:T(8,128)(2,1)S(1)}, bf16[256,512]{1,0:T(8,128)(2,1)}, u32[]{:S(2)}) copy-start(bf16[256,512]{1,0:T(8,128)(2,1)} %get-tuple-element.46.own_ref) | copy-start | bytes 786436
  2.5 13.0 %collective-permute-start.4 = (bf16[256,512]{1,0:T(8,128)(2,1)}, bf16[256,512]{1,0:T(8,128)(2,1)S(1)}, u32[]{:S(2)}, u32[]{:S(2)}) collective-permute-start(bf16[256,512]{1,0:T(8,128)(2,1)} %get-tuple-element.46.own_ref), channel_id=1, source_target_pairs={{0,16},{4,20},{8,24},{12,28},{1,17},{5,21},{9,25},{13,29},{2,18},{... | collective-permute-start | bytes 786440 | tf_op jit(solution)/shard_map/ppermute | solution.py:321
  3.9 11.5 %collective-permute-start.3 = (bf16[256,512]{1,0:T(8,128)(2,1)}, bf16[256,512]{1,0:T(8,128)(2,1)S(1)}, u32[]{:S(2)}, u32[]{:S(2)}) collective-permute-start(bf16[256,512]{1,0:T(8,128)(2,1)} %get-tuple-element.46.own_ref), channel_id=1, source_target_pairs={{0,8},{4,12},{8,16},{12,20},{16,24},{20,28},{1,9},{5,13},{9,17},{1... | collective-permute-start | bytes 786440 | tf_op jit(solution)/shard_map/ppermute | solution.py:321
  5.2 4.5 %collective-permute-start = (bf16[40,512]{1,0:T(8,128)(2,1)}, bf16[40,512]{1,0:T(8,128)(2,1)S(1)}, u32[]{:S(2)}, u32[]{:S(2)}) collective-permute-start(bf16[40,512]{1,0:T(8,128)(2,1)} %get-tuple-element.43), channel_id=1, source_target_pairs={{0,1},{1,0},{2,3},{3,2},{4,5},{5,4},{6,7},{7,6},{8,9},{9,8},{10,11... | collective-permute-start | bytes 122888 | tf_op jit(solution)/shard_map/ppermute | solution.py:305
  6.9 5.9 %collective-permute-start.1 = (bf16[40,512]{1,0:T(8,128)(2,1)}, bf16[40,512]{1,0:T(8,128)(2,1)S(1)}, u32[]{:S(2)}, u32[]{:S(2)}) collective-permute-start(bf16[40,512]{1,0:T(8,128)(2,1)} %get-tuple-element.44), channel_id=1, source_target_pairs={{0,2},{1,3},{2,0},{3,1},{4,6},{5,7},{6,4},{7,5},{8,10},{9,11},{10,... | collective-permute-start | bytes 122888 | tf_op jit(solution)/shard_map/ppermute | solution.py:305
  9.5 6.0 %collective-permute-start.2 = (bf16[40,512]{1,0:T(8,128)(2,1)}, bf16[40,512]{1,0:T(8,128)(2,1)S(1)}, u32[]{:S(2)}, u32[]{:S(2)}) collective-permute-start(bf16[40,512]{1,0:T(8,128)(2,1)} %get-tuple-element.45), channel_id=1, source_target_pairs={{0,3},{1,2},{2,1},{3,0},{4,7},{5,6},{6,5},{7,4},{8,11},{9,10},{10,... | collective-permute-start | bytes 122888 | tf_op jit(solution)/shard_map/ppermute | solution.py:305
  16.3 14.9 %copy-start.1 = (bf16[256,2048]{1,0:T(8,128)(2,1)S(1)}, bf16[256,2048]{1,0:T(8,128)(2,1)}, u32[]{:S(2)}) copy-start(bf16[256,2048]{1,0:T(8,128)(2,1)} %next_ref.1) | copy-start | bytes 3145732
  16.3 14.9 %copy-start.3 = (s32[8]{0:T(128)S(1)}, s32[8]{0:T(128)}, u32[]{:S(2)}) copy-start(s32[8]{0:T(128)} %lengths.1) | copy-start | bytes 100
  16.3 7.9 %collective-permute-start.5 = (bf16[160,512]{1,0:T(8,128)(2,1)S(1)}, bf16[160,512]{1,0:T(8,128)(2,1)S(1)}, u32[]{:S(2)}, u32[]{:S(2)}) collective-permute-start(bf16[160,512]{1,0:T(8,128)(2,1)S(1)} %get-tuple-element.78), channel_id=1, source_target_pairs={{0,8},{4,12},{8,0},{12,4},{16,24},{20,28},{24,16},{28,20},{1,9},{5... | collective-permute-start | bytes 491528 | tf_op jit(solution)/shard_map/ppermute | solution.py:310
  19.9 8.3 %collective-permute-start.6 = (bf16[160,512]{1,0:T(8,128)(2,1)S(1)}, bf16[160,512]{1,0:T(8,128)(2,1)S(1)}, u32[]{:S(2)}, u32[]{:S(2)}) collective-permute-start(bf16[160,512]{1,0:T(8,128)(2,1)S(1)} %get-tuple-element.78), channel_id=1, source_target_pairs={{0,16},{4,20},{8,24},{12,28},{16,0},{20,4},{24,8},{28,12},{1,17},{... | collective-permute-start | bytes 491528 | tf_op jit(solution)/shard_map/ppermute | solution.py:310
  21.7 9.5 %copy-start.2 = (bf16[256,2048]{1,0:T(8,128)(2,1)S(1)}, bf16[256,2048]{1,0:T(8,128)(2,1)}, u32[]{:S(2)}) copy-start(bf16[256,2048]{1,0:T(8,128)(2,1)} %do_ref.1) | copy-start | bytes 3145732
  21.7 6.5 %collective-permute-start.7 = (bf16[160,512]{1,0:T(8,128)(2,1)S(1)}, bf16[160,512]{1,0:T(8,128)(2,1)S(1)}, u32[]{:S(2)}, u32[]{:S(2)}) collective-permute-start(bf16[160,512]{1,0:T(8,128)(2,1)S(1)} %get-tuple-element.78), channel_id=1, source_target_pairs={{0,24},{4,28},{8,16},{12,20},{16,8},{20,12},{24,0},{28,4},{1,25},{... | collective-permute-start | bytes 491528 | tf_op jit(solution)/shard_map/ppermute | solution.py:310
  28.3 2.9 %collective-permute-start.8 = (bf16[1152,512]{1,0:T(8,128)(2,1)S(1)}, bf16[1152,512]{1,0:T(8,128)(2,1)S(1)}, u32[]{:S(2)}, u32[]{:S(2)}) collective-permute-start(bf16[1152,512]{1,0:T(8,128)(2,1)S(1)} %select_dynamic-update-slice_fusion.sent_ref), channel_id=1, source_target_pairs={{0,4},{4,0},{8,12},{12,8},{16,20},{20,16},{24,28},{28,24},{1,5},{5... | collective-permute-start | bytes 3538952 | tf_op jit(solution)/shard_map/ppermute | solution.py:315
  81.1 2.8 %collective-permute-start.9 = (bf16[1152,512]{1,0:T(8,128)(2,1)S(1)}, bf16[1152,512]{1,0:T(8,128)(2,1)S(1)}, u32[]{:S(2)}, u32[]{:S(2)}) collective-permute-start(bf16[1152,512]{1,0:T(8,128)(2,1)S(1)} %get-tuple-element.56), channel_id=1, source_target_pairs={{0,4},{4,0},{8,12},{12,8},{16,20},{20,16},{24,28},{28,24},{1,5},{5... | collective-permute-start | bytes 3538952 | tf_op jit(solution)/shard_map/ppermute | solution.py:315
  84.2 7.1 %collective-permute-start.10 = (bf16[160,512]{1,0:T(8,128)(2,1)S(1)}, bf16[160,512]{1,0:T(8,128)(2,1)S(1)}, u32[]{:S(2)}, u32[]{:S(2)}) collective-permute-start(bf16[160,512]{1,0:T(8,128)(2,1)S(1)} %get-tuple-element.59), channel_id=1, source_target_pairs={{0,8},{4,12},{8,0},{12,4},{16,24},{20,28},{24,16},{28,20},{1,9},{5... | collective-permute-start | bytes 491528 | tf_op jit(solution)/shard_map/ppermute | solution.py:310
  84.7 6.7 %collective-permute-start.11 = (bf16[160,512]{1,0:T(8,128)(2,1)S(1)}, bf16[160,512]{1,0:T(8,128)(2,1)S(1)}, u32[]{:S(2)}, u32[]{:S(2)}) collective-permute-start(bf16[160,512]{1,0:T(8,128)(2,1)S(1)} %get-tuple-element.60), channel_id=1, source_target_pairs={{0,16},{4,20},{8,24},{12,28},{16,0},{20,4},{24,8},{28,12},{1,17},{... | collective-permute-start | bytes 491528 | tf_op jit(solution)/shard_map/ppermute | solution.py:310
  86.3 8.9 %collective-permute-start.12 = (bf16[160,512]{1,0:T(8,128)(2,1)S(1)}, bf16[160,512]{1,0:T(8,128)(2,1)S(1)}, u32[]{:S(2)}, u32[]{:S(2)}) collective-permute-start(bf16[160,512]{1,0:T(8,128)(2,1)S(1)} %get-tuple-element.61), channel_id=1, source_target_pairs={{0,24},{4,28},{8,16},{12,20},{16,8},{20,12},{24,0},{28,4},{1,25},{... | collective-permute-start | bytes 491528 | tf_op jit(solution)/shard_map/ppermute | solution.py:310
  95.1 15.2 %collective-permute-start.13 = (bf16[256,512]{1,0:T(8,128)(2,1)S(1)}, bf16[256,512]{1,0:T(8,128)(2,1)S(1)}, u32[]{:S(2)}, u32[]{:S(2)}) collective-permute-start(bf16[256,512]{1,0:T(8,128)(2,1)S(1)} %get-tuple-element.64), channel_id=1, source_target_pairs={{8,0},{12,4},{16,8},{20,12},{24,16},{28,20},{9,1},{13,5},{17,9},{2... | collective-permute-start | bytes 786440 | tf_op jit(solution)/shard_map/ppermute | solution.py:321
  97.7 12.6 %collective-permute-start.14 = (bf16[256,512]{1,0:T(8,128)(2,1)S(1)}, bf16[256,512]{1,0:T(8,128)(2,1)S(1)}, u32[]{:S(2)}, u32[]{:S(2)}) collective-permute-start(bf16[256,512]{1,0:T(8,128)(2,1)S(1)} %get-tuple-element.65), channel_id=1, source_target_pairs={{16,0},{20,4},{24,8},{28,12},{17,1},{21,5},{25,9},{29,13},{18,2},{... | collective-permute-start | bytes 786440 | tf_op jit(solution)/shard_map/ppermute | solution.py:321
  101.4 4.5 %collective-permute-start.15 = (bf16[40,512]{1,0:T(8,128)(2,1)S(1)}, bf16[40,512]{1,0:T(8,128)(2,1)S(1)}, u32[]{:S(2)}, u32[]{:S(2)}) collective-permute-start(bf16[40,512]{1,0:T(8,128)(2,1)S(1)} %get-tuple-element.71), channel_id=1, source_target_pairs={{0,1},{1,0},{2,3},{3,2},{4,5},{5,4},{6,7},{7,6},{8,9},{9,8},{10,11... | collective-permute-start | bytes 122888 | tf_op jit(solution)/shard_map/ppermute | solution.py:305
  101.9 5.3 %collective-permute-start.16 = (bf16[40,512]{1,0:T(8,128)(2,1)S(1)}, bf16[40,512]{1,0:T(8,128)(2,1)S(1)}, u32[]{:S(2)}, u32[]{:S(2)}) collective-permute-start(bf16[40,512]{1,0:T(8,128)(2,1)S(1)} %get-tuple-element.72), channel_id=1, source_target_pairs={{0,2},{1,3},{2,0},{3,1},{4,6},{5,7},{6,4},{7,5},{8,10},{9,11},{10,... | collective-permute-start | bytes 122888 | tf_op jit(solution)/shard_map/ppermute | solution.py:305
  104.5 5.8 %collective-permute-start.17 = (bf16[40,512]{1,0:T(8,128)(2,1)S(1)}, bf16[40,512]{1,0:T(8,128)(2,1)S(1)}, u32[]{:S(2)}, u32[]{:S(2)}) collective-permute-start(bf16[40,512]{1,0:T(8,128)(2,1)S(1)} %get-tuple-element.73), channel_id=1, source_target_pairs={{0,3},{1,2},{2,1},{3,0},{4,7},{5,6},{6,5},{7,4},{8,11},{9,10},{10,... | collective-permute-start | bytes 122888 | tf_op jit(solution)/shard_map/ppermute | solution.py:305

commit v4 on v2

--- a/solution.py
+++ b/solution.py
@@ -11,7 +11,9 @@
 HD = 128
 CORES = 2
 FAR = 4
-CHUNK = 256
+TILE = 128
+MOST_HEADS = 2
+MOST_SCORES = 4 * 2560 * 256
 NEG = -1e30
 BF16 = jnp.bfloat16
 F32 = jnp.float32
@@ -116,9 +118,11 @@
 def attention_kernel(
     tokens, lengths, q_ref, do_ref, sent_ref, got_ref, own_ref, far_ref,
     o_ref, dq_ref, kept_ref, back_ref,
-    bias, keys, values, keys_t, values_t, s_buf, p_buf, dk, dv,
+    bias, keys, values, keys_t, values_t, q_t, cot_t, q_all, cot_all,
+    s_buf, g_buf, p_buf, d_buf, dk, dv,
 ):
     total_keys = keys.shape[0]
+    heads = q_ref.shape[1] // HD
     prompt_len = total_keys - 5 * tokens
     half = prompt_len // 2
     head = pl.program_id(0)
@@ -129,15 +133,7 @@
     k_cols = pl.ds(pl.multiple_of(head * 2 * HD, HD), HD)
     v_cols = pl.ds(pl.multiple_of(head * 2 * HD + HD, HD), HD)
     resp_at = [prompt_len + i * tokens for i in range(6)]
-    pieces = [
-        (sent_ref, 0, half, 0),
-        (got_ref, 0, half, half),
-        (own_ref, 0, tokens, resp_at[0]),
-        (sent_ref, half, tokens, resp_at[1]),
-        (far_ref, 0, tokens, resp_at[2]),
-        (got_ref, half, tokens, resp_at[3]),
-        (got_ref, half + tokens, tokens, resp_at[4]),
-    ]
+    tiles = [slice(at, at + TILE) for at in range(0, total_keys, TILE)]
 
     @pl.when((step == 0) & (head == 0))
     def _():
@@ -156,13 +152,21 @@
                 jnp.int32, (tokens, tokens), 0
             )
             allowed = (key_pos >= seg_start) & (key_pos <= row_pos)
-            bias[i] = jnp.where(allowed, 0.0, NEG)
+            bias[i * tokens : (i + 1) * tokens] = jnp.where(allowed, 0.0, NEG)
 
     @pl.when(step == 0)
     def _():
         dk[...] = jnp.zeros_like(dk)
         dv[...] = jnp.zeros_like(dv)
-        for ref, start, size, at in pieces:
+        for ref, start, size, at in (
+            (sent_ref, 0, half, 0),
+            (got_ref, 0, half, half),
+            (own_ref, 0, tokens, resp_at[0]),
+            (sent_ref, half, tokens, resp_at[1]),
+            (far_ref, 0, tokens, resp_at[2]),
+            (got_ref, half, tokens, resp_at[3]),
+            (got_ref, half + tokens, tokens, resp_at[4]),
+        ):
             k_rows = ref[start : start + size, k_cols]
             v_rows = ref[start : start + size, v_cols]
             keys[at : at + size] = k_rows
@@ -170,56 +174,70 @@
             keys_t[:, at : at + size] = k_rows.T
             values_t[:, at : at + size] = v_rows.T
 
-    q = q_ref[...]
-    q_t = q.T
-    chunks = [slice(at, at + CHUNK) for at in range(0, total_keys, CHUNK)]
-    top = None
-    for at in chunks:
-        s = dot(keys[at], q_t)
+    def lanes(h):
+        return slice(h * tokens, (h + 1) * tokens)
+
+    def cols(h):
+        return slice(h * HD, (h + 1) * HD)
+
+    for h in range(heads):
+        q_t[:, lanes(h)] = q_ref[:, cols(h)].T
+        cot_t[:, lanes(h)] = do_ref[:, cols(h)].T
+    s_buf[...] = dot(keys[...], q_t[...])
+    g_buf[...] = dot(values[...], cot_t[...])
+
+    def scores(at, h):
+        s = s_buf[at, lanes(h)]
         if at.start >= prompt_len:
-            s = s + bias[(at.start - prompt_len) // tokens]
-        s_buf[at] = s
-        part = jnp.max(s.reshape(CHUNK // 8, 8, tokens), axis=0)
-        top = part if top is None else jnp.maximum(top, part)
-    top = jnp.max(top, axis=0, keepdims=True) * exp_scale
-
-    total = jnp.zeros((8, tokens), F32)
-    out = jnp.zeros((HD, tokens), F32)
-    for at in chunks:
-        p = jnp.exp2(s_buf[at] * exp_scale - top)
-        total = total + jnp.sum(p.reshape(CHUNK // 8, 8, tokens), axis=0)
-        p = p.astype(BF16)
-        p_buf[at] = p
-        out = out + dot(values_t[:, at], p)
-    inverse = 1.0 / jnp.sum(total, axis=0, keepdims=True)
-    out = (out * inverse).astype(BF16)
-    o_ref[...] = out.T
-    cot_t = (do_ref[...].T.astype(F32) * inverse).astype(BF16)
-    delta = jnp.sum(cot_t.astype(F32) * out.astype(F32), axis=0, keepdims=True)
-    cot = cot_t.T
-    dq = jnp.zeros((HD, tokens), F32)
-    for at in chunks:
-        p = p_buf[at]
-        dp = dot(values[at], cot_t)
-        ds = (p.astype(F32) * (dp - delta)).astype(BF16)
-        dq = dq + dot(keys_t[:, at], ds)
-        dv[at] += dot(p, cot)
-        dk[at] += dot(ds, q)
-    dq_ref[...] = (dq * score_scale).T.astype(BF16)
-
-    targets = [
-        (kept_ref, 0, half, 0),
-        (back_ref, 0, half, half),
-        (kept_ref, half + 2 * tokens, tokens, resp_at[0]),
-        (kept_ref, half, tokens, resp_at[1]),
-        (kept_ref, half + tokens, tokens, resp_at[2]),
-        (back_ref, half, tokens, resp_at[3]),
-        (back_ref, half + tokens, tokens, resp_at[4]),
-    ]
+            s = s + bias[at.start - prompt_len : at.stop - prompt_len]
+        return s
+
+    totals = []
+    for h in range(heads):
+        top = None
+        for at in tiles:
+            part = jnp.max(scores(at, h).reshape(TILE // 8, 8, tokens), axis=0)
+            top = part if top is None else jnp.maximum(top, part)
+        top = jnp.max(top, axis=0, keepdims=True) * exp_scale
+        total = None
+        for at in tiles:
+            p = jnp.exp2(scores(at, h) * exp_scale - top)
+            part = jnp.sum(p.reshape(TILE // 8, 8, tokens), axis=0)
+            total = part if total is None else total + part
+            p_buf[at, lanes(h)] = p.astype(BF16)
+        totals.append(total)
+    out_t = dot(values_t[...], p_buf[...])
+    inverses = []
+    for h in range(heads):
+        inverse = 1.0 / jnp.sum(totals[h], axis=0, keepdims=True)
+        inverses.append(inverse)
+        out = (out_t[:, lanes(h)] * inverse).astype(BF16)
+        o_ref[:, cols(h)] = out.T
+        wide = cot_t[:, lanes(h)].astype(F32)
+        delta = jnp.sum(wide * out.astype(F32), axis=0, keepdims=True)
+        cot_all[lanes(h)] = (wide * inverse).astype(BF16).T
+        q_all[lanes(h)] = (q_t[:, lanes(h)].astype(F32) * inverse).astype(BF16).T
+        for at in tiles:
+            p = p_buf[at, lanes(h)].astype(F32)
+            d_buf[at, lanes(h)] = (p * (g_buf[at, lanes(h)] - delta)).astype(BF16)
+    dv[...] += dot(p_buf[...], cot_all[...])
+    dk[...] += dot(d_buf[...], q_all[...])
+    dq_t = dot(keys_t[...], d_buf[...])
+    for h in range(heads):
+        dq = (dq_t[:, lanes(h)] * (inverses[h] * score_scale)).astype(BF16)
+        dq_ref[:, cols(h)] = dq.T
 
     @pl.when(step == last)
     def _():
-        for ref, start, size, at in targets:
+        for ref, start, size, at in (
+            (kept_ref, 0, half, 0),
+            (back_ref, 0, half, half),
+            (kept_ref, half + 2 * tokens, tokens, resp_at[0]),
+            (kept_ref, half, tokens, resp_at[1]),
+            (kept_ref, half + tokens, tokens, resp_at[2]),
+            (back_ref, half, tokens, resp_at[3]),
+            (back_ref, half + tokens, tokens, resp_at[4]),
+        ):
             ref[start : start + size, k_cols] = (dk[at : at + size] * score_scale).astype(ref.dtype)
             ref[start : start + size, v_cols] = dv[at : at + size].astype(ref.dtype)
 
@@ -229,9 +247,14 @@
     half = sent.shape[0] - 2 * tokens
     total_keys = 2 * half + 5 * tokens
     kv_heads = sent.shape[1] // (2 * HD)
-    steps = resp_q.shape[1] // HD // kv_heads
-    head_spec = pl.BlockSpec((tokens, HD), lambda n, g: (0, n * steps + g))
-    pairs = tokens * kv_heads * steps * total_keys
+    q_heads = resp_q.shape[1] // HD
+    heads = 1
+    while heads < MOST_HEADS and 2 * heads * total_keys * tokens <= MOST_SCORES:
+        heads = 2 * heads
+    steps = q_heads // kv_heads // heads
+    lanes = heads * tokens
+    head_spec = pl.BlockSpec((tokens, heads * HD), lambda n, g: (0, n * steps + g))
+    pairs = tokens * q_heads * total_keys
     return pl.pallas_call(
         functools.partial(attention_kernel, tokens),
         grid=(kv_heads, steps),
@@ -244,17 +267,23 @@
             jax.ShapeDtypeStruct((half + 2 * tokens, sent.shape[1]), BF16),
         ],
         scratch_shapes=[
-            pltpu.VMEM((5, tokens, tokens), F32),
+            pltpu.VMEM((5 * tokens, tokens), F32),
             pltpu.VMEM((total_keys, HD), BF16),
             pltpu.VMEM((total_keys, HD), BF16),
             pltpu.VMEM((HD, total_keys), BF16),
             pltpu.VMEM((HD, total_keys), BF16),
-            pltpu.VMEM((total_keys, tokens), F32),
-            pltpu.VMEM((total_keys, tokens), BF16),
+            pltpu.VMEM((HD, lanes), BF16),
+            pltpu.VMEM((HD, lanes), BF16),
+            pltpu.VMEM((lanes, HD), BF16),
+            pltpu.VMEM((lanes, HD), BF16),
+            pltpu.VMEM((total_keys, lanes), F32),
+            pltpu.VMEM((total_keys, lanes), F32),
+            pltpu.VMEM((total_keys, lanes), BF16),
+            pltpu.VMEM((total_keys, lanes), BF16),
             pltpu.VMEM((total_keys, HD), F32),
             pltpu.VMEM((total_keys, HD), F32),
         ],
-        compiler_params=pltpu.CompilerParams(vmem_limit_bytes=44 * 1024 * 1024),
+        compiler_params=pltpu.CompilerParams(vmem_limit_bytes=50 * 1024 * 1024),
         cost_estimate=pl.CostEstimate(
             flops=12 * HD * pairs, bytes_accessed=8 * resp_q.size, transcendentals=pairs
         ),

time: 121 us -> 124 us (1.025)
  local copies, waits for them, and re-layouts: 0.89 us -> 8.91 us
  Pallas kernels: 61.3 us -> 56.8 us
    unnamed x15 -> x19, local copies, waits for them, and re-layouts: 0.88 us -> 8.29 us
    pallas_call x1, Pallas kernels: 58.2 us -> 53.7 us  [attention(): pl.pallas_call(functools.partial(attention_kernel, tokens), grid=(kv_head...]
  transfers between devices with their start and end apart: 18 -> 18, of which waited for: 10 -> 10; matrix products, arithmetic and copies ran while one was open for 0% -> 1% of each run, Pallas kernels for 0% -> 0%
where the time goes in v4:
time: 124 us; the launch traced here: 123 us
  Pallas kernels  56.8 us (46%)
  waiting for transfers between devices  29.2 us (24%)
  starting transfers between devices  26.8 us (22%)
  local copies, waits for them, and re-layouts  8.91 us (7%)
    pallas_call x1, Pallas kernels, attention(): pl.pallas_call(functools.partial(attention_kernel, tokens), grid=(kv_head...  53.7 us
    ppermute x6, waiting for transfers between devices, swap_chips(): lax.ppermute(array, 'seq', [(i, i ^ by * CORES) for i in range(devices)])  13.1 us
    ppermute x6, waiting for transfers between devices, swap_heads(): return lax.ppermute(array, 'head', [(i, i ^ by) for i in range(devices)])  10.3 us
    ppermute x6, starting transfers between devices, swap_heads(): return lax.ppermute(array, 'head', [(i, i ^ by) for i in range(devices)])  8.9 us
    ppermute x6, starting transfers between devices, swap_chips(): lax.ppermute(array, 'seq', [(i, i ^ by * CORES) for i in range(devices)])  8.86 us
    ppermute x4, starting transfers between devices, shift_chips(): lax.ppermute(array, 'seq', [(i, i + by) for i in range(devices) if 0 <= i...  8.83 us
    unnamed x19, local copies, waits for them, and re-layouts  8.29 us
    ppermute x2, waiting for transfers between devices, swap_cores(): return lax.ppermute(array, 'seq', [(i, i ^ 1) for i in range(devices)])  5.77 us
  transfers between devices with their start and end apart: 18, of which 10 were waited for; matrix products, arithmetic and copies ran while one was open for 1% of the time, Pallas kernels for 0%

profile of v4, /device:TPU:6, one launch (start us, length us, event | category | flops | bytes accessed | tf_op | source)
XLA Modules:
  0.0 123.1 jit_solution(2748975125557451691)
XLA Ops:
  0.6 1.9 %pack.1 = (bf16[40,512]{1,0:T(8,128)(2,1)}, bf16[40,512]{1,0:T(8,128)(2,1)}, bf16[40,512]{1,0:T(8,128)(2,1)}, bf16[40,512]{1,0:T(8,128)(2,1)}, bf16[256,512]{1,0:T(8,128)(2,1)}) custom-call(bf16[40,1024]{1,0:T(8,128)(2,1)} %pk_ref.1, bf16[40,1024]{1,0:T(8,128)(2,1)} %pv_ref.1, bf16[256,256]{1,0:T(8,128)(2,1)} %rk_ref.1, bf16[256,256]{1,0:T(8,128)(2,1)} %rv_ref.1), custom_call_target="tpu_custom_call" | custom-call | tf_op jit(solution)/shard_map/pack/pallas_call | solution.py:64
  2.5 1.4 %collective-permute-start.4 = (bf16[256,512]{1,0:T(8,128)(2,1)}, bf16[256,512]{1,0:T(8,128)(2,1)S(1)}, u32[]{:S(2)}, u32[]{:S(2)}) collective-permute-start(bf16[256,512]{1,0:T(8,128)(2,1)} %get-tuple-element.46.own_ref), channel_id=1, source_target_pairs={{0,16},{4,20},{8,24},{12,28},{1,17},{5,21},{9,25},{13,29},{2,18},{... | collective-permute-start | bytes 786440 | tf_op jit(solution)/shard_map/ppermute | solution.py:312
  3.9 1.3 %collective-permute-start.3 = (bf16[256,512]{1,0:T(8,128)(2,1)}, bf16[256,512]{1,0:T(8,128)(2,1)S(1)}, u32[]{:S(2)}, u32[]{:S(2)}) collective-permute-start(bf16[256,512]{1,0:T(8,128)(2,1)} %get-tuple-element.46.own_ref), channel_id=1, source_target_pairs={{0,8},{4,12},{8,16},{12,20},{16,24},{20,28},{1,9},{5,13},{9,17},{1... | collective-permute-start | bytes 786440 | tf_op jit(solution)/shard_map/ppermute | solution.py:312
  5.2 1.6 %collective-permute-start = (bf16[40,512]{1,0:T(8,128)(2,1)}, bf16[40,512]{1,0:T(8,128)(2,1)S(1)}, u32[]{:S(2)}, u32[]{:S(2)}) collective-permute-start(bf16[40,512]{1,0:T(8,128)(2,1)} %get-tuple-element.43), channel_id=1, source_target_pairs={{0,1},{1,0},{2,3},{3,2},{4,5},{5,4},{6,7},{7,6},{8,9},{9,8},{10,11... | collective-permute-start | bytes 122888 | tf_op jit(solution)/shard_map/ppermute | solution.py:296
  6.9 2.6 %collective-permute-start.1 = (bf16[40,512]{1,0:T(8,128)(2,1)}, bf16[40,512]{1,0:T(8,128)(2,1)S(1)}, u32[]{:S(2)}, u32[]{:S(2)}) collective-permute-start(bf16[40,512]{1,0:T(8,128)(2,1)} %get-tuple-element.44), channel_id=1, source_target_pairs={{0,2},{1,3},{2,0},{3,1},{4,6},{5,7},{6,4},{7,5},{8,10},{9,11},{10,... | collective-permute-start | bytes 122888 | tf_op jit(solution)/shard_map/ppermute | solution.py:296
  9.7 3.1 %collective-permute-done.1 = bf16[40,512]{1,0:T(8,128)(2,1)S(1)} collective-permute-done((bf16[40,512]{1,0:T(8,128)(2,1)}, bf16[40,512]{1,0:T(8,128)(2,1)S(1)}, u32[]{:S(2)}, u32[]{:S(2)}) %collective-permute-start.1) | collective-permute-done | bytes 40992 | tf_op jit(solution)/shard_map/ppermute | solution.py:296
  12.8 2.7 %collective-permute-done.2 = bf16[40,512]{1,0:T(8,128)(2,1)S(1)} collective-permute-done((bf16[40,512]{1,0:T(8,128)(2,1)}, bf16[40,512]{1,0:T(8,128)(2,1)S(1)}, u32[]{:S(2)}, u32[]{:S(2)}) %collective-permute-start.2) | collective-permute-done | bytes 40992 | tf_op jit(solution)/shard_map/ppermute | solution.py:296
  15.5 1.4 %constant_dynamic-update-slice_fusion.3 = (bf16[160,512]{1,0:T(8,128)(2,1)S(1)}, bf16[1152,512]{1,0:T(8,128)(2,1)}) fusion(bf16[40,512]{1,0:T(8,128)(2,1)} %get-tuple-element.47), kind=kLoop, calls=%fused_computation.4 | loop fusion | bytes 122880
  18.8 3.5 %collective-permute-start.5 = (bf16[160,512]{1,0:T(8,128)(2,1)S(1)}, bf16[160,512]{1,0:T(8,128)(2,1)S(1)}, u32[]{:S(2)}, u32[]{:S(2)}) collective-permute-start(bf16[160,512]{1,0:T(8,128)(2,1)S(1)} %get-tuple-element.78), channel_id=1, source_target_pairs={{0,8},{4,12},{8,0},{12,4},{16,24},{20,28},{24,16},{28,20},{1,9},{5... | collective-permute-start | bytes 491528 | tf_op jit(solution)/shard_map/ppermute | solution.py:301
  22.2 1.9 %collective-permute-start.6 = (bf16[160,512]{1,0:T(8,128)(2,1)S(1)}, bf16[160,512]{1,0:T(8,128)(2,1)S(1)}, u32[]{:S(2)}, u32[]{:S(2)}) collective-permute-start(bf16[160,512]{1,0:T(8,128)(2,1)S(1)} %get-tuple-element.78), channel_id=1, source_target_pairs={{0,16},{4,20},{8,24},{12,28},{16,0},{20,4},{24,8},{28,12},{1,17},{... | collective-permute-start | bytes 491528 | tf_op jit(solution)/shard_map/ppermute | solution.py:301
  24.1 2.5 %collective-permute-done.5 = bf16[160,512]{1,0:T(8,128)(2,1)S(1)} collective-permute-done((bf16[160,512]{1,0:T(8,128)(2,1)S(1)}, bf16[160,512]{1,0:T(8,128)(2,1)S(1)}, u32[]{:S(2)}, u32[]{:S(2)}) %collective-permute-start.5) | collective-permute-done | bytes 163872 | tf_op jit(solution)/shard_map/ppermute | solution.py:301
  27.2 3.3 %collective-permute-done.6 = bf16[160,512]{1,0:T(8,128)(2,1)S(1)} collective-permute-done((bf16[160,512]{1,0:T(8,128)(2,1)S(1)}, bf16[160,512]{1,0:T(8,128)(2,1)S(1)}, u32[]{:S(2)}, u32[]{:S(2)}) %collective-permute-start.6) | collective-permute-done | bytes 163872 | tf_op jit(solution)/shard_map/ppermute | solution.py:301
  30.5 0.7 constant_dynamic-update-slice_fusion.6
  31.2 0.7 constant_dynamic-update-slice_fusion.5
  31.9 0.7 constant_dynamic-update-slice_fusion.4
  32.6 0.8 select_dynamic-update-slice_fusion.sent_ref
  33.4 3.1 %collective-permute-done.8.got_ref = bf16[1152,512]{1,0:T(8,128)(2,1)S(1)} collective-permute-done((bf16[1152,512]{1,0:T(8,128)(2,1)}, bf16[1152,512]{1,0:T(8,128)(2,1)S(1)}, u32[]{:S(2)}, u32[]{:S(2)}) %collective-permute-start.8) | collective-permute-done | bytes 1179680 | tf_op jit(solution)/shard_map/ppermute | solution.py:306
  36.5 1.0 copy-done.5
  37.5 53.7 %attention.1 = (bf16[256,2048]{1,0:T(8,128)(2,1)}, bf16[256,2048]{1,0:T(8,128)(2,1)}, f32[1408,512]{1,0:T(8,128)}, bf16[1152,512]{1,0:T(8,128)(2,1)S(1)}) custom-call(s32[8]{0:T(128)S(1)} %copy-done.4, bf16[256,2048]{1,0:T(8,128)(2,1)S(1)} %copy-done.2, bf16[256,2048]{1,0:T(8,128)(2,1)S(1)} %copy-done.3, ...), custom_call_target="tpu_custom_call" | custom-call | flops 16106127360 | bytes 4194304 | tf_op jit(solution)/shard_map/attention/pallas_call | solution.py:258
  91.4 2.7 %collective-permute-done.9.got_ref = bf16[1152,512]{1,0:T(8,128)(2,1)S(1)} collective-permute-done((bf16[1152,512]{1,0:T(8,128)(2,1)S(1)}, bf16[1152,512]{1,0:T(8,128)(2,1)S(1)}, u32[]{:S(2)}, u32[]{:S(2)}) %collective-permute-start.9) | collective-permute-done | bytes 1179680 | tf_op jit(solution)/shard_map/ppermute | solution.py:306
  94.1 1.8 %copy-done = f32[1408,512]{1,0:T(8,128)S(1)} copy-done((f32[1408,512]{1,0:T(8,128)S(1)}, f32[1408,512]{1,0:T(8,128)}, u32[]{:S(2)}) %copy-start) | copy-done | bytes 2883608
  96.6 1.6 %collective-permute-start.11 = (bf16[160,512]{1,0:T(8,128)(2,1)S(1)}, bf16[160,512]{1,0:T(8,128)(2,1)S(1)}, u32[]{:S(2)}, u32[]{:S(2)}) collective-permute-start(bf16[160,512]{1,0:T(8,128)(2,1)S(1)} %get-tuple-element.60), channel_id=1, source_target_pairs={{0,16},{4,20},{8,24},{12,28},{16,0},{20,4},{24,8},{28,12},{1,17},{... | collective-permute-start | bytes 491528 | tf_op jit(solution)/shard_map/ppermute | solution.py:301
  98.2 1.6 %collective-permute-start.12 = (bf16[160,512]{1,0:T(8,128)(2,1)S(1)}, bf16[160,512]{1,0:T(8,128)(2,1)S(1)}, u32[]{:S(2)}, u32[]{:S(2)}) collective-permute-start(bf16[160,512]{1,0:T(8,128)(2,1)S(1)} %get-tuple-element.61), channel_id=1, source_target_pairs={{0,24},{4,28},{8,16},{12,20},{16,8},{20,12},{24,0},{28,4},{1,25},{... | collective-permute-start | bytes 491528 | tf_op jit(solution)/shard_map/ppermute | solution.py:301
  99.8 3.6 %collective-permute-done.10.refs_1_ = bf16[160,512]{1,0:T(8,128)(2,1)S(1)} collective-permute-done((bf16[160,512]{1,0:T(8,128)(2,1)S(1)}, bf16[160,512]{1,0:T(8,128)(2,1)S(1)}, u32[]{:S(2)}, u32[]{:S(2)}) %collective-permute-start.10) | collective-permute-done | bytes 163872 | tf_op jit(solution)/shard_map/ppermute | solution.py:301
  103.3 3.8 %collective-permute-done.12.refs_3_ = bf16[160,512]{1,0:T(8,128)(2,1)S(1)} collective-permute-done((bf16[160,512]{1,0:T(8,128)(2,1)S(1)}, bf16[160,512]{1,0:T(8,128)(2,1)S(1)}, u32[]{:S(2)}, u32[]{:S(2)}) %collective-permute-start.12) | collective-permute-done | bytes 163872 | tf_op jit(solution)/shard_map/ppermute | solution.py:301
  107.1 2.6 %collective-permute-start.13 = (bf16[256,512]{1,0:T(8,128)(2,1)S(1)}, bf16[256,512]{1,0:T(8,128)(2,1)S(1)}, u32[]{:S(2)}, u32[]{:S(2)}) collective-permute-start(bf16[256,512]{1,0:T(8,128)(2,1)S(1)} %get-tuple-element.64), channel_id=1, source_target_pairs={{8,0},{12,4},{16,8},{20,12},{24,16},{28,20},{9,1},{13,5},{17,9},{2... | collective-permute-start | bytes 786440 | tf_op jit(solution)/shard_map/ppermute | solution.py:312
  109.7 3.5 %collective-permute-start.14 = (bf16[256,512]{1,0:T(8,128)(2,1)S(1)}, bf16[256,512]{1,0:T(8,128)(2,1)S(1)}, u32[]{:S(2)}, u32[]{:S(2)}) collective-permute-start(bf16[256,512]{1,0:T(8,128)(2,1)S(1)} %get-tuple-element.65), channel_id=1, source_target_pairs={{16,0},{20,4},{24,8},{28,12},{17,1},{21,5},{25,9},{29,13},{18,2},{... | collective-permute-start | bytes 786440 | tf_op jit(solution)/shard_map/ppermute | solution.py:312
  113.9 2.6 %collective-permute-start.16 = (bf16[40,512]{1,0:T(8,128)(2,1)S(1)}, bf16[40,512]{1,0:T(8,128)(2,1)S(1)}, u32[]{:S(2)}, u32[]{:S(2)}) collective-permute-start(bf16[40,512]{1,0:T(8,128)(2,1)S(1)} %get-tuple-element.72), channel_id=1, source_target_pairs={{0,2},{1,3},{2,0},{3,1},{4,6},{5,7},{6,4},{7,5},{8,10},{9,11},{10,... | collective-permute-start | bytes 122888 | tf_op jit(solution)/shard_map/ppermute | solution.py:296
  116.5 1.3 %collective-permute-start.17 = (bf16[40,512]{1,0:T(8,128)(2,1)S(1)}, bf16[40,512]{1,0:T(8,128)(2,1)S(1)}, u32[]{:S(2)}, u32[]{:S(2)}) collective-permute-start(bf16[40,512]{1,0:T(8,128)(2,1)S(1)} %get-tuple-element.73), channel_id=1, source_target_pairs={{0,3},{1,2},{2,1},{3,0},{4,7},{5,6},{6,5},{7,4},{8,11},{9,10},{10,... | collective-permute-start | bytes 122888 | tf_op jit(solution)/shard_map/ppermute | solution.py:296
  117.8 1.4 %collective-permute-done.16.refs_2_ = bf16[40,512]{1,0:T(8,128)(2,1)S(1)} collective-permute-done((bf16[40,512]{1,0:T(8,128)(2,1)S(1)}, bf16[40,512]{1,0:T(8,128)(2,1)S(1)}, u32[]{:S(2)}, u32[]{:S(2)}) %collective-permute-start.16) | collective-permute-done | bytes 40992 | tf_op jit(solution)/shard_map/ppermute | solution.py:296
  119.2 3.1 %collective-permute-done.17.refs_3_ = bf16[40,512]{1,0:T(8,128)(2,1)S(1)} collective-permute-done((bf16[40,512]{1,0:T(8,128)(2,1)S(1)}, bf16[40,512]{1,0:T(8,128)(2,1)S(1)}, u32[]{:S(2)}, u32[]{:S(2)}) %collective-permute-start.17) | collective-permute-done | bytes 40992 | tf_op jit(solution)/shard_map/ppermute | solution.py:296
  122.3 0.8 finish.1
  (30 shorter events, 4.3 us)
Async XLA Ops:
  2.5 30.1 %copy-start.1 = (bf16[256,512]{1,0:T(8,128)(2,1)S(1)}, bf16[256,512]{1,0:T(8,128)(2,1)}, u32[]{:S(2)}) copy-start(bf16[256,512]{1,0:T(8,128)(2,1)} %get-tuple-element.46.own_ref) | copy-start | bytes 786436
  2.5 13.0 %collective-permute-start.4 = (bf16[256,512]{1,0:T(8,128)(2,1)}, bf16[256,512]{1,0:T(8,128)(2,1)S(1)}, u32[]{:S(2)}, u32[]{:S(2)}) collective-permute-start(bf16[256,512]{1,0:T(8,128)(2,1)} %get-tuple-element.46.own_ref), channel_id=1, source_target_pairs={{0,16},{4,20},{8,24},{12,28},{1,17},{5,21},{9,25},{13,29},{2,18},{... | collective-permute-start | bytes 786440 | tf_op jit(solution)/shard_map/ppermute | solution.py:312
  3.9 11.5 %collective-permute-start.3 = (bf16[256,512]{1,0:T(8,128)(2,1)}, bf16[256,512]{1,0:T(8,128)(2,1)S(1)}, u32[]{:S(2)}, u32[]{:S(2)}) collective-permute-start(bf16[256,512]{1,0:T(8,128)(2,1)} %get-tuple-element.46.own_ref), channel_id=1, source_target_pairs={{0,8},{4,12},{8,16},{12,20},{16,24},{20,28},{1,9},{5,13},{9,17},{1... | collective-permute-start | bytes 786440 | tf_op jit(solution)/shard_map/ppermute | solution.py:312
  5.2 4.5 %collective-permute-start = (bf16[40,512]{1,0:T(8,128)(2,1)}, bf16[40,512]{1,0:T(8,128)(2,1)S(1)}, u32[]{:S(2)}, u32[]{:S(2)}) collective-permute-start(bf16[40,512]{1,0:T(8,128)(2,1)} %get-tuple-element.43), channel_id=1, source_target_pairs={{0,1},{1,0},{2,3},{3,2},{4,5},{5,4},{6,7},{7,6},{8,9},{9,8},{10,11... | collective-permute-start | bytes 122888 | tf_op jit(solution)/shard_map/ppermute | solution.py:296
  6.9 5.9 %collective-permute-start.1 = (bf16[40,512]{1,0:T(8,128)(2,1)}, bf16[40,512]{1,0:T(8,128)(2,1)S(1)}, u32[]{:S(2)}, u32[]{:S(2)}) collective-permute-start(bf16[40,512]{1,0:T(8,128)(2,1)} %get-tuple-element.44), channel_id=1, source_target_pairs={{0,2},{1,3},{2,0},{3,1},{4,6},{5,7},{6,4},{7,5},{8,10},{9,11},{10,... | collective-permute-start | bytes 122888 | tf_op jit(solution)/shard_map/ppermute | solution.py:296
  9.5 6.0 %collective-permute-start.2 = (bf16[40,512]{1,0:T(8,128)(2,1)}, bf16[40,512]{1,0:T(8,128)(2,1)S(1)}, u32[]{:S(2)}, u32[]{:S(2)}) collective-permute-start(bf16[40,512]{1,0:T(8,128)(2,1)} %get-tuple-element.45), channel_id=1, source_target_pairs={{0,3},{1,2},{2,1},{3,0},{4,7},{5,6},{6,5},{7,4},{8,11},{9,10},{10,... | collective-permute-start | bytes 122888 | tf_op jit(solution)/shard_map/ppermute | solution.py:296
  18.7 18.8 %copy-start.2 = (bf16[256,2048]{1,0:T(8,128)(2,1)S(1)}, bf16[256,2048]{1,0:T(8,128)(2,1)}, u32[]{:S(2)}) copy-start(bf16[256,2048]{1,0:T(8,128)(2,1)} %q_ref.1) | copy-start | bytes 3145732
  18.7 18.8 %copy-start.3 = (bf16[256,2048]{1,0:T(8,128)(2,1)S(1)}, bf16[256,2048]{1,0:T(8,128)(2,1)}, u32[]{:S(2)}) copy-start(bf16[256,2048]{1,0:T(8,128)(2,1)} %do_ref.1) | copy-start | bytes 3145732
  18.7 18.8 %copy-start.4 = (s32[8]{0:T(128)S(1)}, s32[8]{0:T(128)}, u32[]{:S(2)}) copy-start(s32[8]{0:T(128)} %lengths.1) | copy-start | bytes 100
  18.8 7.8 %collective-permute-start.5 = (bf16[160,512]{1,0:T(8,128)(2,1)S(1)}, bf16[160,512]{1,0:T(8,128)(2,1)S(1)}, u32[]{:S(2)}, u32[]{:S(2)}) collective-permute-start(bf16[160,512]{1,0:T(8,128)(2,1)S(1)} %get-tuple-element.78), channel_id=1, source_target_pairs={{0,8},{4,12},{8,0},{12,4},{16,24},{20,28},{24,16},{28,20},{1,9},{5... | collective-permute-start | bytes 491528 | tf_op jit(solution)/shard_map/ppermute | solution.py:301
  22.2 8.3 %collective-permute-start.6 = (bf16[160,512]{1,0:T(8,128)(2,1)S(1)}, bf16[160,512]{1,0:T(8,128)(2,1)S(1)}, u32[]{:S(2)}, u32[]{:S(2)}) collective-permute-start(bf16[160,512]{1,0:T(8,128)(2,1)S(1)} %get-tuple-element.78), channel_id=1, source_target_pairs={{0,16},{4,20},{8,24},{12,28},{16,0},{20,4},{24,8},{28,12},{1,17},{... | collective-permute-start | bytes 491528 | tf_op jit(solution)/shard_map/ppermute | solution.py:301
  24.1 7.1 %collective-permute-start.7 = (bf16[160,512]{1,0:T(8,128)(2,1)S(1)}, bf16[160,512]{1,0:T(8,128)(2,1)S(1)}, u32[]{:S(2)}, u32[]{:S(2)}) collective-permute-start(bf16[160,512]{1,0:T(8,128)(2,1)S(1)} %get-tuple-element.78), channel_id=1, source_target_pairs={{0,24},{4,28},{8,16},{12,20},{16,8},{20,12},{24,0},{28,4},{1,25},{... | collective-permute-start | bytes 491528 | tf_op jit(solution)/shard_map/ppermute | solution.py:301
  33.4 3.1 %collective-permute-start.8 = (bf16[1152,512]{1,0:T(8,128)(2,1)}, bf16[1152,512]{1,0:T(8,128)(2,1)S(1)}, u32[]{:S(2)}, u32[]{:S(2)}) collective-permute-start(bf16[1152,512]{1,0:T(8,128)(2,1)} %select_dynamic-update-slice_fusion.sent_ref), channel_id=1, source_target_pairs={{0,4},{4,0},{8,12},{12,8},{16,20},{20,16},{24,28},{28,24},{1,5},{5... | collective-permute-start | bytes 3538952 | tf_op jit(solution)/shard_map/ppermute | solution.py:306
  36.5 1.0 copy-start.5
  91.2 2.9 %collective-permute-start.9 = (bf16[1152,512]{1,0:T(8,128)(2,1)S(1)}, bf16[1152,512]{1,0:T(8,128)(2,1)S(1)}, u32[]{:S(2)}, u32[]{:S(2)}) collective-permute-start(bf16[1152,512]{1,0:T(8,128)(2,1)S(1)} %get-tuple-element.56), channel_id=1, source_target_pairs={{0,4},{4,0},{8,12},{12,8},{16,20},{20,16},{24,28},{28,24},{1,5},{5... | collective-permute-start | bytes 3538952 | tf_op jit(solution)/shard_map/ppermute | solution.py:306
  94.1 1.8 %copy-start = (f32[1408,512]{1,0:T(8,128)S(1)}, f32[1408,512]{1,0:T(8,128)}, u32[]{:S(2)}) copy-start(f32[1408,512]{1,0:T(8,128)} %get-tuple-element.55.kept_ref) | copy-start | bytes 8650756
  96.2 7.1 %collective-permute-start.10 = (bf16[160,512]{1,0:T(8,128)(2,1)S(1)}, bf16[160,512]{1,0:T(8,128)(2,1)S(1)}, u32[]{:S(2)}, u32[]{:S(2)}) collective-permute-start(bf16[160,512]{1,0:T(8,128)(2,1)S(1)} %get-tuple-element.59), channel_id=1, source_target_pairs={{0,8},{4,12},{8,0},{12,4},{16,24},{20,28},{24,16},{28,20},{1,9},{5... | collective-permute-start | bytes 491528 | tf_op jit(solution)/shard_map/ppermute | solution.py:301
  96.6 6.7 %collective-permute-start.11 = (bf16[160,512]{1,0:T(8,128)(2,1)S(1)}, bf16[160,512]{1,0:T(8,128)(2,1)S(1)}, u32[]{:S(2)}, u32[]{:S(2)}) collective-permute-start(bf16[160,512]{1,0:T(8,128)(2,1)S(1)} %get-tuple-element.60), channel_id=1, source_target_pairs={{0,16},{4,20},{8,24},{12,28},{16,0},{20,4},{24,8},{28,12},{1,17},{... | collective-permute-start | bytes 491528 | tf_op jit(solution)/shard_map/ppermute | solution.py:301
  98.2 8.9 %collective-permute-start.12 = (bf16[160,512]{1,0:T(8,128)(2,1)S(1)}, bf16[160,512]{1,0:T(8,128)(2,1)S(1)}, u32[]{:S(2)}, u32[]{:S(2)}) collective-permute-start(bf16[160,512]{1,0:T(8,128)(2,1)S(1)} %get-tuple-element.61), channel_id=1, source_target_pairs={{0,24},{4,28},{8,16},{12,20},{16,8},{20,12},{24,0},{28,4},{1,25},{... | collective-permute-start | bytes 491528 | tf_op jit(solution)/shard_map/ppermute | solution.py:301
  107.1 15.2 %collective-permute-start.13 = (bf16[256,512]{1,0:T(8,128)(2,1)S(1)}, bf16[256,512]{1,0:T(8,128)(2,1)S(1)}, u32[]{:S(2)}, u32[]{:S(2)}) collective-permute-start(bf16[256,512]{1,0:T(8,128)(2,1)S(1)} %get-tuple-element.64), channel_id=1, source_target_pairs={{8,0},{12,4},{16,8},{20,12},{24,16},{28,20},{9,1},{13,5},{17,9},{2... | collective-permute-start | bytes 786440 | tf_op jit(solution)/shard_map/ppermute | solution.py:312
  109.7 12.6 %collective-permute-start.14 = (bf16[256,512]{1,0:T(8,128)(2,1)S(1)}, bf16[256,512]{1,0:T(8,128)(2,1)S(1)}, u32[]{:S(2)}, u32[]{:S(2)}) collective-permute-start(bf16[256,512]{1,0:T(8,128)(2,1)S(1)} %get-tuple-element.65), channel_id=1, source_target_pairs={{16,0},{20,4},{24,8},{28,12},{17,1},{21,5},{25,9},{29,13},{18,2},{... | collective-permute-start | bytes 786440 | tf_op jit(solution)/shard_map/ppermute | solution.py:312
  113.3 4.5 %collective-permute-start.15 = (bf16[40,512]{1,0:T(8,128)(2,1)S(1)}, bf16[40,512]{1,0:T(8,128)(2,1)S(1)}, u32[]{:S(2)}, u32[]{:S(2)}) collective-permute-start(bf16[40,512]{1,0:T(8,128)(2,1)S(1)} %get-tuple-element.71), channel_id=1, source_target_pairs={{0,1},{1,0},{2,3},{3,2},{4,5},{5,4},{6,7},{7,6},{8,9},{9,8},{10,11... | collective-permute-start | bytes 122888 | tf_op jit(solution)/shard_map/ppermute | solution.py:296
  113.9 5.3 %collective-permute-start.16 = (bf16[40,512]{1,0:T(8,128)(2,1)S(1)}, bf16[40,512]{1,0:T(8,128)(2,1)S(1)}, u32[]{:S(2)}, u32[]{:S(2)}) collective-permute-start(bf16[40,512]{1,0:T(8,128)(2,1)S(1)} %get-tuple-element.72), channel_id=1, source_target_pairs={{0,2},{1,3},{2,0},{3,1},{4,6},{5,7},{6,4},{7,5},{8,10},{9,11},{10,... | collective-permute-start | bytes 122888 | tf_op jit(solution)/shard_map/ppermute | solution.py:296
  116.5 5.8 %collective-permute-start.17 = (bf16[40,512]{1,0:T(8,128)(2,1)S(1)}, bf16[40,512]{1,0:T(8,128)(2,1)S(1)}, u32[]{:S(2)}, u32[]{:S(2)}) collective-permute-start(bf16[40,512]{1,0:T(8,128)(2,1)S(1)} %get-tuple-element.73), channel_id=1, source_target_pairs={{0,3},{1,2},{2,1},{3,0},{4,7},{5,6},{6,5},{7,4},{8,11},{9,10},{10,... | collective-permute-start | bytes 122888 | tf_op jit(solution)/shard_map/ppermute | solution.py:296

commit v5 on v3

--- a/solution.py
+++ b/solution.py
@@ -12,6 +12,8 @@
 CORES = 2
 FAR = 4
 CHUNK = 256
+ROWS = 64
+MOST_SCORES = 2560 * 256
 NEG = -1e30
 NT = (((1,), (1,)), ((), ()))
 BF16 = jnp.bfloat16
@@ -119,78 +121,150 @@
 
 
 def attention_kernel(
-    tokens, lengths, q_ref, next_ref, do_ref, sent_ref, got_ref, own_ref, far_ref,
+    tokens, halves, steps_per_kv,
+    lengths, q_ref, next_q_ref, do_ref, next_do_ref, sent_ref, got_ref, own_ref, far_ref,
     o_ref, dq_ref, kept_ref, back_ref,
-    bias, keys, values, s_even, s_odd, p_even, p_odd, top_even, dk_t, dv_t,
+    bias, keys, values, s_bufs, g_bufs, p_bufs, d_bufs, inv_bufs, scaled, q_ts, cot_ts, dk_t, dv_t,
 ):
-    total_keys = keys.shape[1]
+    kv_heads, total_keys = keys.shape[0], keys.shape[1]
+    rows = tokens // halves
     prompt_len = total_keys - 5 * tokens
     half = prompt_len // 2
-    head = pl.program_id(0)
-    step = pl.program_id(1)
-    last = pl.num_programs(1) - 1
+    step = pl.program_id(0)
+    last = pl.num_programs(0) - 1
     score_scale = 1.0 / math.sqrt(HD)
     exp_scale = score_scale * math.log2(math.e)
     resp_at = [prompt_len + i * tokens for i in range(6)]
     chunks = [slice(at, at + CHUNK) for at in range(0, total_keys, CHUNK)]
 
-    def front(q, at, which, s_buf, top):
-        s = dot_nt(q, keys[which, at])
-        if at.start >= prompt_len:
-            s = s + bias[(at.start - prompt_len) // tokens]
-        s_buf[:, at] = s
-        for col in range(0, CHUNK, HD):
-            part = s[:, col : col + HD]
-            top = part if top is None else jnp.maximum(top, part)
-        return top
-
-    def middle(at, s_buf, p_buf, top, total, out):
-        p = jnp.exp2(s_buf[:, at] * exp_scale - top)
-        for col in range(0, CHUNK, HD):
-            part = p[:, col : col + HD]
-            total = part if total is None else total + part
-        p = p.astype(BF16)
-        p_buf[:, at] = p
-        more = dot(p, values[head, at])
-        return total, more if out is None else out + more
-
-    def settle(q, cot, total, out):
-        inverse = 1.0 / jnp.sum(total, axis=1, keepdims=True)
-        out = (out * inverse).astype(BF16)
-        wide = cot.astype(F32)
-        delta = jnp.sum(wide * out.astype(F32), axis=1, keepdims=True)
-        cot_t = (wide * inverse).astype(BF16).T
-        q_t = (q.astype(F32) * inverse).astype(BF16).T
-        return inverse, out, delta, cot_t, q_t
-
-    def behind(at, p_buf, cot, delta, cot_t, q_t, dq):
-        p = p_buf[:, at]
-        dp = dot_nt(cot, values[head, at])
-        ds = (p.astype(F32) * (dp - delta)).astype(BF16)
-        dv_t[:, at] += dot(cot_t, p)
-        dk_t[:, at] += dot(q_t, ds)
-        more = dot(ds, keys[head, at])
-        return more if dq is None else dq + more
-
-    @pl.when((step == 0) & (head == 0))
+    def unit(ref, which):
+        if halves == 1:
+            return ref[:, which * HD : (which + 1) * HD]
+        return ref[which * rows : (which + 1) * rows, :HD]
+
+    def kv_of(at_step):
+        return jnp.clip(at_step // steps_per_kv, 0, kv_heads - 1)
+
+    def ahead(which, kv, q, cot):
+        def scores(at):
+            s_bufs[which, :, at] = dot_nt(q, keys[kv, at])
+
+        def grads(at):
+            g_bufs[which, :, at] = dot_nt(cot, values[kv, at])
+
+        return [functools.partial(f, at) for at in chunks for f in (scores, grads)]
+
+    def behind(which, kv, at_step):
+        head = jnp.maximum(at_step, 0) * (2 // halves) + (which if halves == 1 else 0)
+        cols = pl.ds(pl.multiple_of(head * HD, HD), HD)
+        rows_at = slice(0, rows) if halves == 1 else slice(which * rows, (which + 1) * rows)
+
+        def output():
+            out = dot(p_bufs[which], values[kv])
+            o_ref[rows_at, cols] = (out * inv_bufs[which]).astype(BF16)
+
+        def query():
+            dq = dot(d_bufs[which], keys[kv])
+            dq_ref[rows_at, cols] = (dq * (inv_bufs[which] * score_scale)).astype(BF16)
+
+        def value_grad(at):
+            dv_t[kv, :, at] += dot(cot_ts[which], p_bufs[which, :, at])
+
+        def key_grad(at):
+            dk_t[kv, :, at] += dot(q_ts[which], d_bufs[which, :, at])
+
+        work = [functools.partial(f, at) for at in chunks for f in (value_grad, key_grad)]
+        return [output] + work[: len(work) // 2] + [query] + work[len(work) // 2 :]
+
+    def weigh(which, q, cot):
+        work = []
+
+        def scores(r, at):
+            s = s_bufs[which, r, at]
+            if at.start >= prompt_len:
+                row = which * rows * (halves - 1)
+                s = s + bias[r.start + row : r.stop + row, at.start - prompt_len : at.stop - prompt_len]
+            return s
+
+        def parts(x):
+            return [x[:, col : col + HD] for col in range(0, CHUNK, HD)]
+
+        for start in range(0, rows, ROWS):
+            r = slice(start, start + ROWS)
+            state = {}
+
+            def highest(at, r=r, state=state):
+                top = functools.reduce(jnp.maximum, parts(scores(r, at)))
+                state["top"] = jnp.maximum(state["top"], top) if "top" in state else top
+
+            def settle(r=r, state=state):
+                state["top"] = jnp.max(state["top"], axis=1, keepdims=True) * exp_scale
+                state["sum"] = jnp.zeros((ROWS, HD), F32)
+                state["dot"] = jnp.zeros((ROWS, HD), F32)
+
+            def weights(at, r=r, state=state):
+                p = jnp.exp2(scores(r, at) * exp_scale - state["top"])
+                for part in parts(p):
+                    state["sum"] = state["sum"] + part
+                for part in parts(p * g_bufs[which, r, at]):
+                    state["dot"] = state["dot"] + part
+                p_bufs[which, r, at] = p.astype(BF16)
+
+            def finish(r=r, state=state):
+                inverse = 1.0 / jnp.sum(state["sum"], axis=1, keepdims=True)
+                state["delta"] = jnp.sum(state["dot"], axis=1, keepdims=True) * inverse
+                inv_bufs[which, r] = jnp.broadcast_to(inverse, (ROWS, HD))
+                scaled[0, r] = (q[r].astype(F32) * inverse).astype(BF16)
+                scaled[1, r] = (cot[r].astype(F32) * inverse).astype(BF16)
+
+            def slopes(at, r=r, state=state):
+                p = p_bufs[which, r, at].astype(F32)
+                d_bufs[which, r, at] = (p * (g_bufs[which, r, at] - state["delta"])).astype(BF16)
+
+            work += [functools.partial(highest, at) for at in chunks] + [settle]
+            work += [functools.partial(weights, at) for at in chunks] + [finish]
+            work += [functools.partial(slopes, at) for at in chunks]
+
+        def turn():
+            q_ts[which] = scaled[0].T
+            cot_ts[which] = scaled[1].T
+
+        return work + [turn]
+
+    def together(vector, matrix):
+        done = 0
+        for i, work in enumerate(vector):
+            work()
+            while done * len(vector) < (i + 1) * len(matrix):
+                matrix[done]()
+                done += 1
+
+    def mixed(first, second):
+        return [work for pair in zip(first, second) for work in pair] + (
+            first[len(second) :] + second[len(first) :]
+        )
+
+    @pl.when(step == 0)
     def _():
         place = lax.axis_index("seq")
         core = lax.rem(place, CORES)
         first_row = place * tokens
-        row_pos = first_row + lax.broadcasted_iota(jnp.int32, (tokens, tokens), 0)
-        seg_start = jnp.zeros((tokens, tokens), jnp.int32)
+        row_pos = first_row + lax.broadcasted_iota(jnp.int32, (tokens, HD), 0)
+        seg_start = jnp.zeros((tokens, HD), jnp.int32)
         end = jnp.int32(0)
         for i in range(lengths.shape[0]):
             end = end + lengths[i]
             seg_start = jnp.where(row_pos >= end, end, seg_start)
         near = 1 + 2 * core
         for i, distance in enumerate((0, 2, FAR, near, 4 - near)):
-            key_pos = (first_row - distance * tokens) + lax.broadcasted_iota(
-                jnp.int32, (tokens, tokens), 1
-            )
-            allowed = (key_pos >= seg_start) & (key_pos <= row_pos)
-            bias[i] = jnp.where(allowed, 0.0, NEG)
-        for n in range(keys.shape[0]):
+            for col in range(0, tokens, HD):
+                key_pos = (first_row - distance * tokens + col) + lax.broadcasted_iota(
+                    jnp.int32, (tokens, HD), 1
+                )
+                allowed = (key_pos >= seg_start) & (key_pos <= row_pos)
+                at = i * tokens + col
+                bias[:, at : at + HD] = jnp.where(allowed, 0.0, NEG)
+        for n in range(kv_heads):
             k_at, v_at = 2 * n * HD, (2 * n + 1) * HD
             for ref, start, size, at in (
                 (sent_ref, 0, half, 0),
@@ -203,57 +277,51 @@
             ):
                 keys[n, at : at + size] = ref[start : start + size, k_at : k_at + HD]
                 values[n, at : at + size] = ref[start : start + size, v_at : v_at + HD]
-        top = None
-        for at in chunks:
-            top = front(q_ref[:, :HD], at, 0, s_even, top)
-        top_even[...] = top
-
-    @pl.when(step == 0)
-    def _():
         dk_t[...] = jnp.zeros_like(dk_t)
         dv_t[...] = jnp.zeros_like(dv_t)
-
-    q_even, q_odd = q_ref[:, :HD], q_ref[:, HD:]
-    cot_even, cot_odd = do_ref[:, :HD], do_ref[:, HD:]
-    top = jnp.max(top_even[...], axis=1, keepdims=True) * exp_scale
-    total, out, other = None, None, None
-    for at in chunks:
-        total, out = middle(at, s_even, p_even, top, total, out)
-        other = front(q_odd, at, head, s_odd, other)
-    inverse, out, delta, cot_t, q_t = settle(q_even, cot_even, total, out)
-    o_ref[:, :HD] = out
-    top = jnp.max(other, axis=1, keepdims=True) * exp_scale
-    total, out, dq = None, None, None
-    for at in chunks:
-        dq = behind(at, p_even, cot_even, delta, cot_t, q_t, dq)
-        total, out = middle(at, s_odd, p_odd, top, total, out)
-    dq_ref[:, :HD] = (dq * (inverse * score_scale)).astype(BF16)
-    inverse, out, delta, cot_t, q_t = settle(q_odd, cot_odd, total, out)
-    o_ref[:, HD:] = out
-    upcoming = jnp.minimum(head + (step == last).astype(jnp.int32), pl.num_programs(0) - 1)
-    dq, other = None, None
-    for at in chunks:
-        dq = behind(at, p_odd, cot_odd, delta, cot_t, q_t, dq)
-        other = front(next_ref[...], at, upcoming, s_even, other)
-    dq_ref[:, HD:] = (dq * (inverse * score_scale)).astype(BF16)
-    top_even[...] = other
+        for ref in (p_bufs, d_bufs, inv_bufs, q_ts, cot_ts):
+            ref[1] = jnp.zeros(ref.shape[1:], ref.dtype)
+        for work in ahead(0, 0, unit(q_ref, 0), unit(do_ref, 0)):
+            work()
+
+    @pl.when(step < last)
+    def _():
+        kv = kv_of(step)
+        together(
+            weigh(0, unit(q_ref, 0), unit(do_ref, 0)),
+            mixed(
+                behind(1, kv_of(step - 1), step - 1),
+                ahead(1, kv, unit(q_ref, 1), unit(do_ref, 1)),
+            ),
+        )
+        together(
+            weigh(1, unit(q_ref, 1), unit(do_ref, 1)),
+            mixed(
+                behind(0, kv, step),
+                ahead(0, kv_of(step + 1), unit(next_q_ref, 0), unit(next_do_ref, 0)),
+            ),
+        )
 
     @pl.when(step == last)
     def _():
-        k_cols = pl.ds(pl.multiple_of(head * 2 * HD, HD), HD)
-        v_cols = pl.ds(pl.multiple_of(head * 2 * HD + HD, HD), HD)
-        for ref, start, size, at in (
-            (kept_ref, 0, half, 0),
-            (back_ref, 0, half, half),
-            (kept_ref, half + 2 * tokens, tokens, resp_at[0]),
-            (kept_ref, half, tokens, resp_at[1]),
-            (kept_ref, half + tokens, tokens, resp_at[2]),
-            (back_ref, half, tokens, resp_at[3]),
-            (back_ref, half + tokens, tokens, resp_at[4]),
-        ):
-            grad_k = (dk_t[:, at : at + size] * score_scale).T
-            ref[start : start + size, k_cols] = grad_k.astype(ref.dtype)
-            ref[start : start + size, v_cols] = dv_t[:, at : at + size].T.astype(ref.dtype)
+        for work in behind(1, kv_of(step - 1), step - 1):
+            work()
+        for n in range(kv_heads):
+            k_cols = slice(2 * n * HD, (2 * n + 1) * HD)
+            v_cols = slice((2 * n + 1) * HD, (2 * n + 2) * HD)
+            for ref, start, size, at in (
+                (kept_ref, 0, half, 0),
+                (back_ref, 0, half, half),
+                (kept_ref, half + 2 * tokens, tokens, resp_at[0]),
+                (kept_ref, half, tokens, resp_at[1]),
+                (kept_ref, half + tokens, tokens, resp_at[2]),
+                (back_ref, half, tokens, resp_at[3]),
+                (back_ref, half + tokens, tokens, resp_at[4]),
+            ):
+                grad_k = (dk_t[n, :, at : at + size] * score_scale).T
+                ref[start : start + size, k_cols] = grad_k.astype(ref.dtype)
+                grad_v = dv_t[n, :, at : at + size].T
+                ref[start : start + size, v_cols] = grad_v.astype(ref.dtype)
 
 
 def attention(lengths, resp_q, grad_out, sent, got, own, far):
@@ -262,18 +330,21 @@
     total_keys = 2 * half + 5 * tokens
     kv_heads = sent.shape[1] // (2 * HD)
     q_heads = resp_q.shape[1] // HD
-    steps = q_heads // kv_heads // 2
-    pair_spec = pl.BlockSpec((tokens, 2 * HD), lambda n, g: (0, n * steps + g))
-    next_spec = pl.BlockSpec(
-        (tokens, HD), lambda n, g: (0, jnp.minimum((n * steps + g) * 2 + 2, q_heads - 2))
-    )
+    halves = 1 if tokens * total_keys <= MOST_SCORES else 2
+    rows = tokens // halves
+    steps = q_heads * halves // 2
+    width = 2 // halves * HD
+
+    def block(later):
+        return pl.BlockSpec((tokens, width), lambda i: (0, jnp.minimum(i + later, steps - 1)))
+
     pairs = tokens * q_heads * total_keys
     return pl.pallas_call(
-        functools.partial(attention_kernel, tokens),
-        grid=(kv_heads, steps),
-        in_specs=[pl.BlockSpec(memory_space=pltpu.SMEM), pair_spec, next_spec, pair_spec]
+        functools.partial(attention_kernel, tokens, halves, steps // kv_heads),
+        grid=(steps + 1,),
+        in_specs=[pl.BlockSpec(memory_space=pltpu.SMEM), block(0), block(1), block(0), block(1)]
         + whole(4),
-        out_specs=[pair_spec, pair_spec] + whole(2),
+        out_specs=whole(4),
         out_shape=[
             jax.ShapeDtypeStruct(resp_q.shape, BF16),
             jax.ShapeDtypeStruct(resp_q.shape, BF16),
@@ -281,23 +352,26 @@
             jax.ShapeDtypeStruct((half + 2 * tokens, sent.shape[1]), BF16),
         ],
         scratch_shapes=[
-            pltpu.VMEM((5, tokens, tokens), F32),
+            pltpu.VMEM((tokens, 5 * tokens), F32),
             pltpu.VMEM((kv_heads, total_keys, HD), BF16),
             pltpu.VMEM((kv_heads, total_keys, HD), BF16),
-            pltpu.VMEM((tokens, total_keys), F32),
-            pltpu.VMEM((tokens, total_keys), F32),
-            pltpu.VMEM((tokens, total_keys), BF16),
-            pltpu.VMEM((tokens, total_keys), BF16),
-            pltpu.VMEM((tokens, HD), F32),
-            pltpu.VMEM((HD, total_keys), F32),
-            pltpu.VMEM((HD, total_keys), F32),
+            pltpu.VMEM((2, rows, total_keys), F32),
+            pltpu.VMEM((2, rows, total_keys), F32),
+            pltpu.VMEM((2, rows, total_keys), BF16),
+            pltpu.VMEM((2, rows, total_keys), BF16),
+            pltpu.VMEM((2, rows, HD), F32),
+            pltpu.VMEM((2, rows, HD), BF16),
+            pltpu.VMEM((2, HD, rows), BF16),
+            pltpu.VMEM((2, HD, rows), BF16),
+            pltpu.VMEM((kv_heads, HD, total_keys), F32),
+            pltpu.VMEM((kv_heads, HD, total_keys), F32),
         ],
-        compiler_params=pltpu.CompilerParams(vmem_limit_bytes=44 * 1024 * 1024),
+        compiler_params=pltpu.CompilerParams(vmem_limit_bytes=40 * 1024 * 1024),
         cost_estimate=pl.CostEstimate(
             flops=12 * HD * pairs, bytes_accessed=8 * resp_q.size, transcendentals=pairs
         ),
         name="attention",
-    )(lengths, resp_q, resp_q, grad_out, sent, got, own, far)
+    )(lengths, resp_q, resp_q, grad_out, grad_out, sent, got, own, far)
 
 
 def swap_heads(array, by):

time: 112 us -> 115 us (1.027)
  Pallas kernels: 52.9 us -> 55.4 us
    pallas_call x1, Pallas kernels: 49.8 us -> 52.3 us  [attention(): pl.pallas_call(functools.partial(attention_kernel, tokens, halves, steps...]
where the time goes in v5:
time: 115 us; the launch traced here: 114 us
  Pallas kernels  55.4 us (48%)
  waiting for transfers between devices  29.6 us (26%)
  starting transfers between devices  26.9 us (23%)
    pallas_call x1, Pallas kernels, attention(): pl.pallas_call(functools.partial(attention_kernel, tokens, halves, steps...  52.3 us
    ppermute x6, waiting for transfers between devices, swap_chips(): lax.ppermute(array, 'seq', [(i, i ^ by * CORES) for i in range(devices)])  13.8 us
    ppermute x6, waiting for transfers between devices, swap_heads(): return lax.ppermute(array, 'head', [(i, i ^ by) for i in range(devices)])  10.3 us
    ppermute x6, starting transfers between devices, swap_chips(): lax.ppermute(array, 'seq', [(i, i ^ by * CORES) for i in range(devices)])  8.93 us
    ppermute x6, starting transfers between devices, swap_heads(): return lax.ppermute(array, 'head', [(i, i ^ by) for i in range(devices)])  8.9 us
    ppermute x4, starting transfers between devices, shift_chips(): lax.ppermute(array, 'seq', [(i, i + by) for i in range(devices) if 0 <= i...  8.83 us
    ppermute x2, waiting for transfers between devices, swap_cores(): return lax.ppermute(array, 'seq', [(i, i ^ 1) for i in range(devices)])  5.56 us
  transfers between devices with their start and end apart: 18, of which 10 were waited for; matrix products, arithmetic and copies ran while one was open for 0% of the time, Pallas kernels for 0%

profile of v5, /device:TPU:6, one launch (start us, length us, event | category | flops | bytes accessed | tf_op | source)
XLA Modules:
  0.0 113.6 jit_solution(10942699252371310312)
XLA Ops:
  0.6 1.9 %pack.1 = (bf16[40,512]{1,0:T(8,128)(2,1)}, bf16[40,512]{1,0:T(8,128)(2,1)}, bf16[40,512]{1,0:T(8,128)(2,1)}, bf16[40,512]{1,0:T(8,128)(2,1)}, bf16[256,512]{1,0:T(8,128)(2,1)}) custom-call(bf16[40,1024]{1,0:T(8,128)(2,1)} %pk_ref.1, bf16[40,1024]{1,0:T(8,128)(2,1)} %pv_ref.1, bf16[256,256]{1,0:T(8,128)(2,1)} %rk_ref.1, bf16[256,256]{1,0:T(8,128)(2,1)} %rv_ref.1), custom_call_target="tpu_custom_call" | custom-call | tf_op jit(solution)/shard_map/pack/pallas_call | solution.py:69
  2.5 1.4 %collective-permute-start.4 = (bf16[256,512]{1,0:T(8,128)(2,1)}, bf16[256,512]{1,0:T(8,128)(2,1)S(1)}, u32[]{:S(2)}, u32[]{:S(2)}) collective-permute-start(bf16[256,512]{1,0:T(8,128)(2,1)} %get-tuple-element.46.own_ref), channel_id=1, source_target_pairs={{0,16},{4,20},{8,24},{12,28},{1,17},{5,21},{9,25},{13,29},{2,18},{... | collective-permute-start | bytes 786440 | tf_op jit(solution)/shard_map/ppermute | solution.py:395
  3.9 1.3 %collective-permute-start.3 = (bf16[256,512]{1,0:T(8,128)(2,1)}, bf16[256,512]{1,0:T(8,128)(2,1)S(1)}, u32[]{:S(2)}, u32[]{:S(2)}) collective-permute-start(bf16[256,512]{1,0:T(8,128)(2,1)} %get-tuple-element.46.own_ref), channel_id=1, source_target_pairs={{0,8},{4,12},{8,16},{12,20},{16,24},{20,28},{1,9},{5,13},{9,17},{1... | collective-permute-start | bytes 786440 | tf_op jit(solution)/shard_map/ppermute | solution.py:395
  5.2 1.6 %collective-permute-start = (bf16[40,512]{1,0:T(8,128)(2,1)}, bf16[40,512]{1,0:T(8,128)(2,1)S(1)}, u32[]{:S(2)}, u32[]{:S(2)}) collective-permute-start(bf16[40,512]{1,0:T(8,128)(2,1)} %get-tuple-element.43), channel_id=1, source_target_pairs={{0,1},{1,0},{2,3},{3,2},{4,5},{5,4},{6,7},{7,6},{8,9},{9,8},{10,11... | collective-permute-start | bytes 122888 | tf_op jit(solution)/shard_map/ppermute | solution.py:379
  6.9 2.6 %collective-permute-start.1 = (bf16[40,512]{1,0:T(8,128)(2,1)}, bf16[40,512]{1,0:T(8,128)(2,1)S(1)}, u32[]{:S(2)}, u32[]{:S(2)}) collective-permute-start(bf16[40,512]{1,0:T(8,128)(2,1)} %get-tuple-element.44), channel_id=1, source_target_pairs={{0,2},{1,3},{2,0},{3,1},{4,6},{5,7},{6,4},{7,5},{8,10},{9,11},{10,... | collective-permute-start | bytes 122888 | tf_op jit(solution)/shard_map/ppermute | solution.py:379
  9.5 0.2 collective-permute-start.2
  9.7 3.1 %collective-permute-done.1 = bf16[40,512]{1,0:T(8,128)(2,1)S(1)} collective-permute-done((bf16[40,512]{1,0:T(8,128)(2,1)}, bf16[40,512]{1,0:T(8,128)(2,1)S(1)}, u32[]{:S(2)}, u32[]{:S(2)}) %collective-permute-start.1) | collective-permute-done | bytes 40992 | tf_op jit(solution)/shard_map/ppermute | solution.py:379
  12.8 2.7 %collective-permute-done.2 = bf16[40,512]{1,0:T(8,128)(2,1)S(1)} collective-permute-done((bf16[40,512]{1,0:T(8,128)(2,1)}, bf16[40,512]{1,0:T(8,128)(2,1)S(1)}, u32[]{:S(2)}, u32[]{:S(2)}) %collective-permute-start.2) | collective-permute-done | bytes 40992 | tf_op jit(solution)/shard_map/ppermute | solution.py:379
  15.5 0.8 constant_dynamic-update-slice_fusion.3
  16.3 3.5 %collective-permute-start.5 = (bf16[160,512]{1,0:T(8,128)(2,1)S(1)}, bf16[160,512]{1,0:T(8,128)(2,1)S(1)}, u32[]{:S(2)}, u32[]{:S(2)}) collective-permute-start(bf16[160,512]{1,0:T(8,128)(2,1)S(1)} %get-tuple-element.78), channel_id=1, source_target_pairs={{0,8},{4,12},{8,0},{12,4},{16,24},{20,28},{24,16},{28,20},{1,9},{5... | collective-permute-start | bytes 491528 | tf_op jit(solution)/shard_map/ppermute | solution.py:384
  19.9 1.9 %collective-permute-start.6 = (bf16[160,512]{1,0:T(8,128)(2,1)S(1)}, bf16[160,512]{1,0:T(8,128)(2,1)S(1)}, u32[]{:S(2)}, u32[]{:S(2)}) collective-permute-start(bf16[160,512]{1,0:T(8,128)(2,1)S(1)} %get-tuple-element.78), channel_id=1, source_target_pairs={{0,16},{4,20},{8,24},{12,28},{16,0},{20,4},{24,8},{28,12},{1,17},{... | collective-permute-start | bytes 491528 | tf_op jit(solution)/shard_map/ppermute | solution.py:384
  21.7 2.5 %collective-permute-done.5 = bf16[160,512]{1,0:T(8,128)(2,1)S(1)} collective-permute-done((bf16[160,512]{1,0:T(8,128)(2,1)S(1)}, bf16[160,512]{1,0:T(8,128)(2,1)S(1)}, u32[]{:S(2)}, u32[]{:S(2)}) %collective-permute-start.5) | collective-permute-done | bytes 163872 | tf_op jit(solution)/shard_map/ppermute | solution.py:384
  24.2 3.9 %collective-permute-done.6 = bf16[160,512]{1,0:T(8,128)(2,1)S(1)} collective-permute-done((bf16[160,512]{1,0:T(8,128)(2,1)S(1)}, bf16[160,512]{1,0:T(8,128)(2,1)S(1)}, u32[]{:S(2)}, u32[]{:S(2)}) %collective-permute-start.6) | collective-permute-done | bytes 163872 | tf_op jit(solution)/shard_map/ppermute | solution.py:384
  28.4 2.8 %collective-permute-done.8.got_ref = bf16[1152,512]{1,0:T(8,128)(2,1)S(1)} collective-permute-done((bf16[1152,512]{1,0:T(8,128)(2,1)S(1)}, bf16[1152,512]{1,0:T(8,128)(2,1)S(1)}, u32[]{:S(2)}, u32[]{:S(2)}) %collective-permute-start.8) | collective-permute-done | bytes 1179680 | tf_op jit(solution)/shard_map/ppermute | solution.py:389
  31.2 52.3 %attention.1 = (bf16[256,2048]{1,0:T(8,128)(2,1)}, bf16[256,2048]{1,0:T(8,128)(2,1)}, f32[1408,512]{1,0:T(8,128)S(1)}, bf16[1152,512]{1,0:T(8,128)(2,1)S(1)}) custom-call(s32[8]{0:T(128)S(1)} %copy-done.3, bf16[256,2048]{1,0:T(8,128)(2,1)S(1)} %copy-done.1, bf16[256,2048]{1,0:T(8,128)(2,1)S(1)} %copy-done.1, bf16[256,2048]{1,0:T(8,128)(2,1)S(1)} %copy-done.2, ...), custom_call_target="tpu_custom_call" | custom-call | flops 16106127360 | bytes 4194304 | tf_op jit(solution)/shard_map/attention/pallas_call | solution.py:342
  83.6 0.1 collective-permute-start.9
  83.7 2.7 %collective-permute-done.9.got_ref = bf16[1152,512]{1,0:T(8,128)(2,1)S(1)} collective-permute-done((bf16[1152,512]{1,0:T(8,128)(2,1)S(1)}, bf16[1152,512]{1,0:T(8,128)(2,1)S(1)}, u32[]{:S(2)}, u32[]{:S(2)}) %collective-permute-start.9) | collective-permute-done | bytes 1179680 | tf_op jit(solution)/shard_map/ppermute | solution.py:389
  86.4 0.3 merge.1
  86.7 0.4 collective-permute-start.10
  87.2 1.6 %collective-permute-start.11 = (bf16[160,512]{1,0:T(8,128)(2,1)S(1)}, bf16[160,512]{1,0:T(8,128)(2,1)S(1)}, u32[]{:S(2)}, u32[]{:S(2)}) collective-permute-start(bf16[160,512]{1,0:T(8,128)(2,1)S(1)} %get-tuple-element.60), channel_id=1, source_target_pairs={{0,16},{4,20},{8,24},{12,28},{16,0},{20,4},{24,8},{28,12},{1,17},{... | collective-permute-start | bytes 491528 | tf_op jit(solution)/shard_map/ppermute | solution.py:384
  88.8 1.5 %collective-permute-start.12 = (bf16[160,512]{1,0:T(8,128)(2,1)S(1)}, bf16[160,512]{1,0:T(8,128)(2,1)S(1)}, u32[]{:S(2)}, u32[]{:S(2)}) collective-permute-start(bf16[160,512]{1,0:T(8,128)(2,1)S(1)} %get-tuple-element.61), channel_id=1, source_target_pairs={{0,24},{4,28},{8,16},{12,20},{16,8},{20,12},{24,0},{28,4},{1,25},{... | collective-permute-start | bytes 491528 | tf_op jit(solution)/shard_map/ppermute | solution.py:384
  90.3 3.6 %collective-permute-done.10.refs_1_ = bf16[160,512]{1,0:T(8,128)(2,1)S(1)} collective-permute-done((bf16[160,512]{1,0:T(8,128)(2,1)S(1)}, bf16[160,512]{1,0:T(8,128)(2,1)S(1)}, u32[]{:S(2)}, u32[]{:S(2)}) %collective-permute-start.10) | collective-permute-done | bytes 163872 | tf_op jit(solution)/shard_map/ppermute | solution.py:384
  93.9 3.8 %collective-permute-done.12.refs_3_ = bf16[160,512]{1,0:T(8,128)(2,1)S(1)} collective-permute-done((bf16[160,512]{1,0:T(8,128)(2,1)S(1)}, bf16[160,512]{1,0:T(8,128)(2,1)S(1)}, u32[]{:S(2)}, u32[]{:S(2)}) %collective-permute-start.12) | collective-permute-done | bytes 163872 | tf_op jit(solution)/shard_map/ppermute | solution.py:384
  97.6 2.6 %collective-permute-start.13 = (bf16[256,512]{1,0:T(8,128)(2,1)S(1)}, bf16[256,512]{1,0:T(8,128)(2,1)S(1)}, u32[]{:S(2)}, u32[]{:S(2)}) collective-permute-start(bf16[256,512]{1,0:T(8,128)(2,1)S(1)} %get-tuple-element.64), channel_id=1, source_target_pairs={{8,0},{12,4},{16,8},{20,12},{24,16},{28,20},{9,1},{13,5},{17,9},{2... | collective-permute-start | bytes 786440 | tf_op jit(solution)/shard_map/ppermute | solution.py:395
  100.2 3.5 %collective-permute-start.14 = (bf16[256,512]{1,0:T(8,128)(2,1)S(1)}, bf16[256,512]{1,0:T(8,128)(2,1)S(1)}, u32[]{:S(2)}, u32[]{:S(2)}) collective-permute-start(bf16[256,512]{1,0:T(8,128)(2,1)S(1)} %get-tuple-element.65), channel_id=1, source_target_pairs={{16,0},{20,4},{24,8},{28,12},{17,1},{21,5},{25,9},{29,13},{18,2},{... | collective-permute-start | bytes 786440 | tf_op jit(solution)/shard_map/ppermute | solution.py:395
  103.8 0.1 sum_chips.1
  103.9 0.5 collective-permute-start.15
  104.4 2.6 %collective-permute-start.16 = (bf16[40,512]{1,0:T(8,128)(2,1)S(1)}, bf16[40,512]{1,0:T(8,128)(2,1)S(1)}, u32[]{:S(2)}, u32[]{:S(2)}) collective-permute-start(bf16[40,512]{1,0:T(8,128)(2,1)S(1)} %get-tuple-element.72), channel_id=1, source_target_pairs={{0,2},{1,3},{2,0},{3,1},{4,6},{5,7},{6,4},{7,5},{8,10},{9,11},{10,... | collective-permute-start | bytes 122888 | tf_op jit(solution)/shard_map/ppermute | solution.py:379
  107.0 1.3 %collective-permute-start.17 = (bf16[40,512]{1,0:T(8,128)(2,1)S(1)}, bf16[40,512]{1,0:T(8,128)(2,1)S(1)}, u32[]{:S(2)}, u32[]{:S(2)}) collective-permute-start(bf16[40,512]{1,0:T(8,128)(2,1)S(1)} %get-tuple-element.73), channel_id=1, source_target_pairs={{0,3},{1,2},{2,1},{3,0},{4,7},{5,6},{6,5},{7,4},{8,11},{9,10},{10,... | collective-permute-start | bytes 122888 | tf_op jit(solution)/shard_map/ppermute | solution.py:379
  108.3 1.4 %collective-permute-done.16.refs_2_ = bf16[40,512]{1,0:T(8,128)(2,1)S(1)} collective-permute-done((bf16[40,512]{1,0:T(8,128)(2,1)S(1)}, bf16[40,512]{1,0:T(8,128)(2,1)S(1)}, u32[]{:S(2)}, u32[]{:S(2)}) %collective-permute-start.16) | collective-permute-done | bytes 40992 | tf_op jit(solution)/shard_map/ppermute | solution.py:379
  109.8 3.1 %collective-permute-done.17.refs_3_ = bf16[40,512]{1,0:T(8,128)(2,1)S(1)} collective-permute-done((bf16[40,512]{1,0:T(8,128)(2,1)S(1)}, bf16[40,512]{1,0:T(8,128)(2,1)S(1)}, u32[]{:S(2)}, u32[]{:S(2)}) %collective-permute-start.17) | collective-permute-done | bytes 40992 | tf_op jit(solution)/shard_map/ppermute | solution.py:379
  112.8 0.8 finish.1
  (26 shorter events, 0.3 us)
Async XLA Ops:
  2.5 25.7 %copy-start = (bf16[256,512]{1,0:T(8,128)(2,1)S(1)}, bf16[256,512]{1,0:T(8,128)(2,1)}, u32[]{:S(2)}) copy-start(bf16[256,512]{1,0:T(8,128)(2,1)} %get-tuple-element.46.own_ref) | copy-start | bytes 786436
  2.5 13.0 %collective-permute-start.4 = (bf16[256,512]{1,0:T(8,128)(2,1)}, bf16[256,512]{1,0:T(8,128)(2,1)S(1)}, u32[]{:S(2)}, u32[]{:S(2)}) collective-permute-start(bf16[256,512]{1,0:T(8,128)(2,1)} %get-tuple-element.46.own_ref), channel_id=1, source_target_pairs={{0,16},{4,20},{8,24},{12,28},{1,17},{5,21},{9,25},{13,29},{2,18},{... | collective-permute-start | bytes 786440 | tf_op jit(solution)/shard_map/ppermute | solution.py:395
  3.9 11.5 %collective-permute-start.3 = (bf16[256,512]{1,0:T(8,128)(2,1)}, bf16[256,512]{1,0:T(8,128)(2,1)S(1)}, u32[]{:S(2)}, u32[]{:S(2)}) collective-permute-start(bf16[256,512]{1,0:T(8,128)(2,1)} %get-tuple-element.46.own_ref), channel_id=1, source_target_pairs={{0,8},{4,12},{8,16},{12,20},{16,24},{20,28},{1,9},{5,13},{9,17},{1... | collective-permute-start | bytes 786440 | tf_op jit(solution)/shard_map/ppermute | solution.py:395
  5.2 4.5 %collective-permute-start = (bf16[40,512]{1,0:T(8,128)(2,1)}, bf16[40,512]{1,0:T(8,128)(2,1)S(1)}, u32[]{:S(2)}, u32[]{:S(2)}) collective-permute-start(bf16[40,512]{1,0:T(8,128)(2,1)} %get-tuple-element.43), channel_id=1, source_target_pairs={{0,1},{1,0},{2,3},{3,2},{4,5},{5,4},{6,7},{7,6},{8,9},{9,8},{10,11... | collective-permute-start | bytes 122888 | tf_op jit(solution)/shard_map/ppermute | solution.py:379
  6.9 5.9 %collective-permute-start.1 = (bf16[40,512]{1,0:T(8,128)(2,1)}, bf16[40,512]{1,0:T(8,128)(2,1)S(1)}, u32[]{:S(2)}, u32[]{:S(2)}) collective-permute-start(bf16[40,512]{1,0:T(8,128)(2,1)} %get-tuple-element.44), channel_id=1, source_target_pairs={{0,2},{1,3},{2,0},{3,1},{4,6},{5,7},{6,4},{7,5},{8,10},{9,11},{10,... | collective-permute-start | bytes 122888 | tf_op jit(solution)/shard_map/ppermute | solution.py:379
  9.5 6.0 %collective-permute-start.2 = (bf16[40,512]{1,0:T(8,128)(2,1)}, bf16[40,512]{1,0:T(8,128)(2,1)S(1)}, u32[]{:S(2)}, u32[]{:S(2)}) collective-permute-start(bf16[40,512]{1,0:T(8,128)(2,1)} %get-tuple-element.45), channel_id=1, source_target_pairs={{0,3},{1,2},{2,1},{3,0},{4,7},{5,6},{6,5},{7,4},{8,11},{9,10},{10,... | collective-permute-start | bytes 122888 | tf_op jit(solution)/shard_map/ppermute | solution.py:379
  16.3 14.9 %copy-start.1 = (bf16[256,2048]{1,0:T(8,128)(2,1)S(1)}, bf16[256,2048]{1,0:T(8,128)(2,1)}, u32[]{:S(2)}) copy-start(bf16[256,2048]{1,0:T(8,128)(2,1)} %next_q_ref.1) | copy-start | bytes 3145732
  16.3 14.9 %copy-start.3 = (s32[8]{0:T(128)S(1)}, s32[8]{0:T(128)}, u32[]{:S(2)}) copy-start(s32[8]{0:T(128)} %lengths.1) | copy-start | bytes 100
  16.3 7.9 %collective-permute-start.5 = (bf16[160,512]{1,0:T(8,128)(2,1)S(1)}, bf16[160,512]{1,0:T(8,128)(2,1)S(1)}, u32[]{:S(2)}, u32[]{:S(2)}) collective-permute-start(bf16[160,512]{1,0:T(8,128)(2,1)S(1)} %get-tuple-element.78), channel_id=1, source_target_pairs={{0,8},{4,12},{8,0},{12,4},{16,24},{20,28},{24,16},{28,20},{1,9},{5... | collective-permute-start | bytes 491528 | tf_op jit(solution)/shard_map/ppermute | solution.py:384
  19.9 8.3 %collective-permute-start.6 = (bf16[160,512]{1,0:T(8,128)(2,1)S(1)}, bf16[160,512]{1,0:T(8,128)(2,1)S(1)}, u32[]{:S(2)}, u32[]{:S(2)}) collective-permute-start(bf16[160,512]{1,0:T(8,128)(2,1)S(1)} %get-tuple-element.78), channel_id=1, source_target_pairs={{0,16},{4,20},{8,24},{12,28},{16,0},{20,4},{24,8},{28,12},{1,17},{... | collective-permute-start | bytes 491528 | tf_op jit(solution)/shard_map/ppermute | solution.py:384
  21.7 9.5 %copy-start.2 = (bf16[256,2048]{1,0:T(8,128)(2,1)S(1)}, bf16[256,2048]{1,0:T(8,128)(2,1)}, u32[]{:S(2)}) copy-start(bf16[256,2048]{1,0:T(8,128)(2,1)} %next_do_ref.1) | copy-start | bytes 3145732
  21.7 6.5 %collective-permute-start.7 = (bf16[160,512]{1,0:T(8,128)(2,1)S(1)}, bf16[160,512]{1,0:T(8,128)(2,1)S(1)}, u32[]{:S(2)}, u32[]{:S(2)}) collective-permute-start(bf16[160,512]{1,0:T(8,128)(2,1)S(1)} %get-tuple-element.78), channel_id=1, source_target_pairs={{0,24},{4,28},{8,16},{12,20},{16,8},{20,12},{24,0},{28,4},{1,25},{... | collective-permute-start | bytes 491528 | tf_op jit(solution)/shard_map/ppermute | solution.py:384
  28.3 2.9 %collective-permute-start.8 = (bf16[1152,512]{1,0:T(8,128)(2,1)S(1)}, bf16[1152,512]{1,0:T(8,128)(2,1)S(1)}, u32[]{:S(2)}, u32[]{:S(2)}) collective-permute-start(bf16[1152,512]{1,0:T(8,128)(2,1)S(1)} %select_dynamic-update-slice_fusion.sent_ref), channel_id=1, source_target_pairs={{0,4},{4,0},{8,12},{12,8},{16,20},{20,16},{24,28},{28,24},{1,5},{5... | collective-permute-start | bytes 3538952 | tf_op jit(solution)/shard_map/ppermute | solution.py:389
  83.6 2.8 %collective-permute-start.9 = (bf16[1152,512]{1,0:T(8,128)(2,1)S(1)}, bf16[1152,512]{1,0:T(8,128)(2,1)S(1)}, u32[]{:S(2)}, u32[]{:S(2)}) collective-permute-start(bf16[1152,512]{1,0:T(8,128)(2,1)S(1)} %get-tuple-element.56), channel_id=1, source_target_pairs={{0,4},{4,0},{8,12},{12,8},{16,20},{20,16},{24,28},{28,24},{1,5},{5... | collective-permute-start | bytes 3538952 | tf_op jit(solution)/shard_map/ppermute | solution.py:389
  86.7 7.1 %collective-permute-start.10 = (bf16[160,512]{1,0:T(8,128)(2,1)S(1)}, bf16[160,512]{1,0:T(8,128)(2,1)S(1)}, u32[]{:S(2)}, u32[]{:S(2)}) collective-permute-start(bf16[160,512]{1,0:T(8,128)(2,1)S(1)} %get-tuple-element.59), channel_id=1, source_target_pairs={{0,8},{4,12},{8,0},{12,4},{16,24},{20,28},{24,16},{28,20},{1,9},{5... | collective-permute-start | bytes 491528 | tf_op jit(solution)/shard_map/ppermute | solution.py:384
  87.2 6.7 %collective-permute-start.11 = (bf16[160,512]{1,0:T(8,128)(2,1)S(1)}, bf16[160,512]{1,0:T(8,128)(2,1)S(1)}, u32[]{:S(2)}, u32[]{:S(2)}) collective-permute-start(bf16[160,512]{1,0:T(8,128)(2,1)S(1)} %get-tuple-element.60), channel_id=1, source_target_pairs={{0,16},{4,20},{8,24},{12,28},{16,0},{20,4},{24,8},{28,12},{1,17},{... | collective-permute-start | bytes 491528 | tf_op jit(solution)/shard_map/ppermute | solution.py:384
  88.8 8.9 %collective-permute-start.12 = (bf16[160,512]{1,0:T(8,128)(2,1)S(1)}, bf16[160,512]{1,0:T(8,128)(2,1)S(1)}, u32[]{:S(2)}, u32[]{:S(2)}) collective-permute-start(bf16[160,512]{1,0:T(8,128)(2,1)S(1)} %get-tuple-element.61), channel_id=1, source_target_pairs={{0,24},{4,28},{8,16},{12,20},{16,8},{20,12},{24,0},{28,4},{1,25},{... | collective-permute-start | bytes 491528 | tf_op jit(solution)/shard_map/ppermute | solution.py:384
  97.6 15.2 %collective-permute-start.13 = (bf16[256,512]{1,0:T(8,128)(2,1)S(1)}, bf16[256,512]{1,0:T(8,128)(2,1)S(1)}, u32[]{:S(2)}, u32[]{:S(2)}) collective-permute-start(bf16[256,512]{1,0:T(8,128)(2,1)S(1)} %get-tuple-element.64), channel_id=1, source_target_pairs={{8,0},{12,4},{16,8},{20,12},{24,16},{28,20},{9,1},{13,5},{17,9},{2... | collective-permute-start | bytes 786440 | tf_op jit(solution)/shard_map/ppermute | solution.py:395
  100.2 12.6 %collective-permute-start.14 = (bf16[256,512]{1,0:T(8,128)(2,1)S(1)}, bf16[256,512]{1,0:T(8,128)(2,1)S(1)}, u32[]{:S(2)}, u32[]{:S(2)}) collective-permute-start(bf16[256,512]{1,0:T(8,128)(2,1)S(1)} %get-tuple-element.65), channel_id=1, source_target_pairs={{16,0},{20,4},{24,8},{28,12},{17,1},{21,5},{25,9},{29,13},{18,2},{... | collective-permute-start | bytes 786440 | tf_op jit(solution)/shard_map/ppermute | solution.py:395
  103.9 4.5 %collective-permute-start.15 = (bf16[40,512]{1,0:T(8,128)(2,1)S(1)}, bf16[40,512]{1,0:T(8,128)(2,1)S(1)}, u32[]{:S(2)}, u32[]{:S(2)}) collective-permute-start(bf16[40,512]{1,0:T(8,128)(2,1)S(1)} %get-tuple-element.71), channel_id=1, source_target_pairs={{0,1},{1,0},{2,3},{3,2},{4,5},{5,4},{6,7},{7,6},{8,9},{9,8},{10,11... | collective-permute-start | bytes 122888 | tf_op jit(solution)/shard_map/ppermute | solution.py:379
  104.4 5.3 %collective-permute-start.16 = (bf16[40,512]{1,0:T(8,128)(2,1)S(1)}, bf16[40,512]{1,0:T(8,128)(2,1)S(1)}, u32[]{:S(2)}, u32[]{:S(2)}) collective-permute-start(bf16[40,512]{1,0:T(8,128)(2,1)S(1)} %get-tuple-element.72), channel_id=1, source_target_pairs={{0,2},{1,3},{2,0},{3,1},{4,6},{5,7},{6,4},{7,5},{8,10},{9,11},{10,... | collective-permute-start | bytes 122888 | tf_op jit(solution)/shard_map/ppermute | solution.py:379
  107.0 5.8 %collective-permute-start.17 = (bf16[40,512]{1,0:T(8,128)(2,1)S(1)}, bf16[40,512]{1,0:T(8,128)(2,1)S(1)}, u32[]{:S(2)}, u32[]{:S(2)}) collective-permute-start(bf16[40,512]{1,0:T(8,128)(2,1)S(1)} %get-tuple-element.73), channel_id=1, source_target_pairs={{0,3},{1,2},{2,1},{3,0},{4,7},{5,6},{6,5},{7,4},{8,11},{9,10},{10,... | collective-permute-start | bytes 122888 | tf_op jit(solution)/shard_map/ppermute | solution.py:379

commit v6 on v5

--- a/solution.py
+++ b/solution.py
@@ -11,21 +11,16 @@
 HD = 128
 CORES = 2
 FAR = 4
-CHUNK = 256
-ROWS = 64
+CHUNK = 640
+TILE = 64
 MOST_SCORES = 2560 * 256
 NEG = -1e30
-NT = (((1,), (1,)), ((), ()))
 BF16 = jnp.bfloat16
 F32 = jnp.float32
 
 
 def dot(a, b):
     return jnp.dot(a, b, preferred_element_type=F32)
-
-
-def dot_nt(a, b):
-    return lax.dot_general(a, b, NT, preferred_element_type=F32)
 
 
 def whole(count):
@@ -124,7 +119,8 @@
     tokens, halves, steps_per_kv,
     lengths, q_ref, next_q_ref, do_ref, next_do_ref, sent_ref, got_ref, own_ref, far_ref,
     o_ref, dq_ref, kept_ref, back_ref,
-    bias, keys, values, s_bufs, g_bufs, p_bufs, d_bufs, inv_bufs, scaled, q_ts, cot_ts, dk_t, dv_t,
+    bias, keys, values, keys_t, values_t, s_bufs, g_bufs, p_bufs, d_bufs, inv_bufs,
+    q_ts, cot_ts, q_ns, cot_ns, dk, dv,
 ):
     kv_heads, total_keys = keys.shape[0], keys.shape[1]
     rows = tokens // halves
@@ -135,6 +131,7 @@
     score_scale = 1.0 / math.sqrt(HD)
     exp_scale = score_scale * math.log2(math.e)
     resp_at = [prompt_len + i * tokens for i in range(6)]
+    tiles = [slice(at, at + TILE) for at in range(0, total_keys, TILE)]
     chunks = [slice(at, at + CHUNK) for at in range(0, total_keys, CHUNK)]
 
     def unit(ref, which):
@@ -145,91 +142,94 @@
     def kv_of(at_step):
         return jnp.clip(at_step // steps_per_kv, 0, kv_heads - 1)
 
-    def ahead(which, kv, q, cot):
+    def ahead(which, kv, q_from, cot_from):
+        def lift():
+            q_ts[which] = unit(q_from, which).T
+            cot_ts[which] = unit(cot_from, which).T
+
         def scores(at):
-            s_bufs[which, :, at] = dot_nt(q, keys[kv, at])
+            s_bufs[which, at] = dot(keys[kv, at], q_ts[which])
 
         def grads(at):
-            g_bufs[which, :, at] = dot_nt(cot, values[kv, at])
-
-        return [functools.partial(f, at) for at in chunks for f in (scores, grads)]
+            g_bufs[which, at] = dot(values[kv, at], cot_ts[which])
+
+        return [lift] + [functools.partial(f, at) for at in chunks for f in (scores, grads)]
 
     def behind(which, kv, at_step):
         head = jnp.maximum(at_step, 0) * (2 // halves) + (which if halves == 1 else 0)
         cols = pl.ds(pl.multiple_of(head * HD, HD), HD)
         rows_at = slice(0, rows) if halves == 1 else slice(which * rows, (which + 1) * rows)
-
-        def output():
-            out = dot(p_bufs[which], values[kv])
-            o_ref[rows_at, cols] = (out * inv_bufs[which]).astype(BF16)
-
-        def query():
-            dq = dot(d_bufs[which], keys[kv])
-            dq_ref[rows_at, cols] = (dq * (inv_bufs[which] * score_scale)).astype(BF16)
+        cuts = [slice(at, at + total_keys // 2) for at in (0, total_keys // 2)]
+        state = {}
+
+        def output(at):
+            more = dot(values_t[kv, :, at], p_bufs[which, at])
+            state["out"] = state["out"] + more if "out" in state else more
+
+        def query(at):
+            more = dot(keys_t[kv, :, at], d_bufs[which, at])
+            state["dq"] = state["dq"] + more if "dq" in state else more
+
+        def put_output():
+            o_ref[rows_at, cols] = (state["out"] * inv_bufs[which, :1]).astype(BF16).T
+
+        def put_query():
+            dq = state["dq"] * (inv_bufs[which, :1] * score_scale)
+            dq_ref[rows_at, cols] = dq.astype(BF16).T
 
         def value_grad(at):
-            dv_t[kv, :, at] += dot(cot_ts[which], p_bufs[which, :, at])
+            dv[kv, at] += dot(p_bufs[which, at], cot_ns[which])
 
         def key_grad(at):
-            dk_t[kv, :, at] += dot(q_ts[which], d_bufs[which, :, at])
+            dk[kv, at] += dot(d_bufs[which, at], q_ns[which])
 
         work = [functools.partial(f, at) for at in chunks for f in (value_grad, key_grad)]
-        return [output] + work[: len(work) // 2] + [query] + work[len(work) // 2 :]
-
-    def weigh(which, q, cot):
-        work = []
-
-        def scores(r, at):
-            s = s_bufs[which, r, at]
+        first = [functools.partial(output, at) for at in cuts] + [put_output]
+        second = [functools.partial(query, at) for at in cuts] + [put_query]
+        return first + work[: len(work) // 2] + second + work[len(work) // 2 :]
+
+    def weigh(which):
+        state = {}
+
+        def scores(at):
+            s = s_bufs[which, at]
             if at.start >= prompt_len:
                 row = which * rows * (halves - 1)
-                s = s + bias[r.start + row : r.stop + row, at.start - prompt_len : at.stop - prompt_len]
+                s = s + bias[at.start - prompt_len : at.stop - prompt_len, row : row + rows]
             return s
 
-        def parts(x):
-            return [x[:, col : col + HD] for col in range(0, CHUNK, HD)]
-
-        for start in range(0, rows, ROWS):
-            r = slice(start, start + ROWS)
-            state = {}
-
-            def highest(at, r=r, state=state):
-                top = functools.reduce(jnp.maximum, parts(scores(r, at)))
-                state["top"] = jnp.maximum(state["top"], top) if "top" in state else top
-
-            def settle(r=r, state=state):
-                state["top"] = jnp.max(state["top"], axis=1, keepdims=True) * exp_scale
-                state["sum"] = jnp.zeros((ROWS, HD), F32)
-                state["dot"] = jnp.zeros((ROWS, HD), F32)
-
-            def weights(at, r=r, state=state):
-                p = jnp.exp2(scores(r, at) * exp_scale - state["top"])
-                for part in parts(p):
-                    state["sum"] = state["sum"] + part
-                for part in parts(p * g_bufs[which, r, at]):
-                    state["dot"] = state["dot"] + part
-                p_bufs[which, r, at] = p.astype(BF16)
-
-            def finish(r=r, state=state):
-                inverse = 1.0 / jnp.sum(state["sum"], axis=1, keepdims=True)
-                state["delta"] = jnp.sum(state["dot"], axis=1, keepdims=True) * inverse
-                inv_bufs[which, r] = jnp.broadcast_to(inverse, (ROWS, HD))
-                scaled[0, r] = (q[r].astype(F32) * inverse).astype(BF16)
-                scaled[1, r] = (cot[r].astype(F32) * inverse).astype(BF16)
-
-            def slopes(at, r=r, state=state):
-                p = p_bufs[which, r, at].astype(F32)
-                d_bufs[which, r, at] = (p * (g_bufs[which, r, at] - state["delta"])).astype(BF16)
-
-            work += [functools.partial(highest, at) for at in chunks] + [settle]
-            work += [functools.partial(weights, at) for at in chunks] + [finish]
-            work += [functools.partial(slopes, at) for at in chunks]
-
-        def turn():
-            q_ts[which] = scaled[0].T
-            cot_ts[which] = scaled[1].T
-
-        return work + [turn]
+        def folded(x):
+            return x.reshape(TILE // 8, 8, rows)
+
+        def highest(at):
+            top = jnp.max(folded(scores(at)), axis=0)
+            state["top"] = jnp.maximum(state["top"], top) if "top" in state else top
+
+        def settle():
+            state["top"] = jnp.max(state["top"], axis=0, keepdims=True) * exp_scale
+            state["sum"] = jnp.zeros((8, rows), F32)
+            state["dot"] = jnp.zeros((8, rows), F32)
+
+        def weights(at):
+            p = jnp.exp2(scores(at) * exp_scale - state["top"])
+            state["sum"] = state["sum"] + jnp.sum(folded(p), axis=0)
+            state["dot"] = state["dot"] + jnp.sum(folded(p * g_bufs[which, at]), axis=0)
+            p_bufs[which, at] = p.astype(BF16)
+
+        def finish():
+            inverse = 1.0 / jnp.sum(state["sum"], axis=0, keepdims=True)
+            state["delta"] = jnp.sum(state["dot"], axis=0, keepdims=True) * inverse
+            inv_bufs[which] = jnp.broadcast_to(inverse, (8, rows))
+            q_ns[which] = (q_ts[which].astype(F32) * inverse).astype(BF16).T
+            cot_ns[which] = (cot_ts[which].astype(F32) * inverse).astype(BF16).T
+
+        def slopes(at):
+            p = p_bufs[which, at].astype(F32)
+            d_bufs[which, at] = (p * (g_bufs[which, at] - state["delta"])).astype(BF16)
+
+        work = [functools.partial(highest, at) for at in tiles] + [settle]
+        work += [functools.partial(weights, at) for at in tiles] + [finish]
+        return work + [functools.partial(slopes, at) for at in tiles]
 
     def together(vector, matrix):
         done = 0
@@ -249,21 +249,22 @@
         place = lax.axis_index("seq")
         core = lax.rem(place, CORES)
         first_row = place * tokens
-        row_pos = first_row + lax.broadcasted_iota(jnp.int32, (tokens, HD), 0)
-        seg_start = jnp.zeros((tokens, HD), jnp.int32)
+        row_pos = first_row + lax.broadcasted_iota(jnp.int32, (8, tokens), 1)
+        seg_start = jnp.zeros((8, tokens), jnp.int32)
         end = jnp.int32(0)
         for i in range(lengths.shape[0]):
             end = end + lengths[i]
             seg_start = jnp.where(row_pos >= end, end, seg_start)
+        seg_start, row_pos = seg_start[:1], row_pos[:1]
         near = 1 + 2 * core
         for i, distance in enumerate((0, 2, FAR, near, 4 - near)):
-            for col in range(0, tokens, HD):
-                key_pos = (first_row - distance * tokens + col) + lax.broadcasted_iota(
-                    jnp.int32, (tokens, HD), 1
+            for row in range(0, tokens, TILE):
+                key_pos = (first_row - distance * tokens + row) + lax.broadcasted_iota(
+                    jnp.int32, (TILE, tokens), 0
                 )
                 allowed = (key_pos >= seg_start) & (key_pos <= row_pos)
-                at = i * tokens + col
-                bias[:, at : at + HD] = jnp.where(allowed, 0.0, NEG)
+                at = i * tokens + row
+                bias[at : at + TILE] = jnp.where(allowed, 0.0, NEG)
         for n in range(kv_heads):
             k_at, v_at = 2 * n * HD, (2 * n + 1) * HD
             for ref, start, size, at in (
@@ -275,31 +276,29 @@
                 (got_ref, half, tokens, resp_at[3]),
                 (got_ref, half + tokens, tokens, resp_at[4]),
             ):
-                keys[n, at : at + size] = ref[start : start + size, k_at : k_at + HD]
-                values[n, at : at + size] = ref[start : start + size, v_at : v_at + HD]
-        dk_t[...] = jnp.zeros_like(dk_t)
-        dv_t[...] = jnp.zeros_like(dv_t)
-        for ref in (p_bufs, d_bufs, inv_bufs, q_ts, cot_ts):
+                k_rows = ref[start : start + size, k_at : k_at + HD]
+                v_rows = ref[start : start + size, v_at : v_at + HD]
+                keys[n, at : at + size] = k_rows
+                values[n, at : at + size] = v_rows
+                keys_t[n, :, at : at + size] = k_rows.T
+                values_t[n, :, at : at + size] = v_rows.T
+        dk[...] = jnp.zeros_like(dk)
+        dv[...] = jnp.zeros_like(dv)
+        for ref in (p_bufs, d_bufs, inv_bufs, q_ns, cot_ns):
             ref[1] = jnp.zeros(ref.shape[1:], ref.dtype)
-        for work in ahead(0, 0, unit(q_ref, 0), unit(do_ref, 0)):
+        for work in ahead(0, 0, q_ref, do_ref):
             work()
 
     @pl.when(step < last)
     def _():
         kv = kv_of(step)
         together(
-            weigh(0, unit(q_ref, 0), unit(do_ref, 0)),
-            mixed(
-                behind(1, kv_of(step - 1), step - 1),
-                ahead(1, kv, unit(q_ref, 1), unit(do_ref, 1)),
-            ),
+            weigh(0),
+            mixed(behind(1, kv_of(step - 1), step - 1), ahead(1, kv, q_ref, do_ref)),
         )
         together(
-            weigh(1, unit(q_ref, 1), unit(do_ref, 1)),
-            mixed(
-                behind(0, kv, step),
-                ahead(0, kv_of(step + 1), unit(next_q_ref, 0), unit(next_do_ref, 0)),
-            ),
+            weigh(1),
+            mixed(behind(0, kv, step), ahead(0, kv_of(step + 1), next_q_ref, next_do_ref)),
         )
 
     @pl.when(step == last)
@@ -318,10 +317,9 @@
                 (back_ref, half, tokens, resp_at[3]),
                 (back_ref, half + tokens, tokens, resp_at[4]),
             ):
-                grad_k = (dk_t[n, :, at : at + size] * score_scale).T
+                grad_k = dk[n, at : at + size] * score_scale
                 ref[start : start + size, k_cols] = grad_k.astype(ref.dtype)
-                grad_v = dv_t[n, :, at : at + size].T
-                ref[start : start + size, v_cols] = grad_v.astype(ref.dtype)
+                ref[start : start + size, v_cols] = dv[n, at : at + size].astype(ref.dtype)
 
 
 def attention(lengths, resp_q, grad_out, sent, got, own, far):
@@ -352,21 +350,24 @@
             jax.ShapeDtypeStruct((half + 2 * tokens, sent.shape[1]), BF16),
         ],
         scratch_shapes=[
-            pltpu.VMEM((tokens, 5 * tokens), F32),
+            pltpu.VMEM((5 * tokens, tokens), F32),
             pltpu.VMEM((kv_heads, total_keys, HD), BF16),
             pltpu.VMEM((kv_heads, total_keys, HD), BF16),
-            pltpu.VMEM((2, rows, total_keys), F32),
-            pltpu.VMEM((2, rows, total_keys), F32),
-            pltpu.VMEM((2, rows, total_keys), BF16),
-            pltpu.VMEM((2, rows, total_keys), BF16),
-            pltpu.VMEM((2, rows, HD), F32),
-            pltpu.VMEM((2, rows, HD), BF16),
+            pltpu.VMEM((kv_heads, HD, total_keys), BF16),
+            pltpu.VMEM((kv_heads, HD, total_keys), BF16),
+            pltpu.VMEM((2, total_keys, rows), F32),
+            pltpu.VMEM((2, total_keys, rows), F32),
+            pltpu.VMEM((2, total_keys, rows), BF16),
+            pltpu.VMEM((2, total_keys, rows), BF16),
+            pltpu.VMEM((2, 8, rows), F32),
             pltpu.VMEM((2, HD, rows), BF16),
             pltpu.VMEM((2, HD, rows), BF16),
-            pltpu.VMEM((kv_heads, HD, total_keys), F32),
-            pltpu.VMEM((kv_heads, HD, total_keys), F32),
+            pltpu.VMEM((2, rows, HD), BF16),
+            pltpu.VMEM((2, rows, HD), BF16),
+            pltpu.VMEM((kv_heads, total_keys, HD), F32),
+            pltpu.VMEM((kv_heads, total_keys, HD), F32),
         ],
-        compiler_params=pltpu.CompilerParams(vmem_limit_bytes=40 * 1024 * 1024),
+        compiler_params=pltpu.CompilerParams(vmem_limit_bytes=(40 if halves == 1 else 50) << 20),
         cost_estimate=pl.CostEstimate(
             flops=12 * HD * pairs, bytes_accessed=8 * resp_q.size, transcendentals=pairs
         ),

time: 115 us -> 113 us (0.983)
  Pallas kernels: 55.4 us -> 54.1 us
    pallas_call x1, Pallas kernels: 52.3 us -> 51 us  [attention(): pl.pallas_call(functools.partial(attention_kernel, tokens, halves, steps...]
where the time goes in v6:
time: 113 us; the launch traced here: 112 us
  Pallas kernels  54.1 us (48%)
  waiting for transfers between devices  29.6 us (26%)
  starting transfers between devices  26.9 us (24%)
    pallas_call x1, Pallas kernels, attention(): pl.pallas_call(functools.partial(attention_kernel, tokens, halves, steps...  51 us
    ppermute x6, waiting for transfers between devices, swap_chips(): lax.ppermute(array, 'seq', [(i, i ^ by * CORES) for i in range(devices)])  13.7 us
    ppermute x6, waiting for transfers between devices, swap_heads(): return lax.ppermute(array, 'head', [(i, i ^ by) for i in range(devices)])  10.3 us
    ppermute x6, starting transfers between devices, swap_chips(): lax.ppermute(array, 'seq', [(i, i ^ by * CORES) for i in range(devices)])  8.93 us
    ppermute x6, starting transfers between devices, swap_heads(): return lax.ppermute(array, 'head', [(i, i ^ by) for i in range(devices)])  8.9 us
    ppermute x4, starting transfers between devices, shift_chips(): lax.ppermute(array, 'seq', [(i, i + by) for i in range(devices) if 0 <= i...  8.83 us
    ppermute x2, waiting for transfers between devices, swap_cores(): return lax.ppermute(array, 'seq', [(i, i ^ 1) for i in range(devices)])  5.56 us
  transfers between devices with their start and end apart: 18, of which 10 were waited for; matrix products, arithmetic and copies ran while one was open for 0% of the time, Pallas kernels for 0%

profile of v6, /device:TPU:6, one launch (start us, length us, event | category | flops | bytes accessed | tf_op | source)
XLA Modules:
  0.0 112.3 jit_solution(6090825038219567877)
XLA Ops:
  0.6 1.9 %pack.1 = (bf16[40,512]{1,0:T(8,128)(2,1)}, bf16[40,512]{1,0:T(8,128)(2,1)}, bf16[40,512]{1,0:T(8,128)(2,1)}, bf16[40,512]{1,0:T(8,128)(2,1)}, bf16[256,512]{1,0:T(8,128)(2,1)}) custom-call(bf16[40,1024]{1,0:T(8,128)(2,1)} %pk_ref.1, bf16[40,1024]{1,0:T(8,128)(2,1)} %pv_ref.1, bf16[256,256]{1,0:T(8,128)(2,1)} %rk_ref.1, bf16[256,256]{1,0:T(8,128)(2,1)} %rv_ref.1), custom_call_target="tpu_custom_call" | custom-call | tf_op jit(solution)/shard_map/pack/pallas_call | solution.py:64
  2.5 1.4 %collective-permute-start.4 = (bf16[256,512]{1,0:T(8,128)(2,1)}, bf16[256,512]{1,0:T(8,128)(2,1)S(1)}, u32[]{:S(2)}, u32[]{:S(2)}) collective-permute-start(bf16[256,512]{1,0:T(8,128)(2,1)} %get-tuple-element.46.own_ref), channel_id=1, source_target_pairs={{0,16},{4,20},{8,24},{12,28},{1,17},{5,21},{9,25},{13,29},{2,18},{... | collective-permute-start | bytes 786440 | tf_op jit(solution)/shard_map/ppermute | solution.py:396
  3.9 1.3 %collective-permute-start.3 = (bf16[256,512]{1,0:T(8,128)(2,1)}, bf16[256,512]{1,0:T(8,128)(2,1)S(1)}, u32[]{:S(2)}, u32[]{:S(2)}) collective-permute-start(bf16[256,512]{1,0:T(8,128)(2,1)} %get-tuple-element.46.own_ref), channel_id=1, source_target_pairs={{0,8},{4,12},{8,16},{12,20},{16,24},{20,28},{1,9},{5,13},{9,17},{1... | collective-permute-start | bytes 786440 | tf_op jit(solution)/shard_map/ppermute | solution.py:396
  5.2 1.6 %collective-permute-start = (bf16[40,512]{1,0:T(8,128)(2,1)}, bf16[40,512]{1,0:T(8,128)(2,1)S(1)}, u32[]{:S(2)}, u32[]{:S(2)}) collective-permute-start(bf16[40,512]{1,0:T(8,128)(2,1)} %get-tuple-element.43), channel_id=1, source_target_pairs={{0,1},{1,0},{2,3},{3,2},{4,5},{5,4},{6,7},{7,6},{8,9},{9,8},{10,11... | collective-permute-start | bytes 122888 | tf_op jit(solution)/shard_map/ppermute | solution.py:380
  6.9 2.6 %collective-permute-start.1 = (bf16[40,512]{1,0:T(8,128)(2,1)}, bf16[40,512]{1,0:T(8,128)(2,1)S(1)}, u32[]{:S(2)}, u32[]{:S(2)}) collective-permute-start(bf16[40,512]{1,0:T(8,128)(2,1)} %get-tuple-element.44), channel_id=1, source_target_pairs={{0,2},{1,3},{2,0},{3,1},{4,6},{5,7},{6,4},{7,5},{8,10},{9,11},{10,... | collective-permute-start | bytes 122888 | tf_op jit(solution)/shard_map/ppermute | solution.py:380
  9.5 0.2 collective-permute-start.2
  9.7 3.1 %collective-permute-done.1 = bf16[40,512]{1,0:T(8,128)(2,1)S(1)} collective-permute-done((bf16[40,512]{1,0:T(8,128)(2,1)}, bf16[40,512]{1,0:T(8,128)(2,1)S(1)}, u32[]{:S(2)}, u32[]{:S(2)}) %collective-permute-start.1) | collective-permute-done | bytes 40992 | tf_op jit(solution)/shard_map/ppermute | solution.py:380
  12.8 2.7 %collective-permute-done.2 = bf16[40,512]{1,0:T(8,128)(2,1)S(1)} collective-permute-done((bf16[40,512]{1,0:T(8,128)(2,1)}, bf16[40,512]{1,0:T(8,128)(2,1)S(1)}, u32[]{:S(2)}, u32[]{:S(2)}) %collective-permute-start.2) | collective-permute-done | bytes 40992 | tf_op jit(solution)/shard_map/ppermute | solution.py:380
  15.5 0.8 constant_dynamic-update-slice_fusion.3
  16.3 3.5 %collective-permute-start.5 = (bf16[160,512]{1,0:T(8,128)(2,1)S(1)}, bf16[160,512]{1,0:T(8,128)(2,1)S(1)}, u32[]{:S(2)}, u32[]{:S(2)}) collective-permute-start(bf16[160,512]{1,0:T(8,128)(2,1)S(1)} %get-tuple-element.78), channel_id=1, source_target_pairs={{0,8},{4,12},{8,0},{12,4},{16,24},{20,28},{24,16},{28,20},{1,9},{5... | collective-permute-start | bytes 491528 | tf_op jit(solution)/shard_map/ppermute | solution.py:385
  19.9 1.9 %collective-permute-start.6 = (bf16[160,512]{1,0:T(8,128)(2,1)S(1)}, bf16[160,512]{1,0:T(8,128)(2,1)S(1)}, u32[]{:S(2)}, u32[]{:S(2)}) collective-permute-start(bf16[160,512]{1,0:T(8,128)(2,1)S(1)} %get-tuple-element.78), channel_id=1, source_target_pairs={{0,16},{4,20},{8,24},{12,28},{16,0},{20,4},{24,8},{28,12},{1,17},{... | collective-permute-start | bytes 491528 | tf_op jit(solution)/shard_map/ppermute | solution.py:385
  21.7 2.5 %collective-permute-done.5 = bf16[160,512]{1,0:T(8,128)(2,1)S(1)} collective-permute-done((bf16[160,512]{1,0:T(8,128)(2,1)S(1)}, bf16[160,512]{1,0:T(8,128)(2,1)S(1)}, u32[]{:S(2)}, u32[]{:S(2)}) %collective-permute-start.5) | collective-permute-done | bytes 163872 | tf_op jit(solution)/shard_map/ppermute | solution.py:385
  24.2 3.9 %collective-permute-done.6 = bf16[160,512]{1,0:T(8,128)(2,1)S(1)} collective-permute-done((bf16[160,512]{1,0:T(8,128)(2,1)S(1)}, bf16[160,512]{1,0:T(8,128)(2,1)S(1)}, u32[]{:S(2)}, u32[]{:S(2)}) %collective-permute-start.6) | collective-permute-done | bytes 163872 | tf_op jit(solution)/shard_map/ppermute | solution.py:385
  28.4 2.8 %collective-permute-done.8.got_ref = bf16[1152,512]{1,0:T(8,128)(2,1)S(1)} collective-permute-done((bf16[1152,512]{1,0:T(8,128)(2,1)S(1)}, bf16[1152,512]{1,0:T(8,128)(2,1)S(1)}, u32[]{:S(2)}, u32[]{:S(2)}) %collective-permute-start.8) | collective-permute-done | bytes 1179680 | tf_op jit(solution)/shard_map/ppermute | solution.py:390
  31.2 51.0 %attention.1 = (bf16[256,2048]{1,0:T(8,128)(2,1)}, bf16[256,2048]{1,0:T(8,128)(2,1)}, f32[1408,512]{1,0:T(8,128)S(1)}, bf16[1152,512]{1,0:T(8,128)(2,1)S(1)}) custom-call(s32[8]{0:T(128)S(1)} %copy-done.3, bf16[256,2048]{1,0:T(8,128)(2,1)S(1)} %copy-done.1, bf16[256,2048]{1,0:T(8,128)(2,1)S(1)} %copy-done.1, bf16[256,2048]{1,0:T(8,128)(2,1)S(1)} %copy-done.2, ...), custom_call_target="tpu_custom_call" | custom-call | flops 16106127360 | bytes 4194304 | tf_op jit(solution)/shard_map/attention/pallas_call | solution.py:340
  82.3 0.1 collective-permute-start.9
  82.4 2.7 %collective-permute-done.9.got_ref = bf16[1152,512]{1,0:T(8,128)(2,1)S(1)} collective-permute-done((bf16[1152,512]{1,0:T(8,128)(2,1)S(1)}, bf16[1152,512]{1,0:T(8,128)(2,1)S(1)}, u32[]{:S(2)}, u32[]{:S(2)}) %collective-permute-start.9) | collective-permute-done | bytes 1179680 | tf_op jit(solution)/shard_map/ppermute | solution.py:390
  85.1 0.3 merge.1
  85.4 0.4 collective-permute-start.10
  85.9 1.6 %collective-permute-start.11 = (bf16[160,512]{1,0:T(8,128)(2,1)S(1)}, bf16[160,512]{1,0:T(8,128)(2,1)S(1)}, u32[]{:S(2)}, u32[]{:S(2)}) collective-permute-start(bf16[160,512]{1,0:T(8,128)(2,1)S(1)} %get-tuple-element.60), channel_id=1, source_target_pairs={{0,16},{4,20},{8,24},{12,28},{16,0},{20,4},{24,8},{28,12},{1,17},{... | collective-permute-start | bytes 491528 | tf_op jit(solution)/shard_map/ppermute | solution.py:385
  87.4 1.6 %collective-permute-start.12 = (bf16[160,512]{1,0:T(8,128)(2,1)S(1)}, bf16[160,512]{1,0:T(8,128)(2,1)S(1)}, u32[]{:S(2)}, u32[]{:S(2)}) collective-permute-start(bf16[160,512]{1,0:T(8,128)(2,1)S(1)} %get-tuple-element.61), channel_id=1, source_target_pairs={{0,24},{4,28},{8,16},{12,20},{16,8},{20,12},{24,0},{28,4},{1,25},{... | collective-permute-start | bytes 491528 | tf_op jit(solution)/shard_map/ppermute | solution.py:385
  89.0 3.6 %collective-permute-done.10.refs_1_ = bf16[160,512]{1,0:T(8,128)(2,1)S(1)} collective-permute-done((bf16[160,512]{1,0:T(8,128)(2,1)S(1)}, bf16[160,512]{1,0:T(8,128)(2,1)S(1)}, u32[]{:S(2)}, u32[]{:S(2)}) %collective-permute-start.10) | collective-permute-done | bytes 163872 | tf_op jit(solution)/shard_map/ppermute | solution.py:385
  92.6 3.8 %collective-permute-done.12.refs_3_ = bf16[160,512]{1,0:T(8,128)(2,1)S(1)} collective-permute-done((bf16[160,512]{1,0:T(8,128)(2,1)S(1)}, bf16[160,512]{1,0:T(8,128)(2,1)S(1)}, u32[]{:S(2)}, u32[]{:S(2)}) %collective-permute-start.12) | collective-permute-done | bytes 163872 | tf_op jit(solution)/shard_map/ppermute | solution.py:385
  96.3 2.6 %collective-permute-start.13 = (bf16[256,512]{1,0:T(8,128)(2,1)S(1)}, bf16[256,512]{1,0:T(8,128)(2,1)S(1)}, u32[]{:S(2)}, u32[]{:S(2)}) collective-permute-start(bf16[256,512]{1,0:T(8,128)(2,1)S(1)} %get-tuple-element.64), channel_id=1, source_target_pairs={{8,0},{12,4},{16,8},{20,12},{24,16},{28,20},{9,1},{13,5},{17,9},{2... | collective-permute-start | bytes 786440 | tf_op jit(solution)/shard_map/ppermute | solution.py:396
  98.9 3.5 %collective-permute-start.14 = (bf16[256,512]{1,0:T(8,128)(2,1)S(1)}, bf16[256,512]{1,0:T(8,128)(2,1)S(1)}, u32[]{:S(2)}, u32[]{:S(2)}) collective-permute-start(bf16[256,512]{1,0:T(8,128)(2,1)S(1)} %get-tuple-element.65), channel_id=1, source_target_pairs={{16,0},{20,4},{24,8},{28,12},{17,1},{21,5},{25,9},{29,13},{18,2},{... | collective-permute-start | bytes 786440 | tf_op jit(solution)/shard_map/ppermute | solution.py:396
  102.5 0.1 sum_chips.1
  102.6 0.5 collective-permute-start.15
  103.1 2.6 %collective-permute-start.16 = (bf16[40,512]{1,0:T(8,128)(2,1)S(1)}, bf16[40,512]{1,0:T(8,128)(2,1)S(1)}, u32[]{:S(2)}, u32[]{:S(2)}) collective-permute-start(bf16[40,512]{1,0:T(8,128)(2,1)S(1)} %get-tuple-element.72), channel_id=1, source_target_pairs={{0,2},{1,3},{2,0},{3,1},{4,6},{5,7},{6,4},{7,5},{8,10},{9,11},{10,... | collective-permute-start | bytes 122888 | tf_op jit(solution)/shard_map/ppermute | solution.py:380
  105.7 1.3 %collective-permute-start.17 = (bf16[40,512]{1,0:T(8,128)(2,1)S(1)}, bf16[40,512]{1,0:T(8,128)(2,1)S(1)}, u32[]{:S(2)}, u32[]{:S(2)}) collective-permute-start(bf16[40,512]{1,0:T(8,128)(2,1)S(1)} %get-tuple-element.73), channel_id=1, source_target_pairs={{0,3},{1,2},{2,1},{3,0},{4,7},{5,6},{6,5},{7,4},{8,11},{9,10},{10,... | collective-permute-start | bytes 122888 | tf_op jit(solution)/shard_map/ppermute | solution.py:380
  107.0 1.4 %collective-permute-done.16.refs_2_ = bf16[40,512]{1,0:T(8,128)(2,1)S(1)} collective-permute-done((bf16[40,512]{1,0:T(8,128)(2,1)S(1)}, bf16[40,512]{1,0:T(8,128)(2,1)S(1)}, u32[]{:S(2)}, u32[]{:S(2)}) %collective-permute-start.16) | collective-permute-done | bytes 40992 | tf_op jit(solution)/shard_map/ppermute | solution.py:380
  108.4 3.1 %collective-permute-done.17.refs_3_ = bf16[40,512]{1,0:T(8,128)(2,1)S(1)} collective-permute-done((bf16[40,512]{1,0:T(8,128)(2,1)S(1)}, bf16[40,512]{1,0:T(8,128)(2,1)S(1)}, u32[]{:S(2)}, u32[]{:S(2)}) %collective-permute-start.17) | collective-permute-done | bytes 40992 | tf_op jit(solution)/shard_map/ppermute | solution.py:380
  111.5 0.8 finish.1
  (26 shorter events, 0.3 us)
Async XLA Ops:
  2.5 25.7 %copy-start = (bf16[256,512]{1,0:T(8,128)(2,1)S(1)}, bf16[256,512]{1,0:T(8,128)(2,1)}, u32[]{:S(2)}) copy-start(bf16[256,512]{1,0:T(8,128)(2,1)} %get-tuple-element.46.own_ref) | copy-start | bytes 786436
  2.5 13.0 %collective-permute-start.4 = (bf16[256,512]{1,0:T(8,128)(2,1)}, bf16[256,512]{1,0:T(8,128)(2,1)S(1)}, u32[]{:S(2)}, u32[]{:S(2)}) collective-permute-start(bf16[256,512]{1,0:T(8,128)(2,1)} %get-tuple-element.46.own_ref), channel_id=1, source_target_pairs={{0,16},{4,20},{8,24},{12,28},{1,17},{5,21},{9,25},{13,29},{2,18},{... | collective-permute-start | bytes 786440 | tf_op jit(solution)/shard_map/ppermute | solution.py:396
  3.9 11.5 %collective-permute-start.3 = (bf16[256,512]{1,0:T(8,128)(2,1)}, bf16[256,512]{1,0:T(8,128)(2,1)S(1)}, u32[]{:S(2)}, u32[]{:S(2)}) collective-permute-start(bf16[256,512]{1,0:T(8,128)(2,1)} %get-tuple-element.46.own_ref), channel_id=1, source_target_pairs={{0,8},{4,12},{8,16},{12,20},{16,24},{20,28},{1,9},{5,13},{9,17},{1... | collective-permute-start | bytes 786440 | tf_op jit(solution)/shard_map/ppermute | solution.py:396
  5.2 4.5 %collective-permute-start = (bf16[40,512]{1,0:T(8,128)(2,1)}, bf16[40,512]{1,0:T(8,128)(2,1)S(1)}, u32[]{:S(2)}, u32[]{:S(2)}) collective-permute-start(bf16[40,512]{1,0:T(8,128)(2,1)} %get-tuple-element.43), channel_id=1, source_target_pairs={{0,1},{1,0},{2,3},{3,2},{4,5},{5,4},{6,7},{7,6},{8,9},{9,8},{10,11... | collective-permute-start | bytes 122888 | tf_op jit(solution)/shard_map/ppermute | solution.py:380
  6.9 5.9 %collective-permute-start.1 = (bf16[40,512]{1,0:T(8,128)(2,1)}, bf16[40,512]{1,0:T(8,128)(2,1)S(1)}, u32[]{:S(2)}, u32[]{:S(2)}) collective-permute-start(bf16[40,512]{1,0:T(8,128)(2,1)} %get-tuple-element.44), channel_id=1, source_target_pairs={{0,2},{1,3},{2,0},{3,1},{4,6},{5,7},{6,4},{7,5},{8,10},{9,11},{10,... | collective-permute-start | bytes 122888 | tf_op jit(solution)/shard_map/ppermute | solution.py:380
  9.5 6.0 %collective-permute-start.2 = (bf16[40,512]{1,0:T(8,128)(2,1)}, bf16[40,512]{1,0:T(8,128)(2,1)S(1)}, u32[]{:S(2)}, u32[]{:S(2)}) collective-permute-start(bf16[40,512]{1,0:T(8,128)(2,1)} %get-tuple-element.45), channel_id=1, source_target_pairs={{0,3},{1,2},{2,1},{3,0},{4,7},{5,6},{6,5},{7,4},{8,11},{9,10},{10,... | collective-permute-start | bytes 122888 | tf_op jit(solution)/shard_map/ppermute | solution.py:380
  16.3 14.9 %copy-start.1 = (bf16[256,2048]{1,0:T(8,128)(2,1)S(1)}, bf16[256,2048]{1,0:T(8,128)(2,1)}, u32[]{:S(2)}) copy-start(bf16[256,2048]{1,0:T(8,128)(2,1)} %next_q_ref.1) | copy-start | bytes 3145732
  16.3 14.9 %copy-start.3 = (s32[8]{0:T(128)S(1)}, s32[8]{0:T(128)}, u32[]{:S(2)}) copy-start(s32[8]{0:T(128)} %lengths.1) | copy-start | bytes 100
  16.3 7.9 %collective-permute-start.5 = (bf16[160,512]{1,0:T(8,128)(2,1)S(1)}, bf16[160,512]{1,0:T(8,128)(2,1)S(1)}, u32[]{:S(2)}, u32[]{:S(2)}) collective-permute-start(bf16[160,512]{1,0:T(8,128)(2,1)S(1)} %get-tuple-element.78), channel_id=1, source_target_pairs={{0,8},{4,12},{8,0},{12,4},{16,24},{20,28},{24,16},{28,20},{1,9},{5... | collective-permute-start | bytes 491528 | tf_op jit(solution)/shard_map/ppermute | solution.py:385
  19.9 8.3 %collective-permute-start.6 = (bf16[160,512]{1,0:T(8,128)(2,1)S(1)}, bf16[160,512]{1,0:T(8,128)(2,1)S(1)}, u32[]{:S(2)}, u32[]{:S(2)}) collective-permute-start(bf16[160,512]{1,0:T(8,128)(2,1)S(1)} %get-tuple-element.78), channel_id=1, source_target_pairs={{0,16},{4,20},{8,24},{12,28},{16,0},{20,4},{24,8},{28,12},{1,17},{... | collective-permute-start | bytes 491528 | tf_op jit(solution)/shard_map/ppermute | solution.py:385
  21.7 9.5 %copy-start.2 = (bf16[256,2048]{1,0:T(8,128)(2,1)S(1)}, bf16[256,2048]{1,0:T(8,128)(2,1)}, u32[]{:S(2)}) copy-start(bf16[256,2048]{1,0:T(8,128)(2,1)} %next_do_ref.1) | copy-start | bytes 3145732
  21.7 6.5 %collective-permute-start.7 = (bf16[160,512]{1,0:T(8,128)(2,1)S(1)}, bf16[160,512]{1,0:T(8,128)(2,1)S(1)}, u32[]{:S(2)}, u32[]{:S(2)}) collective-permute-start(bf16[160,512]{1,0:T(8,128)(2,1)S(1)} %get-tuple-element.78), channel_id=1, source_target_pairs={{0,24},{4,28},{8,16},{12,20},{16,8},{20,12},{24,0},{28,4},{1,25},{... | collective-permute-start | bytes 491528 | tf_op jit(solution)/shard_map/ppermute | solution.py:385
  28.3 2.9 %collective-permute-start.8 = (bf16[1152,512]{1,0:T(8,128)(2,1)S(1)}, bf16[1152,512]{1,0:T(8,128)(2,1)S(1)}, u32[]{:S(2)}, u32[]{:S(2)}) collective-permute-start(bf16[1152,512]{1,0:T(8,128)(2,1)S(1)} %select_dynamic-update-slice_fusion.sent_ref), channel_id=1, source_target_pairs={{0,4},{4,0},{8,12},{12,8},{16,20},{20,16},{24,28},{28,24},{1,5},{5... | collective-permute-start | bytes 3538952 | tf_op jit(solution)/shard_map/ppermute | solution.py:390
  82.3 2.8 %collective-permute-start.9 = (bf16[1152,512]{1,0:T(8,128)(2,1)S(1)}, bf16[1152,512]{1,0:T(8,128)(2,1)S(1)}, u32[]{:S(2)}, u32[]{:S(2)}) collective-permute-start(bf16[1152,512]{1,0:T(8,128)(2,1)S(1)} %get-tuple-element.56), channel_id=1, source_target_pairs={{0,4},{4,0},{8,12},{12,8},{16,20},{20,16},{24,28},{28,24},{1,5},{5... | collective-permute-start | bytes 3538952 | tf_op jit(solution)/shard_map/ppermute | solution.py:390
  85.4 7.1 %collective-permute-start.10 = (bf16[160,512]{1,0:T(8,128)(2,1)S(1)}, bf16[160,512]{1,0:T(8,128)(2,1)S(1)}, u32[]{:S(2)}, u32[]{:S(2)}) collective-permute-start(bf16[160,512]{1,0:T(8,128)(2,1)S(1)} %get-tuple-element.59), channel_id=1, source_target_pairs={{0,8},{4,12},{8,0},{12,4},{16,24},{20,28},{24,16},{28,20},{1,9},{5... | collective-permute-start | bytes 491528 | tf_op jit(solution)/shard_map/ppermute | solution.py:385
  85.9 6.7 %collective-permute-start.11 = (bf16[160,512]{1,0:T(8,128)(2,1)S(1)}, bf16[160,512]{1,0:T(8,128)(2,1)S(1)}, u32[]{:S(2)}, u32[]{:S(2)}) collective-permute-start(bf16[160,512]{1,0:T(8,128)(2,1)S(1)} %get-tuple-element.60), channel_id=1, source_target_pairs={{0,16},{4,20},{8,24},{12,28},{16,0},{20,4},{24,8},{28,12},{1,17},{... | collective-permute-start | bytes 491528 | tf_op jit(solution)/shard_map/ppermute | solution.py:385
  87.4 8.9 %collective-permute-start.12 = (bf16[160,512]{1,0:T(8,128)(2,1)S(1)}, bf16[160,512]{1,0:T(8,128)(2,1)S(1)}, u32[]{:S(2)}, u32[]{:S(2)}) collective-permute-start(bf16[160,512]{1,0:T(8,128)(2,1)S(1)} %get-tuple-element.61), channel_id=1, source_target_pairs={{0,24},{4,28},{8,16},{12,20},{16,8},{20,12},{24,0},{28,4},{1,25},{... | collective-permute-start | bytes 491528 | tf_op jit(solution)/shard_map/ppermute | solution.py:385
  96.3 15.2 %collective-permute-start.13 = (bf16[256,512]{1,0:T(8,128)(2,1)S(1)}, bf16[256,512]{1,0:T(8,128)(2,1)S(1)}, u32[]{:S(2)}, u32[]{:S(2)}) collective-permute-start(bf16[256,512]{1,0:T(8,128)(2,1)S(1)} %get-tuple-element.64), channel_id=1, source_target_pairs={{8,0},{12,4},{16,8},{20,12},{24,16},{28,20},{9,1},{13,5},{17,9},{2... | collective-permute-start | bytes 786440 | tf_op jit(solution)/shard_map/ppermute | solution.py:396
  98.9 12.6 %collective-permute-start.14 = (bf16[256,512]{1,0:T(8,128)(2,1)S(1)}, bf16[256,512]{1,0:T(8,128)(2,1)S(1)}, u32[]{:S(2)}, u32[]{:S(2)}) collective-permute-start(bf16[256,512]{1,0:T(8,128)(2,1)S(1)} %get-tuple-element.65), channel_id=1, source_target_pairs={{16,0},{20,4},{24,8},{28,12},{17,1},{21,5},{25,9},{29,13},{18,2},{... | collective-permute-start | bytes 786440 | tf_op jit(solution)/shard_map/ppermute | solution.py:396
  102.6 4.5 %collective-permute-start.15 = (bf16[40,512]{1,0:T(8,128)(2,1)S(1)}, bf16[40,512]{1,0:T(8,128)(2,1)S(1)}, u32[]{:S(2)}, u32[]{:S(2)}) collective-permute-start(bf16[40,512]{1,0:T(8,128)(2,1)S(1)} %get-tuple-element.71), channel_id=1, source_target_pairs={{0,1},{1,0},{2,3},{3,2},{4,5},{5,4},{6,7},{7,6},{8,9},{9,8},{10,11... | collective-permute-start | bytes 122888 | tf_op jit(solution)/shard_map/ppermute | solution.py:380
  103.1 5.3 %collective-permute-start.16 = (bf16[40,512]{1,0:T(8,128)(2,1)S(1)}, bf16[40,512]{1,0:T(8,128)(2,1)S(1)}, u32[]{:S(2)}, u32[]{:S(2)}) collective-permute-start(bf16[40,512]{1,0:T(8,128)(2,1)S(1)} %get-tuple-element.72), channel_id=1, source_target_pairs={{0,2},{1,3},{2,0},{3,1},{4,6},{5,7},{6,4},{7,5},{8,10},{9,11},{10,... | collective-permute-start | bytes 122888 | tf_op jit(solution)/shard_map/ppermute | solution.py:380
  105.7 5.8 %collective-permute-start.17 = (bf16[40,512]{1,0:T(8,128)(2,1)S(1)}, bf16[40,512]{1,0:T(8,128)(2,1)S(1)}, u32[]{:S(2)}, u32[]{:S(2)}) collective-permute-start(bf16[40,512]{1,0:T(8,128)(2,1)S(1)} %get-tuple-element.73), channel_id=1, source_target_pairs={{0,3},{1,2},{2,1},{3,0},{4,7},{5,6},{6,5},{7,4},{8,11},{9,10},{10,... | collective-permute-start | bytes 122888 | tf_op jit(solution)/shard_map/ppermute | solution.py:380

commit v7 on v6

--- a/solution.py
+++ b/solution.py
@@ -11,7 +11,7 @@
 HD = 128
 CORES = 2
 FAR = 4
-CHUNK = 640
+CHUNK = 1280
 TILE = 64
 MOST_SCORES = 2560 * 256
 NEG = -1e30
@@ -116,49 +116,70 @@
 
 
 def attention_kernel(
-    tokens, halves, steps_per_kv,
-    lengths, q_ref, next_q_ref, do_ref, next_do_ref, sent_ref, got_ref, own_ref, far_ref,
+    halves, lengths, q_ref, do_ref, sent_ref, got_ref, own_ref, far_ref,
     o_ref, dq_ref, kept_ref, back_ref,
-    bias, keys, values, keys_t, values_t, s_bufs, g_bufs, p_bufs, d_bufs, inv_bufs,
+    bias, keys, values, keys_t, values_t, s_bufs, g_bufs, p_bufs, d_bufs, top_bufs, inv_bufs,
     q_ts, cot_ts, q_ns, cot_ns, dk, dv,
 ):
     kv_heads, total_keys = keys.shape[0], keys.shape[1]
+    tokens, q_cols = q_ref.shape
     rows = tokens // halves
     prompt_len = total_keys - 5 * tokens
     half = prompt_len // 2
-    step = pl.program_id(0)
-    last = pl.num_programs(0) - 1
+    steps = q_cols // HD * halves // 2
+    steps_per_kv = steps // kv_heads
     score_scale = 1.0 / math.sqrt(HD)
     exp_scale = score_scale * math.log2(math.e)
     resp_at = [prompt_len + i * tokens for i in range(6)]
     tiles = [slice(at, at + TILE) for at in range(0, total_keys, TILE)]
     chunks = [slice(at, at + CHUNK) for at in range(0, total_keys, CHUNK)]
 
-    def unit(ref, which):
-        if halves == 1:
-            return ref[:, which * HD : (which + 1) * HD]
-        return ref[which * rows : (which + 1) * rows, :HD]
-
-    def kv_of(at_step):
-        return jnp.clip(at_step // steps_per_kv, 0, kv_heads - 1)
-
-    def ahead(which, kv, q_from, cot_from):
+    def place_of(which, step):
+        head = step * 2 + which if halves == 1 else step
+        row = 0 if halves == 1 else which * rows
+        return slice(row, row + rows), pl.ds(pl.multiple_of(head * HD, HD), HD)
+
+    def kv_of(step):
+        return jnp.clip(step // steps_per_kv, 0, kv_heads - 1)
+
+    def bias_at(which, at, size):
+        row = which * rows * (halves - 1)
+        return bias[at - prompt_len : at - prompt_len + size, row : row + rows]
+
+    def folded(x):
+        return x.reshape(x.shape[0] // 8, 8, rows)
+
+    def ahead(which, step):
+        kv = kv_of(step)
+        where = place_of(which, jnp.minimum(step, steps - 1))
+
         def lift():
-            q_ts[which] = unit(q_from, which).T
-            cot_ts[which] = unit(cot_from, which).T
+            q_ts[which] = q_ref[where].T
+            cot_ts[which] = do_ref[where].T
 
         def scores(at):
-            s_bufs[which, at] = dot(keys[kv, at], q_ts[which])
+            whole_s = dot(keys[kv, at], q_ts[which])
+            top = None
+            for start in range(at.start, at.stop, TILE):
+                s = whole_s[start - at.start : start - at.start + TILE]
+                if start >= prompt_len:
+                    s = s + bias_at(which, start, TILE)
+                s_bufs[which, start : start + TILE] = s
+                part = jnp.max(folded(s), axis=0)
+                top = part if top is None else jnp.maximum(top, part)
+            if at.start == 0:
+                top_bufs[which] = top
+            else:
+                top_bufs[which] = jnp.maximum(top_bufs[which], top)
 
         def grads(at):
             g_bufs[which, at] = dot(values[kv, at], cot_ts[which])
 
         return [lift] + [functools.partial(f, at) for at in chunks for f in (scores, grads)]
 
-    def behind(which, kv, at_step):
-        head = jnp.maximum(at_step, 0) * (2 // halves) + (which if halves == 1 else 0)
-        cols = pl.ds(pl.multiple_of(head * HD, HD), HD)
-        rows_at = slice(0, rows) if halves == 1 else slice(which * rows, (which + 1) * rows)
+    def behind(which, step):
+        kv = kv_of(step)
+        where = place_of(which, jnp.maximum(step, 0))
         cuts = [slice(at, at + total_keys // 2) for at in (0, total_keys // 2)]
         state = {}
 
@@ -171,11 +192,11 @@
             state["dq"] = state["dq"] + more if "dq" in state else more
 
         def put_output():
-            o_ref[rows_at, cols] = (state["out"] * inv_bufs[which, :1]).astype(BF16).T
+            o_ref[where] = (state["out"] * inv_bufs[which, :1]).astype(BF16).T
 
         def put_query():
             dq = state["dq"] * (inv_bufs[which, :1] * score_scale)
-            dq_ref[rows_at, cols] = dq.astype(BF16).T
+            dq_ref[where] = dq.astype(BF16).T
 
         def value_grad(at):
             dv[kv, at] += dot(p_bufs[which, at], cot_ns[which])
@@ -191,27 +212,13 @@
     def weigh(which):
         state = {}
 
-        def scores(at):
-            s = s_bufs[which, at]
-            if at.start >= prompt_len:
-                row = which * rows * (halves - 1)
-                s = s + bias[at.start - prompt_len : at.stop - prompt_len, row : row + rows]
-            return s
-
-        def folded(x):
-            return x.reshape(TILE // 8, 8, rows)
-
-        def highest(at):
-            top = jnp.max(folded(scores(at)), axis=0)
-            state["top"] = jnp.maximum(state["top"], top) if "top" in state else top
-
         def settle():
-            state["top"] = jnp.max(state["top"], axis=0, keepdims=True) * exp_scale
+            state["top"] = jnp.max(top_bufs[which], axis=0, keepdims=True) * exp_scale
             state["sum"] = jnp.zeros((8, rows), F32)
             state["dot"] = jnp.zeros((8, rows), F32)
 
         def weights(at):
-            p = jnp.exp2(scores(at) * exp_scale - state["top"])
+            p = jnp.exp2(s_bufs[which, at] * exp_scale - state["top"])
             state["sum"] = state["sum"] + jnp.sum(folded(p), axis=0)
             state["dot"] = state["dot"] + jnp.sum(folded(p * g_bufs[which, at]), axis=0)
             p_bufs[which, at] = p.astype(BF16)
@@ -227,8 +234,7 @@
             p = p_bufs[which, at].astype(F32)
             d_bufs[which, at] = (p * (g_bufs[which, at] - state["delta"])).astype(BF16)
 
-        work = [functools.partial(highest, at) for at in tiles] + [settle]
-        work += [functools.partial(weights, at) for at in tiles] + [finish]
+        work = [settle] + [functools.partial(weights, at) for at in tiles] + [finish]
         return work + [functools.partial(slopes, at) for at in tiles]
 
     def together(vector, matrix):
@@ -244,82 +250,72 @@
             first[len(second) :] + second[len(first) :]
         )
 
-    @pl.when(step == 0)
-    def _():
-        place = lax.axis_index("seq")
-        core = lax.rem(place, CORES)
-        first_row = place * tokens
-        row_pos = first_row + lax.broadcasted_iota(jnp.int32, (8, tokens), 1)
-        seg_start = jnp.zeros((8, tokens), jnp.int32)
-        end = jnp.int32(0)
-        for i in range(lengths.shape[0]):
-            end = end + lengths[i]
-            seg_start = jnp.where(row_pos >= end, end, seg_start)
-        seg_start, row_pos = seg_start[:1], row_pos[:1]
-        near = 1 + 2 * core
-        for i, distance in enumerate((0, 2, FAR, near, 4 - near)):
-            for row in range(0, tokens, TILE):
-                key_pos = (first_row - distance * tokens + row) + lax.broadcasted_iota(
-                    jnp.int32, (TILE, tokens), 0
-                )
-                allowed = (key_pos >= seg_start) & (key_pos <= row_pos)
-                at = i * tokens + row
-                bias[at : at + TILE] = jnp.where(allowed, 0.0, NEG)
-        for n in range(kv_heads):
-            k_at, v_at = 2 * n * HD, (2 * n + 1) * HD
-            for ref, start, size, at in (
-                (sent_ref, 0, half, 0),
-                (got_ref, 0, half, half),
-                (own_ref, 0, tokens, resp_at[0]),
-                (sent_ref, half, tokens, resp_at[1]),
-                (far_ref, 0, tokens, resp_at[2]),
-                (got_ref, half, tokens, resp_at[3]),
-                (got_ref, half + tokens, tokens, resp_at[4]),
-            ):
-                k_rows = ref[start : start + size, k_at : k_at + HD]
-                v_rows = ref[start : start + size, v_at : v_at + HD]
-                keys[n, at : at + size] = k_rows
-                values[n, at : at + size] = v_rows
-                keys_t[n, :, at : at + size] = k_rows.T
-                values_t[n, :, at : at + size] = v_rows.T
-        dk[...] = jnp.zeros_like(dk)
-        dv[...] = jnp.zeros_like(dv)
-        for ref in (p_bufs, d_bufs, inv_bufs, q_ns, cot_ns):
-            ref[1] = jnp.zeros(ref.shape[1:], ref.dtype)
-        for work in ahead(0, 0, q_ref, do_ref):
-            work()
-
-    @pl.when(step < last)
-    def _():
-        kv = kv_of(step)
-        together(
-            weigh(0),
-            mixed(behind(1, kv_of(step - 1), step - 1), ahead(1, kv, q_ref, do_ref)),
-        )
-        together(
-            weigh(1),
-            mixed(behind(0, kv, step), ahead(0, kv_of(step + 1), next_q_ref, next_do_ref)),
-        )
-
-    @pl.when(step == last)
-    def _():
-        for work in behind(1, kv_of(step - 1), step - 1):
-            work()
-        for n in range(kv_heads):
-            k_cols = slice(2 * n * HD, (2 * n + 1) * HD)
-            v_cols = slice((2 * n + 1) * HD, (2 * n + 2) * HD)
-            for ref, start, size, at in (
-                (kept_ref, 0, half, 0),
-                (back_ref, 0, half, half),
-                (kept_ref, half + 2 * tokens, tokens, resp_at[0]),
-                (kept_ref, half, tokens, resp_at[1]),
-                (kept_ref, half + tokens, tokens, resp_at[2]),
-                (back_ref, half, tokens, resp_at[3]),
-                (back_ref, half + tokens, tokens, resp_at[4]),
-            ):
-                grad_k = dk[n, at : at + size] * score_scale
-                ref[start : start + size, k_cols] = grad_k.astype(ref.dtype)
-                ref[start : start + size, v_cols] = dv[n, at : at + size].astype(ref.dtype)
+    place = lax.axis_index("seq")
+    core = lax.rem(place, CORES)
+    first_row = place * tokens
+    row_pos = first_row + lax.broadcasted_iota(jnp.int32, (8, tokens), 1)
+    seg_start = jnp.zeros((8, tokens), jnp.int32)
+    end = jnp.int32(0)
+    for i in range(lengths.shape[0]):
+        end = end + lengths[i]
+        seg_start = jnp.where(row_pos >= end, end, seg_start)
+    seg_start, row_pos = seg_start[:1], row_pos[:1]
+    near = 1 + 2 * core
+    for i, distance in enumerate((0, 2, FAR, near, 4 - near)):
+        for row in range(0, tokens, TILE):
+            key_pos = (first_row - distance * tokens + row) + lax.broadcasted_iota(
+                jnp.int32, (TILE, tokens), 0
+            )
+            allowed = (key_pos >= seg_start) & (key_pos <= row_pos)
+            at = i * tokens + row
+            bias[at : at + TILE] = jnp.where(allowed, 0.0, NEG)
+    for n in range(kv_heads):
+        k_at, v_at = 2 * n * HD, (2 * n + 1) * HD
+        for ref, start, size, at in (
+            (sent_ref, 0, half, 0),
+            (got_ref, 0, half, half),
+            (own_ref, 0, tokens, resp_at[0]),
+            (sent_ref, half, tokens, resp_at[1]),
+            (far_ref, 0, tokens, resp_at[2]),
+            (got_ref, half, tokens, resp_at[3]),
+            (got_ref, half + tokens, tokens, resp_at[4]),
+        ):
+            k_rows = ref[start : start + size, k_at : k_at + HD]
+            v_rows = ref[start : start + size, v_at : v_at + HD]
+            keys[n, at : at + size] = k_rows
+            values[n, at : at + size] = v_rows
+            keys_t[n, :, at : at + size] = k_rows.T
+            values_t[n, :, at : at + size] = v_rows.T
+    dk[...] = jnp.zeros_like(dk)
+    dv[...] = jnp.zeros_like(dv)
+    for ref in (p_bufs, d_bufs, inv_bufs, q_ns, cot_ns):
+        ref[1] = jnp.zeros(ref.shape[1:], ref.dtype)
+    for work in ahead(0, 0):
+        work()
+
+    def pair(step, carry):
+        together(weigh(0), mixed(behind(1, step - 1), ahead(1, step)))
+        together(weigh(1), mixed(behind(0, step), ahead(0, step + 1)))
+        return carry
+
+    lax.fori_loop(0, steps, pair, 0)
+    for work in behind(1, steps - 1):
+        work()
+    for n in range(kv_heads):
+        k_cols = slice(2 * n * HD, (2 * n + 1) * HD)
+        v_cols = slice((2 * n + 1) * HD, (2 * n + 2) * HD)
+        for ref, start, size, at in (
+            (kept_ref, 0, half, 0),
+            (back_ref, 0, half, half),
+            (kept_ref, half + 2 * tokens, tokens, resp_at[0]),
+            (kept_ref, half, tokens, resp_at[1]),
+            (kept_ref, half + tokens, tokens, resp_at[2]),
+            (back_ref, half, tokens, resp_at[3]),
+            (back_ref, half + tokens, tokens, resp_at[4]),
+        ):
+            grad_k = dk[n, at : at + size] * score_scale
+            ref[start : start + size, k_cols] = grad_k.astype(ref.dtype)
+            ref[start : start + size, v_cols] = dv[n, at : at + size].astype(ref.dtype)
 
 
 def attention(lengths, resp_q, grad_out, sent, got, own, far):
@@ -330,18 +326,10 @@
     q_heads = resp_q.shape[1] // HD
     halves = 1 if tokens * total_keys <= MOST_SCORES else 2
     rows = tokens // halves
-    steps = q_heads * halves // 2
-    width = 2 // halves * HD
-
-    def block(later):
-        return pl.BlockSpec((tokens, width), lambda i: (0, jnp.minimum(i + later, steps - 1)))
-
     pairs = tokens * q_heads * total_keys
     return pl.pallas_call(
-        functools.partial(attention_kernel, tokens, halves, steps // kv_heads),
-        grid=(steps + 1,),
-        in_specs=[pl.BlockSpec(memory_space=pltpu.SMEM), block(0), block(1), block(0), block(1)]
-        + whole(4),
+        functools.partial(attention_kernel, halves),
+        in_specs=[pl.BlockSpec(memory_space=pltpu.SMEM)] + whole(6),
         out_specs=whole(4),
         out_shape=[
             jax.ShapeDtypeStruct(resp_q.shape, BF16),
@@ -360,6 +348,7 @@
             pltpu.VMEM((2, total_keys, rows), BF16),
             pltpu.VMEM((2, total_keys, rows), BF16),
             pltpu.VMEM((2, 8, rows), F32),
+            pltpu.VMEM((2, 8, rows), F32),
             pltpu.VMEM((2, HD, rows), BF16),
             pltpu.VMEM((2, HD, rows), BF16),
             pltpu.VMEM((2, rows, HD), BF16),
@@ -367,12 +356,12 @@
             pltpu.VMEM((kv_heads, total_keys, HD), F32),
             pltpu.VMEM((kv_heads, total_keys, HD), F32),
         ],
-        compiler_params=pltpu.CompilerParams(vmem_limit_bytes=(40 if halves == 1 else 50) << 20),
+        compiler_params=pltpu.CompilerParams(vmem_limit_bytes=(36 if halves == 1 else 48) << 20),
         cost_estimate=pl.CostEstimate(
             flops=12 * HD * pairs, bytes_accessed=8 * resp_q.size, transcendentals=pairs
         ),
         name="attention",
-    )(lengths, resp_q, resp_q, grad_out, grad_out, sent, got, own, far)
+    )(lengths, resp_q, grad_out, sent, got, own, far)
 
 
 def swap_heads(array, by):

time: 113 us -> 109 us (0.965)
  Pallas kernels: 54.1 us -> 49.8 us
    pallas_call x1, Pallas kernels: 51 us -> 46.8 us  [attention(): pl.pallas_call(functools.partial(attention_kernel, halves), in_specs=[pl....]
where the time goes in v7:
time: 109 us; the launch traced here: 108 us
  Pallas kernels  49.8 us (46%)
  waiting for transfers between devices  29.6 us (27%)
  starting transfers between devices  26.9 us (25%)
    pallas_call x1, Pallas kernels, attention(): pl.pallas_call(functools.partial(attention_kernel, halves), in_specs=[pl....  46.8 us
    ppermute x6, waiting for transfers between devices, swap_chips(): lax.ppermute(array, 'seq', [(i, i ^ by * CORES) for i in range(devices)])  13.8 us
    ppermute x6, waiting for transfers between devices, swap_heads(): return lax.ppermute(array, 'head', [(i, i ^ by) for i in range(devices)])  10.3 us
    ppermute x6, starting transfers between devices, swap_chips(): lax.ppermute(array, 'seq', [(i, i ^ by * CORES) for i in range(devices)])  8.93 us
    ppermute x6, starting transfers between devices, swap_heads(): return lax.ppermute(array, 'head', [(i, i ^ by) for i in range(devices)])  8.9 us
    ppermute x4, starting transfers between devices, shift_chips(): lax.ppermute(array, 'seq', [(i, i + by) for i in range(devices) if 0 <= i...  8.83 us
    ppermute x2, waiting for transfers between devices, swap_cores(): return lax.ppermute(array, 'seq', [(i, i ^ 1) for i in range(devices)])  5.55 us
  transfers between devices with their start and end apart: 18, of which 10 were waited for; matrix products, arithmetic and copies ran while one was open for 0% of the time, Pallas kernels for 0%

profile of v7, /device:TPU:6, one launch (start us, length us, event | category | flops | bytes accessed | tf_op | source)
XLA Modules:
  0.0 108.0 jit_solution(9928628011545930196)
XLA Ops:
  0.6 1.9 %pack.1 = (bf16[40,512]{1,0:T(8,128)(2,1)}, bf16[40,512]{1,0:T(8,128)(2,1)}, bf16[40,512]{1,0:T(8,128)(2,1)}, bf16[40,512]{1,0:T(8,128)(2,1)}, bf16[256,512]{1,0:T(8,128)(2,1)}) custom-call(bf16[40,1024]{1,0:T(8,128)(2,1)} %pk_ref.1, bf16[40,1024]{1,0:T(8,128)(2,1)} %pv_ref.1, bf16[256,256]{1,0:T(8,128)(2,1)} %rk_ref.1, bf16[256,256]{1,0:T(8,128)(2,1)} %rv_ref.1), custom_call_target="tpu_custom_call" | custom-call | tf_op jit(solution)/shard_map/pack/pallas_call | solution.py:64
  2.5 1.4 %collective-permute-start.4 = (bf16[256,512]{1,0:T(8,128)(2,1)}, bf16[256,512]{1,0:T(8,128)(2,1)S(1)}, u32[]{:S(2)}, u32[]{:S(2)}) collective-permute-start(bf16[256,512]{1,0:T(8,128)(2,1)} %get-tuple-element.46.own_ref), channel_id=1, source_target_pairs={{0,16},{4,20},{8,24},{12,28},{1,17},{5,21},{9,25},{13,29},{2,18},{... | collective-permute-start | bytes 786440 | tf_op jit(solution)/shard_map/ppermute | solution.py:385
  3.9 1.3 %collective-permute-start.3 = (bf16[256,512]{1,0:T(8,128)(2,1)}, bf16[256,512]{1,0:T(8,128)(2,1)S(1)}, u32[]{:S(2)}, u32[]{:S(2)}) collective-permute-start(bf16[256,512]{1,0:T(8,128)(2,1)} %get-tuple-element.46.own_ref), channel_id=1, source_target_pairs={{0,8},{4,12},{8,16},{12,20},{16,24},{20,28},{1,9},{5,13},{9,17},{1... | collective-permute-start | bytes 786440 | tf_op jit(solution)/shard_map/ppermute | solution.py:385
  5.2 1.6 %collective-permute-start = (bf16[40,512]{1,0:T(8,128)(2,1)}, bf16[40,512]{1,0:T(8,128)(2,1)S(1)}, u32[]{:S(2)}, u32[]{:S(2)}) collective-permute-start(bf16[40,512]{1,0:T(8,128)(2,1)} %get-tuple-element.43), channel_id=1, source_target_pairs={{0,1},{1,0},{2,3},{3,2},{4,5},{5,4},{6,7},{7,6},{8,9},{9,8},{10,11... | collective-permute-start | bytes 122888 | tf_op jit(solution)/shard_map/ppermute | solution.py:369
  6.9 2.6 %collective-permute-start.1 = (bf16[40,512]{1,0:T(8,128)(2,1)}, bf16[40,512]{1,0:T(8,128)(2,1)S(1)}, u32[]{:S(2)}, u32[]{:S(2)}) collective-permute-start(bf16[40,512]{1,0:T(8,128)(2,1)} %get-tuple-element.44), channel_id=1, source_target_pairs={{0,2},{1,3},{2,0},{3,1},{4,6},{5,7},{6,4},{7,5},{8,10},{9,11},{10,... | collective-permute-start | bytes 122888 | tf_op jit(solution)/shard_map/ppermute | solution.py:369
  9.5 0.2 collective-permute-start.2
  9.7 3.1 %collective-permute-done.1 = bf16[40,512]{1,0:T(8,128)(2,1)S(1)} collective-permute-done((bf16[40,512]{1,0:T(8,128)(2,1)}, bf16[40,512]{1,0:T(8,128)(2,1)S(1)}, u32[]{:S(2)}, u32[]{:S(2)}) %collective-permute-start.1) | collective-permute-done | bytes 40992 | tf_op jit(solution)/shard_map/ppermute | solution.py:369
  12.8 2.7 %collective-permute-done.2 = bf16[40,512]{1,0:T(8,128)(2,1)S(1)} collective-permute-done((bf16[40,512]{1,0:T(8,128)(2,1)}, bf16[40,512]{1,0:T(8,128)(2,1)S(1)}, u32[]{:S(2)}, u32[]{:S(2)}) %collective-permute-start.2) | collective-permute-done | bytes 40992 | tf_op jit(solution)/shard_map/ppermute | solution.py:369
  15.5 0.8 constant_dynamic-update-slice_fusion.3
  16.3 3.5 %collective-permute-start.5 = (bf16[160,512]{1,0:T(8,128)(2,1)S(1)}, bf16[160,512]{1,0:T(8,128)(2,1)S(1)}, u32[]{:S(2)}, u32[]{:S(2)}) collective-permute-start(bf16[160,512]{1,0:T(8,128)(2,1)S(1)} %get-tuple-element.78), channel_id=1, source_target_pairs={{0,8},{4,12},{8,0},{12,4},{16,24},{20,28},{24,16},{28,20},{1,9},{5... | collective-permute-start | bytes 491528 | tf_op jit(solution)/shard_map/ppermute | solution.py:374
  19.9 1.9 %collective-permute-start.6 = (bf16[160,512]{1,0:T(8,128)(2,1)S(1)}, bf16[160,512]{1,0:T(8,128)(2,1)S(1)}, u32[]{:S(2)}, u32[]{:S(2)}) collective-permute-start(bf16[160,512]{1,0:T(8,128)(2,1)S(1)} %get-tuple-element.78), channel_id=1, source_target_pairs={{0,16},{4,20},{8,24},{12,28},{16,0},{20,4},{24,8},{28,12},{1,17},{... | collective-permute-start | bytes 491528 | tf_op jit(solution)/shard_map/ppermute | solution.py:374
  21.7 2.5 %collective-permute-done.5 = bf16[160,512]{1,0:T(8,128)(2,1)S(1)} collective-permute-done((bf16[160,512]{1,0:T(8,128)(2,1)S(1)}, bf16[160,512]{1,0:T(8,128)(2,1)S(1)}, u32[]{:S(2)}, u32[]{:S(2)}) %collective-permute-start.5) | collective-permute-done | bytes 163872 | tf_op jit(solution)/shard_map/ppermute | solution.py:374
  24.2 3.9 %collective-permute-done.6 = bf16[160,512]{1,0:T(8,128)(2,1)S(1)} collective-permute-done((bf16[160,512]{1,0:T(8,128)(2,1)S(1)}, bf16[160,512]{1,0:T(8,128)(2,1)S(1)}, u32[]{:S(2)}, u32[]{:S(2)}) %collective-permute-start.6) | collective-permute-done | bytes 163872 | tf_op jit(solution)/shard_map/ppermute | solution.py:374
  28.4 2.8 %collective-permute-done.8.got_ref = bf16[1152,512]{1,0:T(8,128)(2,1)S(1)} collective-permute-done((bf16[1152,512]{1,0:T(8,128)(2,1)S(1)}, bf16[1152,512]{1,0:T(8,128)(2,1)S(1)}, u32[]{:S(2)}, u32[]{:S(2)}) %collective-permute-start.8) | collective-permute-done | bytes 1179680 | tf_op jit(solution)/shard_map/ppermute | solution.py:379
  31.2 46.8 %attention.1 = (bf16[256,2048]{1,0:T(8,128)(2,1)}, bf16[256,2048]{1,0:T(8,128)(2,1)}, f32[1408,512]{1,0:T(8,128)S(1)}, bf16[1152,512]{1,0:T(8,128)(2,1)S(1)}) custom-call(s32[8]{0:T(128)S(1)} %copy-done.3, bf16[256,2048]{1,0:T(8,128)(2,1)S(1)} %copy-done.1, bf16[256,2048]{1,0:T(8,128)(2,1)S(1)} %copy-done.2, ...), custom_call_target="tpu_custom_call" | custom-call | flops 16106127360 | bytes 4194304 | tf_op jit(solution)/shard_map/attention/pallas_call | solution.py:330
  78.0 0.1 collective-permute-start.9
  78.2 2.7 %collective-permute-done.9.got_ref = bf16[1152,512]{1,0:T(8,128)(2,1)S(1)} collective-permute-done((bf16[1152,512]{1,0:T(8,128)(2,1)S(1)}, bf16[1152,512]{1,0:T(8,128)(2,1)S(1)}, u32[]{:S(2)}, u32[]{:S(2)}) %collective-permute-start.9) | collective-permute-done | bytes 1179680 | tf_op jit(solution)/shard_map/ppermute | solution.py:379
  80.9 0.3 merge.1
  81.1 0.4 collective-permute-start.10
  81.6 1.6 %collective-permute-start.11 = (bf16[160,512]{1,0:T(8,128)(2,1)S(1)}, bf16[160,512]{1,0:T(8,128)(2,1)S(1)}, u32[]{:S(2)}, u32[]{:S(2)}) collective-permute-start(bf16[160,512]{1,0:T(8,128)(2,1)S(1)} %get-tuple-element.60), channel_id=1, source_target_pairs={{0,16},{4,20},{8,24},{12,28},{16,0},{20,4},{24,8},{28,12},{1,17},{... | collective-permute-start | bytes 491528 | tf_op jit(solution)/shard_map/ppermute | solution.py:374
  83.2 1.5 %collective-permute-start.12 = (bf16[160,512]{1,0:T(8,128)(2,1)S(1)}, bf16[160,512]{1,0:T(8,128)(2,1)S(1)}, u32[]{:S(2)}, u32[]{:S(2)}) collective-permute-start(bf16[160,512]{1,0:T(8,128)(2,1)S(1)} %get-tuple-element.61), channel_id=1, source_target_pairs={{0,24},{4,28},{8,16},{12,20},{16,8},{20,12},{24,0},{28,4},{1,25},{... | collective-permute-start | bytes 491528 | tf_op jit(solution)/shard_map/ppermute | solution.py:374
  84.7 3.6 %collective-permute-done.10.refs_1_ = bf16[160,512]{1,0:T(8,128)(2,1)S(1)} collective-permute-done((bf16[160,512]{1,0:T(8,128)(2,1)S(1)}, bf16[160,512]{1,0:T(8,128)(2,1)S(1)}, u32[]{:S(2)}, u32[]{:S(2)}) %collective-permute-start.10) | collective-permute-done | bytes 163872 | tf_op jit(solution)/shard_map/ppermute | solution.py:374
  88.2 3.8 %collective-permute-done.12.refs_3_ = bf16[160,512]{1,0:T(8,128)(2,1)S(1)} collective-permute-done((bf16[160,512]{1,0:T(8,128)(2,1)S(1)}, bf16[160,512]{1,0:T(8,128)(2,1)S(1)}, u32[]{:S(2)}, u32[]{:S(2)}) %collective-permute-start.12) | collective-permute-done | bytes 163872 | tf_op jit(solution)/shard_map/ppermute | solution.py:374
  92.0 2.6 %collective-permute-start.13 = (bf16[256,512]{1,0:T(8,128)(2,1)S(1)}, bf16[256,512]{1,0:T(8,128)(2,1)S(1)}, u32[]{:S(2)}, u32[]{:S(2)}) collective-permute-start(bf16[256,512]{1,0:T(8,128)(2,1)S(1)} %get-tuple-element.64), channel_id=1, source_target_pairs={{8,0},{12,4},{16,8},{20,12},{24,16},{28,20},{9,1},{13,5},{17,9},{2... | collective-permute-start | bytes 786440 | tf_op jit(solution)/shard_map/ppermute | solution.py:385
  94.6 3.5 %collective-permute-start.14 = (bf16[256,512]{1,0:T(8,128)(2,1)S(1)}, bf16[256,512]{1,0:T(8,128)(2,1)S(1)}, u32[]{:S(2)}, u32[]{:S(2)}) collective-permute-start(bf16[256,512]{1,0:T(8,128)(2,1)S(1)} %get-tuple-element.65), channel_id=1, source_target_pairs={{16,0},{20,4},{24,8},{28,12},{17,1},{21,5},{25,9},{29,13},{18,2},{... | collective-permute-start | bytes 786440 | tf_op jit(solution)/shard_map/ppermute | solution.py:385
  98.2 0.1 sum_chips.1
  98.3 0.6 collective-permute-start.15
  98.8 2.6 %collective-permute-start.16 = (bf16[40,512]{1,0:T(8,128)(2,1)S(1)}, bf16[40,512]{1,0:T(8,128)(2,1)S(1)}, u32[]{:S(2)}, u32[]{:S(2)}) collective-permute-start(bf16[40,512]{1,0:T(8,128)(2,1)S(1)} %get-tuple-element.72), channel_id=1, source_target_pairs={{0,2},{1,3},{2,0},{3,1},{4,6},{5,7},{6,4},{7,5},{8,10},{9,11},{10,... | collective-permute-start | bytes 122888 | tf_op jit(solution)/shard_map/ppermute | solution.py:369
  101.4 1.3 %collective-permute-start.17 = (bf16[40,512]{1,0:T(8,128)(2,1)S(1)}, bf16[40,512]{1,0:T(8,128)(2,1)S(1)}, u32[]{:S(2)}, u32[]{:S(2)}) collective-permute-start(bf16[40,512]{1,0:T(8,128)(2,1)S(1)} %get-tuple-element.73), channel_id=1, source_target_pairs={{0,3},{1,2},{2,1},{3,0},{4,7},{5,6},{6,5},{7,4},{8,11},{9,10},{10,... | collective-permute-start | bytes 122888 | tf_op jit(solution)/shard_map/ppermute | solution.py:369
  102.7 1.4 %collective-permute-done.16.refs_2_ = bf16[40,512]{1,0:T(8,128)(2,1)S(1)} collective-permute-done((bf16[40,512]{1,0:T(8,128)(2,1)S(1)}, bf16[40,512]{1,0:T(8,128)(2,1)S(1)}, u32[]{:S(2)}, u32[]{:S(2)}) %collective-permute-start.16) | collective-permute-done | bytes 40992 | tf_op jit(solution)/shard_map/ppermute | solution.py:369
  104.2 3.0 %collective-permute-done.17.refs_3_ = bf16[40,512]{1,0:T(8,128)(2,1)S(1)} collective-permute-done((bf16[40,512]{1,0:T(8,128)(2,1)S(1)}, bf16[40,512]{1,0:T(8,128)(2,1)S(1)}, u32[]{:S(2)}, u32[]{:S(2)}) %collective-permute-start.17) | collective-permute-done | bytes 40992 | tf_op jit(solution)/shard_map/ppermute | solution.py:369
  107.2 0.8 finish.1
  (26 shorter events, 0.3 us)
Async XLA Ops:
  2.5 25.7 %copy-start = (bf16[256,512]{1,0:T(8,128)(2,1)S(1)}, bf16[256,512]{1,0:T(8,128)(2,1)}, u32[]{:S(2)}) copy-start(bf16[256,512]{1,0:T(8,128)(2,1)} %get-tuple-element.46.own_ref) | copy-start | bytes 786436
  2.5 13.0 %collective-permute-start.4 = (bf16[256,512]{1,0:T(8,128)(2,1)}, bf16[256,512]{1,0:T(8,128)(2,1)S(1)}, u32[]{:S(2)}, u32[]{:S(2)}) collective-permute-start(bf16[256,512]{1,0:T(8,128)(2,1)} %get-tuple-element.46.own_ref), channel_id=1, source_target_pairs={{0,16},{4,20},{8,24},{12,28},{1,17},{5,21},{9,25},{13,29},{2,18},{... | collective-permute-start | bytes 786440 | tf_op jit(solution)/shard_map/ppermute | solution.py:385
  3.9 11.5 %collective-permute-start.3 = (bf16[256,512]{1,0:T(8,128)(2,1)}, bf16[256,512]{1,0:T(8,128)(2,1)S(1)}, u32[]{:S(2)}, u32[]{:S(2)}) collective-permute-start(bf16[256,512]{1,0:T(8,128)(2,1)} %get-tuple-element.46.own_ref), channel_id=1, source_target_pairs={{0,8},{4,12},{8,16},{12,20},{16,24},{20,28},{1,9},{5,13},{9,17},{1... | collective-permute-start | bytes 786440 | tf_op jit(solution)/shard_map/ppermute | solution.py:385
  5.2 4.5 %collective-permute-start = (bf16[40,512]{1,0:T(8,128)(2,1)}, bf16[40,512]{1,0:T(8,128)(2,1)S(1)}, u32[]{:S(2)}, u32[]{:S(2)}) collective-permute-start(bf16[40,512]{1,0:T(8,128)(2,1)} %get-tuple-element.43), channel_id=1, source_target_pairs={{0,1},{1,0},{2,3},{3,2},{4,5},{5,4},{6,7},{7,6},{8,9},{9,8},{10,11... | collective-permute-start | bytes 122888 | tf_op jit(solution)/shard_map/ppermute | solution.py:369
  6.9 5.9 %collective-permute-start.1 = (bf16[40,512]{1,0:T(8,128)(2,1)}, bf16[40,512]{1,0:T(8,128)(2,1)S(1)}, u32[]{:S(2)}, u32[]{:S(2)}) collective-permute-start(bf16[40,512]{1,0:T(8,128)(2,1)} %get-tuple-element.44), channel_id=1, source_target_pairs={{0,2},{1,3},{2,0},{3,1},{4,6},{5,7},{6,4},{7,5},{8,10},{9,11},{10,... | collective-permute-start | bytes 122888 | tf_op jit(solution)/shard_map/ppermute | solution.py:369
  9.5 6.0 %collective-permute-start.2 = (bf16[40,512]{1,0:T(8,128)(2,1)}, bf16[40,512]{1,0:T(8,128)(2,1)S(1)}, u32[]{:S(2)}, u32[]{:S(2)}) collective-permute-start(bf16[40,512]{1,0:T(8,128)(2,1)} %get-tuple-element.45), channel_id=1, source_target_pairs={{0,3},{1,2},{2,1},{3,0},{4,7},{5,6},{6,5},{7,4},{8,11},{9,10},{10,... | collective-permute-start | bytes 122888 | tf_op jit(solution)/shard_map/ppermute | solution.py:369
  16.3 14.9 %copy-start.1 = (bf16[256,2048]{1,0:T(8,128)(2,1)S(1)}, bf16[256,2048]{1,0:T(8,128)(2,1)}, u32[]{:S(2)}) copy-start(bf16[256,2048]{1,0:T(8,128)(2,1)} %q_ref.1) | copy-start | bytes 3145732
  16.3 14.9 %copy-start.3 = (s32[8]{0:T(128)S(1)}, s32[8]{0:T(128)}, u32[]{:S(2)}) copy-start(s32[8]{0:T(128)} %lengths.1) | copy-start | bytes 100
  16.3 7.9 %collective-permute-start.5 = (bf16[160,512]{1,0:T(8,128)(2,1)S(1)}, bf16[160,512]{1,0:T(8,128)(2,1)S(1)}, u32[]{:S(2)}, u32[]{:S(2)}) collective-permute-start(bf16[160,512]{1,0:T(8,128)(2,1)S(1)} %get-tuple-element.78), channel_id=1, source_target_pairs={{0,8},{4,12},{8,0},{12,4},{16,24},{20,28},{24,16},{28,20},{1,9},{5... | collective-permute-start | bytes 491528 | tf_op jit(solution)/shard_map/ppermute | solution.py:374
  19.9 8.3 %collective-permute-start.6 = (bf16[160,512]{1,0:T(8,128)(2,1)S(1)}, bf16[160,512]{1,0:T(8,128)(2,1)S(1)}, u32[]{:S(2)}, u32[]{:S(2)}) collective-permute-start(bf16[160,512]{1,0:T(8,128)(2,1)S(1)} %get-tuple-element.78), channel_id=1, source_target_pairs={{0,16},{4,20},{8,24},{12,28},{16,0},{20,4},{24,8},{28,12},{1,17},{... | collective-permute-start | bytes 491528 | tf_op jit(solution)/shard_map/ppermute | solution.py:374
  21.7 9.5 %copy-start.2 = (bf16[256,2048]{1,0:T(8,128)(2,1)S(1)}, bf16[256,2048]{1,0:T(8,128)(2,1)}, u32[]{:S(2)}) copy-start(bf16[256,2048]{1,0:T(8,128)(2,1)} %do_ref.1) | copy-start | bytes 3145732
  21.7 6.5 %collective-permute-start.7 = (bf16[160,512]{1,0:T(8,128)(2,1)S(1)}, bf16[160,512]{1,0:T(8,128)(2,1)S(1)}, u32[]{:S(2)}, u32[]{:S(2)}) collective-permute-start(bf16[160,512]{1,0:T(8,128)(2,1)S(1)} %get-tuple-element.78), channel_id=1, source_target_pairs={{0,24},{4,28},{8,16},{12,20},{16,8},{20,12},{24,0},{28,4},{1,25},{... | collective-permute-start | bytes 491528 | tf_op jit(solution)/shard_map/ppermute | solution.py:374
  28.3 2.9 %collective-permute-start.8 = (bf16[1152,512]{1,0:T(8,128)(2,1)S(1)}, bf16[1152,512]{1,0:T(8,128)(2,1)S(1)}, u32[]{:S(2)}, u32[]{:S(2)}) collective-permute-start(bf16[1152,512]{1,0:T(8,128)(2,1)S(1)} %select_dynamic-update-slice_fusion.sent_ref), channel_id=1, source_target_pairs={{0,4},{4,0},{8,12},{12,8},{16,20},{20,16},{24,28},{28,24},{1,5},{5... | collective-permute-start | bytes 3538952 | tf_op jit(solution)/shard_map/ppermute | solution.py:379
  78.0 2.8 %collective-permute-start.9 = (bf16[1152,512]{1,0:T(8,128)(2,1)S(1)}, bf16[1152,512]{1,0:T(8,128)(2,1)S(1)}, u32[]{:S(2)}, u32[]{:S(2)}) collective-permute-start(bf16[1152,512]{1,0:T(8,128)(2,1)S(1)} %get-tuple-element.56), channel_id=1, source_target_pairs={{0,4},{4,0},{8,12},{12,8},{16,20},{20,16},{24,28},{28,24},{1,5},{5... | collective-permute-start | bytes 3538952 | tf_op jit(solution)/shard_map/ppermute | solution.py:379
  81.1 7.1 %collective-permute-start.10 = (bf16[160,512]{1,0:T(8,128)(2,1)S(1)}, bf16[160,512]{1,0:T(8,128)(2,1)S(1)}, u32[]{:S(2)}, u32[]{:S(2)}) collective-permute-start(bf16[160,512]{1,0:T(8,128)(2,1)S(1)} %get-tuple-element.59), channel_id=1, source_target_pairs={{0,8},{4,12},{8,0},{12,4},{16,24},{20,28},{24,16},{28,20},{1,9},{5... | collective-permute-start | bytes 491528 | tf_op jit(solution)/shard_map/ppermute | solution.py:374
  81.6 6.7 %collective-permute-start.11 = (bf16[160,512]{1,0:T(8,128)(2,1)S(1)}, bf16[160,512]{1,0:T(8,128)(2,1)S(1)}, u32[]{:S(2)}, u32[]{:S(2)}) collective-permute-start(bf16[160,512]{1,0:T(8,128)(2,1)S(1)} %get-tuple-element.60), channel_id=1, source_target_pairs={{0,16},{4,20},{8,24},{12,28},{16,0},{20,4},{24,8},{28,12},{1,17},{... | collective-permute-start | bytes 491528 | tf_op jit(solution)/shard_map/ppermute | solution.py:374
  83.2 8.9 %collective-permute-start.12 = (bf16[160,512]{1,0:T(8,128)(2,1)S(1)}, bf16[160,512]{1,0:T(8,128)(2,1)S(1)}, u32[]{:S(2)}, u32[]{:S(2)}) collective-permute-start(bf16[160,512]{1,0:T(8,128)(2,1)S(1)} %get-tuple-element.61), channel_id=1, source_target_pairs={{0,24},{4,28},{8,16},{12,20},{16,8},{20,12},{24,0},{28,4},{1,25},{... | collective-permute-start | bytes 491528 | tf_op jit(solution)/shard_map/ppermute | solution.py:374
  92.0 15.2 %collective-permute-start.13 = (bf16[256,512]{1,0:T(8,128)(2,1)S(1)}, bf16[256,512]{1,0:T(8,128)(2,1)S(1)}, u32[]{:S(2)}, u32[]{:S(2)}) collective-permute-start(bf16[256,512]{1,0:T(8,128)(2,1)S(1)} %get-tuple-element.64), channel_id=1, source_target_pairs={{8,0},{12,4},{16,8},{20,12},{24,16},{28,20},{9,1},{13,5},{17,9},{2... | collective-permute-start | bytes 786440 | tf_op jit(solution)/shard_map/ppermute | solution.py:385
  94.6 12.6 %collective-permute-start.14 = (bf16[256,512]{1,0:T(8,128)(2,1)S(1)}, bf16[256,512]{1,0:T(8,128)(2,1)S(1)}, u32[]{:S(2)}, u32[]{:S(2)}) collective-permute-start(bf16[256,512]{1,0:T(8,128)(2,1)S(1)} %get-tuple-element.65), channel_id=1, source_target_pairs={{16,0},{20,4},{24,8},{28,12},{17,1},{21,5},{25,9},{29,13},{18,2},{... | collective-permute-start | bytes 786440 | tf_op jit(solution)/shard_map/ppermute | solution.py:385
  98.3 4.5 %collective-permute-start.15 = (bf16[40,512]{1,0:T(8,128)(2,1)S(1)}, bf16[40,512]{1,0:T(8,128)(2,1)S(1)}, u32[]{:S(2)}, u32[]{:S(2)}) collective-permute-start(bf16[40,512]{1,0:T(8,128)(2,1)S(1)} %get-tuple-element.71), channel_id=1, source_target_pairs={{0,1},{1,0},{2,3},{3,2},{4,5},{5,4},{6,7},{7,6},{8,9},{9,8},{10,11... | collective-permute-start | bytes 122888 | tf_op jit(solution)/shard_map/ppermute | solution.py:369
  98.8 5.3 %collective-permute-start.16 = (bf16[40,512]{1,0:T(8,128)(2,1)S(1)}, bf16[40,512]{1,0:T(8,128)(2,1)S(1)}, u32[]{:S(2)}, u32[]{:S(2)}) collective-permute-start(bf16[40,512]{1,0:T(8,128)(2,1)S(1)} %get-tuple-element.72), channel_id=1, source_target_pairs={{0,2},{1,3},{2,0},{3,1},{4,6},{5,7},{6,4},{7,5},{8,10},{9,11},{10,... | collective-permute-start | bytes 122888 | tf_op jit(solution)/shard_map/ppermute | solution.py:369
  101.4 5.8 %collective-permute-start.17 = (bf16[40,512]{1,0:T(8,128)(2,1)S(1)}, bf16[40,512]{1,0:T(8,128)(2,1)S(1)}, u32[]{:S(2)}, u32[]{:S(2)}) collective-permute-start(bf16[40,512]{1,0:T(8,128)(2,1)S(1)} %get-tuple-element.73), channel_id=1, source_target_pairs={{0,3},{1,2},{2,1},{3,0},{4,7},{5,6},{6,5},{7,4},{8,11},{9,10},{10,... | collective-permute-start | bytes 122888 | tf_op jit(solution)/shard_map/ppermute | solution.py:369

commit v8 on v7

--- a/solution.py
+++ b/solution.py
@@ -73,7 +73,7 @@
 
 
 def merge_kernel(parts, rows, kept_ref, got_ref, *outs):
-    pieces, back1, back2, own = outs[:parts], outs[parts], outs[parts + 1], outs[parts + 2]
+    pieces, back1, back2, own = outs[:parts], outs[parts:-3], outs[-3:-1], outs[-1]
     core = lax.rem(lax.axis_index("seq"), CORES)
     to_own = jnp.where(core == 0, 1.0, 0.0)
     half = kept_ref.shape[0] - 3 * rows
@@ -82,9 +82,12 @@
         at = slice(k * share, (k + 1) * share)
         piece[...] = (kept_ref[at] + got_ref[at].astype(F32)).astype(BF16)
     one, two, three = half + rows, half + 2 * rows, half + 3 * rows
-    back1[...] = (kept_ref[half:one] + got_ref[half:one].astype(F32)).astype(BF16)
+    near = (kept_ref[half:one] + got_ref[half:one].astype(F32)).astype(BF16)
     chosen = got_ref[one:two].astype(F32)
-    back2[...] = (kept_ref[one:two] + chosen * (1.0 - to_own)).astype(BF16)
+    far = (kept_ref[one:two] + chosen * (1.0 - to_own)).astype(BF16)
+    for i in range(2):
+        back1[i][...] = near[i * rows // 2 : (i + 1) * rows // 2]
+        back2[i][...] = far[i * rows // 2 : (i + 1) * rows // 2]
     own[...] = kept_ref[two:three] + chosen * to_own
 
 
@@ -99,8 +102,8 @@
         out[...] = total[k * share : (k + 1) * share].astype(BF16)
 
 
-def finish_kernel(own_ref, one_ref, two_ref, *refs):
-    pieces, (gk_ref, gv_ref, rk_ref, rv_ref) = refs[:-4], refs[-4:]
+def finish_kernel(own_ref, *refs):
+    near, far, pieces, (gk_ref, gv_ref, rk_ref, rv_ref) = refs[:2], refs[2:4], refs[4:-4], refs[-4:]
     head = lax.axis_index("head")
     width = pieces[0].shape[1]
     for k, piece in enumerate(pieces):
@@ -109,10 +112,14 @@
             at = pl.multiple_of(start + n * HD, HD)
             gk_ref[:, pl.ds(at, HD)] = piece[:, 2 * n * HD : (2 * n + 1) * HD]
             gv_ref[:, pl.ds(at, HD)] = piece[:, (2 * n + 1) * HD : (2 * n + 2) * HD]
-    total = (own_ref[...] + one_ref[...].astype(F32) + two_ref[...].astype(F32)).astype(BF16)
-    for n in range(width // (2 * HD)):
-        rk_ref[:, n * HD : (n + 1) * HD] = total[:, 2 * n * HD : (2 * n + 1) * HD]
-        rv_ref[:, n * HD : (n + 1) * HD] = total[:, (2 * n + 1) * HD : (2 * n + 2) * HD]
+    rows = near[0].shape[0]
+    for i in range(2):
+        at = slice(i * rows, (i + 1) * rows)
+        total = own_ref[at] + near[i][...].astype(F32) + far[i][...].astype(F32)
+        total = total.astype(BF16)
+        for n in range(width // (2 * HD)):
+            rk_ref[at, n * HD : (n + 1) * HD] = total[:, 2 * n * HD : (2 * n + 1) * HD]
+            rv_ref[at, n * HD : (n + 1) * HD] = total[:, (2 * n + 1) * HD : (2 * n + 2) * HD]
 
 
 def attention_kernel(
@@ -231,8 +238,8 @@
             cot_ns[which] = (cot_ts[which].astype(F32) * inverse).astype(BF16).T
 
         def slopes(at):
-            p = p_bufs[which, at].astype(F32)
-            d_bufs[which, at] = (p * (g_bufs[which, at] - state["delta"])).astype(BF16)
+            slope = (g_bufs[which, at] - state["delta"]).astype(BF16)
+            d_bufs[which, at] = p_bufs[which, at] * slope
 
         work = [settle] + [functools.partial(weights, at) for at in tiles] + [finish]
         return work + [functools.partial(slopes, at) for at in tiles]
@@ -397,7 +404,7 @@
     pieces = [pieces[0]] + [swap_heads(pieces[k], k) for k in range(1, groups)]
     near = shift_chips(own, 1)
     far = shift_chips(own, 2)
-    pieces, near, far = lax.optimization_barrier((pieces, near, far))
+    pieces[1:], near, far = lax.optimization_barrier((pieces[1:], near, far))
     mine = jnp.concatenate(pieces, axis=0)
     parts = [mine] + [swap_chips(mine, k) for k in range(1, chips)]
     chosen = jnp.where(core == 1, far, own)
@@ -410,18 +417,18 @@
 
     back = swap_cores(back)
     share = groups * block
-    *parts, near, far, own = local_call(
+    *parts, own = local_call(
         functools.partial(merge_kernel, chips, tokens),
         "merge",
         [kept, back],
         [((share, wide), BF16)] * chips
-        + [((tokens, wide), BF16)] * 2
+        + [((tokens // 2, wide), BF16)] * 4
         + [((tokens, wide), F32)],
     )
+    near, far, parts = parts[chips : chips + 2], parts[chips + 2 :], parts[:chips]
     parts = [parts[0]] + [swap_chips(parts[k], k) for k in range(1, chips)]
-    parts, near, far = lax.optimization_barrier((parts, near, far))
-    near = shift_chips(near, -1)
-    far = shift_chips(far, -2)
+    near = [shift_chips(part, -1) for part in near]
+    far = [shift_chips(part, -2) for part in far]
     pieces = local_call(
         functools.partial(sum_kernel, chips),
         "sum_chips",
@@ -433,7 +440,7 @@
     grad_k_prompt, grad_v_prompt, grad_k_resp, grad_v_resp = local_call(
         finish_kernel,
         "finish",
-        [own, near, far] + pieces,
+        [own] + near + far + pieces,
         [(prompt_k.shape, BF16)] * 2 + [((tokens, kv_cols), BF16)] * 2,
     )
     return (resp_out, grad_q, grad_k_resp, grad_v_resp, grad_k_prompt, grad_v_prompt)

time: 109 us -> 107 us (0.982)
  waiting for transfers between devices: 29.6 us -> 19.4 us
  starting transfers between devices: 26.9 us -> 36.2 us
    ppermute x4 -> x6, starting transfers between devices: 8.83 us -> 18.2 us  [shift_chips(): lax.ppermute(array, 'seq', [(i, i + by) for i in range(devices) if 0 <= i...]
    ppermute x6, waiting for transfers between devices: 13.8 us -> 6.44 us  [swap_chips(): lax.ppermute(array, 'seq', [(i, i ^ by * CORES) for i in range(devices)])]
    ppermute x6, waiting for transfers between devices: 10.3 us -> 7.4 us  [swap_heads(): return lax.ppermute(array, 'head', [(i, i ^ by) for i in range(devices)])]
  transfers between devices with their start and end apart: 18 -> 20, of which waited for: 10 -> 8; matrix products, arithmetic and copies ran while one was open for 0% -> 1% of each run, Pallas kernels for 0% -> 0%
where the time goes in v8:
time: 107 us; the launch traced here: 106 us
  Pallas kernels  48.9 us (46%)
  starting transfers between devices  36.2 us (34%)
  waiting for transfers between devices  19.4 us (18%)
    pallas_call x1, Pallas kernels, attention(): pl.pallas_call(functools.partial(attention_kernel, halves), in_specs=[pl....  45.9 us
    ppermute x6, starting transfers between devices, shift_chips(): lax.ppermute(array, 'seq', [(i, i + by) for i in range(devices) if 0 <= i...  18.2 us
    ppermute x6, starting transfers between devices, swap_chips(): lax.ppermute(array, 'seq', [(i, i ^ by * CORES) for i in range(devices)])  8.93 us
    ppermute x6, starting transfers between devices, swap_heads(): return lax.ppermute(array, 'head', [(i, i ^ by) for i in range(devices)])  8.88 us
    ppermute x6, waiting for transfers between devices, swap_heads(): return lax.ppermute(array, 'head', [(i, i ^ by) for i in range(devices)])  7.4 us
    ppermute x6, waiting for transfers between devices, swap_chips(): lax.ppermute(array, 'seq', [(i, i ^ by * CORES) for i in range(devices)])  6.44 us
    ppermute x2, waiting for transfers between devices, swap_cores(): return lax.ppermute(array, 'seq', [(i, i ^ 1) for i in range(devices)])  5.55 us
  transfers between devices with their start and end apart: 20, of which 8 were waited for; matrix products, arithmetic and copies ran while one was open for 1% of the time, Pallas kernels for 0%

profile of v8, /device:TPU:6, one launch (start us, length us, event | category | flops | bytes accessed | tf_op | source)
XLA Modules:
  0.0 106.4 jit_solution(14748925699575344412)
XLA Ops:
  0.6 1.9 %pack.1 = (bf16[40,512]{1,0:T(8,128)(2,1)}, bf16[40,512]{1,0:T(8,128)(2,1)}, bf16[40,512]{1,0:T(8,128)(2,1)}, bf16[40,512]{1,0:T(8,128)(2,1)}, bf16[256,512]{1,0:T(8,128)(2,1)}) custom-call(bf16[40,1024]{1,0:T(8,128)(2,1)} %pk_ref.1, bf16[40,1024]{1,0:T(8,128)(2,1)} %pv_ref.1, bf16[256,256]{1,0:T(8,128)(2,1)} %rk_ref.1, bf16[256,256]{1,0:T(8,128)(2,1)} %rv_ref.1), custom_call_target="tpu_custom_call" | custom-call | tf_op jit(solution)/shard_map/pack/pallas_call | solution.py:64
  2.5 1.4 %collective-permute-start.4 = (bf16[256,512]{1,0:T(8,128)(2,1)}, bf16[256,512]{1,0:T(8,128)(2,1)S(1)}, u32[]{:S(2)}, u32[]{:S(2)}) collective-permute-start(bf16[256,512]{1,0:T(8,128)(2,1)} %get-tuple-element.41.own_ref), channel_id=1, source_target_pairs={{0,16},{4,20},{8,24},{12,28},{1,17},{5,21},{9,25},{13,29},{2,18},{... | collective-permute-start | bytes 786440 | tf_op jit(solution)/shard_map/ppermute | solution.py:392
  3.9 1.3 %collective-permute-start.3 = (bf16[256,512]{1,0:T(8,128)(2,1)}, bf16[256,512]{1,0:T(8,128)(2,1)S(1)}, u32[]{:S(2)}, u32[]{:S(2)}) collective-permute-start(bf16[256,512]{1,0:T(8,128)(2,1)} %get-tuple-element.41.own_ref), channel_id=1, source_target_pairs={{0,8},{4,12},{8,16},{12,20},{16,24},{20,28},{1,9},{5,13},{9,17},{1... | collective-permute-start | bytes 786440 | tf_op jit(solution)/shard_map/ppermute | solution.py:392
  5.2 1.6 %collective-permute-start = (bf16[40,512]{1,0:T(8,128)(2,1)}, bf16[40,512]{1,0:T(8,128)(2,1)S(1)}, u32[]{:S(2)}, u32[]{:S(2)}) collective-permute-start(bf16[40,512]{1,0:T(8,128)(2,1)} %get-tuple-element.38), channel_id=1, source_target_pairs={{0,1},{1,0},{2,3},{3,2},{4,5},{5,4},{6,7},{7,6},{8,9},{9,8},{10,11... | collective-permute-start | bytes 122888 | tf_op jit(solution)/shard_map/ppermute | solution.py:376
  6.9 2.6 %collective-permute-start.1 = (bf16[40,512]{1,0:T(8,128)(2,1)}, bf16[40,512]{1,0:T(8,128)(2,1)S(1)}, u32[]{:S(2)}, u32[]{:S(2)}) collective-permute-start(bf16[40,512]{1,0:T(8,128)(2,1)} %get-tuple-element.39), channel_id=1, source_target_pairs={{0,2},{1,3},{2,0},{3,1},{4,6},{5,7},{6,4},{7,5},{8,10},{9,11},{10,... | collective-permute-start | bytes 122888 | tf_op jit(solution)/shard_map/ppermute | solution.py:376
  9.5 0.2 collective-permute-start.2
  9.7 0.8 constant_dynamic-update-slice_fusion.3
  10.5 2.3 %collective-permute-done.1 = bf16[40,512]{1,0:T(8,128)(2,1)S(1)} collective-permute-done((bf16[40,512]{1,0:T(8,128)(2,1)}, bf16[40,512]{1,0:T(8,128)(2,1)S(1)}, u32[]{:S(2)}, u32[]{:S(2)}) %collective-permute-start.1) | collective-permute-done | bytes 40992 | tf_op jit(solution)/shard_map/ppermute | solution.py:376
  12.8 2.7 %collective-permute-done.2 = bf16[40,512]{1,0:T(8,128)(2,1)S(1)} collective-permute-done((bf16[40,512]{1,0:T(8,128)(2,1)}, bf16[40,512]{1,0:T(8,128)(2,1)S(1)}, u32[]{:S(2)}, u32[]{:S(2)}) %collective-permute-start.2) | collective-permute-done | bytes 40992 | tf_op jit(solution)/shard_map/ppermute | solution.py:376
  15.6 3.5 %collective-permute-start.5 = (bf16[160,512]{1,0:T(8,128)(2,1)S(1)}, bf16[160,512]{1,0:T(8,128)(2,1)S(1)}, u32[]{:S(2)}, u32[]{:S(2)}) collective-permute-start(bf16[160,512]{1,0:T(8,128)(2,1)S(1)} %get-tuple-element.68), channel_id=1, source_target_pairs={{0,8},{4,12},{8,0},{12,4},{16,24},{20,28},{24,16},{28,20},{1,9},{5... | collective-permute-start | bytes 491528 | tf_op jit(solution)/shard_map/ppermute | solution.py:381
  19.1 1.9 %collective-permute-start.6 = (bf16[160,512]{1,0:T(8,128)(2,1)S(1)}, bf16[160,512]{1,0:T(8,128)(2,1)S(1)}, u32[]{:S(2)}, u32[]{:S(2)}) collective-permute-start(bf16[160,512]{1,0:T(8,128)(2,1)S(1)} %get-tuple-element.68), channel_id=1, source_target_pairs={{0,16},{4,20},{8,24},{12,28},{16,0},{20,4},{24,8},{28,12},{1,17},{... | collective-permute-start | bytes 491528 | tf_op jit(solution)/shard_map/ppermute | solution.py:381
  20.9 2.5 %collective-permute-done.5 = bf16[160,512]{1,0:T(8,128)(2,1)S(1)} collective-permute-done((bf16[160,512]{1,0:T(8,128)(2,1)S(1)}, bf16[160,512]{1,0:T(8,128)(2,1)S(1)}, u32[]{:S(2)}, u32[]{:S(2)}) %collective-permute-start.5) | collective-permute-done | bytes 163872 | tf_op jit(solution)/shard_map/ppermute | solution.py:381
  23.4 3.9 %collective-permute-done.6 = bf16[160,512]{1,0:T(8,128)(2,1)S(1)} collective-permute-done((bf16[160,512]{1,0:T(8,128)(2,1)S(1)}, bf16[160,512]{1,0:T(8,128)(2,1)S(1)}, u32[]{:S(2)}, u32[]{:S(2)}) %collective-permute-start.6) | collective-permute-done | bytes 163872 | tf_op jit(solution)/shard_map/ppermute | solution.py:381
  27.5 0.1 collective-permute-start.8
  27.6 2.8 %collective-permute-done.8.got_ref = bf16[1152,512]{1,0:T(8,128)(2,1)S(1)} collective-permute-done((bf16[1152,512]{1,0:T(8,128)(2,1)S(1)}, bf16[1152,512]{1,0:T(8,128)(2,1)S(1)}, u32[]{:S(2)}, u32[]{:S(2)}) %collective-permute-start.8) | collective-permute-done | bytes 1179680 | tf_op jit(solution)/shard_map/ppermute | solution.py:386
  30.5 45.9 %attention.1 = (bf16[256,2048]{1,0:T(8,128)(2,1)}, bf16[256,2048]{1,0:T(8,128)(2,1)}, f32[1408,512]{1,0:T(8,128)S(1)}, bf16[1152,512]{1,0:T(8,128)(2,1)S(1)}) custom-call(s32[8]{0:T(128)S(1)} %copy-done.3, bf16[256,2048]{1,0:T(8,128)(2,1)S(1)} %copy-done.1, bf16[256,2048]{1,0:T(8,128)(2,1)S(1)} %copy-done.2, ...), custom_call_target="tpu_custom_call" | custom-call | flops 16106127360 | bytes 4194304 | tf_op jit(solution)/shard_map/attention/pallas_call | solution.py:337
  76.3 0.1 collective-permute-start.9
  76.5 2.7 %collective-permute-done.9.got_ref = bf16[1152,512]{1,0:T(8,128)(2,1)S(1)} collective-permute-done((bf16[1152,512]{1,0:T(8,128)(2,1)S(1)}, bf16[1152,512]{1,0:T(8,128)(2,1)S(1)}, u32[]{:S(2)}, u32[]{:S(2)}) %collective-permute-start.9) | collective-permute-done | bytes 1179680 | tf_op jit(solution)/shard_map/ppermute | solution.py:386
  79.2 0.3 merge.1
  79.4 0.4 collective-permute-start.14
  79.9 1.6 %collective-permute-start.15 = (bf16[160,512]{1,0:T(8,128)(2,1)S(1)}, bf16[160,512]{1,0:T(8,128)(2,1)S(1)}, u32[]{:S(2)}, u32[]{:S(2)}) collective-permute-start(bf16[160,512]{1,0:T(8,128)(2,1)S(1)} %get-tuple-element.58), channel_id=1, source_target_pairs={{0,16},{4,20},{8,24},{12,28},{16,0},{20,4},{24,8},{28,12},{1,17},{... | collective-permute-start | bytes 491528 | tf_op jit(solution)/shard_map/ppermute | solution.py:381
  81.4 1.5 %collective-permute-start.16 = (bf16[160,512]{1,0:T(8,128)(2,1)S(1)}, bf16[160,512]{1,0:T(8,128)(2,1)S(1)}, u32[]{:S(2)}, u32[]{:S(2)}) collective-permute-start(bf16[160,512]{1,0:T(8,128)(2,1)S(1)} %get-tuple-element.59), channel_id=1, source_target_pairs={{0,24},{4,28},{8,16},{12,20},{16,8},{20,12},{24,0},{28,4},{1,25},{... | collective-permute-start | bytes 491528 | tf_op jit(solution)/shard_map/ppermute | solution.py:381
  83.0 2.3 %collective-permute-start.10 = (bf16[128,512]{1,0:T(8,128)(2,1)S(1)}, bf16[128,512]{1,0:T(8,128)(2,1)S(1)}, u32[]{:S(2)}, u32[]{:S(2)}) collective-permute-start(bf16[128,512]{1,0:T(8,128)(2,1)S(1)} %get-tuple-element.52), channel_id=1, source_target_pairs={{8,0},{12,4},{16,8},{20,12},{24,16},{28,20},{9,1},{13,5},{17,9},{2... | collective-permute-start | bytes 393224 | tf_op jit(solution)/shard_map/ppermute | solution.py:392
  85.3 4.6 %collective-permute-start.11 = (bf16[128,512]{1,0:T(8,128)(2,1)S(1)}, bf16[128,512]{1,0:T(8,128)(2,1)S(1)}, u32[]{:S(2)}, u32[]{:S(2)}) collective-permute-start(bf16[128,512]{1,0:T(8,128)(2,1)S(1)} %get-tuple-element.53), channel_id=1, source_target_pairs={{8,0},{12,4},{16,8},{20,12},{24,16},{28,20},{9,1},{13,5},{17,9},{2... | collective-permute-start | bytes 393224 | tf_op jit(solution)/shard_map/ppermute | solution.py:392
  89.9 1.3 %collective-permute-start.12 = (bf16[128,512]{1,0:T(8,128)(2,1)S(1)}, bf16[128,512]{1,0:T(8,128)(2,1)S(1)}, u32[]{:S(2)}, u32[]{:S(2)}) collective-permute-start(bf16[128,512]{1,0:T(8,128)(2,1)S(1)} %get-tuple-element.54), channel_id=1, source_target_pairs={{16,0},{20,4},{24,8},{28,12},{17,1},{21,5},{25,9},{29,13},{18,2},{... | collective-permute-start | bytes 393224 | tf_op jit(solution)/shard_map/ppermute | solution.py:392
  91.2 7.3 %collective-permute-start.13 = (bf16[128,512]{1,0:T(8,128)(2,1)S(1)}, bf16[128,512]{1,0:T(8,128)(2,1)S(1)}, u32[]{:S(2)}, u32[]{:S(2)}) collective-permute-start(bf16[128,512]{1,0:T(8,128)(2,1)S(1)} %get-tuple-element.55), channel_id=1, source_target_pairs={{16,0},{20,4},{24,8},{28,12},{17,1},{21,5},{25,9},{29,13},{18,2},{... | collective-permute-start | bytes 393224 | tf_op jit(solution)/shard_map/ppermute | solution.py:392
  98.6 0.1 sum_chips.1
  98.7 0.1 collective-permute-start.17
  98.9 4.3 %collective-permute-start.19 = (bf16[40,512]{1,0:T(8,128)(2,1)S(1)}, bf16[40,512]{1,0:T(8,128)(2,1)S(1)}, u32[]{:S(2)}, u32[]{:S(2)}) collective-permute-start(bf16[40,512]{1,0:T(8,128)(2,1)S(1)} %get-tuple-element.63), channel_id=1, source_target_pairs={{0,3},{1,2},{2,1},{3,0},{4,7},{5,6},{6,5},{7,4},{8,11},{9,10},{10,... | collective-permute-start | bytes 122888 | tf_op jit(solution)/shard_map/ppermute | solution.py:376
  103.2 0.6 collective-permute-done.18.refs_6_
  103.7 1.8 %collective-permute-done.19.refs_7_ = bf16[40,512]{1,0:T(8,128)(2,1)S(1)} collective-permute-done((bf16[40,512]{1,0:T(8,128)(2,1)S(1)}, bf16[40,512]{1,0:T(8,128)(2,1)S(1)}, u32[]{:S(2)}, u32[]{:S(2)}) %collective-permute-start.19) | collective-permute-done | bytes 40992 | tf_op jit(solution)/shard_map/ppermute | solution.py:376
  105.6 0.8 finish.1
  (30 shorter events, 0.3 us)
Async XLA Ops:
  2.5 24.9 %copy-start = (bf16[256,512]{1,0:T(8,128)(2,1)S(1)}, bf16[256,512]{1,0:T(8,128)(2,1)}, u32[]{:S(2)}) copy-start(bf16[256,512]{1,0:T(8,128)(2,1)} %get-tuple-element.41.own_ref) | copy-start | bytes 786436
  2.5 13.0 %collective-permute-start.4 = (bf16[256,512]{1,0:T(8,128)(2,1)}, bf16[256,512]{1,0:T(8,128)(2,1)S(1)}, u32[]{:S(2)}, u32[]{:S(2)}) collective-permute-start(bf16[256,512]{1,0:T(8,128)(2,1)} %get-tuple-element.41.own_ref), channel_id=1, source_target_pairs={{0,16},{4,20},{8,24},{12,28},{1,17},{5,21},{9,25},{13,29},{2,18},{... | collective-permute-start | bytes 786440 | tf_op jit(solution)/shard_map/ppermute | solution.py:392
  3.9 11.5 %collective-permute-start.3 = (bf16[256,512]{1,0:T(8,128)(2,1)}, bf16[256,512]{1,0:T(8,128)(2,1)S(1)}, u32[]{:S(2)}, u32[]{:S(2)}) collective-permute-start(bf16[256,512]{1,0:T(8,128)(2,1)} %get-tuple-element.41.own_ref), channel_id=1, source_target_pairs={{0,8},{4,12},{8,16},{12,20},{16,24},{20,28},{1,9},{5,13},{9,17},{1... | collective-permute-start | bytes 786440 | tf_op jit(solution)/shard_map/ppermute | solution.py:392
  5.2 5.2 %collective-permute-start = (bf16[40,512]{1,0:T(8,128)(2,1)}, bf16[40,512]{1,0:T(8,128)(2,1)S(1)}, u32[]{:S(2)}, u32[]{:S(2)}) collective-permute-start(bf16[40,512]{1,0:T(8,128)(2,1)} %get-tuple-element.38), channel_id=1, source_target_pairs={{0,1},{1,0},{2,3},{3,2},{4,5},{5,4},{6,7},{7,6},{8,9},{9,8},{10,11... | collective-permute-start | bytes 122888 | tf_op jit(solution)/shard_map/ppermute | solution.py:376
  6.9 5.9 %collective-permute-start.1 = (bf16[40,512]{1,0:T(8,128)(2,1)}, bf16[40,512]{1,0:T(8,128)(2,1)S(1)}, u32[]{:S(2)}, u32[]{:S(2)}) collective-permute-start(bf16[40,512]{1,0:T(8,128)(2,1)} %get-tuple-element.39), channel_id=1, source_target_pairs={{0,2},{1,3},{2,0},{3,1},{4,6},{5,7},{6,4},{7,5},{8,10},{9,11},{10,... | collective-permute-start | bytes 122888 | tf_op jit(solution)/shard_map/ppermute | solution.py:376
  9.5 6.0 %collective-permute-start.2 = (bf16[40,512]{1,0:T(8,128)(2,1)}, bf16[40,512]{1,0:T(8,128)(2,1)S(1)}, u32[]{:S(2)}, u32[]{:S(2)}) collective-permute-start(bf16[40,512]{1,0:T(8,128)(2,1)} %get-tuple-element.40), channel_id=1, source_target_pairs={{0,3},{1,2},{2,1},{3,0},{4,7},{5,6},{6,5},{7,4},{8,11},{9,10},{10,... | collective-permute-start | bytes 122888 | tf_op jit(solution)/shard_map/ppermute | solution.py:376
  15.5 14.9 %copy-start.1 = (bf16[256,2048]{1,0:T(8,128)(2,1)S(1)}, bf16[256,2048]{1,0:T(8,128)(2,1)}, u32[]{:S(2)}) copy-start(bf16[256,2048]{1,0:T(8,128)(2,1)} %q_ref.1) | copy-start | bytes 3145732
  15.5 14.9 %copy-start.3 = (s32[8]{0:T(128)S(1)}, s32[8]{0:T(128)}, u32[]{:S(2)}) copy-start(s32[8]{0:T(128)} %lengths.1) | copy-start | bytes 100
  15.6 7.9 %collective-permute-start.5 = (bf16[160,512]{1,0:T(8,128)(2,1)S(1)}, bf16[160,512]{1,0:T(8,128)(2,1)S(1)}, u32[]{:S(2)}, u32[]{:S(2)}) collective-permute-start(bf16[160,512]{1,0:T(8,128)(2,1)S(1)} %get-tuple-element.68), channel_id=1, source_target_pairs={{0,8},{4,12},{8,0},{12,4},{16,24},{20,28},{24,16},{28,20},{1,9},{5... | collective-permute-start | bytes 491528 | tf_op jit(solution)/shard_map/ppermute | solution.py:381
  19.1 8.3 %collective-permute-start.6 = (bf16[160,512]{1,0:T(8,128)(2,1)S(1)}, bf16[160,512]{1,0:T(8,128)(2,1)S(1)}, u32[]{:S(2)}, u32[]{:S(2)}) collective-permute-start(bf16[160,512]{1,0:T(8,128)(2,1)S(1)} %get-tuple-element.68), channel_id=1, source_target_pairs={{0,16},{4,20},{8,24},{12,28},{16,0},{20,4},{24,8},{28,12},{1,17},{... | collective-permute-start | bytes 491528 | tf_op jit(solution)/shard_map/ppermute | solution.py:381
  20.9 9.5 %copy-start.2 = (bf16[256,2048]{1,0:T(8,128)(2,1)S(1)}, bf16[256,2048]{1,0:T(8,128)(2,1)}, u32[]{:S(2)}) copy-start(bf16[256,2048]{1,0:T(8,128)(2,1)} %do_ref.1) | copy-start | bytes 3145732
  20.9 6.5 %collective-permute-start.7 = (bf16[160,512]{1,0:T(8,128)(2,1)S(1)}, bf16[160,512]{1,0:T(8,128)(2,1)S(1)}, u32[]{:S(2)}, u32[]{:S(2)}) collective-permute-start(bf16[160,512]{1,0:T(8,128)(2,1)S(1)} %get-tuple-element.68), channel_id=1, source_target_pairs={{0,24},{4,28},{8,16},{12,20},{16,8},{20,12},{24,0},{28,4},{1,25},{... | collective-permute-start | bytes 491528 | tf_op jit(solution)/shard_map/ppermute | solution.py:381
  27.5 2.9 %collective-permute-start.8 = (bf16[1152,512]{1,0:T(8,128)(2,1)S(1)}, bf16[1152,512]{1,0:T(8,128)(2,1)S(1)}, u32[]{:S(2)}, u32[]{:S(2)}) collective-permute-start(bf16[1152,512]{1,0:T(8,128)(2,1)S(1)} %select_dynamic-update-slice_fusion.sent_ref), channel_id=1, source_target_pairs={{0,4},{4,0},{8,12},{12,8},{16,20},{20,16},{24,28},{28,24},{1,5},{5... | collective-permute-start | bytes 3538952 | tf_op jit(solution)/shard_map/ppermute | solution.py:386
  76.3 2.8 %collective-permute-start.9 = (bf16[1152,512]{1,0:T(8,128)(2,1)S(1)}, bf16[1152,512]{1,0:T(8,128)(2,1)S(1)}, u32[]{:S(2)}, u32[]{:S(2)}) collective-permute-start(bf16[1152,512]{1,0:T(8,128)(2,1)S(1)} %get-tuple-element.50), channel_id=1, source_target_pairs={{0,4},{4,0},{8,12},{12,8},{16,20},{20,16},{24,28},{28,24},{1,5},{5... | collective-permute-start | bytes 3538952 | tf_op jit(solution)/shard_map/ppermute | solution.py:386
  79.4 10.5 %collective-permute-start.14 = (bf16[160,512]{1,0:T(8,128)(2,1)S(1)}, bf16[160,512]{1,0:T(8,128)(2,1)S(1)}, u32[]{:S(2)}, u32[]{:S(2)}) collective-permute-start(bf16[160,512]{1,0:T(8,128)(2,1)S(1)} %get-tuple-element.57), channel_id=1, source_target_pairs={{0,8},{4,12},{8,0},{12,4},{16,24},{20,28},{24,16},{28,20},{1,9},{5... | collective-permute-start | bytes 491528 | tf_op jit(solution)/shard_map/ppermute | solution.py:381
  79.9 11.4 %collective-permute-start.15 = (bf16[160,512]{1,0:T(8,128)(2,1)S(1)}, bf16[160,512]{1,0:T(8,128)(2,1)S(1)}, u32[]{:S(2)}, u32[]{:S(2)}) collective-permute-start(bf16[160,512]{1,0:T(8,128)(2,1)S(1)} %get-tuple-element.58), channel_id=1, source_target_pairs={{0,16},{4,20},{8,24},{12,28},{16,0},{20,4},{24,8},{28,12},{1,17},{... | collective-permute-start | bytes 491528 | tf_op jit(solution)/shard_map/ppermute | solution.py:381
  81.4 17.1 %collective-permute-start.16 = (bf16[160,512]{1,0:T(8,128)(2,1)S(1)}, bf16[160,512]{1,0:T(8,128)(2,1)S(1)}, u32[]{:S(2)}, u32[]{:S(2)}) collective-permute-start(bf16[160,512]{1,0:T(8,128)(2,1)S(1)} %get-tuple-element.59), channel_id=1, source_target_pairs={{0,24},{4,28},{8,16},{12,20},{16,8},{20,12},{24,0},{28,4},{1,25},{... | collective-permute-start | bytes 491528 | tf_op jit(solution)/shard_map/ppermute | solution.py:381
  83.0 15.8 %collective-permute-start.10 = (bf16[128,512]{1,0:T(8,128)(2,1)S(1)}, bf16[128,512]{1,0:T(8,128)(2,1)S(1)}, u32[]{:S(2)}, u32[]{:S(2)}) collective-permute-start(bf16[128,512]{1,0:T(8,128)(2,1)S(1)} %get-tuple-element.52), channel_id=1, source_target_pairs={{8,0},{12,4},{16,8},{20,12},{24,16},{28,20},{9,1},{13,5},{17,9},{2... | collective-permute-start | bytes 393224 | tf_op jit(solution)/shard_map/ppermute | solution.py:392
  85.3 13.6 %collective-permute-start.11 = (bf16[128,512]{1,0:T(8,128)(2,1)S(1)}, bf16[128,512]{1,0:T(8,128)(2,1)S(1)}, u32[]{:S(2)}, u32[]{:S(2)}) collective-permute-start(bf16[128,512]{1,0:T(8,128)(2,1)S(1)} %get-tuple-element.53), channel_id=1, source_target_pairs={{8,0},{12,4},{16,8},{20,12},{24,16},{28,20},{9,1},{13,5},{17,9},{2... | collective-permute-start | bytes 393224 | tf_op jit(solution)/shard_map/ppermute | solution.py:392
  89.9 13.2 %collective-permute-start.12 = (bf16[128,512]{1,0:T(8,128)(2,1)S(1)}, bf16[128,512]{1,0:T(8,128)(2,1)S(1)}, u32[]{:S(2)}, u32[]{:S(2)}) collective-permute-start(bf16[128,512]{1,0:T(8,128)(2,1)S(1)} %get-tuple-element.54), channel_id=1, source_target_pairs={{16,0},{20,4},{24,8},{28,12},{17,1},{21,5},{25,9},{29,13},{18,2},{... | collective-permute-start | bytes 393224 | tf_op jit(solution)/shard_map/ppermute | solution.py:392
  91.2 11.9 %collective-permute-start.13 = (bf16[128,512]{1,0:T(8,128)(2,1)S(1)}, bf16[128,512]{1,0:T(8,128)(2,1)S(1)}, u32[]{:S(2)}, u32[]{:S(2)}) collective-permute-start(bf16[128,512]{1,0:T(8,128)(2,1)S(1)} %get-tuple-element.55), channel_id=1, source_target_pairs={{16,0},{20,4},{24,8},{28,12},{17,1},{21,5},{25,9},{29,13},{18,2},{... | collective-permute-start | bytes 393224 | tf_op jit(solution)/shard_map/ppermute | solution.py:392
  98.7 4.5 %collective-permute-start.17 = (bf16[40,512]{1,0:T(8,128)(2,1)S(1)}, bf16[40,512]{1,0:T(8,128)(2,1)S(1)}, u32[]{:S(2)}, u32[]{:S(2)}) collective-permute-start(bf16[40,512]{1,0:T(8,128)(2,1)S(1)} %get-tuple-element.61), channel_id=1, source_target_pairs={{0,1},{1,0},{2,3},{3,2},{4,5},{5,4},{6,7},{7,6},{8,9},{9,8},{10,11... | collective-permute-start | bytes 122888 | tf_op jit(solution)/shard_map/ppermute | solution.py:376
  98.8 5.0 %collective-permute-start.18 = (bf16[40,512]{1,0:T(8,128)(2,1)S(1)}, bf16[40,512]{1,0:T(8,128)(2,1)S(1)}, u32[]{:S(2)}, u32[]{:S(2)}) collective-permute-start(bf16[40,512]{1,0:T(8,128)(2,1)S(1)} %get-tuple-element.62), channel_id=1, source_target_pairs={{0,2},{1,3},{2,0},{3,1},{4,6},{5,7},{6,4},{7,5},{8,10},{9,11},{10,... | collective-permute-start | bytes 122888 | tf_op jit(solution)/shard_map/ppermute | solution.py:376
  98.9 6.7 %collective-permute-start.19 = (bf16[40,512]{1,0:T(8,128)(2,1)S(1)}, bf16[40,512]{1,0:T(8,128)(2,1)S(1)}, u32[]{:S(2)}, u32[]{:S(2)}) collective-permute-start(bf16[40,512]{1,0:T(8,128)(2,1)S(1)} %get-tuple-element.63), channel_id=1, source_target_pairs={{0,3},{1,2},{2,1},{3,0},{4,7},{5,6},{6,5},{7,4},{8,11},{9,10},{10,... | collective-permute-start | bytes 122888 | tf_op jit(solution)/shard_map/ppermute | solution.py:376

commit v9 on v8

--- a/solution.py
+++ b/solution.py
@@ -122,11 +122,25 @@
             rv_ref[at, n * HD : (n + 1) * HD] = total[:, (2 * n + 1) * HD : (2 * n + 2) * HD]
 
 
+def kv_pieces(tokens, total_keys, sent_ref, got_ref, own_ref, far_ref):
+    prompt_len = total_keys - 5 * tokens
+    half = prompt_len // 2
+    return [
+        (sent_ref, 0, half, 0),
+        (got_ref, 0, half, half),
+        (own_ref, 0, tokens, prompt_len),
+        (sent_ref, half, tokens, prompt_len + tokens),
+        (far_ref, 0, tokens, prompt_len + 2 * tokens),
+        (got_ref, half, tokens, prompt_len + 3 * tokens),
+        (got_ref, half + tokens, tokens, prompt_len + 4 * tokens),
+    ]
+
+
 def attention_kernel(
     halves, lengths, q_ref, do_ref, sent_ref, got_ref, own_ref, far_ref,
-    o_ref, dq_ref, kept_ref, back_ref,
-    bias, keys, values, keys_t, values_t, s_bufs, g_bufs, p_bufs, d_bufs, top_bufs, inv_bufs,
-    q_ts, cot_ts, q_ns, cot_ns, dk, dv,
+    kept_ref, back_ref, inv_ref, p_ref, d_ref,
+    bias, keys, values, s_bufs, g_bufs, p_bufs, d_bufs, top_bufs,
+    q_ts, cot_ts, q_ns, cot_ns, dk, dv, sems,
 ):
     kv_heads, total_keys = keys.shape[0], keys.shape[1]
     tokens, q_cols = q_ref.shape
@@ -137,7 +151,7 @@
     steps_per_kv = steps // kv_heads
     score_scale = 1.0 / math.sqrt(HD)
     exp_scale = score_scale * math.log2(math.e)
-    resp_at = [prompt_len + i * tokens for i in range(6)]
+    resp_at = [prompt_len + i * tokens for i in range(5)]
     tiles = [slice(at, at + TILE) for at in range(0, total_keys, TILE)]
     chunks = [slice(at, at + CHUNK) for at in range(0, total_keys, CHUNK)]
 
@@ -186,24 +200,6 @@
 
     def behind(which, step):
         kv = kv_of(step)
-        where = place_of(which, jnp.maximum(step, 0))
-        cuts = [slice(at, at + total_keys // 2) for at in (0, total_keys // 2)]
-        state = {}
-
-        def output(at):
-            more = dot(values_t[kv, :, at], p_bufs[which, at])
-            state["out"] = state["out"] + more if "out" in state else more
-
-        def query(at):
-            more = dot(keys_t[kv, :, at], d_bufs[which, at])
-            state["dq"] = state["dq"] + more if "dq" in state else more
-
-        def put_output():
-            o_ref[where] = (state["out"] * inv_bufs[which, :1]).astype(BF16).T
-
-        def put_query():
-            dq = state["dq"] * (inv_bufs[which, :1] * score_scale)
-            dq_ref[where] = dq.astype(BF16).T
 
         def value_grad(at):
             dv[kv, at] += dot(p_bufs[which, at], cot_ns[which])
@@ -211,12 +207,24 @@
         def key_grad(at):
             dk[kv, at] += dot(d_bufs[which, at], q_ns[which])
 
-        work = [functools.partial(f, at) for at in chunks for f in (value_grad, key_grad)]
-        first = [functools.partial(output, at) for at in cuts] + [put_output]
-        second = [functools.partial(query, at) for at in cuts] + [put_query]
-        return first + work[: len(work) // 2] + second + work[len(work) // 2 :]
-
-    def weigh(which):
+        return [functools.partial(f, at) for at in chunks for f in (value_grad, key_grad)]
+
+    def kept_copies(which, step):
+        index = 2 * step + which
+        return [
+            pltpu.make_async_copy(p_bufs.at[which], p_ref.at[index], sems.at[which, 0]),
+            pltpu.make_async_copy(d_bufs.at[which], d_ref.at[index], sems.at[which, 1]),
+        ]
+
+    def send(which, step):
+        for copy in kept_copies(which, step):
+            copy.start()
+
+    def finish_sending(which, step):
+        for copy in kept_copies(which, step):
+            copy.wait()
+
+    def weigh(which, step):
         state = {}
 
         def settle():
@@ -233,7 +241,7 @@
         def finish():
             inverse = 1.0 / jnp.sum(state["sum"], axis=0, keepdims=True)
             state["delta"] = jnp.sum(state["dot"], axis=0, keepdims=True) * inverse
-            inv_bufs[which] = jnp.broadcast_to(inverse, (8, rows))
+            inv_ref[2 * step + which] = jnp.broadcast_to(inverse, (8, rows))
             q_ns[which] = (q_ts[which].astype(F32) * inverse).astype(BF16).T
             cot_ns[which] = (cot_ts[which].astype(F32) * inverse).astype(BF16).T
 
@@ -278,36 +286,38 @@
             bias[at : at + TILE] = jnp.where(allowed, 0.0, NEG)
     for n in range(kv_heads):
         k_at, v_at = 2 * n * HD, (2 * n + 1) * HD
-        for ref, start, size, at in (
-            (sent_ref, 0, half, 0),
-            (got_ref, 0, half, half),
-            (own_ref, 0, tokens, resp_at[0]),
-            (sent_ref, half, tokens, resp_at[1]),
-            (far_ref, 0, tokens, resp_at[2]),
-            (got_ref, half, tokens, resp_at[3]),
-            (got_ref, half + tokens, tokens, resp_at[4]),
-        ):
-            k_rows = ref[start : start + size, k_at : k_at + HD]
-            v_rows = ref[start : start + size, v_at : v_at + HD]
-            keys[n, at : at + size] = k_rows
-            values[n, at : at + size] = v_rows
-            keys_t[n, :, at : at + size] = k_rows.T
-            values_t[n, :, at : at + size] = v_rows.T
+        for ref, start, size, at in kv_pieces(tokens, total_keys, sent_ref, got_ref, own_ref, far_ref):
+            keys[n, at : at + size] = ref[start : start + size, k_at : k_at + HD]
+            values[n, at : at + size] = ref[start : start + size, v_at : v_at + HD]
     dk[...] = jnp.zeros_like(dk)
     dv[...] = jnp.zeros_like(dv)
-    for ref in (p_bufs, d_bufs, inv_bufs, q_ns, cot_ns):
+    for ref in (p_bufs, d_bufs, q_ns, cot_ns):
         ref[1] = jnp.zeros(ref.shape[1:], ref.dtype)
     for work in ahead(0, 0):
         work()
 
     def pair(step, carry):
-        together(weigh(0), mixed(behind(1, step - 1), ahead(1, step)))
-        together(weigh(1), mixed(behind(0, step), ahead(0, step + 1)))
+        @pl.when(step > 0)
+        def _():
+            send(1, step - 1)
+            finish_sending(0, step - 1)
+
+        together(weigh(0, step), mixed(behind(1, step - 1), ahead(1, step)))
+
+        @pl.when(step > 0)
+        def _():
+            finish_sending(1, step - 1)
+
+        send(0, step)
+        together(weigh(1, step), mixed(behind(0, step), ahead(0, step + 1)))
         return carry
 
     lax.fori_loop(0, steps, pair, 0)
+    send(1, steps - 1)
     for work in behind(1, steps - 1):
         work()
+    finish_sending(0, steps - 1)
+    finish_sending(1, steps - 1)
     for n in range(kv_heads):
         k_cols = slice(2 * n * HD, (2 * n + 1) * HD)
         v_cols = slice((2 * n + 1) * HD, (2 * n + 2) * HD)
@@ -333,28 +343,28 @@
     q_heads = resp_q.shape[1] // HD
     halves = 1 if tokens * total_keys <= MOST_SCORES else 2
     rows = tokens // halves
+    units = q_heads * halves
     pairs = tokens * q_heads * total_keys
-    return pl.pallas_call(
+    stored = jax.ShapeDtypeStruct((units, total_keys, rows), BF16)
+    kept, back, inverses, weights, slopes = pl.pallas_call(
         functools.partial(attention_kernel, halves),
         in_specs=[pl.BlockSpec(memory_space=pltpu.SMEM)] + whole(6),
-        out_specs=whole(4),
+        out_specs=whole(3) + [pl.BlockSpec(memory_space=pl.ANY)] * 2,
         out_shape=[
-            jax.ShapeDtypeStruct(resp_q.shape, BF16),
-            jax.ShapeDtypeStruct(resp_q.shape, BF16),
             jax.ShapeDtypeStruct((half + 3 * tokens, sent.shape[1]), F32),
             jax.ShapeDtypeStruct((half + 2 * tokens, sent.shape[1]), BF16),
+            jax.ShapeDtypeStruct((units, 8, rows), F32),
+            stored,
+            stored,
         ],
         scratch_shapes=[
             pltpu.VMEM((5 * tokens, tokens), F32),
             pltpu.VMEM((kv_heads, total_keys, HD), BF16),
             pltpu.VMEM((kv_heads, total_keys, HD), BF16),
-            pltpu.VMEM((kv_heads, HD, total_keys), BF16),
-            pltpu.VMEM((kv_heads, HD, total_keys), BF16),
             pltpu.VMEM((2, total_keys, rows), F32),
             pltpu.VMEM((2, total_keys, rows), F32),
             pltpu.VMEM((2, total_keys, rows), BF16),
             pltpu.VMEM((2, total_keys, rows), BF16),
-            pltpu.VMEM((2, 8, rows), F32),
             pltpu.VMEM((2, 8, rows), F32),
             pltpu.VMEM((2, HD, rows), BF16),
             pltpu.VMEM((2, HD, rows), BF16),
@@ -362,13 +372,60 @@
             pltpu.VMEM((2, rows, HD), BF16),
             pltpu.VMEM((kv_heads, total_keys, HD), F32),
             pltpu.VMEM((kv_heads, total_keys, HD), F32),
+            pltpu.SemaphoreType.DMA((2, 2)),
         ],
-        compiler_params=pltpu.CompilerParams(vmem_limit_bytes=(36 if halves == 1 else 48) << 20),
+        compiler_params=pltpu.CompilerParams(
+            vmem_limit_bytes=(34 if halves == 1 else 44) << 20
+        ),
         cost_estimate=pl.CostEstimate(
-            flops=12 * HD * pairs, bytes_accessed=8 * resp_q.size, transcendentals=pairs
+            flops=16 * HD * pairs, bytes_accessed=8 * resp_q.size, transcendentals=pairs
         ),
         name="attention",
     )(lengths, resp_q, grad_out, sent, got, own, far)
+
+    def rows_of_tokens(name, column, scale, stored):
+        per_kv = units // kv_heads
+        return pl.pallas_call(
+            functools.partial(product_kernel, tokens, per_kv, column, scale),
+            grid=(units,),
+            in_specs=[
+                pl.BlockSpec((1, total_keys, rows), lambda u: (u, 0, 0)),
+                pl.BlockSpec((1, 8, rows), lambda u: (u, 0, 0)),
+            ]
+            + whole(4),
+            out_specs=pl.BlockSpec((rows, HD), lambda u: (u % halves, u // halves)),
+            out_shape=jax.ShapeDtypeStruct(resp_q.shape, BF16),
+            scratch_shapes=[pltpu.VMEM((kv_heads, HD, total_keys), BF16)],
+            compiler_params=pltpu.CompilerParams(vmem_limit_bytes=48 << 20),
+            cost_estimate=pl.CostEstimate(
+                flops=8 * HD * pairs, bytes_accessed=2 * pairs, transcendentals=0
+            ),
+            name=name,
+        )(stored, inverses, sent, got, own, far)
+
+    resp_out = rows_of_tokens("output", HD, 1.0, weights)
+    grad_q = rows_of_tokens("grad_query", 0, 1.0 / math.sqrt(HD), slopes)
+    return resp_out, grad_q, kept, back
+
+
+def product_kernel(
+    tokens, per_kv, column, scale, stored_ref, inv_ref, sent_ref, got_ref, own_ref, far_ref,
+    out_ref, rows_t,
+):
+    kv_heads, total_keys = rows_t.shape[0], rows_t.shape[2]
+    index = pl.program_id(0)
+
+    @pl.when(index == 0)
+    def _():
+        for n in range(kv_heads):
+            cols = slice(2 * n * HD + column, 2 * n * HD + column + HD)
+            for ref, start, size, at in kv_pieces(
+                tokens, total_keys, sent_ref, got_ref, own_ref, far_ref
+            ):
+                rows_t[n, :, at : at + size] = ref[start : start + size, cols].T
+
+    out = dot(rows_t[index // per_kv], stored_ref[0])
+    out_ref[...] = (out * (inv_ref[0, :1] * scale)).astype(BF16).T
 
 
 def swap_heads(array, by):

time: 107 us -> 135 us (1.26)
  Pallas kernels: 48.9 us -> 83.9 us
  starting transfers between devices: 36.2 us -> 30.9 us
  waiting for transfers between devices: 19.4 us -> 17 us
    pallas_call x0 -> x2, Pallas kernels: none -> 32.5 us  [rows_of_tokens(): pl.pallas_call(functools.partial(product_kernel, tokens, per_kv, column,...]
    ppermute x6, starting transfers between devices: 18.2 us -> 12.8 us  [shift_chips(): lax.ppermute(array, 'seq', [(i, i + by) for i in range(devices) if 0 <= i...]
    pallas_call x1, Pallas kernels: 45.9 us -> 48.3 us  [attention(): pl.pallas_call(functools.partial(attention_kernel, halves), in_specs=[pl....]
    ppermute x6, waiting for transfers between devices: 7.4 us -> 5.01 us  [swap_heads(): return lax.ppermute(array, 'head', [(i, i ^ by) for i in range(devices)])]
  transfers between devices with their start and end apart: 20 -> 20, of which waited for: 8 -> 6; matrix products, arithmetic and copies ran while one was open for 1% -> 1% of each run, Pallas kernels for 0% -> 24%
where the time goes in v9:
time: 135 us; the launch traced here: 134 us
  Pallas kernels  83.9 us (62%)
  starting transfers between devices  30.9 us (23%)
  waiting for transfers between devices  17 us (13%)
    pallas_call x1, Pallas kernels, attention(): pl.pallas_call(functools.partial(attention_kernel, halves), in_specs=[pl....  48.3 us
    pallas_call x2, Pallas kernels, rows_of_tokens(): pl.pallas_call(functools.partial(product_kernel, tokens, per_kv, column,...  32.5 us
    ppermute x6, starting transfers between devices, shift_chips(): lax.ppermute(array, 'seq', [(i, i + by) for i in range(devices) if 0 <= i...  12.8 us
    ppermute x6, starting transfers between devices, swap_chips(): lax.ppermute(array, 'seq', [(i, i ^ by * CORES) for i in range(devices)])  8.93 us
    ppermute x6, starting transfers between devices, swap_heads(): return lax.ppermute(array, 'head', [(i, i ^ by) for i in range(devices)])  8.91 us
    ppermute x6, waiting for transfers between devices, swap_chips(): lax.ppermute(array, 'seq', [(i, i ^ by * CORES) for i in range(devices)])  6.44 us
    ppermute x2, waiting for transfers between devices, swap_cores(): return lax.ppermute(array, 'seq', [(i, i ^ 1) for i in range(devices)])  5.55 us
    ppermute x6, waiting for transfers between devices, swap_heads(): return lax.ppermute(array, 'head', [(i, i ^ by) for i in range(devices)])  5.01 us
  transfers between devices with their start and end apart: 20, of which 6 were waited for; matrix products, arithmetic and copies ran while one was open for 1% of the time, Pallas kernels for 24%

profile of v9, /device:TPU:6, one launch (start us, length us, event | category | flops | bytes accessed | tf_op | source)
XLA Modules:
  0.0 133.6 jit_solution(18187814553106921532)
XLA Ops:
  0.6 1.9 %pack.1 = (bf16[40,512]{1,0:T(8,128)(2,1)}, bf16[40,512]{1,0:T(8,128)(2,1)}, bf16[40,512]{1,0:T(8,128)(2,1)}, bf16[40,512]{1,0:T(8,128)(2,1)}, bf16[256,512]{1,0:T(8,128)(2,1)}) custom-call(bf16[40,1024]{1,0:T(8,128)(2,1)} %pk_ref.1, bf16[40,1024]{1,0:T(8,128)(2,1)} %pv_ref.1, bf16[256,256]{1,0:T(8,128)(2,1)} %rk_ref.1, bf16[256,256]{1,0:T(8,128)(2,1)} %rv_ref.1), custom_call_target="tpu_custom_call" | custom-call | tf_op jit(solution)/shard_map/pack/pallas_call | solution.py:64
  2.5 1.4 %collective-permute-start.4 = (bf16[256,512]{1,0:T(8,128)(2,1)}, bf16[256,512]{1,0:T(8,128)(2,1)S(1)}, u32[]{:S(2)}, u32[]{:S(2)}) collective-permute-start(bf16[256,512]{1,0:T(8,128)(2,1)} %get-tuple-element.42.own_ref), channel_id=1, source_target_pairs={{0,16},{4,20},{8,24},{12,28},{1,17},{5,21},{9,25},{13,29},{2,18},{... | collective-permute-start | bytes 786440 | tf_op jit(solution)/shard_map/ppermute | solution.py:449
  3.9 1.3 collective-permute-start.3
  5.2 1.6 %collective-permute-start = (bf16[40,512]{1,0:T(8,128)(2,1)}, bf16[40,512]{1,0:T(8,128)(2,1)S(1)}, u32[]{:S(2)}, u32[]{:S(2)}) collective-permute-start(bf16[40,512]{1,0:T(8,128)(2,1)} %get-tuple-element.39), channel_id=1, source_target_pairs={{0,1},{1,0},{2,3},{3,2},{4,5},{5,4},{6,7},{7,6},{8,9},{9,8},{10,11... | collective-permute-start | bytes 122888 | tf_op jit(solution)/shard_map/ppermute | solution.py:433
  6.9 2.6 %collective-permute-start.1 = (bf16[40,512]{1,0:T(8,128)(2,1)}, bf16[40,512]{1,0:T(8,128)(2,1)S(1)}, u32[]{:S(2)}, u32[]{:S(2)}) collective-permute-start(bf16[40,512]{1,0:T(8,128)(2,1)} %get-tuple-element.40), channel_id=1, source_target_pairs={{0,2},{1,3},{2,0},{3,1},{4,6},{5,7},{6,4},{7,5},{8,10},{9,11},{10,... | collective-permute-start | bytes 122888 | tf_op jit(solution)/shard_map/ppermute | solution.py:433
  9.5 0.2 collective-permute-start.2
  9.7 0.8 constant_dynamic-update-slice_fusion.3
  10.5 2.3 %collective-permute-done.1 = bf16[40,512]{1,0:T(8,128)(2,1)S(1)} collective-permute-done((bf16[40,512]{1,0:T(8,128)(2,1)}, bf16[40,512]{1,0:T(8,128)(2,1)S(1)}, u32[]{:S(2)}, u32[]{:S(2)}) %collective-permute-start.1) | collective-permute-done | bytes 40992 | tf_op jit(solution)/shard_map/ppermute | solution.py:433
  12.8 2.7 %collective-permute-done.2 = bf16[40,512]{1,0:T(8,128)(2,1)S(1)} collective-permute-done((bf16[40,512]{1,0:T(8,128)(2,1)}, bf16[40,512]{1,0:T(8,128)(2,1)S(1)}, u32[]{:S(2)}, u32[]{:S(2)}) %collective-permute-start.2) | collective-permute-done | bytes 40992 | tf_op jit(solution)/shard_map/ppermute | solution.py:433
  15.6 3.5 %collective-permute-start.5 = (bf16[160,512]{1,0:T(8,128)(2,1)S(1)}, bf16[160,512]{1,0:T(8,128)(2,1)S(1)}, u32[]{:S(2)}, u32[]{:S(2)}) collective-permute-start(bf16[160,512]{1,0:T(8,128)(2,1)S(1)} %get-tuple-element.70), channel_id=1, source_target_pairs={{0,8},{4,12},{8,0},{12,4},{16,24},{20,28},{24,16},{28,20},{1,9},{5... | collective-permute-start | bytes 491528 | tf_op jit(solution)/shard_map/ppermute | solution.py:438
  19.1 1.9 %collective-permute-start.6 = (bf16[160,512]{1,0:T(8,128)(2,1)S(1)}, bf16[160,512]{1,0:T(8,128)(2,1)S(1)}, u32[]{:S(2)}, u32[]{:S(2)}) collective-permute-start(bf16[160,512]{1,0:T(8,128)(2,1)S(1)} %get-tuple-element.70), channel_id=1, source_target_pairs={{0,16},{4,20},{8,24},{12,28},{16,0},{20,4},{24,8},{28,12},{1,17},{... | collective-permute-start | bytes 491528 | tf_op jit(solution)/shard_map/ppermute | solution.py:438
  20.9 2.5 %collective-permute-done.5 = bf16[160,512]{1,0:T(8,128)(2,1)S(1)} collective-permute-done((bf16[160,512]{1,0:T(8,128)(2,1)S(1)}, bf16[160,512]{1,0:T(8,128)(2,1)S(1)}, u32[]{:S(2)}, u32[]{:S(2)}) %collective-permute-start.5) | collective-permute-done | bytes 163872 | tf_op jit(solution)/shard_map/ppermute | solution.py:438
  23.4 3.9 %collective-permute-done.6 = bf16[160,512]{1,0:T(8,128)(2,1)S(1)} collective-permute-done((bf16[160,512]{1,0:T(8,128)(2,1)S(1)}, bf16[160,512]{1,0:T(8,128)(2,1)S(1)}, u32[]{:S(2)}, u32[]{:S(2)}) %collective-permute-start.6) | collective-permute-done | bytes 163872 | tf_op jit(solution)/shard_map/ppermute | solution.py:438
  27.5 0.1 collective-permute-start.8
  27.6 2.8 %collective-permute-done.8.got_ref = bf16[1152,512]{1,0:T(8,128)(2,1)S(1)} collective-permute-done((bf16[1152,512]{1,0:T(8,128)(2,1)S(1)}, bf16[1152,512]{1,0:T(8,128)(2,1)S(1)}, u32[]{:S(2)}, u32[]{:S(2)}) %collective-permute-start.8) | collective-permute-done | bytes 1179680 | tf_op jit(solution)/shard_map/ppermute | solution.py:443
  30.5 48.3 %attention.1 = (f32[1408,512]{1,0:T(8,128)S(1)}, bf16[1152,512]{1,0:T(8,128)(2,1)S(1)}, f32[16,8,256]{2,1,0:T(8,128)S(1)}, bf16[16,2560,256]{2,1,0:T(8,128)(2,1)}, bf16[16,2560,256]{2,1,0:T(8,128)(2,1)}) custom-call(s32[8]{0:T(128)S(1)} %copy-done.3, bf16[256,2048]{1,0:T(8,128)(2,1)S(1)} %copy-done.1, bf16[256,2048]{1,0:T(8,128)(2,1)S(1)} %copy-done.2, ...), custom_call_target="tpu_custom_call" | custom-call | flops 21474836480 | bytes 4194304 | tf_op jit(solution)/shard_map/attention/pallas_call | solution.py:349
  78.8 0.2 collective-permute-start.9
  79.0 2.7 %collective-permute-done.9.got_ref = bf16[1152,512]{1,0:T(8,128)(2,1)S(1)} collective-permute-done((bf16[1152,512]{1,0:T(8,128)(2,1)S(1)}, bf16[1152,512]{1,0:T(8,128)(2,1)S(1)}, u32[]{:S(2)}, u32[]{:S(2)}) %collective-permute-start.9) | collective-permute-done | bytes 1179680 | tf_op jit(solution)/shard_map/ppermute | solution.py:443
  81.7 0.3 merge.1
  81.9 2.3 %collective-permute-start.10 = (bf16[128,512]{1,0:T(8,128)(2,1)S(1)}, bf16[128,512]{1,0:T(8,128)(2,1)S(1)}, u32[]{:S(2)}, u32[]{:S(2)}) collective-permute-start(bf16[128,512]{1,0:T(8,128)(2,1)S(1)} %get-tuple-element.54), channel_id=1, source_target_pairs={{8,0},{12,4},{16,8},{20,12},{24,16},{28,20},{9,1},{13,5},{17,9},{2... | collective-permute-start | bytes 393224 | tf_op jit(solution)/shard_map/ppermute | solution.py:449
  84.2 4.6 %collective-permute-start.11 = (bf16[128,512]{1,0:T(8,128)(2,1)S(1)}, bf16[128,512]{1,0:T(8,128)(2,1)S(1)}, u32[]{:S(2)}, u32[]{:S(2)}) collective-permute-start(bf16[128,512]{1,0:T(8,128)(2,1)S(1)} %get-tuple-element.55), channel_id=1, source_target_pairs={{8,0},{12,4},{16,8},{20,12},{24,16},{28,20},{9,1},{13,5},{17,9},{2... | collective-permute-start | bytes 393224 | tf_op jit(solution)/shard_map/ppermute | solution.py:449
  88.9 0.4 collective-permute-start.14
  89.2 3.2 %collective-permute-start.16 = (bf16[160,512]{1,0:T(8,128)(2,1)S(1)}, bf16[160,512]{1,0:T(8,128)(2,1)S(1)}, u32[]{:S(2)}, u32[]{:S(2)}) collective-permute-start(bf16[160,512]{1,0:T(8,128)(2,1)S(1)} %get-tuple-element.61), channel_id=1, source_target_pairs={{0,24},{4,28},{8,16},{12,20},{16,8},{20,12},{24,0},{28,4},{1,25},{... | collective-permute-start | bytes 491528 | tf_op jit(solution)/shard_map/ppermute | solution.py:438
  92.4 16.3 %output.1 = bf16[256,2048]{1,0:T(8,128)(2,1)} custom-call(bf16[16,2560,256]{2,1,0:T(8,128)(2,1)} %get-tuple-element.48.stored_ref, f32[16,8,256]{2,1,0:T(8,128)S(1)} %get-tuple-element.49.inv_ref, bf16[1152,512]{1,0:T(8,128)(2,1)S(1)} %select_dynamic-update-slice_fusion.sent_ref, bf16[1152,512]{1,0:T(8,128)(2,1)S(1)} %collective-permute-done.8.got_ref, ...), custom_call_target="tpu_custom_call" | custom-call | flops 10737418240 | bytes 20971520 | tf_op jit(solution)/shard_map/output/pallas_call | solution.py:388
  108.7 1.9 %collective-permute-start.12 = (bf16[128,512]{1,0:T(8,128)(2,1)S(1)}, bf16[128,512]{1,0:T(8,128)(2,1)S(1)}, u32[]{:S(2)}, u32[]{:S(2)}) collective-permute-start(bf16[128,512]{1,0:T(8,128)(2,1)S(1)} %get-tuple-element.56), channel_id=1, source_target_pairs={{16,0},{20,4},{24,8},{28,12},{17,1},{21,5},{25,9},{29,13},{18,2},{... | collective-permute-start | bytes 393224 | tf_op jit(solution)/shard_map/ppermute | solution.py:449
  110.6 1.3 collective-permute-start.13
  111.9 0.1 sum_chips.1
  112.0 0.5 collective-permute-start.17
  112.6 2.6 %collective-permute-start.18 = (bf16[40,512]{1,0:T(8,128)(2,1)S(1)}, bf16[40,512]{1,0:T(8,128)(2,1)S(1)}, u32[]{:S(2)}, u32[]{:S(2)}) collective-permute-start(bf16[40,512]{1,0:T(8,128)(2,1)S(1)} %get-tuple-element.64), channel_id=1, source_target_pairs={{0,2},{1,3},{2,0},{3,1},{4,6},{5,7},{6,4},{7,5},{8,10},{9,11},{10,... | collective-permute-start | bytes 122888 | tf_op jit(solution)/shard_map/ppermute | solution.py:433
  115.2 1.3 collective-permute-start.19
  116.5 16.3 %grad_query.1 = bf16[256,2048]{1,0:T(8,128)(2,1)} custom-call(bf16[16,2560,256]{2,1,0:T(8,128)(2,1)} %get-tuple-element.50.stored_ref, f32[16,8,256]{2,1,0:T(8,128)S(1)} %get-tuple-element.49.inv_ref, bf16[1152,512]{1,0:T(8,128)(2,1)S(1)} %select_dynamic-update-slice_fusion.sent_ref, bf16[1152,512]{1,0:T(8,128)(2,1)S(1)} %collective-permute-done.8.got_ref, ...), custom_call_target="tpu_custom_call" | custom-call | flops 10737418240 | bytes 20971520 | tf_op jit(solution)/shard_map/grad_query/pallas_call | solution.py:388
  132.8 0.8 finish.1
  (32 shorter events, 0.2 us)
Async XLA Ops:
  2.5 24.9 %copy-start = (bf16[256,512]{1,0:T(8,128)(2,1)S(1)}, bf16[256,512]{1,0:T(8,128)(2,1)}, u32[]{:S(2)}) copy-start(bf16[256,512]{1,0:T(8,128)(2,1)} %get-tuple-element.42.own_ref) | copy-start | bytes 786436
  2.5 13.0 %collective-permute-start.4 = (bf16[256,512]{1,0:T(8,128)(2,1)}, bf16[256,512]{1,0:T(8,128)(2,1)S(1)}, u32[]{:S(2)}, u32[]{:S(2)}) collective-permute-start(bf16[256,512]{1,0:T(8,128)(2,1)} %get-tuple-element.42.own_ref), channel_id=1, source_target_pairs={{0,16},{4,20},{8,24},{12,28},{1,17},{5,21},{9,25},{13,29},{2,18},{... | collective-permute-start | bytes 786440 | tf_op jit(solution)/shard_map/ppermute | solution.py:449
  3.9 11.5 %collective-permute-start.3 = (bf16[256,512]{1,0:T(8,128)(2,1)}, bf16[256,512]{1,0:T(8,128)(2,1)S(1)}, u32[]{:S(2)}, u32[]{:S(2)}) collective-permute-start(bf16[256,512]{1,0:T(8,128)(2,1)} %get-tuple-element.42.own_ref), channel_id=1, source_target_pairs={{0,8},{4,12},{8,16},{12,20},{16,24},{20,28},{1,9},{5,13},{9,17},{1... | collective-permute-start | bytes 786440 | tf_op jit(solution)/shard_map/ppermute | solution.py:449
  5.2 5.2 %collective-permute-start = (bf16[40,512]{1,0:T(8,128)(2,1)}, bf16[40,512]{1,0:T(8,128)(2,1)S(1)}, u32[]{:S(2)}, u32[]{:S(2)}) collective-permute-start(bf16[40,512]{1,0:T(8,128)(2,1)} %get-tuple-element.39), channel_id=1, source_target_pairs={{0,1},{1,0},{2,3},{3,2},{4,5},{5,4},{6,7},{7,6},{8,9},{9,8},{10,11... | collective-permute-start | bytes 122888 | tf_op jit(solution)/shard_map/ppermute | solution.py:433
  6.9 5.9 %collective-permute-start.1 = (bf16[40,512]{1,0:T(8,128)(2,1)}, bf16[40,512]{1,0:T(8,128)(2,1)S(1)}, u32[]{:S(2)}, u32[]{:S(2)}) collective-permute-start(bf16[40,512]{1,0:T(8,128)(2,1)} %get-tuple-element.40), channel_id=1, source_target_pairs={{0,2},{1,3},{2,0},{3,1},{4,6},{5,7},{6,4},{7,5},{8,10},{9,11},{10,... | collective-permute-start | bytes 122888 | tf_op jit(solution)/shard_map/ppermute | solution.py:433
  9.5 6.0 %collective-permute-start.2 = (bf16[40,512]{1,0:T(8,128)(2,1)}, bf16[40,512]{1,0:T(8,128)(2,1)S(1)}, u32[]{:S(2)}, u32[]{:S(2)}) collective-permute-start(bf16[40,512]{1,0:T(8,128)(2,1)} %get-tuple-element.41), channel_id=1, source_target_pairs={{0,3},{1,2},{2,1},{3,0},{4,7},{5,6},{6,5},{7,4},{8,11},{9,10},{10,... | collective-permute-start | bytes 122888 | tf_op jit(solution)/shard_map/ppermute | solution.py:433
  15.5 14.9 %copy-start.1 = (bf16[256,2048]{1,0:T(8,128)(2,1)S(1)}, bf16[256,2048]{1,0:T(8,128)(2,1)}, u32[]{:S(2)}) copy-start(bf16[256,2048]{1,0:T(8,128)(2,1)} %q_ref.1) | copy-start | bytes 3145732
  15.5 14.9 %copy-start.3 = (s32[8]{0:T(128)S(1)}, s32[8]{0:T(128)}, u32[]{:S(2)}) copy-start(s32[8]{0:T(128)} %lengths.1) | copy-start | bytes 100
  15.6 7.9 %collective-permute-start.5 = (bf16[160,512]{1,0:T(8,128)(2,1)S(1)}, bf16[160,512]{1,0:T(8,128)(2,1)S(1)}, u32[]{:S(2)}, u32[]{:S(2)}) collective-permute-start(bf16[160,512]{1,0:T(8,128)(2,1)S(1)} %get-tuple-element.70), channel_id=1, source_target_pairs={{0,8},{4,12},{8,0},{12,4},{16,24},{20,28},{24,16},{28,20},{1,9},{5... | collective-permute-start | bytes 491528 | tf_op jit(solution)/shard_map/ppermute | solution.py:438
  19.1 8.3 %collective-permute-start.6 = (bf16[160,512]{1,0:T(8,128)(2,1)S(1)}, bf16[160,512]{1,0:T(8,128)(2,1)S(1)}, u32[]{:S(2)}, u32[]{:S(2)}) collective-permute-start(bf16[160,512]{1,0:T(8,128)(2,1)S(1)} %get-tuple-element.70), channel_id=1, source_target_pairs={{0,16},{4,20},{8,24},{12,28},{16,0},{20,4},{24,8},{28,12},{1,17},{... | collective-permute-start | bytes 491528 | tf_op jit(solution)/shard_map/ppermute | solution.py:438
  20.9 9.5 %copy-start.2 = (bf16[256,2048]{1,0:T(8,128)(2,1)S(1)}, bf16[256,2048]{1,0:T(8,128)(2,1)}, u32[]{:S(2)}) copy-start(bf16[256,2048]{1,0:T(8,128)(2,1)} %do_ref.1) | copy-start | bytes 3145732
  20.9 6.5 %collective-permute-start.7 = (bf16[160,512]{1,0:T(8,128)(2,1)S(1)}, bf16[160,512]{1,0:T(8,128)(2,1)S(1)}, u32[]{:S(2)}, u32[]{:S(2)}) collective-permute-start(bf16[160,512]{1,0:T(8,128)(2,1)S(1)} %get-tuple-element.70), channel_id=1, source_target_pairs={{0,24},{4,28},{8,16},{12,20},{16,8},{20,12},{24,0},{28,4},{1,25},{... | collective-permute-start | bytes 491528 | tf_op jit(solution)/shard_map/ppermute | solution.py:438
  27.5 2.9 %collective-permute-start.8 = (bf16[1152,512]{1,0:T(8,128)(2,1)S(1)}, bf16[1152,512]{1,0:T(8,128)(2,1)S(1)}, u32[]{:S(2)}, u32[]{:S(2)}) collective-permute-start(bf16[1152,512]{1,0:T(8,128)(2,1)S(1)} %select_dynamic-update-slice_fusion.sent_ref), channel_id=1, source_target_pairs={{0,4},{4,0},{8,12},{12,8},{16,20},{20,16},{24,28},{28,24},{1,5},{5... | collective-permute-start | bytes 3538952 | tf_op jit(solution)/shard_map/ppermute | solution.py:443
  78.8 2.9 %collective-permute-start.9 = (bf16[1152,512]{1,0:T(8,128)(2,1)S(1)}, bf16[1152,512]{1,0:T(8,128)(2,1)S(1)}, u32[]{:S(2)}, u32[]{:S(2)}) collective-permute-start(bf16[1152,512]{1,0:T(8,128)(2,1)S(1)} %get-tuple-element.52), channel_id=1, source_target_pairs={{0,4},{4,0},{8,12},{12,8},{16,20},{20,16},{24,28},{28,24},{1,5},{5... | collective-permute-start | bytes 3538952 | tf_op jit(solution)/shard_map/ppermute | solution.py:443
  81.9 30.6 %collective-permute-start.10 = (bf16[128,512]{1,0:T(8,128)(2,1)S(1)}, bf16[128,512]{1,0:T(8,128)(2,1)S(1)}, u32[]{:S(2)}, u32[]{:S(2)}) collective-permute-start(bf16[128,512]{1,0:T(8,128)(2,1)S(1)} %get-tuple-element.54), channel_id=1, source_target_pairs={{8,0},{12,4},{16,8},{20,12},{24,16},{28,20},{9,1},{13,5},{17,9},{2... | collective-permute-start | bytes 393224 | tf_op jit(solution)/shard_map/ppermute | solution.py:449
  84.2 31.0 %collective-permute-start.11 = (bf16[128,512]{1,0:T(8,128)(2,1)S(1)}, bf16[128,512]{1,0:T(8,128)(2,1)S(1)}, u32[]{:S(2)}, u32[]{:S(2)}) collective-permute-start(bf16[128,512]{1,0:T(8,128)(2,1)S(1)} %get-tuple-element.55), channel_id=1, source_target_pairs={{8,0},{12,4},{16,8},{20,12},{24,16},{28,20},{9,1},{13,5},{17,9},{2... | collective-permute-start | bytes 393224 | tf_op jit(solution)/shard_map/ppermute | solution.py:449
  88.9 19.8 %collective-permute-start.14 = (bf16[160,512]{1,0:T(8,128)(2,1)S(1)}, bf16[160,512]{1,0:T(8,128)(2,1)S(1)}, u32[]{:S(2)}, u32[]{:S(2)}) collective-permute-start(bf16[160,512]{1,0:T(8,128)(2,1)S(1)} %get-tuple-element.59), channel_id=1, source_target_pairs={{0,8},{4,12},{8,0},{12,4},{16,24},{20,28},{24,16},{28,20},{1,9},{5... | collective-permute-start | bytes 491528 | tf_op jit(solution)/shard_map/ppermute | solution.py:438
  89.2 21.4 %collective-permute-start.15 = (bf16[160,512]{1,0:T(8,128)(2,1)S(1)}, bf16[160,512]{1,0:T(8,128)(2,1)S(1)}, u32[]{:S(2)}, u32[]{:S(2)}) collective-permute-start(bf16[160,512]{1,0:T(8,128)(2,1)S(1)} %get-tuple-element.60), channel_id=1, source_target_pairs={{0,16},{4,20},{8,24},{12,28},{16,0},{20,4},{24,8},{28,12},{1,17},{... | collective-permute-start | bytes 491528 | tf_op jit(solution)/shard_map/ppermute | solution.py:438
  89.2 22.7 %collective-permute-start.16 = (bf16[160,512]{1,0:T(8,128)(2,1)S(1)}, bf16[160,512]{1,0:T(8,128)(2,1)S(1)}, u32[]{:S(2)}, u32[]{:S(2)}) collective-permute-start(bf16[160,512]{1,0:T(8,128)(2,1)S(1)} %get-tuple-element.61), channel_id=1, source_target_pairs={{0,24},{4,28},{8,16},{12,20},{16,8},{20,12},{24,0},{28,4},{1,25},{... | collective-permute-start | bytes 491528 | tf_op jit(solution)/shard_map/ppermute | solution.py:438
  108.7 24.1 %collective-permute-start.12 = (bf16[128,512]{1,0:T(8,128)(2,1)S(1)}, bf16[128,512]{1,0:T(8,128)(2,1)S(1)}, u32[]{:S(2)}, u32[]{:S(2)}) collective-permute-start(bf16[128,512]{1,0:T(8,128)(2,1)S(1)} %get-tuple-element.56), channel_id=1, source_target_pairs={{16,0},{20,4},{24,8},{28,12},{17,1},{21,5},{25,9},{29,13},{18,2},{... | collective-permute-start | bytes 393224 | tf_op jit(solution)/shard_map/ppermute | solution.py:449
  110.6 22.1 %collective-permute-start.13 = (bf16[128,512]{1,0:T(8,128)(2,1)S(1)}, bf16[128,512]{1,0:T(8,128)(2,1)S(1)}, u32[]{:S(2)}, u32[]{:S(2)}) collective-permute-start(bf16[128,512]{1,0:T(8,128)(2,1)S(1)} %get-tuple-element.57), channel_id=1, source_target_pairs={{16,0},{20,4},{24,8},{28,12},{17,1},{21,5},{25,9},{29,13},{18,2},{... | collective-permute-start | bytes 393224 | tf_op jit(solution)/shard_map/ppermute | solution.py:449
  112.0 20.7 %collective-permute-start.17 = (bf16[40,512]{1,0:T(8,128)(2,1)S(1)}, bf16[40,512]{1,0:T(8,128)(2,1)S(1)}, u32[]{:S(2)}, u32[]{:S(2)}) collective-permute-start(bf16[40,512]{1,0:T(8,128)(2,1)S(1)} %get-tuple-element.63), channel_id=1, source_target_pairs={{0,1},{1,0},{2,3},{3,2},{4,5},{5,4},{6,7},{7,6},{8,9},{9,8},{10,11... | collective-permute-start | bytes 122888 | tf_op jit(solution)/shard_map/ppermute | solution.py:433
  112.6 20.2 %collective-permute-start.18 = (bf16[40,512]{1,0:T(8,128)(2,1)S(1)}, bf16[40,512]{1,0:T(8,128)(2,1)S(1)}, u32[]{:S(2)}, u32[]{:S(2)}) collective-permute-start(bf16[40,512]{1,0:T(8,128)(2,1)S(1)} %get-tuple-element.64), channel_id=1, source_target_pairs={{0,2},{1,3},{2,0},{3,1},{4,6},{5,7},{6,4},{7,5},{8,10},{9,11},{10,... | collective-permute-start | bytes 122888 | tf_op jit(solution)/shard_map/ppermute | solution.py:433
  115.2 17.6 %collective-permute-start.19 = (bf16[40,512]{1,0:T(8,128)(2,1)S(1)}, bf16[40,512]{1,0:T(8,128)(2,1)S(1)}, u32[]{:S(2)}, u32[]{:S(2)}) collective-permute-start(bf16[40,512]{1,0:T(8,128)(2,1)S(1)} %get-tuple-element.65), channel_id=1, source_target_pairs={{0,3},{1,2},{2,1},{3,0},{4,7},{5,6},{6,5},{7,4},{8,11},{9,10},{10,... | collective-permute-start | bytes 122888 | tf_op jit(solution)/shard_map/ppermute | solution.py:433

commit v10 on v8

--- a/solution.py
+++ b/solution.py
@@ -11,7 +11,9 @@
 HD = 128
 CORES = 2
 FAR = 4
-CHUNK = 1280
+CHUNK = 256
+LONGER = 640
+SAFE_SCORE = 40.0
 TILE = 64
 MOST_SCORES = 2560 * 256
 NEG = -1e30
@@ -125,7 +127,7 @@
 def attention_kernel(
     halves, lengths, q_ref, do_ref, sent_ref, got_ref, own_ref, far_ref,
     o_ref, dq_ref, kept_ref, back_ref,
-    bias, keys, values, keys_t, values_t, s_bufs, g_bufs, p_bufs, d_bufs, top_bufs, inv_bufs,
+    bias, keys, values, keys_t, values_t, s_buf, p_bufs, d_bufs, inv_bufs,
     q_ts, cot_ts, q_ns, cot_ns, dk, dv,
 ):
     kv_heads, total_keys = keys.shape[0], keys.shape[1]
@@ -138,8 +140,9 @@
     score_scale = 1.0 / math.sqrt(HD)
     exp_scale = score_scale * math.log2(math.e)
     resp_at = [prompt_len + i * tokens for i in range(6)]
-    tiles = [slice(at, at + TILE) for at in range(0, total_keys, TILE)]
     chunks = [slice(at, at + CHUNK) for at in range(0, total_keys, CHUNK)]
+    longer = [slice(at, at + LONGER) for at in range(0, total_keys, LONGER)]
+    cuts = [slice(at, at + total_keys // 2) for at in (0, total_keys // 2)]
 
     def place_of(which, step):
         head = step * 2 + which if halves == 1 else step
@@ -156,93 +159,127 @@
     def folded(x):
         return x.reshape(x.shape[0] // 8, 8, rows)
 
-    def ahead(which, step):
+    def within(at):
+        return [slice(start, start + TILE) for start in range(at.start, at.stop, TILE)]
+
+    def weigh(which, step, fast):
         kv = kv_of(step)
-        where = place_of(which, jnp.minimum(step, steps - 1))
+        where = place_of(which, step)
+        state = {"sum": jnp.zeros((8, rows), F32)}
 
         def lift():
             q_ts[which] = q_ref[where].T
             cot_ts[which] = do_ref[where].T
 
-        def scores(at):
-            whole_s = dot(keys[kv, at], q_ts[which])
-            top = None
-            for start in range(at.start, at.stop, TILE):
-                s = whole_s[start - at.start : start - at.start + TILE]
-                if start >= prompt_len:
-                    s = s + bias_at(which, start, TILE)
-                s_bufs[which, start : start + TILE] = s
-                part = jnp.max(folded(s), axis=0)
-                top = part if top is None else jnp.maximum(top, part)
-            if at.start == 0:
-                top_bufs[which] = top
-            else:
-                top_bufs[which] = jnp.maximum(top_bufs[which], top)
-
-        def grads(at):
-            g_bufs[which, at] = dot(values[kv, at], cot_ts[which])
-
-        return [lift] + [functools.partial(f, at) for at in chunks for f in (scores, grads)]
-
-    def behind(which, step):
+        def masked(s, at, tile):
+            s = s[tile.start - at.start : tile.stop - at.start]
+            return s if tile.start < prompt_len else s + bias_at(which, tile.start, TILE)
+
+        def put(tile, p):
+            state["sum"] = state["sum"] + jnp.sum(folded(p), axis=0)
+            p_bufs[which, tile] = p.astype(BF16)
+
+        def direct(at):
+            s = dot(keys[kv, at], q_ts[which])
+            for tile in within(at):
+                put(tile, jnp.exp2(masked(s, at, tile) * exp_scale))
+
+        def highest(at):
+            s = dot(keys[kv, at], q_ts[which])
+            for tile in within(at):
+                part = masked(s, at, tile)
+                s_buf[tile] = part
+                top = jnp.max(folded(part), axis=0)
+                state["top"] = jnp.maximum(state["top"], top) if "top" in state else top
+
+        def settle():
+            state["top"] = jnp.max(state["top"], axis=0, keepdims=True) * exp_scale
+
+        def reduced(at):
+            for tile in within(at):
+                put(tile, jnp.exp2(s_buf[tile] * exp_scale - state["top"]))
+
+        def finish():
+            inverse = 1.0 / jnp.sum(state["sum"], axis=0, keepdims=True)
+            inv_bufs[which] = jnp.broadcast_to(inverse, (8, rows))
+            q_ns[which] = (q_ts[which].astype(F32) * inverse).astype(BF16).T
+            cot_ns[which] = (cot_ts[which].astype(F32) * inverse).astype(BF16).T
+
+        if fast:
+            return [lift] + [functools.partial(direct, at) for at in chunks], finish
+        work = [lift] + [functools.partial(highest, at) for at in chunks] + [settle]
+        return work + [functools.partial(reduced, at) for at in chunks], finish
+
+    def settled(which, step, state):
         kv = kv_of(step)
         where = place_of(which, jnp.maximum(step, 0))
-        cuts = [slice(at, at + total_keys // 2) for at in (0, total_keys // 2)]
-        state = {}
 
         def output(at):
             more = dot(values_t[kv, :, at], p_bufs[which, at])
             state["out"] = state["out"] + more if "out" in state else more
 
+        def put():
+            out = (state["out"] * inv_bufs[which, :1]).astype(BF16)
+            o_ref[where] = out.T
+            wide = cot_ts[which].astype(F32)
+            state["delta"] = jnp.sum(wide * out.astype(F32), axis=0, keepdims=True)
+
+        return [functools.partial(output, at) for at in cuts] + [put]
+
+    def slopes(which, step, state):
+        kv = kv_of(step)
+
+        def slope(at):
+            grads = dot(values[kv, at], cot_ts[which])
+            for tile in within(at):
+                part = grads[tile.start - at.start : tile.stop - at.start] - state["delta"]
+                d_bufs[which, tile] = p_bufs[which, tile] * part.astype(BF16)
+
+        return [functools.partial(slope, at) for at in chunks]
+
+    def value_grads(which, step):
+        kv = kv_of(step)
+
+        def value_grad(at):
+            dv[kv, at] += dot(p_bufs[which, at], cot_ns[which])
+
+        return [functools.partial(value_grad, at) for at in longer]
+
+    def key_grads(which, step):
+        kv = kv_of(step)
+
+        def key_grad(at):
+            dk[kv, at] += dot(d_bufs[which, at], q_ns[which])
+
+        return [functools.partial(key_grad, at) for at in longer]
+
+    def query_grads(which, step):
+        kv = kv_of(step)
+        where = place_of(which, jnp.maximum(step, 0))
+        state = {}
+
         def query(at):
             more = dot(keys_t[kv, :, at], d_bufs[which, at])
             state["dq"] = state["dq"] + more if "dq" in state else more
 
-        def put_output():
-            o_ref[where] = (state["out"] * inv_bufs[which, :1]).astype(BF16).T
-
-        def put_query():
+        def put():
             dq = state["dq"] * (inv_bufs[which, :1] * score_scale)
             dq_ref[where] = dq.astype(BF16).T
 
-        def value_grad(at):
-            dv[kv, at] += dot(p_bufs[which, at], cot_ns[which])
-
-        def key_grad(at):
-            dk[kv, at] += dot(d_bufs[which, at], q_ns[which])
-
-        work = [functools.partial(f, at) for at in chunks for f in (value_grad, key_grad)]
-        first = [functools.partial(output, at) for at in cuts] + [put_output]
-        second = [functools.partial(query, at) for at in cuts] + [put_query]
-        return first + work[: len(work) // 2] + second + work[len(work) // 2 :]
-
-    def weigh(which):
+        return [functools.partial(query, at) for at in cuts] + [put]
+
+    def slot(which, step, fast):
+        before, before_step = 1 - which, step - 1 + which
         state = {}
-
-        def settle():
-            state["top"] = jnp.max(top_bufs[which], axis=0, keepdims=True) * exp_scale
-            state["sum"] = jnp.zeros((8, rows), F32)
-            state["dot"] = jnp.zeros((8, rows), F32)
-
-        def weights(at):
-            p = jnp.exp2(s_bufs[which, at] * exp_scale - state["top"])
-            state["sum"] = state["sum"] + jnp.sum(folded(p), axis=0)
-            state["dot"] = state["dot"] + jnp.sum(folded(p * g_bufs[which, at]), axis=0)
-            p_bufs[which, at] = p.astype(BF16)
-
-        def finish():
-            inverse = 1.0 / jnp.sum(state["sum"], axis=0, keepdims=True)
-            state["delta"] = jnp.sum(state["dot"], axis=0, keepdims=True) * inverse
-            inv_bufs[which] = jnp.broadcast_to(inverse, (8, rows))
-            q_ns[which] = (q_ts[which].astype(F32) * inverse).astype(BF16).T
-            cot_ns[which] = (cot_ts[which].astype(F32) * inverse).astype(BF16).T
-
-        def slopes(at):
-            slope = (g_bufs[which, at] - state["delta"]).astype(BF16)
-            d_bufs[which, at] = p_bufs[which, at] * slope
-
-        work = [settle] + [functools.partial(weights, at) for at in tiles] + [finish]
-        return work + [functools.partial(slopes, at) for at in tiles]
+        work, finish = weigh(which, step, fast)
+        late = key_grads(which, step - 1)
+        first = settled(before, before_step, state) + query_grads(which, step - 1)
+        together(work, first + late[: len(late) // 2])
+        together(
+            slopes(before, before_step, state),
+            late[len(late) // 2 :] + value_grads(before, before_step),
+        )
+        finish()
 
     def together(vector, matrix):
         done = 0
@@ -251,11 +288,6 @@
             while done * len(vector) < (i + 1) * len(matrix):
                 matrix[done]()
                 done += 1
-
-    def mixed(first, second):
-        return [work for pair in zip(first, second) for work in pair] + (
-            first[len(second) :] + second[len(first) :]
-        )
 
     place = lax.axis_index("seq")
     core = lax.rem(place, CORES)
@@ -295,18 +327,38 @@
             values_t[n, :, at : at + size] = v_rows.T
     dk[...] = jnp.zeros_like(dk)
     dv[...] = jnp.zeros_like(dv)
-    for ref in (p_bufs, d_bufs, inv_bufs, q_ns, cot_ns):
-        ref[1] = jnp.zeros(ref.shape[1:], ref.dtype)
-    for work in ahead(0, 0):
+    p_bufs[1] = jnp.zeros(p_bufs.shape[1:], BF16)
+    cot_ts[1] = jnp.zeros(cot_ts.shape[1:], BF16)
+    for ref in (d_bufs, inv_bufs, q_ns, cot_ns):
+        ref[...] = jnp.zeros_like(ref)
+    q_most = jnp.zeros((tokens, 1), F32)
+    for at in range(0, q_cols, HD):
+        part = q_ref[:, at : at + HD].astype(F32)
+        q_most = jnp.maximum(q_most, jnp.sum(part * part, axis=1, keepdims=True))
+    k_most = jnp.zeros((CHUNK, 1), F32)
+    for n in range(kv_heads):
+        for at in chunks:
+            part = keys[n, at].astype(F32)
+            k_most = jnp.maximum(k_most, jnp.sum(part * part, axis=1, keepdims=True))
+    most = jnp.max(q_most) * jnp.max(k_most) * (score_scale * score_scale)
+    small = most <= SAFE_SCORE * SAFE_SCORE
+    def run(fast):
+        def pair(step, carry):
+            slot(0, step, fast)
+            slot(1, step, fast)
+            return carry
+
+        lax.fori_loop(0, steps, pair, 0)
+
+    pl.when(small)(functools.partial(run, True))
+    pl.when(jnp.logical_not(small))(functools.partial(run, False))
+    state = {}
+    for work in settled(1, steps - 1, state) + query_grads(0, steps - 1):
         work()
-
-    def pair(step, carry):
-        together(weigh(0), mixed(behind(1, step - 1), ahead(1, step)))
-        together(weigh(1), mixed(behind(0, step), ahead(0, step + 1)))
-        return carry
-
-    lax.fori_loop(0, steps, pair, 0)
-    for work in behind(1, steps - 1):
+    together(
+        slopes(1, steps - 1, state), key_grads(0, steps - 1) + value_grads(1, steps - 1)
+    )
+    for work in key_grads(1, steps - 1) + query_grads(1, steps - 1):
         work()
     for n in range(kv_heads):
         k_cols = slice(2 * n * HD, (2 * n + 1) * HD)
@@ -350,11 +402,9 @@
             pltpu.VMEM((kv_heads, total_keys, HD), BF16),
             pltpu.VMEM((kv_heads, HD, total_keys), BF16),
             pltpu.VMEM((kv_heads, HD, total_keys), BF16),
-            pltpu.VMEM((2, total_keys, rows), F32),
-            pltpu.VMEM((2, total_keys, rows), F32),
+            pltpu.VMEM((total_keys, rows), F32),
             pltpu.VMEM((2, total_keys, rows), BF16),
             pltpu.VMEM((2, total_keys, rows), BF16),
-            pltpu.VMEM((2, 8, rows), F32),
             pltpu.VMEM((2, 8, rows), F32),
             pltpu.VMEM((2, HD, rows), BF16),
             pltpu.VMEM((2, HD, rows), BF16),

time: 107 us -> 105 us (0.981)
  Pallas kernels: 48.9 us -> 47.6 us
    pallas_call x1, Pallas kernels: 45.9 us -> 44.5 us  [attention(): pl.pallas_call(functools.partial(attention_kernel, halves), in_specs=[pl....]
where the time goes in v10:
time: 105 us
  Pallas kernels  47.6 us (45%)
  starting transfers between devices  36.3 us (35%)
  waiting for transfers between devices  19.4 us (18%)
    pallas_call x1, Pallas kernels, attention(): pl.pallas_call(functools.partial(attention_kernel, halves), in_specs=[pl....  44.5 us
    ppermute x6, starting transfers between devices, shift_chips(): lax.ppermute(array, 'seq', [(i, i + by) for i in range(devices) if 0 <= i...  18.3 us
    ppermute x6, starting transfers between devices, swap_chips(): lax.ppermute(array, 'seq', [(i, i ^ by * CORES) for i in range(devices)])  8.93 us
    ppermute x6, starting transfers between devices, swap_heads(): return lax.ppermute(array, 'head', [(i, i ^ by) for i in range(devices)])  8.88 us
    ppermute x6, waiting for transfers between devices, swap_heads(): return lax.ppermute(array, 'head', [(i, i ^ by) for i in range(devices)])  7.4 us
    ppermute x6, waiting for transfers between devices, swap_chips(): lax.ppermute(array, 'seq', [(i, i ^ by * CORES) for i in range(devices)])  6.44 us
    ppermute x2, waiting for transfers between devices, swap_cores(): return lax.ppermute(array, 'seq', [(i, i ^ 1) for i in range(devices)])  5.55 us
  transfers between devices with their start and end apart: 20, of which 8 were waited for; matrix products, arithmetic and copies ran while one was open for 1% of the time, Pallas kernels for 0%

profile of v10, /device:TPU:6, one launch (start us, length us, event | category | flops | bytes accessed | tf_op | source)
XLA Modules:
  0.0 105.0 jit_solution(14044541634149729497)
XLA Ops:
  0.6 1.9 %pack.1 = (bf16[40,512]{1,0:T(8,128)(2,1)}, bf16[40,512]{1,0:T(8,128)(2,1)}, bf16[40,512]{1,0:T(8,128)(2,1)}, bf16[40,512]{1,0:T(8,128)(2,1)}, bf16[256,512]{1,0:T(8,128)(2,1)}) custom-call(bf16[40,1024]{1,0:T(8,128)(2,1)} %pk_ref.1, bf16[40,1024]{1,0:T(8,128)(2,1)} %pv_ref.1, bf16[256,256]{1,0:T(8,128)(2,1)} %rk_ref.1, bf16[256,256]{1,0:T(8,128)(2,1)} %rv_ref.1), custom_call_target="tpu_custom_call" | custom-call | tf_op jit(solution)/shard_map/pack/pallas_call | solution.py:66
  2.5 1.4 %collective-permute-start.4 = (bf16[256,512]{1,0:T(8,128)(2,1)}, bf16[256,512]{1,0:T(8,128)(2,1)S(1)}, u32[]{:S(2)}, u32[]{:S(2)}) collective-permute-start(bf16[256,512]{1,0:T(8,128)(2,1)} %get-tuple-element.41.own_ref), channel_id=1, source_target_pairs={{0,16},{4,20},{8,24},{12,28},{1,17},{5,21},{9,25},{13,29},{2,18},{... | collective-permute-start | bytes 786440 | tf_op jit(solution)/shard_map/ppermute | solution.py:442
  3.9 1.3 %collective-permute-start.3 = (bf16[256,512]{1,0:T(8,128)(2,1)}, bf16[256,512]{1,0:T(8,128)(2,1)S(1)}, u32[]{:S(2)}, u32[]{:S(2)}) collective-permute-start(bf16[256,512]{1,0:T(8,128)(2,1)} %get-tuple-element.41.own_ref), channel_id=1, source_target_pairs={{0,8},{4,12},{8,16},{12,20},{16,24},{20,28},{1,9},{5,13},{9,17},{1... | collective-permute-start | bytes 786440 | tf_op jit(solution)/shard_map/ppermute | solution.py:442
  5.2 1.6 %collective-permute-start = (bf16[40,512]{1,0:T(8,128)(2,1)}, bf16[40,512]{1,0:T(8,128)(2,1)S(1)}, u32[]{:S(2)}, u32[]{:S(2)}) collective-permute-start(bf16[40,512]{1,0:T(8,128)(2,1)} %get-tuple-element.38), channel_id=1, source_target_pairs={{0,1},{1,0},{2,3},{3,2},{4,5},{5,4},{6,7},{7,6},{8,9},{9,8},{10,11... | collective-permute-start | bytes 122888 | tf_op jit(solution)/shard_map/ppermute | solution.py:426
  6.9 2.6 %collective-permute-start.1 = (bf16[40,512]{1,0:T(8,128)(2,1)}, bf16[40,512]{1,0:T(8,128)(2,1)S(1)}, u32[]{:S(2)}, u32[]{:S(2)}) collective-permute-start(bf16[40,512]{1,0:T(8,128)(2,1)} %get-tuple-element.39), channel_id=1, source_target_pairs={{0,2},{1,3},{2,0},{3,1},{4,6},{5,7},{6,4},{7,5},{8,10},{9,11},{10,... | collective-permute-start | bytes 122888 | tf_op jit(solution)/shard_map/ppermute | solution.py:426
  9.5 0.2 collective-permute-start.2
  9.7 0.8 constant_dynamic-update-slice_fusion.3
  10.5 2.3 %collective-permute-done.1 = bf16[40,512]{1,0:T(8,128)(2,1)S(1)} collective-permute-done((bf16[40,512]{1,0:T(8,128)(2,1)}, bf16[40,512]{1,0:T(8,128)(2,1)S(1)}, u32[]{:S(2)}, u32[]{:S(2)}) %collective-permute-start.1) | collective-permute-done | bytes 40992 | tf_op jit(solution)/shard_map/ppermute | solution.py:426
  12.8 2.7 %collective-permute-done.2 = bf16[40,512]{1,0:T(8,128)(2,1)S(1)} collective-permute-done((bf16[40,512]{1,0:T(8,128)(2,1)}, bf16[40,512]{1,0:T(8,128)(2,1)S(1)}, u32[]{:S(2)}, u32[]{:S(2)}) %collective-permute-start.2) | collective-permute-done | bytes 40992 | tf_op jit(solution)/shard_map/ppermute | solution.py:426
  15.6 3.5 %collective-permute-start.5 = (bf16[160,512]{1,0:T(8,128)(2,1)S(1)}, bf16[160,512]{1,0:T(8,128)(2,1)S(1)}, u32[]{:S(2)}, u32[]{:S(2)}) collective-permute-start(bf16[160,512]{1,0:T(8,128)(2,1)S(1)} %get-tuple-element.68), channel_id=1, source_target_pairs={{0,8},{4,12},{8,0},{12,4},{16,24},{20,28},{24,16},{28,20},{1,9},{5... | collective-permute-start | bytes 491528 | tf_op jit(solution)/shard_map/ppermute | solution.py:431
  19.1 1.9 %collective-permute-start.6 = (bf16[160,512]{1,0:T(8,128)(2,1)S(1)}, bf16[160,512]{1,0:T(8,128)(2,1)S(1)}, u32[]{:S(2)}, u32[]{:S(2)}) collective-permute-start(bf16[160,512]{1,0:T(8,128)(2,1)S(1)} %get-tuple-element.68), channel_id=1, source_target_pairs={{0,16},{4,20},{8,24},{12,28},{16,0},{20,4},{24,8},{28,12},{1,17},{... | collective-permute-start | bytes 491528 | tf_op jit(solution)/shard_map/ppermute | solution.py:431
  20.9 2.5 %collective-permute-done.5 = bf16[160,512]{1,0:T(8,128)(2,1)S(1)} collective-permute-done((bf16[160,512]{1,0:T(8,128)(2,1)S(1)}, bf16[160,512]{1,0:T(8,128)(2,1)S(1)}, u32[]{:S(2)}, u32[]{:S(2)}) %collective-permute-start.5) | collective-permute-done | bytes 163872 | tf_op jit(solution)/shard_map/ppermute | solution.py:431
  23.4 3.9 %collective-permute-done.6 = bf16[160,512]{1,0:T(8,128)(2,1)S(1)} collective-permute-done((bf16[160,512]{1,0:T(8,128)(2,1)S(1)}, bf16[160,512]{1,0:T(8,128)(2,1)S(1)}, u32[]{:S(2)}, u32[]{:S(2)}) %collective-permute-start.6) | collective-permute-done | bytes 163872 | tf_op jit(solution)/shard_map/ppermute | solution.py:431
  27.5 0.1 collective-permute-start.8
  27.6 2.8 %collective-permute-done.8.got_ref = bf16[1152,512]{1,0:T(8,128)(2,1)S(1)} collective-permute-done((bf16[1152,512]{1,0:T(8,128)(2,1)S(1)}, bf16[1152,512]{1,0:T(8,128)(2,1)S(1)}, u32[]{:S(2)}, u32[]{:S(2)}) %collective-permute-start.8) | collective-permute-done | bytes 1179680 | tf_op jit(solution)/shard_map/ppermute | solution.py:436
  30.5 44.5 %attention.1 = (bf16[256,2048]{1,0:T(8,128)(2,1)}, bf16[256,2048]{1,0:T(8,128)(2,1)}, f32[1408,512]{1,0:T(8,128)S(1)}, bf16[1152,512]{1,0:T(8,128)(2,1)S(1)}) custom-call(s32[8]{0:T(128)S(1)} %copy-done.3, bf16[256,2048]{1,0:T(8,128)(2,1)S(1)} %copy-done.1, bf16[256,2048]{1,0:T(8,128)(2,1)S(1)} %copy-done.2, ...), custom_call_target="tpu_custom_call" | custom-call | flops 16106127360 | bytes 4194304 | tf_op jit(solution)/shard_map/attention/pallas_call | solution.py:389
  75.0 0.1 collective-permute-start.9
  75.1 2.7 %collective-permute-done.9.got_ref = bf16[1152,512]{1,0:T(8,128)(2,1)S(1)} collective-permute-done((bf16[1152,512]{1,0:T(8,128)(2,1)S(1)}, bf16[1152,512]{1,0:T(8,128)(2,1)S(1)}, u32[]{:S(2)}, u32[]{:S(2)}) %collective-permute-start.9) | collective-permute-done | bytes 1179680 | tf_op jit(solution)/shard_map/ppermute | solution.py:436
  77.8 0.3 merge.1
  78.1 0.4 collective-permute-start.14
  78.5 1.6 %collective-permute-start.15 = (bf16[160,512]{1,0:T(8,128)(2,1)S(1)}, bf16[160,512]{1,0:T(8,128)(2,1)S(1)}, u32[]{:S(2)}, u32[]{:S(2)}) collective-permute-start(bf16[160,512]{1,0:T(8,128)(2,1)S(1)} %get-tuple-element.58), channel_id=1, source_target_pairs={{0,16},{4,20},{8,24},{12,28},{16,0},{20,4},{24,8},{28,12},{1,17},{... | collective-permute-start | bytes 491528 | tf_op jit(solution)/shard_map/ppermute | solution.py:431
  80.1 1.5 %collective-permute-start.16 = (bf16[160,512]{1,0:T(8,128)(2,1)S(1)}, bf16[160,512]{1,0:T(8,128)(2,1)S(1)}, u32[]{:S(2)}, u32[]{:S(2)}) collective-permute-start(bf16[160,512]{1,0:T(8,128)(2,1)S(1)} %get-tuple-element.59), channel_id=1, source_target_pairs={{0,24},{4,28},{8,16},{12,20},{16,8},{20,12},{24,0},{28,4},{1,25},{... | collective-permute-start | bytes 491528 | tf_op jit(solution)/shard_map/ppermute | solution.py:431
  81.6 2.3 %collective-permute-start.10 = (bf16[128,512]{1,0:T(8,128)(2,1)S(1)}, bf16[128,512]{1,0:T(8,128)(2,1)S(1)}, u32[]{:S(2)}, u32[]{:S(2)}) collective-permute-start(bf16[128,512]{1,0:T(8,128)(2,1)S(1)} %get-tuple-element.52), channel_id=1, source_target_pairs={{8,0},{12,4},{16,8},{20,12},{24,16},{28,20},{9,1},{13,5},{17,9},{2... | collective-permute-start | bytes 393224 | tf_op jit(solution)/shard_map/ppermute | solution.py:442
  83.9 4.7 %collective-permute-start.11 = (bf16[128,512]{1,0:T(8,128)(2,1)S(1)}, bf16[128,512]{1,0:T(8,128)(2,1)S(1)}, u32[]{:S(2)}, u32[]{:S(2)}) collective-permute-start(bf16[128,512]{1,0:T(8,128)(2,1)S(1)} %get-tuple-element.53), channel_id=1, source_target_pairs={{8,0},{12,4},{16,8},{20,12},{24,16},{28,20},{9,1},{13,5},{17,9},{2... | collective-permute-start | bytes 393224 | tf_op jit(solution)/shard_map/ppermute | solution.py:442
  88.6 1.3 %collective-permute-start.12 = (bf16[128,512]{1,0:T(8,128)(2,1)S(1)}, bf16[128,512]{1,0:T(8,128)(2,1)S(1)}, u32[]{:S(2)}, u32[]{:S(2)}) collective-permute-start(bf16[128,512]{1,0:T(8,128)(2,1)S(1)} %get-tuple-element.54), channel_id=1, source_target_pairs={{16,0},{20,4},{24,8},{28,12},{17,1},{21,5},{25,9},{29,13},{18,2},{... | collective-permute-start | bytes 393224 | tf_op jit(solution)/shard_map/ppermute | solution.py:442
  89.9 7.3 %collective-permute-start.13 = (bf16[128,512]{1,0:T(8,128)(2,1)S(1)}, bf16[128,512]{1,0:T(8,128)(2,1)S(1)}, u32[]{:S(2)}, u32[]{:S(2)}) collective-permute-start(bf16[128,512]{1,0:T(8,128)(2,1)S(1)} %get-tuple-element.55), channel_id=1, source_target_pairs={{16,0},{20,4},{24,8},{28,12},{17,1},{21,5},{25,9},{29,13},{18,2},{... | collective-permute-start | bytes 393224 | tf_op jit(solution)/shard_map/ppermute | solution.py:442
  97.3 0.1 sum_chips.1
  97.4 0.1 collective-permute-start.18
  97.5 4.3 %collective-permute-start.19 = (bf16[40,512]{1,0:T(8,128)(2,1)S(1)}, bf16[40,512]{1,0:T(8,128)(2,1)S(1)}, u32[]{:S(2)}, u32[]{:S(2)}) collective-permute-start(bf16[40,512]{1,0:T(8,128)(2,1)S(1)} %get-tuple-element.63), channel_id=1, source_target_pairs={{0,3},{1,2},{2,1},{3,0},{4,7},{5,6},{6,5},{7,4},{8,11},{9,10},{10,... | collective-permute-start | bytes 122888 | tf_op jit(solution)/shard_map/ppermute | solution.py:426
  101.8 0.6 collective-permute-done.18.refs_6_
  102.4 1.8 %collective-permute-done.19.refs_7_ = bf16[40,512]{1,0:T(8,128)(2,1)S(1)} collective-permute-done((bf16[40,512]{1,0:T(8,128)(2,1)S(1)}, bf16[40,512]{1,0:T(8,128)(2,1)S(1)}, u32[]{:S(2)}, u32[]{:S(2)}) %collective-permute-start.19) | collective-permute-done | bytes 40992 | tf_op jit(solution)/shard_map/ppermute | solution.py:426
  104.2 0.8 finish.1
  (30 shorter events, 0.3 us)
Async XLA Ops:
  2.5 24.9 %copy-start = (bf16[256,512]{1,0:T(8,128)(2,1)S(1)}, bf16[256,512]{1,0:T(8,128)(2,1)}, u32[]{:S(2)}) copy-start(bf16[256,512]{1,0:T(8,128)(2,1)} %get-tuple-element.41.own_ref) | copy-start | bytes 786436
  2.5 13.0 %collective-permute-start.4 = (bf16[256,512]{1,0:T(8,128)(2,1)}, bf16[256,512]{1,0:T(8,128)(2,1)S(1)}, u32[]{:S(2)}, u32[]{:S(2)}) collective-permute-start(bf16[256,512]{1,0:T(8,128)(2,1)} %get-tuple-element.41.own_ref), channel_id=1, source_target_pairs={{0,16},{4,20},{8,24},{12,28},{1,17},{5,21},{9,25},{13,29},{2,18},{... | collective-permute-start | bytes 786440 | tf_op jit(solution)/shard_map/ppermute | solution.py:442
  3.9 11.5 %collective-permute-start.3 = (bf16[256,512]{1,0:T(8,128)(2,1)}, bf16[256,512]{1,0:T(8,128)(2,1)S(1)}, u32[]{:S(2)}, u32[]{:S(2)}) collective-permute-start(bf16[256,512]{1,0:T(8,128)(2,1)} %get-tuple-element.41.own_ref), channel_id=1, source_target_pairs={{0,8},{4,12},{8,16},{12,20},{16,24},{20,28},{1,9},{5,13},{9,17},{1... | collective-permute-start | bytes 786440 | tf_op jit(solution)/shard_map/ppermute | solution.py:442
  5.2 5.2 %collective-permute-start = (bf16[40,512]{1,0:T(8,128)(2,1)}, bf16[40,512]{1,0:T(8,128)(2,1)S(1)}, u32[]{:S(2)}, u32[]{:S(2)}) collective-permute-start(bf16[40,512]{1,0:T(8,128)(2,1)} %get-tuple-element.38), channel_id=1, source_target_pairs={{0,1},{1,0},{2,3},{3,2},{4,5},{5,4},{6,7},{7,6},{8,9},{9,8},{10,11... | collective-permute-start | bytes 122888 | tf_op jit(solution)/shard_map/ppermute | solution.py:426
  6.9 5.9 %collective-permute-start.1 = (bf16[40,512]{1,0:T(8,128)(2,1)}, bf16[40,512]{1,0:T(8,128)(2,1)S(1)}, u32[]{:S(2)}, u32[]{:S(2)}) collective-permute-start(bf16[40,512]{1,0:T(8,128)(2,1)} %get-tuple-element.39), channel_id=1, source_target_pairs={{0,2},{1,3},{2,0},{3,1},{4,6},{5,7},{6,4},{7,5},{8,10},{9,11},{10,... | collective-permute-start | bytes 122888 | tf_op jit(solution)/shard_map/ppermute | solution.py:426
  9.5 6.0 %collective-permute-start.2 = (bf16[40,512]{1,0:T(8,128)(2,1)}, bf16[40,512]{1,0:T(8,128)(2,1)S(1)}, u32[]{:S(2)}, u32[]{:S(2)}) collective-permute-start(bf16[40,512]{1,0:T(8,128)(2,1)} %get-tuple-element.40), channel_id=1, source_target_pairs={{0,3},{1,2},{2,1},{3,0},{4,7},{5,6},{6,5},{7,4},{8,11},{9,10},{10,... | collective-permute-start | bytes 122888 | tf_op jit(solution)/shard_map/ppermute | solution.py:426
  15.5 14.9 %copy-start.1 = (bf16[256,2048]{1,0:T(8,128)(2,1)S(1)}, bf16[256,2048]{1,0:T(8,128)(2,1)}, u32[]{:S(2)}) copy-start(bf16[256,2048]{1,0:T(8,128)(2,1)} %q_ref.1) | copy-start | bytes 3145732
  15.5 14.9 %copy-start.3 = (s32[8]{0:T(128)S(1)}, s32[8]{0:T(128)}, u32[]{:S(2)}) copy-start(s32[8]{0:T(128)} %lengths.1) | copy-start | bytes 100
  15.6 7.9 %collective-permute-start.5 = (bf16[160,512]{1,0:T(8,128)(2,1)S(1)}, bf16[160,512]{1,0:T(8,128)(2,1)S(1)}, u32[]{:S(2)}, u32[]{:S(2)}) collective-permute-start(bf16[160,512]{1,0:T(8,128)(2,1)S(1)} %get-tuple-element.68), channel_id=1, source_target_pairs={{0,8},{4,12},{8,0},{12,4},{16,24},{20,28},{24,16},{28,20},{1,9},{5... | collective-permute-start | bytes 491528 | tf_op jit(solution)/shard_map/ppermute | solution.py:431
  19.1 8.3 %collective-permute-start.6 = (bf16[160,512]{1,0:T(8,128)(2,1)S(1)}, bf16[160,512]{1,0:T(8,128)(2,1)S(1)}, u32[]{:S(2)}, u32[]{:S(2)}) collective-permute-start(bf16[160,512]{1,0:T(8,128)(2,1)S(1)} %get-tuple-element.68), channel_id=1, source_target_pairs={{0,16},{4,20},{8,24},{12,28},{16,0},{20,4},{24,8},{28,12},{1,17},{... | collective-permute-start | bytes 491528 | tf_op jit(solution)/shard_map/ppermute | solution.py:431
  20.9 9.5 %copy-start.2 = (bf16[256,2048]{1,0:T(8,128)(2,1)S(1)}, bf16[256,2048]{1,0:T(8,128)(2,1)}, u32[]{:S(2)}) copy-start(bf16[256,2048]{1,0:T(8,128)(2,1)} %do_ref.1) | copy-start | bytes 3145732
  20.9 6.5 %collective-permute-start.7 = (bf16[160,512]{1,0:T(8,128)(2,1)S(1)}, bf16[160,512]{1,0:T(8,128)(2,1)S(1)}, u32[]{:S(2)}, u32[]{:S(2)}) collective-permute-start(bf16[160,512]{1,0:T(8,128)(2,1)S(1)} %get-tuple-element.68), channel_id=1, source_target_pairs={{0,24},{4,28},{8,16},{12,20},{16,8},{20,12},{24,0},{28,4},{1,25},{... | collective-permute-start | bytes 491528 | tf_op jit(solution)/shard_map/ppermute | solution.py:431
  27.5 2.9 %collective-permute-start.8 = (bf16[1152,512]{1,0:T(8,128)(2,1)S(1)}, bf16[1152,512]{1,0:T(8,128)(2,1)S(1)}, u32[]{:S(2)}, u32[]{:S(2)}) collective-permute-start(bf16[1152,512]{1,0:T(8,128)(2,1)S(1)} %select_dynamic-update-slice_fusion.sent_ref), channel_id=1, source_target_pairs={{0,4},{4,0},{8,12},{12,8},{16,20},{20,16},{24,28},{28,24},{1,5},{5... | collective-permute-start | bytes 3538952 | tf_op jit(solution)/shard_map/ppermute | solution.py:436
  75.0 2.8 %collective-permute-start.9 = (bf16[1152,512]{1,0:T(8,128)(2,1)S(1)}, bf16[1152,512]{1,0:T(8,128)(2,1)S(1)}, u32[]{:S(2)}, u32[]{:S(2)}) collective-permute-start(bf16[1152,512]{1,0:T(8,128)(2,1)S(1)} %get-tuple-element.50), channel_id=1, source_target_pairs={{0,4},{4,0},{8,12},{12,8},{16,20},{20,16},{24,28},{28,24},{1,5},{5... | collective-permute-start | bytes 3538952 | tf_op jit(solution)/shard_map/ppermute | solution.py:436
  78.1 10.5 %collective-permute-start.14 = (bf16[160,512]{1,0:T(8,128)(2,1)S(1)}, bf16[160,512]{1,0:T(8,128)(2,1)S(1)}, u32[]{:S(2)}, u32[]{:S(2)}) collective-permute-start(bf16[160,512]{1,0:T(8,128)(2,1)S(1)} %get-tuple-element.57), channel_id=1, source_target_pairs={{0,8},{4,12},{8,0},{12,4},{16,24},{20,28},{24,16},{28,20},{1,9},{5... | collective-permute-start | bytes 491528 | tf_op jit(solution)/shard_map/ppermute | solution.py:431
  78.5 11.4 %collective-permute-start.15 = (bf16[160,512]{1,0:T(8,128)(2,1)S(1)}, bf16[160,512]{1,0:T(8,128)(2,1)S(1)}, u32[]{:S(2)}, u32[]{:S(2)}) collective-permute-start(bf16[160,512]{1,0:T(8,128)(2,1)S(1)} %get-tuple-element.58), channel_id=1, source_target_pairs={{0,16},{4,20},{8,24},{12,28},{16,0},{20,4},{24,8},{28,12},{1,17},{... | collective-permute-start | bytes 491528 | tf_op jit(solution)/shard_map/ppermute | solution.py:431
  80.1 17.2 %collective-permute-start.16 = (bf16[160,512]{1,0:T(8,128)(2,1)S(1)}, bf16[160,512]{1,0:T(8,128)(2,1)S(1)}, u32[]{:S(2)}, u32[]{:S(2)}) collective-permute-start(bf16[160,512]{1,0:T(8,128)(2,1)S(1)} %get-tuple-element.59), channel_id=1, source_target_pairs={{0,24},{4,28},{8,16},{12,20},{16,8},{20,12},{24,0},{28,4},{1,25},{... | collective-permute-start | bytes 491528 | tf_op jit(solution)/shard_map/ppermute | solution.py:431
  81.6 15.8 %collective-permute-start.10 = (bf16[128,512]{1,0:T(8,128)(2,1)S(1)}, bf16[128,512]{1,0:T(8,128)(2,1)S(1)}, u32[]{:S(2)}, u32[]{:S(2)}) collective-permute-start(bf16[128,512]{1,0:T(8,128)(2,1)S(1)} %get-tuple-element.52), channel_id=1, source_target_pairs={{8,0},{12,4},{16,8},{20,12},{24,16},{28,20},{9,1},{13,5},{17,9},{2... | collective-permute-start | bytes 393224 | tf_op jit(solution)/shard_map/ppermute | solution.py:442
  83.9 13.6 %collective-permute-start.11 = (bf16[128,512]{1,0:T(8,128)(2,1)S(1)}, bf16[128,512]{1,0:T(8,128)(2,1)S(1)}, u32[]{:S(2)}, u32[]{:S(2)}) collective-permute-start(bf16[128,512]{1,0:T(8,128)(2,1)S(1)} %get-tuple-element.53), channel_id=1, source_target_pairs={{8,0},{12,4},{16,8},{20,12},{24,16},{28,20},{9,1},{13,5},{17,9},{2... | collective-permute-start | bytes 393224 | tf_op jit(solution)/shard_map/ppermute | solution.py:442
  88.6 13.2 %collective-permute-start.12 = (bf16[128,512]{1,0:T(8,128)(2,1)S(1)}, bf16[128,512]{1,0:T(8,128)(2,1)S(1)}, u32[]{:S(2)}, u32[]{:S(2)}) collective-permute-start(bf16[128,512]{1,0:T(8,128)(2,1)S(1)} %get-tuple-element.54), channel_id=1, source_target_pairs={{16,0},{20,4},{24,8},{28,12},{17,1},{21,5},{25,9},{29,13},{18,2},{... | collective-permute-start | bytes 393224 | tf_op jit(solution)/shard_map/ppermute | solution.py:442
  89.9 11.9 %collective-permute-start.13 = (bf16[128,512]{1,0:T(8,128)(2,1)S(1)}, bf16[128,512]{1,0:T(8,128)(2,1)S(1)}, u32[]{:S(2)}, u32[]{:S(2)}) collective-permute-start(bf16[128,512]{1,0:T(8,128)(2,1)S(1)} %get-tuple-element.55), channel_id=1, source_target_pairs={{16,0},{20,4},{24,8},{28,12},{17,1},{21,5},{25,9},{29,13},{18,2},{... | collective-permute-start | bytes 393224 | tf_op jit(solution)/shard_map/ppermute | solution.py:442
  97.3 4.5 %collective-permute-start.17 = (bf16[40,512]{1,0:T(8,128)(2,1)S(1)}, bf16[40,512]{1,0:T(8,128)(2,1)S(1)}, u32[]{:S(2)}, u32[]{:S(2)}) collective-permute-start(bf16[40,512]{1,0:T(8,128)(2,1)S(1)} %get-tuple-element.61), channel_id=1, source_target_pairs={{0,1},{1,0},{2,3},{3,2},{4,5},{5,4},{6,7},{7,6},{8,9},{9,8},{10,11... | collective-permute-start | bytes 122888 | tf_op jit(solution)/shard_map/ppermute | solution.py:426
  97.4 5.0 %collective-permute-start.18 = (bf16[40,512]{1,0:T(8,128)(2,1)S(1)}, bf16[40,512]{1,0:T(8,128)(2,1)S(1)}, u32[]{:S(2)}, u32[]{:S(2)}) collective-permute-start(bf16[40,512]{1,0:T(8,128)(2,1)S(1)} %get-tuple-element.62), channel_id=1, source_target_pairs={{0,2},{1,3},{2,0},{3,1},{4,6},{5,7},{6,4},{7,5},{8,10},{9,11},{10,... | collective-permute-start | bytes 122888 | tf_op jit(solution)/shard_map/ppermute | solution.py:426
  97.5 6.7 %collective-permute-start.19 = (bf16[40,512]{1,0:T(8,128)(2,1)S(1)}, bf16[40,512]{1,0:T(8,128)(2,1)S(1)}, u32[]{:S(2)}, u32[]{:S(2)}) collective-permute-start(bf16[40,512]{1,0:T(8,128)(2,1)S(1)} %get-tuple-element.63), channel_id=1, source_target_pairs={{0,3},{1,2},{2,1},{3,0},{4,7},{5,6},{6,5},{7,4},{8,11},{9,10},{10,... | collective-permute-start | bytes 122888 | tf_op jit(solution)/shard_map/ppermute | solution.py:426

commit v11 on v10

--- a/solution.py
+++ b/solution.py
@@ -29,10 +29,10 @@
     return [pl.BlockSpec(memory_space=pltpu.VMEM)] * count
 
 
-def local_call(kernel, name, inputs, outputs, scratch=()):
+def local_call(kernel, name, inputs, outputs, scratch=(), scalars=0):
     return pl.pallas_call(
         kernel,
-        in_specs=whole(len(inputs)),
+        in_specs=[pl.BlockSpec(memory_space=pltpu.SMEM)] * scalars + whole(len(inputs) - scalars),
         out_specs=whole(len(outputs)),
         out_shape=[jax.ShapeDtypeStruct(shape, kind) for shape, kind in outputs],
         scratch_shapes=list(scratch),
@@ -124,171 +124,8 @@
             rv_ref[at, n * HD : (n + 1) * HD] = total[:, (2 * n + 1) * HD : (2 * n + 2) * HD]
 
 
-def attention_kernel(
-    halves, lengths, q_ref, do_ref, sent_ref, got_ref, own_ref, far_ref,
-    o_ref, dq_ref, kept_ref, back_ref,
-    bias, keys, values, keys_t, values_t, s_buf, p_bufs, d_bufs, inv_bufs,
-    q_ts, cot_ts, q_ns, cot_ns, dk, dv,
-):
-    kv_heads, total_keys = keys.shape[0], keys.shape[1]
+def mask_kernel(lengths, q_ref, bias, most_ref):
     tokens, q_cols = q_ref.shape
-    rows = tokens // halves
-    prompt_len = total_keys - 5 * tokens
-    half = prompt_len // 2
-    steps = q_cols // HD * halves // 2
-    steps_per_kv = steps // kv_heads
-    score_scale = 1.0 / math.sqrt(HD)
-    exp_scale = score_scale * math.log2(math.e)
-    resp_at = [prompt_len + i * tokens for i in range(6)]
-    chunks = [slice(at, at + CHUNK) for at in range(0, total_keys, CHUNK)]
-    longer = [slice(at, at + LONGER) for at in range(0, total_keys, LONGER)]
-    cuts = [slice(at, at + total_keys // 2) for at in (0, total_keys // 2)]
-
-    def place_of(which, step):
-        head = step * 2 + which if halves == 1 else step
-        row = 0 if halves == 1 else which * rows
-        return slice(row, row + rows), pl.ds(pl.multiple_of(head * HD, HD), HD)
-
-    def kv_of(step):
-        return jnp.clip(step // steps_per_kv, 0, kv_heads - 1)
-
-    def bias_at(which, at, size):
-        row = which * rows * (halves - 1)
-        return bias[at - prompt_len : at - prompt_len + size, row : row + rows]
-
-    def folded(x):
-        return x.reshape(x.shape[0] // 8, 8, rows)
-
-    def within(at):
-        return [slice(start, start + TILE) for start in range(at.start, at.stop, TILE)]
-
-    def weigh(which, step, fast):
-        kv = kv_of(step)
-        where = place_of(which, step)
-        state = {"sum": jnp.zeros((8, rows), F32)}
-
-        def lift():
-            q_ts[which] = q_ref[where].T
-            cot_ts[which] = do_ref[where].T
-
-        def masked(s, at, tile):
-            s = s[tile.start - at.start : tile.stop - at.start]
-            return s if tile.start < prompt_len else s + bias_at(which, tile.start, TILE)
-
-        def put(tile, p):
-            state["sum"] = state["sum"] + jnp.sum(folded(p), axis=0)
-            p_bufs[which, tile] = p.astype(BF16)
-
-        def direct(at):
-            s = dot(keys[kv, at], q_ts[which])
-            for tile in within(at):
-                put(tile, jnp.exp2(masked(s, at, tile) * exp_scale))
-
-        def highest(at):
-            s = dot(keys[kv, at], q_ts[which])
-            for tile in within(at):
-                part = masked(s, at, tile)
-                s_buf[tile] = part
-                top = jnp.max(folded(part), axis=0)
-                state["top"] = jnp.maximum(state["top"], top) if "top" in state else top
-
-        def settle():
-            state["top"] = jnp.max(state["top"], axis=0, keepdims=True) * exp_scale
-
-        def reduced(at):
-            for tile in within(at):
-                put(tile, jnp.exp2(s_buf[tile] * exp_scale - state["top"]))
-
-        def finish():
-            inverse = 1.0 / jnp.sum(state["sum"], axis=0, keepdims=True)
-            inv_bufs[which] = jnp.broadcast_to(inverse, (8, rows))
-            q_ns[which] = (q_ts[which].astype(F32) * inverse).astype(BF16).T
-            cot_ns[which] = (cot_ts[which].astype(F32) * inverse).astype(BF16).T
-
-        if fast:
-            return [lift] + [functools.partial(direct, at) for at in chunks], finish
-        work = [lift] + [functools.partial(highest, at) for at in chunks] + [settle]
-        return work + [functools.partial(reduced, at) for at in chunks], finish
-
-    def settled(which, step, state):
-        kv = kv_of(step)
-        where = place_of(which, jnp.maximum(step, 0))
-
-        def output(at):
-            more = dot(values_t[kv, :, at], p_bufs[which, at])
-            state["out"] = state["out"] + more if "out" in state else more
-
-        def put():
-            out = (state["out"] * inv_bufs[which, :1]).astype(BF16)
-            o_ref[where] = out.T
-            wide = cot_ts[which].astype(F32)
-            state["delta"] = jnp.sum(wide * out.astype(F32), axis=0, keepdims=True)
-
-        return [functools.partial(output, at) for at in cuts] + [put]
-
-    def slopes(which, step, state):
-        kv = kv_of(step)
-
-        def slope(at):
-            grads = dot(values[kv, at], cot_ts[which])
-            for tile in within(at):
-                part = grads[tile.start - at.start : tile.stop - at.start] - state["delta"]
-                d_bufs[which, tile] = p_bufs[which, tile] * part.astype(BF16)
-
-        return [functools.partial(slope, at) for at in chunks]
-
-    def value_grads(which, step):
-        kv = kv_of(step)
-
-        def value_grad(at):
-            dv[kv, at] += dot(p_bufs[which, at], cot_ns[which])
-
-        return [functools.partial(value_grad, at) for at in longer]
-
-    def key_grads(which, step):
-        kv = kv_of(step)
-
-        def key_grad(at):
-            dk[kv, at] += dot(d_bufs[which, at], q_ns[which])
-
-        return [functools.partial(key_grad, at) for at in longer]
-
-    def query_grads(which, step):
-        kv = kv_of(step)
-        where = place_of(which, jnp.maximum(step, 0))
-        state = {}
-
-        def query(at):
-            more = dot(keys_t[kv, :, at], d_bufs[which, at])
-            state["dq"] = state["dq"] + more if "dq" in state else more
-
-        def put():
-            dq = state["dq"] * (inv_bufs[which, :1] * score_scale)
-            dq_ref[where] = dq.astype(BF16).T
-
-        return [functools.partial(query, at) for at in cuts] + [put]
-
-    def slot(which, step, fast):
-        before, before_step = 1 - which, step - 1 + which
-        state = {}
-        work, finish = weigh(which, step, fast)
-        late = key_grads(which, step - 1)
-        first = settled(before, before_step, state) + query_grads(which, step - 1)
-        together(work, first + late[: len(late) // 2])
-        together(
-            slopes(before, before_step, state),
-            late[len(late) // 2 :] + value_grads(before, before_step),
-        )
-        finish()
-
-    def together(vector, matrix):
-        done = 0
-        for i, work in enumerate(vector):
-            work()
-            while done * len(vector) < (i + 1) * len(matrix):
-                matrix[done]()
-                done += 1
-
     place = lax.axis_index("seq")
     core = lax.rem(place, CORES)
     first_row = place * tokens
@@ -308,39 +145,238 @@
             allowed = (key_pos >= seg_start) & (key_pos <= row_pos)
             at = i * tokens + row
             bias[at : at + TILE] = jnp.where(allowed, 0.0, NEG)
+    most = jnp.zeros((tokens, 1), F32)
+    for at in range(0, q_cols, HD):
+        part = q_ref[:, at : at + HD].astype(F32)
+        most = jnp.maximum(most, jnp.sum(part * part, axis=1, keepdims=True))
+    most_ref[...] = jnp.broadcast_to(jnp.max(most, axis=0, keepdims=True), most_ref.shape)
+
+
+def largest(ref, most, cols):
+    for at in range(0, ref.shape[0], HD):
+        part = ref[at : at + HD, cols].astype(F32)
+        most = jnp.maximum(most, jnp.sum(part * part, axis=1, keepdims=True))
+    return most
+
+
+def turn_kernel(kv_heads, sent_ref, own_ref, far_ref, turned, most_ref):
+    tokens = own_ref.shape[0]
+    most = jnp.zeros((HD, 1), F32)
+    for n in range(2 * kv_heads):
+        cols = slice(n * HD, (n + 1) * HD)
+        at = 0
+        for ref, size in ((sent_ref, sent_ref.shape[0] - tokens), (far_ref, tokens), (own_ref, tokens)):
+            turned[n, :, at : at + size] = ref[:size, cols].T
+            at += size
+            if n % 2 == 0:
+                most = largest(ref, most, cols)
+    most_ref[...] = jnp.broadcast_to(jnp.max(most, axis=0, keepdims=True), most_ref.shape)
+
+
+def attention_kernel(
+    halves, q_ref, do_ref, sent_ref, got_ref, own_ref, far_ref,
+    bias, turned, q_most, k_most,
+    o_ref, dq_ref, kept_ref, back_ref,
+    keys, values, keys_t, values_t, s_buf, p_bufs, d_bufs, inv_bufs,
+    q_ts, cot_ts, q_ns, cot_ns, dk, dv,
+):
+    kv_heads, total_keys = keys.shape[0], keys.shape[1]
+    tokens, q_cols = q_ref.shape
+    rows = tokens // halves
+    prompt_len = total_keys - 5 * tokens
+    half = prompt_len // 2
+    steps = q_cols // HD * halves // 2
+    steps_per_kv = steps // kv_heads
+    score_scale = 1.0 / math.sqrt(HD)
+    exp_scale = score_scale * math.log2(math.e)
+    resp_at = [prompt_len + i * tokens for i in range(6)]
+    chunks = [slice(at, at + CHUNK) for at in range(0, total_keys, CHUNK)]
+    longer = [slice(at, at + LONGER) for at in range(0, total_keys, LONGER)]
+    cuts = [slice(at, at + total_keys // 2) for at in (0, total_keys // 2)]
+
+    def columns(head):
+        if isinstance(head, int):
+            return slice(head * HD, (head + 1) * HD)
+        return pl.ds(pl.multiple_of(head * HD, HD), HD)
+
+    def place_of(which, step):
+        head = step * 2 + which if halves == 1 else step
+        row = 0 if halves == 1 else which * rows
+        return slice(row, row + rows), columns(head)
+
+    def kv_of(step):
+        return step // steps_per_kv
+
+    def bias_at(which, at, size):
+        row = which * rows * (halves - 1)
+        return bias[at - prompt_len : at - prompt_len + size, row : row + rows]
+
+    def folded(x):
+        return x.reshape(x.shape[0] // 8, 8, rows)
+
+    def within(at):
+        return [slice(start, start + TILE) for start in range(at.start, at.stop, TILE)]
+
+    def weigh(which, step, fast):
+        kv = kv_of(step)
+        where = place_of(which, step)
+        state = {"sum": jnp.zeros((8, rows), F32)}
+
+        def lift():
+            q_ts[which] = q_ref[where].T
+            cot_ts[which] = do_ref[where].T
+
+        def masked(s, at, tile):
+            s = s[tile.start - at.start : tile.stop - at.start]
+            return s if tile.start < prompt_len else s + bias_at(which, tile.start, TILE)
+
+        def put(tile, p):
+            state["sum"] = state["sum"] + jnp.sum(folded(p), axis=0)
+            p_bufs[which, tile] = p.astype(BF16)
+
+        def direct(at):
+            s = dot(keys[kv, at], q_ts[which])
+            for tile in within(at):
+                put(tile, jnp.exp2(masked(s, at, tile) * exp_scale))
+
+        def highest(at):
+            s = dot(keys[kv, at], q_ts[which])
+            for tile in within(at):
+                part = masked(s, at, tile)
+                s_buf[tile] = part
+                top = jnp.max(folded(part), axis=0)
+                state["top"] = jnp.maximum(state["top"], top) if "top" in state else top
+
+        def settle():
+            state["top"] = jnp.max(state["top"], axis=0, keepdims=True) * exp_scale
+
+        def reduced(at):
+            for tile in within(at):
+                put(tile, jnp.exp2(s_buf[tile] * exp_scale - state["top"]))
+
+        def finish():
+            inverse = 1.0 / jnp.sum(state["sum"], axis=0, keepdims=True)
+            inv_bufs[which] = jnp.broadcast_to(inverse, (8, rows))
+            q_ns[which] = (q_ts[which].astype(F32) * inverse).astype(BF16).T
+            cot_ns[which] = (cot_ts[which].astype(F32) * inverse).astype(BF16).T
+
+        if fast:
+            return [lift] + [functools.partial(direct, at) for at in chunks], finish
+        work = [lift] + [functools.partial(highest, at) for at in chunks] + [settle]
+        return work + [functools.partial(reduced, at) for at in chunks], finish
+
+    def settled(which, step, state):
+        kv = kv_of(step)
+        where = place_of(which, step)
+
+        def output(at):
+            more = dot(values_t[kv, :, at], p_bufs[which, at])
+            state["out"] = state["out"] + more if "out" in state else more
+
+        def put():
+            out = (state["out"] * inv_bufs[which, :1]).astype(BF16)
+            o_ref[where] = out.T
+            wide = cot_ts[which].astype(F32)
+            state["delta"] = jnp.sum(wide * out.astype(F32), axis=0, keepdims=True)
+
+        return [functools.partial(output, at) for at in cuts] + [put]
+
+    def slopes(which, step, state):
+        kv = kv_of(step)
+
+        def slope(at):
+            grads = dot(values[kv, at], cot_ts[which])
+            for tile in within(at):
+                part = grads[tile.start - at.start : tile.stop - at.start] - state["delta"]
+                d_bufs[which, tile] = p_bufs[which, tile] * part.astype(BF16)
+
+        return [functools.partial(slope, at) for at in chunks]
+
+    def value_grads(which, step):
+        kv = kv_of(step)
+
+        def value_grad(at):
+            dv[kv, at] += dot(p_bufs[which, at], cot_ns[which])
+
+        return [functools.partial(value_grad, at) for at in longer]
+
+    def key_grads(which, step):
+        kv = kv_of(step)
+
+        def key_grad(at):
+            dk[kv, at] += dot(d_bufs[which, at], q_ns[which])
+
+        return [functools.partial(key_grad, at) for at in longer]
+
+    def query_grads(which, step):
+        kv = kv_of(step)
+        where = place_of(which, step)
+        state = {}
+
+        def query(at):
+            more = dot(keys_t[kv, :, at], d_bufs[which, at])
+            state["dq"] = state["dq"] + more if "dq" in state else more
+
+        def put():
+            dq = state["dq"] * (inv_bufs[which, :1] * score_scale)
+            dq_ref[where] = dq.astype(BF16).T
+
+        return [functools.partial(query, at) for at in cuts] + [put]
+
+    def slot(which, step, fast):
+        before, before_step = 1 - which, step - 1 + which
+        state = {}
+        work, finish = weigh(which, step, fast)
+        started = not isinstance(step, int)
+        late = key_grads(which, step - 1) if started else []
+        first = query_grads(which, step - 1) if started else []
+        if started or which == 1:
+            first = settled(before, before_step, state) + first
+        together(work, first + late[: len(late) // 2])
+        if started or which == 1:
+            together(
+                slopes(before, before_step, state),
+                late[len(late) // 2 :] + value_grads(before, before_step),
+            )
+        finish()
+
+    def together(vector, matrix):
+        done = 0
+        for i, work in enumerate(vector):
+            work()
+            while done * len(vector) < (i + 1) * len(matrix):
+                matrix[done]()
+                done += 1
+
+    most = jnp.zeros((HD, 1), F32)
     for n in range(kv_heads):
-        k_at, v_at = 2 * n * HD, (2 * n + 1) * HD
-        for ref, start, size, at in (
-            (sent_ref, 0, half, 0),
-            (got_ref, 0, half, half),
-            (own_ref, 0, tokens, resp_at[0]),
-            (sent_ref, half, tokens, resp_at[1]),
-            (far_ref, 0, tokens, resp_at[2]),
-            (got_ref, half, tokens, resp_at[3]),
-            (got_ref, half + tokens, tokens, resp_at[4]),
+        k_cols = slice(2 * n * HD, (2 * n + 1) * HD)
+        v_cols = slice((2 * n + 1) * HD, (2 * n + 2) * HD)
+        for ref, start, size, at, turned_at in (
+            (sent_ref, 0, half, 0, 0),
+            (got_ref, 0, half, half, None),
+            (own_ref, 0, tokens, resp_at[0], half + 2 * tokens),
+            (sent_ref, half, tokens, resp_at[1], half),
+            (far_ref, 0, tokens, resp_at[2], half + tokens),
+            (got_ref, half, tokens, resp_at[3], None),
+            (got_ref, half + tokens, tokens, resp_at[4], None),
         ):
-            k_rows = ref[start : start + size, k_at : k_at + HD]
-            v_rows = ref[start : start + size, v_at : v_at + HD]
+            k_rows = ref[start : start + size, k_cols]
+            v_rows = ref[start : start + size, v_cols]
             keys[n, at : at + size] = k_rows
             values[n, at : at + size] = v_rows
-            keys_t[n, :, at : at + size] = k_rows.T
-            values_t[n, :, at : at + size] = v_rows.T
+            if turned_at is None:
+                keys_t[n, :, at : at + size] = k_rows.T
+                values_t[n, :, at : at + size] = v_rows.T
+            else:
+                there = slice(turned_at, turned_at + size)
+                keys_t[n, :, at : at + size] = turned[2 * n, :, there]
+                values_t[n, :, at : at + size] = turned[2 * n + 1, :, there]
+        most = largest(got_ref, most, k_cols)
     dk[...] = jnp.zeros_like(dk)
     dv[...] = jnp.zeros_like(dv)
-    p_bufs[1] = jnp.zeros(p_bufs.shape[1:], BF16)
-    cot_ts[1] = jnp.zeros(cot_ts.shape[1:], BF16)
-    for ref in (d_bufs, inv_bufs, q_ns, cot_ns):
-        ref[...] = jnp.zeros_like(ref)
-    q_most = jnp.zeros((tokens, 1), F32)
-    for at in range(0, q_cols, HD):
-        part = q_ref[:, at : at + HD].astype(F32)
-        q_most = jnp.maximum(q_most, jnp.sum(part * part, axis=1, keepdims=True))
-    k_most = jnp.zeros((CHUNK, 1), F32)
-    for n in range(kv_heads):
-        for at in chunks:
-            part = keys[n, at].astype(F32)
-            k_most = jnp.maximum(k_most, jnp.sum(part * part, axis=1, keepdims=True))
-    most = jnp.max(q_most) * jnp.max(k_most) * (score_scale * score_scale)
+    keys_most = jnp.maximum(jnp.max(most), jnp.max(k_most[...]))
+    most = jnp.max(q_most[...]) * keys_most * (score_scale * score_scale)
     small = most <= SAFE_SCORE * SAFE_SCORE
     def run(fast):
         def pair(step, carry):
@@ -348,7 +384,9 @@
             slot(1, step, fast)
             return carry
 
-        lax.fori_loop(0, steps, pair, 0)
+        slot(0, 0, fast)
+        slot(1, 0, fast)
+        lax.fori_loop(1, steps, pair, 0)
 
     pl.when(small)(functools.partial(run, True))
     pl.when(jnp.logical_not(small))(functools.partial(run, False))
@@ -386,9 +424,19 @@
     halves = 1 if tokens * total_keys <= MOST_SCORES else 2
     rows = tokens // halves
     pairs = tokens * q_heads * total_keys
+    most = ((8, HD), F32)
+    bias, q_most = local_call(
+        mask_kernel, "mask", [lengths, resp_q], [((5 * tokens, tokens), F32), most], scalars=1
+    )
+    turned, k_most = local_call(
+        functools.partial(turn_kernel, kv_heads),
+        "turn",
+        [sent, own, far],
+        [((2 * kv_heads, HD, half + 3 * tokens), BF16), most],
+    )
     return pl.pallas_call(
         functools.partial(attention_kernel, halves),
-        in_specs=[pl.BlockSpec(memory_space=pltpu.SMEM)] + whole(6),
+        in_specs=whole(10),
         out_specs=whole(4),
         out_shape=[
             jax.ShapeDtypeStruct(resp_q.shape, BF16),
@@ -397,7 +445,6 @@
             jax.ShapeDtypeStruct((half + 2 * tokens, sent.shape[1]), BF16),
         ],
         scratch_shapes=[
-            pltpu.VMEM((5 * tokens, tokens), F32),
             pltpu.VMEM((kv_heads, total_keys, HD), BF16),
             pltpu.VMEM((kv_heads, total_keys, HD), BF16),
             pltpu.VMEM((kv_heads, HD, total_keys), BF16),
@@ -418,7 +465,7 @@
             flops=12 * HD * pairs, bytes_accessed=8 * resp_q.size, transcendentals=pairs
         ),
         name="attention",
-    )(lengths, resp_q, grad_out, sent, got, own, far)
+    )(resp_q, grad_out, sent, got, own, far, bias, turned, q_most, k_most)
 
 
 def swap_heads(array, by):

time: 105 us -> 101 us (0.962)
  waiting for transfers between devices: 19.4 us -> 17.2 us
  Pallas kernels: 47.6 us -> 45.5 us
    ppermute x2, waiting for transfers between devices: 5.55 us -> 3.35 us  [swap_cores(): return lax.ppermute(array, 'seq', [(i, i ^ 1) for i in range(devices)])]
    pallas_call x4 -> x6, Pallas kernels: 45.7 us -> 43.6 us  [the longest x1 40.2 us: attention(): pl.pallas_call(functools.partial(attention_kernel, halves), in_specs=whol...]
  transfers between devices with their start and end apart: 20 -> 20, of which waited for: 8 -> 8; matrix products, arithmetic and copies ran while one was open for 1% -> 1% of each run, Pallas kernels for 0% -> 2%
where the time goes in v11:
time: 101 us
  Pallas kernels  45.5 us (45%)
  starting transfers between devices  36.2 us (36%)
  waiting for transfers between devices  17.2 us (17%)
    pallas_call x1, Pallas kernels, attention(): pl.pallas_call(functools.partial(attention_kernel, halves), in_specs=whol...  40.2 us
    ppermute x6, starting transfers between devices, shift_chips(): lax.ppermute(array, 'seq', [(i, i + by) for i in range(devices) if 0 <= i...  18.2 us
    ppermute x6, starting transfers between devices, swap_chips(): lax.ppermute(array, 'seq', [(i, i ^ by * CORES) for i in range(devices)])  8.93 us
    ppermute x6, starting transfers between devices, swap_heads(): return lax.ppermute(array, 'head', [(i, i ^ by) for i in range(devices)])  8.88 us
    ppermute x6, waiting for transfers between devices, swap_heads(): return lax.ppermute(array, 'head', [(i, i ^ by) for i in range(devices)])  7.4 us
    ppermute x6, waiting for transfers between devices, swap_chips(): lax.ppermute(array, 'seq', [(i, i ^ by * CORES) for i in range(devices)])  6.44 us
    pallas_call x5, Pallas kernels, local_call(): pl.pallas_call(kernel, in_specs=[pl.BlockSpec(memory_space=pltpu.SMEM)] *...  3.4 us
    ppermute x2, waiting for transfers between devices, swap_cores(): return lax.ppermute(array, 'seq', [(i, i ^ 1) for i in range(devices)])  3.35 us
  transfers between devices with their start and end apart: 20, of which 8 were waited for; matrix products, arithmetic and copies ran while one was open for 1% of the time, Pallas kernels for 2%

profile of v11, /device:TPU:6, one launch (start us, length us, event | category | flops | bytes accessed | tf_op | source)
XLA Modules:
  0.0 100.8 jit_solution(9738928710813786302)
XLA Ops:
  0.6 1.9 %pack.1 = (bf16[40,512]{1,0:T(8,128)(2,1)}, bf16[40,512]{1,0:T(8,128)(2,1)}, bf16[40,512]{1,0:T(8,128)(2,1)}, bf16[40,512]{1,0:T(8,128)(2,1)}, bf16[256,512]{1,0:T(8,128)(2,1)}) custom-call(bf16[40,1024]{1,0:T(8,128)(2,1)} %pk_ref.1, bf16[40,1024]{1,0:T(8,128)(2,1)} %pv_ref.1, bf16[256,256]{1,0:T(8,128)(2,1)} %rk_ref.1, bf16[256,256]{1,0:T(8,128)(2,1)} %rv_ref.1), custom_call_target="tpu_custom_call" | custom-call | tf_op jit(solution)/shard_map/pack/pallas_call | solution.py:66
  2.5 1.4 %collective-permute-start.4 = (bf16[256,512]{1,0:T(8,128)(2,1)}, bf16[256,512]{1,0:T(8,128)(2,1)S(1)}, u32[]{:S(2)}, u32[]{:S(2)}) collective-permute-start(bf16[256,512]{1,0:T(8,128)(2,1)} %get-tuple-element.45.own_ref), channel_id=1, source_target_pairs={{0,16},{4,20},{8,24},{12,28},{1,17},{5,21},{9,25},{13,29},{2,18},{... | collective-permute-start | bytes 786440 | tf_op jit(solution)/shard_map/ppermute | solution.py:489
  3.9 1.3 %collective-permute-start.3 = (bf16[256,512]{1,0:T(8,128)(2,1)}, bf16[256,512]{1,0:T(8,128)(2,1)S(1)}, u32[]{:S(2)}, u32[]{:S(2)}) collective-permute-start(bf16[256,512]{1,0:T(8,128)(2,1)} %get-tuple-element.45.own_ref), channel_id=1, source_target_pairs={{0,8},{4,12},{8,16},{12,20},{16,24},{20,28},{1,9},{5,13},{9,17},{1... | collective-permute-start | bytes 786440 | tf_op jit(solution)/shard_map/ppermute | solution.py:489
  5.2 1.6 %collective-permute-start = (bf16[40,512]{1,0:T(8,128)(2,1)}, bf16[40,512]{1,0:T(8,128)(2,1)S(1)}, u32[]{:S(2)}, u32[]{:S(2)}) collective-permute-start(bf16[40,512]{1,0:T(8,128)(2,1)} %get-tuple-element.42), channel_id=1, source_target_pairs={{0,1},{1,0},{2,3},{3,2},{4,5},{5,4},{6,7},{7,6},{8,9},{9,8},{10,11... | collective-permute-start | bytes 122888 | tf_op jit(solution)/shard_map/ppermute | solution.py:473
  6.9 2.6 %collective-permute-start.1 = (bf16[40,512]{1,0:T(8,128)(2,1)}, bf16[40,512]{1,0:T(8,128)(2,1)S(1)}, u32[]{:S(2)}, u32[]{:S(2)}) collective-permute-start(bf16[40,512]{1,0:T(8,128)(2,1)} %get-tuple-element.43), channel_id=1, source_target_pairs={{0,2},{1,3},{2,0},{3,1},{4,6},{5,7},{6,4},{7,5},{8,10},{9,11},{10,... | collective-permute-start | bytes 122888 | tf_op jit(solution)/shard_map/ppermute | solution.py:473
  9.5 0.2 collective-permute-start.2
  9.7 0.8 constant_dynamic-update-slice_fusion.3
  10.5 2.3 %collective-permute-done.1 = bf16[40,512]{1,0:T(8,128)(2,1)S(1)} collective-permute-done((bf16[40,512]{1,0:T(8,128)(2,1)}, bf16[40,512]{1,0:T(8,128)(2,1)S(1)}, u32[]{:S(2)}, u32[]{:S(2)}) %collective-permute-start.1) | collective-permute-done | bytes 40992 | tf_op jit(solution)/shard_map/ppermute | solution.py:473
  12.8 2.7 %collective-permute-done.2 = bf16[40,512]{1,0:T(8,128)(2,1)S(1)} collective-permute-done((bf16[40,512]{1,0:T(8,128)(2,1)}, bf16[40,512]{1,0:T(8,128)(2,1)S(1)}, u32[]{:S(2)}, u32[]{:S(2)}) %collective-permute-start.2) | collective-permute-done | bytes 40992 | tf_op jit(solution)/shard_map/ppermute | solution.py:473
  15.6 3.5 %collective-permute-start.5 = (bf16[160,512]{1,0:T(8,128)(2,1)S(1)}, bf16[160,512]{1,0:T(8,128)(2,1)S(1)}, u32[]{:S(2)}, u32[]{:S(2)}) collective-permute-start(bf16[160,512]{1,0:T(8,128)(2,1)S(1)} %get-tuple-element.76), channel_id=1, source_target_pairs={{0,8},{4,12},{8,0},{12,4},{16,24},{20,28},{24,16},{28,20},{1,9},{5... | collective-permute-start | bytes 491528 | tf_op jit(solution)/shard_map/ppermute | solution.py:478
  19.1 1.9 %collective-permute-start.6 = (bf16[160,512]{1,0:T(8,128)(2,1)S(1)}, bf16[160,512]{1,0:T(8,128)(2,1)S(1)}, u32[]{:S(2)}, u32[]{:S(2)}) collective-permute-start(bf16[160,512]{1,0:T(8,128)(2,1)S(1)} %get-tuple-element.76), channel_id=1, source_target_pairs={{0,16},{4,20},{8,24},{12,28},{16,0},{20,4},{24,8},{28,12},{1,17},{... | collective-permute-start | bytes 491528 | tf_op jit(solution)/shard_map/ppermute | solution.py:478
  20.9 2.5 %collective-permute-done.5 = bf16[160,512]{1,0:T(8,128)(2,1)S(1)} collective-permute-done((bf16[160,512]{1,0:T(8,128)(2,1)S(1)}, bf16[160,512]{1,0:T(8,128)(2,1)S(1)}, u32[]{:S(2)}, u32[]{:S(2)}) %collective-permute-start.5) | collective-permute-done | bytes 163872 | tf_op jit(solution)/shard_map/ppermute | solution.py:478
  23.4 3.9 %collective-permute-done.6 = bf16[160,512]{1,0:T(8,128)(2,1)S(1)} collective-permute-done((bf16[160,512]{1,0:T(8,128)(2,1)S(1)}, bf16[160,512]{1,0:T(8,128)(2,1)S(1)}, u32[]{:S(2)}, u32[]{:S(2)}) %collective-permute-start.6) | collective-permute-done | bytes 163872 | tf_op jit(solution)/shard_map/ppermute | solution.py:478
  27.6 1.3 %mask.1 = (f32[1280,256]{1,0:T(8,128)S(1)}, f32[8,128]{1,0:T(8,128)S(1)}) custom-call(s32[8]{0:T(128)S(1)} %copy-done.2, bf16[256,2048]{1,0:T(8,128)(2,1)S(1)} %copy-done), custom_call_target="tpu_custom_call" | custom-call | tf_op jit(solution)/shard_map/mask/pallas_call | solution.py:33
  28.9 0.9 turn.1
  29.8 0.6 collective-permute-done.8.got_ref
  30.5 40.2 %attention.1 = (bf16[256,2048]{1,0:T(8,128)(2,1)}, bf16[256,2048]{1,0:T(8,128)(2,1)}, f32[1408,512]{1,0:T(8,128)S(1)}, bf16[1152,512]{1,0:T(8,128)(2,1)S(1)}) custom-call(bf16[256,2048]{1,0:T(8,128)(2,1)S(1)} %copy-done, bf16[256,2048]{1,0:T(8,128)(2,1)S(1)} %copy-done.3, bf16[1152,512]{1,0:T(8,128)(2,1)S(1)} %select_dynamic-update-slice_fusion.sent_ref, ...), custom_call_target="tpu_custom_call" | custom-call | flops 16106127360 | bytes 4194304 | tf_op jit(solution)/shard_map/attention/pallas_call | solution.py:437
  70.7 0.1 collective-permute-start.9
  70.8 2.7 %collective-permute-done.9.got_ref = bf16[1152,512]{1,0:T(8,128)(2,1)S(1)} collective-permute-done((bf16[1152,512]{1,0:T(8,128)(2,1)S(1)}, bf16[1152,512]{1,0:T(8,128)(2,1)S(1)}, u32[]{:S(2)}, u32[]{:S(2)}) %collective-permute-start.9) | collective-permute-done | bytes 1179680 | tf_op jit(solution)/shard_map/ppermute | solution.py:483
  73.6 0.3 merge.1
  73.9 0.4 collective-permute-start.14
  74.3 1.6 %collective-permute-start.15 = (bf16[160,512]{1,0:T(8,128)(2,1)S(1)}, bf16[160,512]{1,0:T(8,128)(2,1)S(1)}, u32[]{:S(2)}, u32[]{:S(2)}) collective-permute-start(bf16[160,512]{1,0:T(8,128)(2,1)S(1)} %get-tuple-element.66), channel_id=1, source_target_pairs={{0,16},{4,20},{8,24},{12,28},{16,0},{20,4},{24,8},{28,12},{1,17},{... | collective-permute-start | bytes 491528 | tf_op jit(solution)/shard_map/ppermute | solution.py:478
  75.9 1.6 %collective-permute-start.16 = (bf16[160,512]{1,0:T(8,128)(2,1)S(1)}, bf16[160,512]{1,0:T(8,128)(2,1)S(1)}, u32[]{:S(2)}, u32[]{:S(2)}) collective-permute-start(bf16[160,512]{1,0:T(8,128)(2,1)S(1)} %get-tuple-element.67), channel_id=1, source_target_pairs={{0,24},{4,28},{8,16},{12,20},{16,8},{20,12},{24,0},{28,4},{1,25},{... | collective-permute-start | bytes 491528 | tf_op jit(solution)/shard_map/ppermute | solution.py:478
  77.4 2.3 %collective-permute-start.10 = (bf16[128,512]{1,0:T(8,128)(2,1)S(1)}, bf16[128,512]{1,0:T(8,128)(2,1)S(1)}, u32[]{:S(2)}, u32[]{:S(2)}) collective-permute-start(bf16[128,512]{1,0:T(8,128)(2,1)S(1)} %get-tuple-element.60), channel_id=1, source_target_pairs={{8,0},{12,4},{16,8},{20,12},{24,16},{28,20},{9,1},{13,5},{17,9},{2... | collective-permute-start | bytes 393224 | tf_op jit(solution)/shard_map/ppermute | solution.py:489
  79.7 4.6 %collective-permute-start.11 = (bf16[128,512]{1,0:T(8,128)(2,1)S(1)}, bf16[128,512]{1,0:T(8,128)(2,1)S(1)}, u32[]{:S(2)}, u32[]{:S(2)}) collective-permute-start(bf16[128,512]{1,0:T(8,128)(2,1)S(1)} %get-tuple-element.61), channel_id=1, source_target_pairs={{8,0},{12,4},{16,8},{20,12},{24,16},{28,20},{9,1},{13,5},{17,9},{2... | collective-permute-start | bytes 393224 | tf_op jit(solution)/shard_map/ppermute | solution.py:489
  84.3 1.3 %collective-permute-start.12 = (bf16[128,512]{1,0:T(8,128)(2,1)S(1)}, bf16[128,512]{1,0:T(8,128)(2,1)S(1)}, u32[]{:S(2)}, u32[]{:S(2)}) collective-permute-start(bf16[128,512]{1,0:T(8,128)(2,1)S(1)} %get-tuple-element.62), channel_id=1, source_target_pairs={{16,0},{20,4},{24,8},{28,12},{17,1},{21,5},{25,9},{29,13},{18,2},{... | collective-permute-start | bytes 393224 | tf_op jit(solution)/shard_map/ppermute | solution.py:489
  85.7 7.3 %collective-permute-start.13 = (bf16[128,512]{1,0:T(8,128)(2,1)S(1)}, bf16[128,512]{1,0:T(8,128)(2,1)S(1)}, u32[]{:S(2)}, u32[]{:S(2)}) collective-permute-start(bf16[128,512]{1,0:T(8,128)(2,1)S(1)} %get-tuple-element.63), channel_id=1, source_target_pairs={{16,0},{20,4},{24,8},{28,12},{17,1},{21,5},{25,9},{29,13},{18,2},{... | collective-permute-start | bytes 393224 | tf_op jit(solution)/shard_map/ppermute | solution.py:489
  93.0 0.1 sum_chips.1
  93.3 4.3 %collective-permute-start.19 = (bf16[40,512]{1,0:T(8,128)(2,1)S(1)}, bf16[40,512]{1,0:T(8,128)(2,1)S(1)}, u32[]{:S(2)}, u32[]{:S(2)}) collective-permute-start(bf16[40,512]{1,0:T(8,128)(2,1)S(1)} %get-tuple-element.71), channel_id=1, source_target_pairs={{0,3},{1,2},{2,1},{3,0},{4,7},{5,6},{6,5},{7,4},{8,11},{9,10},{10,... | collective-permute-start | bytes 122888 | tf_op jit(solution)/shard_map/ppermute | solution.py:473
  97.6 0.6 collective-permute-done.18.refs_6_
  98.1 1.8 %collective-permute-done.19.refs_7_ = bf16[40,512]{1,0:T(8,128)(2,1)S(1)} collective-permute-done((bf16[40,512]{1,0:T(8,128)(2,1)S(1)}, bf16[40,512]{1,0:T(8,128)(2,1)S(1)}, u32[]{:S(2)}, u32[]{:S(2)}) %collective-permute-start.19) | collective-permute-done | bytes 40992 | tf_op jit(solution)/shard_map/ppermute | solution.py:473
  100.0 0.8 finish.1
  (32 shorter events, 0.4 us)
Async XLA Ops:
  2.5 24.9 %copy-start.1 = (bf16[256,512]{1,0:T(8,128)(2,1)S(1)}, bf16[256,512]{1,0:T(8,128)(2,1)}, u32[]{:S(2)}) copy-start(bf16[256,512]{1,0:T(8,128)(2,1)} %get-tuple-element.45.own_ref) | copy-start | bytes 786436
  2.5 13.0 %collective-permute-start.4 = (bf16[256,512]{1,0:T(8,128)(2,1)}, bf16[256,512]{1,0:T(8,128)(2,1)S(1)}, u32[]{:S(2)}, u32[]{:S(2)}) collective-permute-start(bf16[256,512]{1,0:T(8,128)(2,1)} %get-tuple-element.45.own_ref), channel_id=1, source_target_pairs={{0,16},{4,20},{8,24},{12,28},{1,17},{5,21},{9,25},{13,29},{2,18},{... | collective-permute-start | bytes 786440 | tf_op jit(solution)/shard_map/ppermute | solution.py:489
  3.9 11.5 %collective-permute-start.3 = (bf16[256,512]{1,0:T(8,128)(2,1)}, bf16[256,512]{1,0:T(8,128)(2,1)S(1)}, u32[]{:S(2)}, u32[]{:S(2)}) collective-permute-start(bf16[256,512]{1,0:T(8,128)(2,1)} %get-tuple-element.45.own_ref), channel_id=1, source_target_pairs={{0,8},{4,12},{8,16},{12,20},{16,24},{20,28},{1,9},{5,13},{9,17},{1... | collective-permute-start | bytes 786440 | tf_op jit(solution)/shard_map/ppermute | solution.py:489
  5.2 5.2 %collective-permute-start = (bf16[40,512]{1,0:T(8,128)(2,1)}, bf16[40,512]{1,0:T(8,128)(2,1)S(1)}, u32[]{:S(2)}, u32[]{:S(2)}) collective-permute-start(bf16[40,512]{1,0:T(8,128)(2,1)} %get-tuple-element.42), channel_id=1, source_target_pairs={{0,1},{1,0},{2,3},{3,2},{4,5},{5,4},{6,7},{7,6},{8,9},{9,8},{10,11... | collective-permute-start | bytes 122888 | tf_op jit(solution)/shard_map/ppermute | solution.py:473
  6.9 5.9 %collective-permute-start.1 = (bf16[40,512]{1,0:T(8,128)(2,1)}, bf16[40,512]{1,0:T(8,128)(2,1)S(1)}, u32[]{:S(2)}, u32[]{:S(2)}) collective-permute-start(bf16[40,512]{1,0:T(8,128)(2,1)} %get-tuple-element.43), channel_id=1, source_target_pairs={{0,2},{1,3},{2,0},{3,1},{4,6},{5,7},{6,4},{7,5},{8,10},{9,11},{10,... | collective-permute-start | bytes 122888 | tf_op jit(solution)/shard_map/ppermute | solution.py:473
  9.5 6.0 %collective-permute-start.2 = (bf16[40,512]{1,0:T(8,128)(2,1)}, bf16[40,512]{1,0:T(8,128)(2,1)S(1)}, u32[]{:S(2)}, u32[]{:S(2)}) collective-permute-start(bf16[40,512]{1,0:T(8,128)(2,1)} %get-tuple-element.44), channel_id=1, source_target_pairs={{0,3},{1,2},{2,1},{3,0},{4,7},{5,6},{6,5},{7,4},{8,11},{9,10},{10,... | collective-permute-start | bytes 122888 | tf_op jit(solution)/shard_map/ppermute | solution.py:473
  15.5 12.1 %copy-start = (bf16[256,2048]{1,0:T(8,128)(2,1)S(1)}, bf16[256,2048]{1,0:T(8,128)(2,1)}, u32[]{:S(2)}) copy-start(bf16[256,2048]{1,0:T(8,128)(2,1)} %q_ref.3) | copy-start | bytes 3145732
  15.5 12.1 %copy-start.2 = (s32[8]{0:T(128)S(1)}, s32[8]{0:T(128)}, u32[]{:S(2)}) copy-start(s32[8]{0:T(128)} %lengths.1) | copy-start | bytes 100
  15.6 7.9 %collective-permute-start.5 = (bf16[160,512]{1,0:T(8,128)(2,1)S(1)}, bf16[160,512]{1,0:T(8,128)(2,1)S(1)}, u32[]{:S(2)}, u32[]{:S(2)}) collective-permute-start(bf16[160,512]{1,0:T(8,128)(2,1)S(1)} %get-tuple-element.76), channel_id=1, source_target_pairs={{0,8},{4,12},{8,0},{12,4},{16,24},{20,28},{24,16},{28,20},{1,9},{5... | collective-permute-start | bytes 491528 | tf_op jit(solution)/shard_map/ppermute | solution.py:478
  19.1 8.3 %collective-permute-start.6 = (bf16[160,512]{1,0:T(8,128)(2,1)S(1)}, bf16[160,512]{1,0:T(8,128)(2,1)S(1)}, u32[]{:S(2)}, u32[]{:S(2)}) collective-permute-start(bf16[160,512]{1,0:T(8,128)(2,1)S(1)} %get-tuple-element.76), channel_id=1, source_target_pairs={{0,16},{4,20},{8,24},{12,28},{16,0},{20,4},{24,8},{28,12},{1,17},{... | collective-permute-start | bytes 491528 | tf_op jit(solution)/shard_map/ppermute | solution.py:478
  20.9 6.5 %collective-permute-start.7 = (bf16[160,512]{1,0:T(8,128)(2,1)S(1)}, bf16[160,512]{1,0:T(8,128)(2,1)S(1)}, u32[]{:S(2)}, u32[]{:S(2)}) collective-permute-start(bf16[160,512]{1,0:T(8,128)(2,1)S(1)} %get-tuple-element.76), channel_id=1, source_target_pairs={{0,24},{4,28},{8,16},{12,20},{16,8},{20,12},{24,0},{28,4},{1,25},{... | collective-permute-start | bytes 491528 | tf_op jit(solution)/shard_map/ppermute | solution.py:478
  27.5 2.9 %copy-start.3 = (bf16[256,2048]{1,0:T(8,128)(2,1)S(1)}, bf16[256,2048]{1,0:T(8,128)(2,1)}, u32[]{:S(2)}) copy-start(bf16[256,2048]{1,0:T(8,128)(2,1)} %do_ref.1) | copy-start | bytes 3145732
  27.5 2.9 %collective-permute-start.8 = (bf16[1152,512]{1,0:T(8,128)(2,1)S(1)}, bf16[1152,512]{1,0:T(8,128)(2,1)S(1)}, u32[]{:S(2)}, u32[]{:S(2)}) collective-permute-start(bf16[1152,512]{1,0:T(8,128)(2,1)S(1)} %select_dynamic-update-slice_fusion.sent_ref), channel_id=1, source_target_pairs={{0,4},{4,0},{8,12},{12,8},{16,20},{20,16},{24,28},{28,24},{1,5},{5... | collective-permute-start | bytes 3538952 | tf_op jit(solution)/shard_map/ppermute | solution.py:483
  70.7 2.8 %collective-permute-start.9 = (bf16[1152,512]{1,0:T(8,128)(2,1)S(1)}, bf16[1152,512]{1,0:T(8,128)(2,1)S(1)}, u32[]{:S(2)}, u32[]{:S(2)}) collective-permute-start(bf16[1152,512]{1,0:T(8,128)(2,1)S(1)} %get-tuple-element.58), channel_id=1, source_target_pairs={{0,4},{4,0},{8,12},{12,8},{16,20},{20,16},{24,28},{28,24},{1,5},{5... | collective-permute-start | bytes 3538952 | tf_op jit(solution)/shard_map/ppermute | solution.py:483
  73.9 10.5 %collective-permute-start.14 = (bf16[160,512]{1,0:T(8,128)(2,1)S(1)}, bf16[160,512]{1,0:T(8,128)(2,1)S(1)}, u32[]{:S(2)}, u32[]{:S(2)}) collective-permute-start(bf16[160,512]{1,0:T(8,128)(2,1)S(1)} %get-tuple-element.65), channel_id=1, source_target_pairs={{0,8},{4,12},{8,0},{12,4},{16,24},{20,28},{24,16},{28,20},{1,9},{5... | collective-permute-start | bytes 491528 | tf_op jit(solution)/shard_map/ppermute | solution.py:478
  74.3 11.4 %collective-permute-start.15 = (bf16[160,512]{1,0:T(8,128)(2,1)S(1)}, bf16[160,512]{1,0:T(8,128)(2,1)S(1)}, u32[]{:S(2)}, u32[]{:S(2)}) collective-permute-start(bf16[160,512]{1,0:T(8,128)(2,1)S(1)} %get-tuple-element.66), channel_id=1, source_target_pairs={{0,16},{4,20},{8,24},{12,28},{16,0},{20,4},{24,8},{28,12},{1,17},{... | collective-permute-start | bytes 491528 | tf_op jit(solution)/shard_map/ppermute | solution.py:478
  75.9 17.1 %collective-permute-start.16 = (bf16[160,512]{1,0:T(8,128)(2,1)S(1)}, bf16[160,512]{1,0:T(8,128)(2,1)S(1)}, u32[]{:S(2)}, u32[]{:S(2)}) collective-permute-start(bf16[160,512]{1,0:T(8,128)(2,1)S(1)} %get-tuple-element.67), channel_id=1, source_target_pairs={{0,24},{4,28},{8,16},{12,20},{16,8},{20,12},{24,0},{28,4},{1,25},{... | collective-permute-start | bytes 491528 | tf_op jit(solution)/shard_map/ppermute | solution.py:478
  77.4 15.7 %collective-permute-start.10 = (bf16[128,512]{1,0:T(8,128)(2,1)S(1)}, bf16[128,512]{1,0:T(8,128)(2,1)S(1)}, u32[]{:S(2)}, u32[]{:S(2)}) collective-permute-start(bf16[128,512]{1,0:T(8,128)(2,1)S(1)} %get-tuple-element.60), channel_id=1, source_target_pairs={{8,0},{12,4},{16,8},{20,12},{24,16},{28,20},{9,1},{13,5},{17,9},{2... | collective-permute-start | bytes 393224 | tf_op jit(solution)/shard_map/ppermute | solution.py:489
  79.7 13.6 %collective-permute-start.11 = (bf16[128,512]{1,0:T(8,128)(2,1)S(1)}, bf16[128,512]{1,0:T(8,128)(2,1)S(1)}, u32[]{:S(2)}, u32[]{:S(2)}) collective-permute-start(bf16[128,512]{1,0:T(8,128)(2,1)S(1)} %get-tuple-element.61), channel_id=1, source_target_pairs={{8,0},{12,4},{16,8},{20,12},{24,16},{28,20},{9,1},{13,5},{17,9},{2... | collective-permute-start | bytes 393224 | tf_op jit(solution)/shard_map/ppermute | solution.py:489
  84.3 13.2 %collective-permute-start.12 = (bf16[128,512]{1,0:T(8,128)(2,1)S(1)}, bf16[128,512]{1,0:T(8,128)(2,1)S(1)}, u32[]{:S(2)}, u32[]{:S(2)}) collective-permute-start(bf16[128,512]{1,0:T(8,128)(2,1)S(1)} %get-tuple-element.62), channel_id=1, source_target_pairs={{16,0},{20,4},{24,8},{28,12},{17,1},{21,5},{25,9},{29,13},{18,2},{... | collective-permute-start | bytes 393224 | tf_op jit(solution)/shard_map/ppermute | solution.py:489
  85.7 11.9 %collective-permute-start.13 = (bf16[128,512]{1,0:T(8,128)(2,1)S(1)}, bf16[128,512]{1,0:T(8,128)(2,1)S(1)}, u32[]{:S(2)}, u32[]{:S(2)}) collective-permute-start(bf16[128,512]{1,0:T(8,128)(2,1)S(1)} %get-tuple-element.63), channel_id=1, source_target_pairs={{16,0},{20,4},{24,8},{28,12},{17,1},{21,5},{25,9},{29,13},{18,2},{... | collective-permute-start | bytes 393224 | tf_op jit(solution)/shard_map/ppermute | solution.py:489
  93.1 4.5 %collective-permute-start.17 = (bf16[40,512]{1,0:T(8,128)(2,1)S(1)}, bf16[40,512]{1,0:T(8,128)(2,1)S(1)}, u32[]{:S(2)}, u32[]{:S(2)}) collective-permute-start(bf16[40,512]{1,0:T(8,128)(2,1)S(1)} %get-tuple-element.69), channel_id=1, source_target_pairs={{0,1},{1,0},{2,3},{3,2},{4,5},{5,4},{6,7},{7,6},{8,9},{9,8},{10,11... | collective-permute-start | bytes 122888 | tf_op jit(solution)/shard_map/ppermute | solution.py:473
  93.2 5.0 %collective-permute-start.18 = (bf16[40,512]{1,0:T(8,128)(2,1)S(1)}, bf16[40,512]{1,0:T(8,128)(2,1)S(1)}, u32[]{:S(2)}, u32[]{:S(2)}) collective-permute-start(bf16[40,512]{1,0:T(8,128)(2,1)S(1)} %get-tuple-element.70), channel_id=1, source_target_pairs={{0,2},{1,3},{2,0},{3,1},{4,6},{5,7},{6,4},{7,5},{8,10},{9,11},{10,... | collective-permute-start | bytes 122888 | tf_op jit(solution)/shard_map/ppermute | solution.py:473
  93.3 6.7 %collective-permute-start.19 = (bf16[40,512]{1,0:T(8,128)(2,1)S(1)}, bf16[40,512]{1,0:T(8,128)(2,1)S(1)}, u32[]{:S(2)}, u32[]{:S(2)}) collective-permute-start(bf16[40,512]{1,0:T(8,128)(2,1)S(1)} %get-tuple-element.71), channel_id=1, source_target_pairs={{0,3},{1,2},{2,1},{3,0},{4,7},{5,6},{6,5},{7,4},{8,11},{9,10},{10,... | collective-permute-start | bytes 122888 | tf_op jit(solution)/shard_map/ppermute | solution.py:473

commit v12 on v11

--- a/solution.py
+++ b/solution.py
@@ -220,7 +220,7 @@
     def weigh(which, step, fast):
         kv = kv_of(step)
         where = place_of(which, step)
-        state = {"sum": jnp.zeros((8, rows), F32)}
+        state = {}
 
         def lift():
             q_ts[which] = q_ref[where].T
@@ -231,7 +231,6 @@
             return s if tile.start < prompt_len else s + bias_at(which, tile.start, TILE)
 
         def put(tile, p):
-            state["sum"] = state["sum"] + jnp.sum(folded(p), axis=0)
             p_bufs[which, tile] = p.astype(BF16)
 
         def direct(at):
@@ -254,16 +253,10 @@
             for tile in within(at):
                 put(tile, jnp.exp2(s_buf[tile] * exp_scale - state["top"]))
 
-        def finish():
-            inverse = 1.0 / jnp.sum(state["sum"], axis=0, keepdims=True)
-            inv_bufs[which] = jnp.broadcast_to(inverse, (8, rows))
-            q_ns[which] = (q_ts[which].astype(F32) * inverse).astype(BF16).T
-            cot_ns[which] = (cot_ts[which].astype(F32) * inverse).astype(BF16).T
-
         if fast:
-            return [lift] + [functools.partial(direct, at) for at in chunks], finish
+            return [lift] + [functools.partial(direct, at) for at in chunks]
         work = [lift] + [functools.partial(highest, at) for at in chunks] + [settle]
-        return work + [functools.partial(reduced, at) for at in chunks], finish
+        return work + [functools.partial(reduced, at) for at in chunks]
 
     def settled(which, step, state):
         kv = kv_of(step)
@@ -274,10 +267,14 @@
             state["out"] = state["out"] + more if "out" in state else more
 
         def put():
-            out = (state["out"] * inv_bufs[which, :1]).astype(BF16)
+            inverse = 1.0 / state["out"][HD : HD + 1]
+            inv_bufs[which] = jnp.broadcast_to(inverse, (8, rows))
+            out = (state["out"][:HD] * inverse).astype(BF16)
             o_ref[where] = out.T
+            q_ns[which] = (q_ts[which].astype(F32) * inverse).astype(BF16).T
             wide = cot_ts[which].astype(F32)
             state["delta"] = jnp.sum(wide * out.astype(F32), axis=0, keepdims=True)
+            cot_ns[which] = (wide * inverse).astype(BF16).T
 
         return [functools.partial(output, at) for at in cuts] + [put]
 
@@ -326,7 +323,7 @@
     def slot(which, step, fast):
         before, before_step = 1 - which, step - 1 + which
         state = {}
-        work, finish = weigh(which, step, fast)
+        work = weigh(which, step, fast)
         started = not isinstance(step, int)
         late = key_grads(which, step - 1) if started else []
         first = query_grads(which, step - 1) if started else []
@@ -338,7 +335,6 @@
                 slopes(before, before_step, state),
                 late[len(late) // 2 :] + value_grads(before, before_step),
             )
-        finish()
 
     def together(vector, matrix):
         done = 0
@@ -367,11 +363,12 @@
             values[n, at : at + size] = v_rows
             if turned_at is None:
                 keys_t[n, :, at : at + size] = k_rows.T
-                values_t[n, :, at : at + size] = v_rows.T
+                values_t[n, :HD, at : at + size] = v_rows.T
             else:
                 there = slice(turned_at, turned_at + size)
                 keys_t[n, :, at : at + size] = turned[2 * n, :, there]
-                values_t[n, :, at : at + size] = turned[2 * n + 1, :, there]
+                values_t[n, :HD, at : at + size] = turned[2 * n + 1, :, there]
+        values_t[n, HD:] = jnp.ones((16, total_keys), BF16)
         most = largest(got_ref, most, k_cols)
     dk[...] = jnp.zeros_like(dk)
     dv[...] = jnp.zeros_like(dv)
@@ -448,7 +445,7 @@
             pltpu.VMEM((kv_heads, total_keys, HD), BF16),
             pltpu.VMEM((kv_heads, total_keys, HD), BF16),
             pltpu.VMEM((kv_heads, HD, total_keys), BF16),
-            pltpu.VMEM((kv_heads, HD, total_keys), BF16),
+            pltpu.VMEM((kv_heads, HD + 16, total_keys), BF16),
             pltpu.VMEM((total_keys, rows), F32),
             pltpu.VMEM((2, total_keys, rows), BF16),
             pltpu.VMEM((2, total_keys, rows), BF16),

time: 101 us -> 98.9 us (0.979)
  Pallas kernels: 45.5 us -> 43.3 us
    pallas_call x1, Pallas kernels: 40.2 us -> 38 us  [attention(): pl.pallas_call(functools.partial(attention_kernel, halves), in_specs=whol...]
where the time goes in v12:
time: 98.9 us; the launch traced here: 98.5 us
  Pallas kernels  43.3 us (44%)
  starting transfers between devices  36.2 us (37%)
  waiting for transfers between devices  17.2 us (17%)
    pallas_call x1, Pallas kernels, attention(): pl.pallas_call(functools.partial(attention_kernel, halves), in_specs=whol...  38 us
    ppermute x6, starting transfers between devices, shift_chips(): lax.ppermute(array, 'seq', [(i, i + by) for i in range(devices) if 0 <= i...  18.2 us
    ppermute x6, starting transfers between devices, swap_chips(): lax.ppermute(array, 'seq', [(i, i ^ by * CORES) for i in range(devices)])  8.93 us
    ppermute x6, starting transfers between devices, swap_heads(): return lax.ppermute(array, 'head', [(i, i ^ by) for i in range(devices)])  8.88 us
    ppermute x6, waiting for transfers between devices, swap_heads(): return lax.ppermute(array, 'head', [(i, i ^ by) for i in range(devices)])  7.4 us
    ppermute x6, waiting for transfers between devices, swap_chips(): lax.ppermute(array, 'seq', [(i, i ^ by * CORES) for i in range(devices)])  6.44 us
    pallas_call x5, Pallas kernels, local_call(): pl.pallas_call(kernel, in_specs=[pl.BlockSpec(memory_space=pltpu.SMEM)] *...  3.4 us
    ppermute x2, waiting for transfers between devices, swap_cores(): return lax.ppermute(array, 'seq', [(i, i ^ 1) for i in range(devices)])  3.32 us
  transfers between devices with their start and end apart: 20, of which 8 were waited for; matrix products, arithmetic and copies ran while one was open for 1% of the time, Pallas kernels for 2%

profile of v12, /device:TPU:6, one launch (start us, length us, event | category | flops | bytes accessed | tf_op | source)
XLA Modules:
  0.0 98.5 jit_solution(4100642145789018882)
XLA Ops:
  0.6 1.9 %pack.1 = (bf16[40,512]{1,0:T(8,128)(2,1)}, bf16[40,512]{1,0:T(8,128)(2,1)}, bf16[40,512]{1,0:T(8,128)(2,1)}, bf16[40,512]{1,0:T(8,128)(2,1)}, bf16[256,512]{1,0:T(8,128)(2,1)}) custom-call(bf16[40,1024]{1,0:T(8,128)(2,1)} %pk_ref.1, bf16[40,1024]{1,0:T(8,128)(2,1)} %pv_ref.1, bf16[256,256]{1,0:T(8,128)(2,1)} %rk_ref.1, bf16[256,256]{1,0:T(8,128)(2,1)} %rv_ref.1), custom_call_target="tpu_custom_call" | custom-call | tf_op jit(solution)/shard_map/pack/pallas_call | solution.py:66
  2.5 1.4 %collective-permute-start.4 = (bf16[256,512]{1,0:T(8,128)(2,1)}, bf16[256,512]{1,0:T(8,128)(2,1)S(1)}, u32[]{:S(2)}, u32[]{:S(2)}) collective-permute-start(bf16[256,512]{1,0:T(8,128)(2,1)} %get-tuple-element.45.own_ref), channel_id=1, source_target_pairs={{0,16},{4,20},{8,24},{12,28},{1,17},{5,21},{9,25},{13,29},{2,18},{... | collective-permute-start | bytes 786440 | tf_op jit(solution)/shard_map/ppermute | solution.py:486
  3.9 1.3 %collective-permute-start.3 = (bf16[256,512]{1,0:T(8,128)(2,1)}, bf16[256,512]{1,0:T(8,128)(2,1)S(1)}, u32[]{:S(2)}, u32[]{:S(2)}) collective-permute-start(bf16[256,512]{1,0:T(8,128)(2,1)} %get-tuple-element.45.own_ref), channel_id=1, source_target_pairs={{0,8},{4,12},{8,16},{12,20},{16,24},{20,28},{1,9},{5,13},{9,17},{1... | collective-permute-start | bytes 786440 | tf_op jit(solution)/shard_map/ppermute | solution.py:486
  5.2 1.6 %collective-permute-start = (bf16[40,512]{1,0:T(8,128)(2,1)}, bf16[40,512]{1,0:T(8,128)(2,1)S(1)}, u32[]{:S(2)}, u32[]{:S(2)}) collective-permute-start(bf16[40,512]{1,0:T(8,128)(2,1)} %get-tuple-element.42), channel_id=1, source_target_pairs={{0,1},{1,0},{2,3},{3,2},{4,5},{5,4},{6,7},{7,6},{8,9},{9,8},{10,11... | collective-permute-start | bytes 122888 | tf_op jit(solution)/shard_map/ppermute | solution.py:470
  6.9 2.6 %collective-permute-start.1 = (bf16[40,512]{1,0:T(8,128)(2,1)}, bf16[40,512]{1,0:T(8,128)(2,1)S(1)}, u32[]{:S(2)}, u32[]{:S(2)}) collective-permute-start(bf16[40,512]{1,0:T(8,128)(2,1)} %get-tuple-element.43), channel_id=1, source_target_pairs={{0,2},{1,3},{2,0},{3,1},{4,6},{5,7},{6,4},{7,5},{8,10},{9,11},{10,... | collective-permute-start | bytes 122888 | tf_op jit(solution)/shard_map/ppermute | solution.py:470
  9.5 0.2 collective-permute-start.2
  9.7 0.8 constant_dynamic-update-slice_fusion.3
  10.5 2.3 %collective-permute-done.1 = bf16[40,512]{1,0:T(8,128)(2,1)S(1)} collective-permute-done((bf16[40,512]{1,0:T(8,128)(2,1)}, bf16[40,512]{1,0:T(8,128)(2,1)S(1)}, u32[]{:S(2)}, u32[]{:S(2)}) %collective-permute-start.1) | collective-permute-done | bytes 40992 | tf_op jit(solution)/shard_map/ppermute | solution.py:470
  12.8 2.7 %collective-permute-done.2 = bf16[40,512]{1,0:T(8,128)(2,1)S(1)} collective-permute-done((bf16[40,512]{1,0:T(8,128)(2,1)}, bf16[40,512]{1,0:T(8,128)(2,1)S(1)}, u32[]{:S(2)}, u32[]{:S(2)}) %collective-permute-start.2) | collective-permute-done | bytes 40992 | tf_op jit(solution)/shard_map/ppermute | solution.py:470
  15.6 3.5 %collective-permute-start.5 = (bf16[160,512]{1,0:T(8,128)(2,1)S(1)}, bf16[160,512]{1,0:T(8,128)(2,1)S(1)}, u32[]{:S(2)}, u32[]{:S(2)}) collective-permute-start(bf16[160,512]{1,0:T(8,128)(2,1)S(1)} %get-tuple-element.76), channel_id=1, source_target_pairs={{0,8},{4,12},{8,0},{12,4},{16,24},{20,28},{24,16},{28,20},{1,9},{5... | collective-permute-start | bytes 491528 | tf_op jit(solution)/shard_map/ppermute | solution.py:475
  19.1 1.9 %collective-permute-start.6 = (bf16[160,512]{1,0:T(8,128)(2,1)S(1)}, bf16[160,512]{1,0:T(8,128)(2,1)S(1)}, u32[]{:S(2)}, u32[]{:S(2)}) collective-permute-start(bf16[160,512]{1,0:T(8,128)(2,1)S(1)} %get-tuple-element.76), channel_id=1, source_target_pairs={{0,16},{4,20},{8,24},{12,28},{16,0},{20,4},{24,8},{28,12},{1,17},{... | collective-permute-start | bytes 491528 | tf_op jit(solution)/shard_map/ppermute | solution.py:475
  20.9 2.5 %collective-permute-done.5 = bf16[160,512]{1,0:T(8,128)(2,1)S(1)} collective-permute-done((bf16[160,512]{1,0:T(8,128)(2,1)S(1)}, bf16[160,512]{1,0:T(8,128)(2,1)S(1)}, u32[]{:S(2)}, u32[]{:S(2)}) %collective-permute-start.5) | collective-permute-done | bytes 163872 | tf_op jit(solution)/shard_map/ppermute | solution.py:475
  23.4 3.9 %collective-permute-done.6 = bf16[160,512]{1,0:T(8,128)(2,1)S(1)} collective-permute-done((bf16[160,512]{1,0:T(8,128)(2,1)S(1)}, bf16[160,512]{1,0:T(8,128)(2,1)S(1)}, u32[]{:S(2)}, u32[]{:S(2)}) %collective-permute-start.6) | collective-permute-done | bytes 163872 | tf_op jit(solution)/shard_map/ppermute | solution.py:475
  27.6 1.3 %mask.1 = (f32[1280,256]{1,0:T(8,128)S(1)}, f32[8,128]{1,0:T(8,128)S(1)}) custom-call(s32[8]{0:T(128)S(1)} %copy-done.2, bf16[256,2048]{1,0:T(8,128)(2,1)S(1)} %copy-done), custom_call_target="tpu_custom_call" | custom-call | tf_op jit(solution)/shard_map/mask/pallas_call | solution.py:33
  28.9 0.9 turn.1
  29.8 0.6 collective-permute-done.8.got_ref
  30.5 38.0 %attention.1 = (bf16[256,2048]{1,0:T(8,128)(2,1)}, bf16[256,2048]{1,0:T(8,128)(2,1)}, f32[1408,512]{1,0:T(8,128)S(1)}, bf16[1152,512]{1,0:T(8,128)(2,1)S(1)}) custom-call(bf16[256,2048]{1,0:T(8,128)(2,1)S(1)} %copy-done, bf16[256,2048]{1,0:T(8,128)(2,1)S(1)} %copy-done.3, bf16[1152,512]{1,0:T(8,128)(2,1)S(1)} %select_dynamic-update-slice_fusion.sent_ref, ...), custom_call_target="tpu_custom_call" | custom-call | flops 16106127360 | bytes 4194304 | tf_op jit(solution)/shard_map/attention/pallas_call | solution.py:434
  68.5 0.1 collective-permute-start.9
  68.6 2.7 %collective-permute-done.9.got_ref = bf16[1152,512]{1,0:T(8,128)(2,1)S(1)} collective-permute-done((bf16[1152,512]{1,0:T(8,128)(2,1)S(1)}, bf16[1152,512]{1,0:T(8,128)(2,1)S(1)}, u32[]{:S(2)}, u32[]{:S(2)}) %collective-permute-start.9) | collective-permute-done | bytes 1179680 | tf_op jit(solution)/shard_map/ppermute | solution.py:480
  71.3 0.3 merge.1
  71.6 0.4 collective-permute-start.14
  72.1 1.6 %collective-permute-start.15 = (bf16[160,512]{1,0:T(8,128)(2,1)S(1)}, bf16[160,512]{1,0:T(8,128)(2,1)S(1)}, u32[]{:S(2)}, u32[]{:S(2)}) collective-permute-start(bf16[160,512]{1,0:T(8,128)(2,1)S(1)} %get-tuple-element.66), channel_id=1, source_target_pairs={{0,16},{4,20},{8,24},{12,28},{16,0},{20,4},{24,8},{28,12},{1,17},{... | collective-permute-start | bytes 491528 | tf_op jit(solution)/shard_map/ppermute | solution.py:475
  73.6 1.5 %collective-permute-start.16 = (bf16[160,512]{1,0:T(8,128)(2,1)S(1)}, bf16[160,512]{1,0:T(8,128)(2,1)S(1)}, u32[]{:S(2)}, u32[]{:S(2)}) collective-permute-start(bf16[160,512]{1,0:T(8,128)(2,1)S(1)} %get-tuple-element.67), channel_id=1, source_target_pairs={{0,24},{4,28},{8,16},{12,20},{16,8},{20,12},{24,0},{28,4},{1,25},{... | collective-permute-start | bytes 491528 | tf_op jit(solution)/shard_map/ppermute | solution.py:475
  75.2 2.3 %collective-permute-start.10 = (bf16[128,512]{1,0:T(8,128)(2,1)S(1)}, bf16[128,512]{1,0:T(8,128)(2,1)S(1)}, u32[]{:S(2)}, u32[]{:S(2)}) collective-permute-start(bf16[128,512]{1,0:T(8,128)(2,1)S(1)} %get-tuple-element.60), channel_id=1, source_target_pairs={{8,0},{12,4},{16,8},{20,12},{24,16},{28,20},{9,1},{13,5},{17,9},{2... | collective-permute-start | bytes 393224 | tf_op jit(solution)/shard_map/ppermute | solution.py:486
  77.5 4.6 %collective-permute-start.11 = (bf16[128,512]{1,0:T(8,128)(2,1)S(1)}, bf16[128,512]{1,0:T(8,128)(2,1)S(1)}, u32[]{:S(2)}, u32[]{:S(2)}) collective-permute-start(bf16[128,512]{1,0:T(8,128)(2,1)S(1)} %get-tuple-element.61), channel_id=1, source_target_pairs={{8,0},{12,4},{16,8},{20,12},{24,16},{28,20},{9,1},{13,5},{17,9},{2... | collective-permute-start | bytes 393224 | tf_op jit(solution)/shard_map/ppermute | solution.py:486
  82.1 1.3 %collective-permute-start.12 = (bf16[128,512]{1,0:T(8,128)(2,1)S(1)}, bf16[128,512]{1,0:T(8,128)(2,1)S(1)}, u32[]{:S(2)}, u32[]{:S(2)}) collective-permute-start(bf16[128,512]{1,0:T(8,128)(2,1)S(1)} %get-tuple-element.62), channel_id=1, source_target_pairs={{16,0},{20,4},{24,8},{28,12},{17,1},{21,5},{25,9},{29,13},{18,2},{... | collective-permute-start | bytes 393224 | tf_op jit(solution)/shard_map/ppermute | solution.py:486
  83.4 7.3 %collective-permute-start.13 = (bf16[128,512]{1,0:T(8,128)(2,1)S(1)}, bf16[128,512]{1,0:T(8,128)(2,1)S(1)}, u32[]{:S(2)}, u32[]{:S(2)}) collective-permute-start(bf16[128,512]{1,0:T(8,128)(2,1)S(1)} %get-tuple-element.63), channel_id=1, source_target_pairs={{16,0},{20,4},{24,8},{28,12},{17,1},{21,5},{25,9},{29,13},{18,2},{... | collective-permute-start | bytes 393224 | tf_op jit(solution)/shard_map/ppermute | solution.py:486
  90.8 0.1 sum_chips.1
  91.0 4.3 %collective-permute-start.19 = (bf16[40,512]{1,0:T(8,128)(2,1)S(1)}, bf16[40,512]{1,0:T(8,128)(2,1)S(1)}, u32[]{:S(2)}, u32[]{:S(2)}) collective-permute-start(bf16[40,512]{1,0:T(8,128)(2,1)S(1)} %get-tuple-element.71), channel_id=1, source_target_pairs={{0,3},{1,2},{2,1},{3,0},{4,7},{5,6},{6,5},{7,4},{8,11},{9,10},{10,... | collective-permute-start | bytes 122888 | tf_op jit(solution)/shard_map/ppermute | solution.py:470
  95.3 0.6 collective-permute-done.18.refs_6_
  95.9 1.8 %collective-permute-done.19.refs_7_ = bf16[40,512]{1,0:T(8,128)(2,1)S(1)} collective-permute-done((bf16[40,512]{1,0:T(8,128)(2,1)S(1)}, bf16[40,512]{1,0:T(8,128)(2,1)S(1)}, u32[]{:S(2)}, u32[]{:S(2)}) %collective-permute-start.19) | collective-permute-done | bytes 40992 | tf_op jit(solution)/shard_map/ppermute | solution.py:470
  97.7 0.8 finish.1
  (32 shorter events, 0.4 us)
Async XLA Ops:
  2.5 24.9 %copy-start.1 = (bf16[256,512]{1,0:T(8,128)(2,1)S(1)}, bf16[256,512]{1,0:T(8,128)(2,1)}, u32[]{:S(2)}) copy-start(bf16[256,512]{1,0:T(8,128)(2,1)} %get-tuple-element.45.own_ref) | copy-start | bytes 786436
  2.5 13.0 %collective-permute-start.4 = (bf16[256,512]{1,0:T(8,128)(2,1)}, bf16[256,512]{1,0:T(8,128)(2,1)S(1)}, u32[]{:S(2)}, u32[]{:S(2)}) collective-permute-start(bf16[256,512]{1,0:T(8,128)(2,1)} %get-tuple-element.45.own_ref), channel_id=1, source_target_pairs={{0,16},{4,20},{8,24},{12,28},{1,17},{5,21},{9,25},{13,29},{2,18},{... | collective-permute-start | bytes 786440 | tf_op jit(solution)/shard_map/ppermute | solution.py:486
  3.9 11.5 %collective-permute-start.3 = (bf16[256,512]{1,0:T(8,128)(2,1)}, bf16[256,512]{1,0:T(8,128)(2,1)S(1)}, u32[]{:S(2)}, u32[]{:S(2)}) collective-permute-start(bf16[256,512]{1,0:T(8,128)(2,1)} %get-tuple-element.45.own_ref), channel_id=1, source_target_pairs={{0,8},{4,12},{8,16},{12,20},{16,24},{20,28},{1,9},{5,13},{9,17},{1... | collective-permute-start | bytes 786440 | tf_op jit(solution)/shard_map/ppermute | solution.py:486
  5.2 5.2 %collective-permute-start = (bf16[40,512]{1,0:T(8,128)(2,1)}, bf16[40,512]{1,0:T(8,128)(2,1)S(1)}, u32[]{:S(2)}, u32[]{:S(2)}) collective-permute-start(bf16[40,512]{1,0:T(8,128)(2,1)} %get-tuple-element.42), channel_id=1, source_target_pairs={{0,1},{1,0},{2,3},{3,2},{4,5},{5,4},{6,7},{7,6},{8,9},{9,8},{10,11... | collective-permute-start | bytes 122888 | tf_op jit(solution)/shard_map/ppermute | solution.py:470
  6.9 5.9 %collective-permute-start.1 = (bf16[40,512]{1,0:T(8,128)(2,1)}, bf16[40,512]{1,0:T(8,128)(2,1)S(1)}, u32[]{:S(2)}, u32[]{:S(2)}) collective-permute-start(bf16[40,512]{1,0:T(8,128)(2,1)} %get-tuple-element.43), channel_id=1, source_target_pairs={{0,2},{1,3},{2,0},{3,1},{4,6},{5,7},{6,4},{7,5},{8,10},{9,11},{10,... | collective-permute-start | bytes 122888 | tf_op jit(solution)/shard_map/ppermute | solution.py:470
  9.5 6.0 %collective-permute-start.2 = (bf16[40,512]{1,0:T(8,128)(2,1)}, bf16[40,512]{1,0:T(8,128)(2,1)S(1)}, u32[]{:S(2)}, u32[]{:S(2)}) collective-permute-start(bf16[40,512]{1,0:T(8,128)(2,1)} %get-tuple-element.44), channel_id=1, source_target_pairs={{0,3},{1,2},{2,1},{3,0},{4,7},{5,6},{6,5},{7,4},{8,11},{9,10},{10,... | collective-permute-start | bytes 122888 | tf_op jit(solution)/shard_map/ppermute | solution.py:470
  15.5 12.1 %copy-start = (bf16[256,2048]{1,0:T(8,128)(2,1)S(1)}, bf16[256,2048]{1,0:T(8,128)(2,1)}, u32[]{:S(2)}) copy-start(bf16[256,2048]{1,0:T(8,128)(2,1)} %q_ref.3) | copy-start | bytes 3145732
  15.5 12.1 %copy-start.2 = (s32[8]{0:T(128)S(1)}, s32[8]{0:T(128)}, u32[]{:S(2)}) copy-start(s32[8]{0:T(128)} %lengths.1) | copy-start | bytes 100
  15.6 7.9 %collective-permute-start.5 = (bf16[160,512]{1,0:T(8,128)(2,1)S(1)}, bf16[160,512]{1,0:T(8,128)(2,1)S(1)}, u32[]{:S(2)}, u32[]{:S(2)}) collective-permute-start(bf16[160,512]{1,0:T(8,128)(2,1)S(1)} %get-tuple-element.76), channel_id=1, source_target_pairs={{0,8},{4,12},{8,0},{12,4},{16,24},{20,28},{24,16},{28,20},{1,9},{5... | collective-permute-start | bytes 491528 | tf_op jit(solution)/shard_map/ppermute | solution.py:475
  19.1 8.3 %collective-permute-start.6 = (bf16[160,512]{1,0:T(8,128)(2,1)S(1)}, bf16[160,512]{1,0:T(8,128)(2,1)S(1)}, u32[]{:S(2)}, u32[]{:S(2)}) collective-permute-start(bf16[160,512]{1,0:T(8,128)(2,1)S(1)} %get-tuple-element.76), channel_id=1, source_target_pairs={{0,16},{4,20},{8,24},{12,28},{16,0},{20,4},{24,8},{28,12},{1,17},{... | collective-permute-start | bytes 491528 | tf_op jit(solution)/shard_map/ppermute | solution.py:475
  20.9 6.5 %collective-permute-start.7 = (bf16[160,512]{1,0:T(8,128)(2,1)S(1)}, bf16[160,512]{1,0:T(8,128)(2,1)S(1)}, u32[]{:S(2)}, u32[]{:S(2)}) collective-permute-start(bf16[160,512]{1,0:T(8,128)(2,1)S(1)} %get-tuple-element.76), channel_id=1, source_target_pairs={{0,24},{4,28},{8,16},{12,20},{16,8},{20,12},{24,0},{28,4},{1,25},{... | collective-permute-start | bytes 491528 | tf_op jit(solution)/shard_map/ppermute | solution.py:475
  27.5 2.9 %copy-start.3 = (bf16[256,2048]{1,0:T(8,128)(2,1)S(1)}, bf16[256,2048]{1,0:T(8,128)(2,1)}, u32[]{:S(2)}) copy-start(bf16[256,2048]{1,0:T(8,128)(2,1)} %do_ref.1) | copy-start | bytes 3145732
  27.5 2.9 %collective-permute-start.8 = (bf16[1152,512]{1,0:T(8,128)(2,1)S(1)}, bf16[1152,512]{1,0:T(8,128)(2,1)S(1)}, u32[]{:S(2)}, u32[]{:S(2)}) collective-permute-start(bf16[1152,512]{1,0:T(8,128)(2,1)S(1)} %select_dynamic-update-slice_fusion.sent_ref), channel_id=1, source_target_pairs={{0,4},{4,0},{8,12},{12,8},{16,20},{20,16},{24,28},{28,24},{1,5},{5... | collective-permute-start | bytes 3538952 | tf_op jit(solution)/shard_map/ppermute | solution.py:480
  68.5 2.8 %collective-permute-start.9 = (bf16[1152,512]{1,0:T(8,128)(2,1)S(1)}, bf16[1152,512]{1,0:T(8,128)(2,1)S(1)}, u32[]{:S(2)}, u32[]{:S(2)}) collective-permute-start(bf16[1152,512]{1,0:T(8,128)(2,1)S(1)} %get-tuple-element.58), channel_id=1, source_target_pairs={{0,4},{4,0},{8,12},{12,8},{16,20},{20,16},{24,28},{28,24},{1,5},{5... | collective-permute-start | bytes 3538952 | tf_op jit(solution)/shard_map/ppermute | solution.py:480
  71.6 10.5 %collective-permute-start.14 = (bf16[160,512]{1,0:T(8,128)(2,1)S(1)}, bf16[160,512]{1,0:T(8,128)(2,1)S(1)}, u32[]{:S(2)}, u32[]{:S(2)}) collective-permute-start(bf16[160,512]{1,0:T(8,128)(2,1)S(1)} %get-tuple-element.65), channel_id=1, source_target_pairs={{0,8},{4,12},{8,0},{12,4},{16,24},{20,28},{24,16},{28,20},{1,9},{5... | collective-permute-start | bytes 491528 | tf_op jit(solution)/shard_map/ppermute | solution.py:475
  72.1 11.4 %collective-permute-start.15 = (bf16[160,512]{1,0:T(8,128)(2,1)S(1)}, bf16[160,512]{1,0:T(8,128)(2,1)S(1)}, u32[]{:S(2)}, u32[]{:S(2)}) collective-permute-start(bf16[160,512]{1,0:T(8,128)(2,1)S(1)} %get-tuple-element.66), channel_id=1, source_target_pairs={{0,16},{4,20},{8,24},{12,28},{16,0},{20,4},{24,8},{28,12},{1,17},{... | collective-permute-start | bytes 491528 | tf_op jit(solution)/shard_map/ppermute | solution.py:475
  73.6 17.1 %collective-permute-start.16 = (bf16[160,512]{1,0:T(8,128)(2,1)S(1)}, bf16[160,512]{1,0:T(8,128)(2,1)S(1)}, u32[]{:S(2)}, u32[]{:S(2)}) collective-permute-start(bf16[160,512]{1,0:T(8,128)(2,1)S(1)} %get-tuple-element.67), channel_id=1, source_target_pairs={{0,24},{4,28},{8,16},{12,20},{16,8},{20,12},{24,0},{28,4},{1,25},{... | collective-permute-start | bytes 491528 | tf_op jit(solution)/shard_map/ppermute | solution.py:475
  75.2 15.8 %collective-permute-start.10 = (bf16[128,512]{1,0:T(8,128)(2,1)S(1)}, bf16[128,512]{1,0:T(8,128)(2,1)S(1)}, u32[]{:S(2)}, u32[]{:S(2)}) collective-permute-start(bf16[128,512]{1,0:T(8,128)(2,1)S(1)} %get-tuple-element.60), channel_id=1, source_target_pairs={{8,0},{12,4},{16,8},{20,12},{24,16},{28,20},{9,1},{13,5},{17,9},{2... | collective-permute-start | bytes 393224 | tf_op jit(solution)/shard_map/ppermute | solution.py:486
  77.5 13.6 %collective-permute-start.11 = (bf16[128,512]{1,0:T(8,128)(2,1)S(1)}, bf16[128,512]{1,0:T(8,128)(2,1)S(1)}, u32[]{:S(2)}, u32[]{:S(2)}) collective-permute-start(bf16[128,512]{1,0:T(8,128)(2,1)S(1)} %get-tuple-element.61), channel_id=1, source_target_pairs={{8,0},{12,4},{16,8},{20,12},{24,16},{28,20},{9,1},{13,5},{17,9},{2... | collective-permute-start | bytes 393224 | tf_op jit(solution)/shard_map/ppermute | solution.py:486
  82.1 13.2 %collective-permute-start.12 = (bf16[128,512]{1,0:T(8,128)(2,1)S(1)}, bf16[128,512]{1,0:T(8,128)(2,1)S(1)}, u32[]{:S(2)}, u32[]{:S(2)}) collective-permute-start(bf16[128,512]{1,0:T(8,128)(2,1)S(1)} %get-tuple-element.62), channel_id=1, source_target_pairs={{16,0},{20,4},{24,8},{28,12},{17,1},{21,5},{25,9},{29,13},{18,2},{... | collective-permute-start | bytes 393224 | tf_op jit(solution)/shard_map/ppermute | solution.py:486
  83.4 11.9 %collective-permute-start.13 = (bf16[128,512]{1,0:T(8,128)(2,1)S(1)}, bf16[128,512]{1,0:T(8,128)(2,1)S(1)}, u32[]{:S(2)}, u32[]{:S(2)}) collective-permute-start(bf16[128,512]{1,0:T(8,128)(2,1)S(1)} %get-tuple-element.63), channel_id=1, source_target_pairs={{16,0},{20,4},{24,8},{28,12},{17,1},{21,5},{25,9},{29,13},{18,2},{... | collective-permute-start | bytes 393224 | tf_op jit(solution)/shard_map/ppermute | solution.py:486
  90.9 4.5 %collective-permute-start.17 = (bf16[40,512]{1,0:T(8,128)(2,1)S(1)}, bf16[40,512]{1,0:T(8,128)(2,1)S(1)}, u32[]{:S(2)}, u32[]{:S(2)}) collective-permute-start(bf16[40,512]{1,0:T(8,128)(2,1)S(1)} %get-tuple-element.69), channel_id=1, source_target_pairs={{0,1},{1,0},{2,3},{3,2},{4,5},{5,4},{6,7},{7,6},{8,9},{9,8},{10,11... | collective-permute-start | bytes 122888 | tf_op jit(solution)/shard_map/ppermute | solution.py:470
  91.0 5.0 %collective-permute-start.18 = (bf16[40,512]{1,0:T(8,128)(2,1)S(1)}, bf16[40,512]{1,0:T(8,128)(2,1)S(1)}, u32[]{:S(2)}, u32[]{:S(2)}) collective-permute-start(bf16[40,512]{1,0:T(8,128)(2,1)S(1)} %get-tuple-element.70), channel_id=1, source_target_pairs={{0,2},{1,3},{2,0},{3,1},{4,6},{5,7},{6,4},{7,5},{8,10},{9,11},{10,... | collective-permute-start | bytes 122888 | tf_op jit(solution)/shard_map/ppermute | solution.py:470
  91.0 6.7 %collective-permute-start.19 = (bf16[40,512]{1,0:T(8,128)(2,1)S(1)}, bf16[40,512]{1,0:T(8,128)(2,1)S(1)}, u32[]{:S(2)}, u32[]{:S(2)}) collective-permute-start(bf16[40,512]{1,0:T(8,128)(2,1)S(1)} %get-tuple-element.71), channel_id=1, source_target_pairs={{0,3},{1,2},{2,1},{3,0},{4,7},{5,6},{6,5},{7,4},{8,11},{9,10},{10,... | collective-permute-start | bytes 122888 | tf_op jit(solution)/shard_map/ppermute | solution.py:470

commit v13 on v11

--- a/solution.py
+++ b/solution.py
@@ -11,8 +11,8 @@
 HD = 128
 CORES = 2
 FAR = 4
-CHUNK = 256
-LONGER = 640
+CHUNK = 640
+LONGER = 1280
 SAFE_SCORE = 40.0
 TILE = 64
 MOST_SCORES = 2560 * 256

time: 101 us -> 101 us (level)
  no operation moved by 1% of the time
where the time goes in v13:
time: 101 us
  Pallas kernels  45.4 us (45%)
  starting transfers between devices  36.2 us (36%)
  waiting for transfers between devices  17.2 us (17%)
    pallas_call x1, Pallas kernels, attention(): pl.pallas_call(functools.partial(attention_kernel, halves), in_specs=whol...  40.2 us
    ppermute x6, starting transfers between devices, shift_chips(): lax.ppermute(array, 'seq', [(i, i + by) for i in range(devices) if 0 <= i...  18.2 us
    ppermute x6, starting transfers between devices, swap_chips(): lax.ppermute(array, 'seq', [(i, i ^ by * CORES) for i in range(devices)])  8.93 us
    ppermute x6, starting transfers between devices, swap_heads(): return lax.ppermute(array, 'head', [(i, i ^ by) for i in range(devices)])  8.88 us
    ppermute x6, waiting for transfers between devices, swap_heads(): return lax.ppermute(array, 'head', [(i, i ^ by) for i in range(devices)])  7.4 us
    ppermute x6, waiting for transfers between devices, swap_chips(): lax.ppermute(array, 'seq', [(i, i ^ by * CORES) for i in range(devices)])  6.44 us
    pallas_call x5, Pallas kernels, local_call(): pl.pallas_call(kernel, in_specs=[pl.BlockSpec(memory_space=pltpu.SMEM)] *...  3.4 us
    ppermute x2, waiting for transfers between devices, swap_cores(): return lax.ppermute(array, 'seq', [(i, i ^ 1) for i in range(devices)])  3.33 us
  transfers between devices with their start and end apart: 20, of which 8 were waited for; matrix products, arithmetic and copies ran while one was open for 1% of the time, Pallas kernels for 2%

profile of v13, /device:TPU:6, one launch (start us, length us, event | category | flops | bytes accessed | tf_op | source)
XLA Modules:
  0.0 100.7 jit_solution(11101598056679492076)
XLA Ops:
  0.6 1.9 %pack.1 = (bf16[40,512]{1,0:T(8,128)(2,1)}, bf16[40,512]{1,0:T(8,128)(2,1)}, bf16[40,512]{1,0:T(8,128)(2,1)}, bf16[40,512]{1,0:T(8,128)(2,1)}, bf16[256,512]{1,0:T(8,128)(2,1)}) custom-call(bf16[40,1024]{1,0:T(8,128)(2,1)} %pk_ref.1, bf16[40,1024]{1,0:T(8,128)(2,1)} %pv_ref.1, bf16[256,256]{1,0:T(8,128)(2,1)} %rk_ref.1, bf16[256,256]{1,0:T(8,128)(2,1)} %rv_ref.1), custom_call_target="tpu_custom_call" | custom-call | tf_op jit(solution)/shard_map/pack/pallas_call | solution.py:66
  2.5 1.4 %collective-permute-start.4 = (bf16[256,512]{1,0:T(8,128)(2,1)}, bf16[256,512]{1,0:T(8,128)(2,1)S(1)}, u32[]{:S(2)}, u32[]{:S(2)}) collective-permute-start(bf16[256,512]{1,0:T(8,128)(2,1)} %get-tuple-element.45.own_ref), channel_id=1, source_target_pairs={{0,16},{4,20},{8,24},{12,28},{1,17},{5,21},{9,25},{13,29},{2,18},{... | collective-permute-start | bytes 786440 | tf_op jit(solution)/shard_map/ppermute | solution.py:489
  3.9 1.3 %collective-permute-start.3 = (bf16[256,512]{1,0:T(8,128)(2,1)}, bf16[256,512]{1,0:T(8,128)(2,1)S(1)}, u32[]{:S(2)}, u32[]{:S(2)}) collective-permute-start(bf16[256,512]{1,0:T(8,128)(2,1)} %get-tuple-element.45.own_ref), channel_id=1, source_target_pairs={{0,8},{4,12},{8,16},{12,20},{16,24},{20,28},{1,9},{5,13},{9,17},{1... | collective-permute-start | bytes 786440 | tf_op jit(solution)/shard_map/ppermute | solution.py:489
  5.2 1.6 %collective-permute-start = (bf16[40,512]{1,0:T(8,128)(2,1)}, bf16[40,512]{1,0:T(8,128)(2,1)S(1)}, u32[]{:S(2)}, u32[]{:S(2)}) collective-permute-start(bf16[40,512]{1,0:T(8,128)(2,1)} %get-tuple-element.42), channel_id=1, source_target_pairs={{0,1},{1,0},{2,3},{3,2},{4,5},{5,4},{6,7},{7,6},{8,9},{9,8},{10,11... | collective-permute-start | bytes 122888 | tf_op jit(solution)/shard_map/ppermute | solution.py:473
  6.9 2.6 %collective-permute-start.1 = (bf16[40,512]{1,0:T(8,128)(2,1)}, bf16[40,512]{1,0:T(8,128)(2,1)S(1)}, u32[]{:S(2)}, u32[]{:S(2)}) collective-permute-start(bf16[40,512]{1,0:T(8,128)(2,1)} %get-tuple-element.43), channel_id=1, source_target_pairs={{0,2},{1,3},{2,0},{3,1},{4,6},{5,7},{6,4},{7,5},{8,10},{9,11},{10,... | collective-permute-start | bytes 122888 | tf_op jit(solution)/shard_map/ppermute | solution.py:473
  9.5 0.2 collective-permute-start.2
  9.7 0.8 constant_dynamic-update-slice_fusion.3
  10.5 2.3 %collective-permute-done.1 = bf16[40,512]{1,0:T(8,128)(2,1)S(1)} collective-permute-done((bf16[40,512]{1,0:T(8,128)(2,1)}, bf16[40,512]{1,0:T(8,128)(2,1)S(1)}, u32[]{:S(2)}, u32[]{:S(2)}) %collective-permute-start.1) | collective-permute-done | bytes 40992 | tf_op jit(solution)/shard_map/ppermute | solution.py:473
  12.8 2.7 %collective-permute-done.2 = bf16[40,512]{1,0:T(8,128)(2,1)S(1)} collective-permute-done((bf16[40,512]{1,0:T(8,128)(2,1)}, bf16[40,512]{1,0:T(8,128)(2,1)S(1)}, u32[]{:S(2)}, u32[]{:S(2)}) %collective-permute-start.2) | collective-permute-done | bytes 40992 | tf_op jit(solution)/shard_map/ppermute | solution.py:473
  15.6 3.5 %collective-permute-start.5 = (bf16[160,512]{1,0:T(8,128)(2,1)S(1)}, bf16[160,512]{1,0:T(8,128)(2,1)S(1)}, u32[]{:S(2)}, u32[]{:S(2)}) collective-permute-start(bf16[160,512]{1,0:T(8,128)(2,1)S(1)} %get-tuple-element.76), channel_id=1, source_target_pairs={{0,8},{4,12},{8,0},{12,4},{16,24},{20,28},{24,16},{28,20},{1,9},{5... | collective-permute-start | bytes 491528 | tf_op jit(solution)/shard_map/ppermute | solution.py:478
  19.1 1.9 %collective-permute-start.6 = (bf16[160,512]{1,0:T(8,128)(2,1)S(1)}, bf16[160,512]{1,0:T(8,128)(2,1)S(1)}, u32[]{:S(2)}, u32[]{:S(2)}) collective-permute-start(bf16[160,512]{1,0:T(8,128)(2,1)S(1)} %get-tuple-element.76), channel_id=1, source_target_pairs={{0,16},{4,20},{8,24},{12,28},{16,0},{20,4},{24,8},{28,12},{1,17},{... | collective-permute-start | bytes 491528 | tf_op jit(solution)/shard_map/ppermute | solution.py:478
  20.9 2.5 %collective-permute-done.5 = bf16[160,512]{1,0:T(8,128)(2,1)S(1)} collective-permute-done((bf16[160,512]{1,0:T(8,128)(2,1)S(1)}, bf16[160,512]{1,0:T(8,128)(2,1)S(1)}, u32[]{:S(2)}, u32[]{:S(2)}) %collective-permute-start.5) | collective-permute-done | bytes 163872 | tf_op jit(solution)/shard_map/ppermute | solution.py:478
  23.4 3.9 %collective-permute-done.6 = bf16[160,512]{1,0:T(8,128)(2,1)S(1)} collective-permute-done((bf16[160,512]{1,0:T(8,128)(2,1)S(1)}, bf16[160,512]{1,0:T(8,128)(2,1)S(1)}, u32[]{:S(2)}, u32[]{:S(2)}) %collective-permute-start.6) | collective-permute-done | bytes 163872 | tf_op jit(solution)/shard_map/ppermute | solution.py:478
  27.6 1.3 %mask.1 = (f32[1280,256]{1,0:T(8,128)S(1)}, f32[8,128]{1,0:T(8,128)S(1)}) custom-call(s32[8]{0:T(128)S(1)} %copy-done.2, bf16[256,2048]{1,0:T(8,128)(2,1)S(1)} %copy-done), custom_call_target="tpu_custom_call" | custom-call | tf_op jit(solution)/shard_map/mask/pallas_call | solution.py:33
  28.9 0.9 turn.1
  29.8 0.6 collective-permute-done.8.got_ref
  30.5 40.2 %attention.1 = (bf16[256,2048]{1,0:T(8,128)(2,1)}, bf16[256,2048]{1,0:T(8,128)(2,1)}, f32[1408,512]{1,0:T(8,128)S(1)}, bf16[1152,512]{1,0:T(8,128)(2,1)S(1)}) custom-call(bf16[256,2048]{1,0:T(8,128)(2,1)S(1)} %copy-done, bf16[256,2048]{1,0:T(8,128)(2,1)S(1)} %copy-done.3, bf16[1152,512]{1,0:T(8,128)(2,1)S(1)} %select_dynamic-update-slice_fusion.sent_ref, ...), custom_call_target="tpu_custom_call" | custom-call | flops 16106127360 | bytes 4194304 | tf_op jit(solution)/shard_map/attention/pallas_call | solution.py:437
  70.6 0.1 collective-permute-start.9
  70.7 2.7 %collective-permute-done.9.got_ref = bf16[1152,512]{1,0:T(8,128)(2,1)S(1)} collective-permute-done((bf16[1152,512]{1,0:T(8,128)(2,1)S(1)}, bf16[1152,512]{1,0:T(8,128)(2,1)S(1)}, u32[]{:S(2)}, u32[]{:S(2)}) %collective-permute-start.9) | collective-permute-done | bytes 1179680 | tf_op jit(solution)/shard_map/ppermute | solution.py:483
  73.5 0.3 merge.1
  73.8 0.4 collective-permute-start.14
  74.2 1.6 %collective-permute-start.15 = (bf16[160,512]{1,0:T(8,128)(2,1)S(1)}, bf16[160,512]{1,0:T(8,128)(2,1)S(1)}, u32[]{:S(2)}, u32[]{:S(2)}) collective-permute-start(bf16[160,512]{1,0:T(8,128)(2,1)S(1)} %get-tuple-element.66), channel_id=1, source_target_pairs={{0,16},{4,20},{8,24},{12,28},{16,0},{20,4},{24,8},{28,12},{1,17},{... | collective-permute-start | bytes 491528 | tf_op jit(solution)/shard_map/ppermute | solution.py:478
  75.8 1.6 %collective-permute-start.16 = (bf16[160,512]{1,0:T(8,128)(2,1)S(1)}, bf16[160,512]{1,0:T(8,128)(2,1)S(1)}, u32[]{:S(2)}, u32[]{:S(2)}) collective-permute-start(bf16[160,512]{1,0:T(8,128)(2,1)S(1)} %get-tuple-element.67), channel_id=1, source_target_pairs={{0,24},{4,28},{8,16},{12,20},{16,8},{20,12},{24,0},{28,4},{1,25},{... | collective-permute-start | bytes 491528 | tf_op jit(solution)/shard_map/ppermute | solution.py:478
  77.3 2.3 %collective-permute-start.10 = (bf16[128,512]{1,0:T(8,128)(2,1)S(1)}, bf16[128,512]{1,0:T(8,128)(2,1)S(1)}, u32[]{:S(2)}, u32[]{:S(2)}) collective-permute-start(bf16[128,512]{1,0:T(8,128)(2,1)S(1)} %get-tuple-element.60), channel_id=1, source_target_pairs={{8,0},{12,4},{16,8},{20,12},{24,16},{28,20},{9,1},{13,5},{17,9},{2... | collective-permute-start | bytes 393224 | tf_op jit(solution)/shard_map/ppermute | solution.py:489
  79.6 4.6 %collective-permute-start.11 = (bf16[128,512]{1,0:T(8,128)(2,1)S(1)}, bf16[128,512]{1,0:T(8,128)(2,1)S(1)}, u32[]{:S(2)}, u32[]{:S(2)}) collective-permute-start(bf16[128,512]{1,0:T(8,128)(2,1)S(1)} %get-tuple-element.61), channel_id=1, source_target_pairs={{8,0},{12,4},{16,8},{20,12},{24,16},{28,20},{9,1},{13,5},{17,9},{2... | collective-permute-start | bytes 393224 | tf_op jit(solution)/shard_map/ppermute | solution.py:489
  84.3 1.3 %collective-permute-start.12 = (bf16[128,512]{1,0:T(8,128)(2,1)S(1)}, bf16[128,512]{1,0:T(8,128)(2,1)S(1)}, u32[]{:S(2)}, u32[]{:S(2)}) collective-permute-start(bf16[128,512]{1,0:T(8,128)(2,1)S(1)} %get-tuple-element.62), channel_id=1, source_target_pairs={{16,0},{20,4},{24,8},{28,12},{17,1},{21,5},{25,9},{29,13},{18,2},{... | collective-permute-start | bytes 393224 | tf_op jit(solution)/shard_map/ppermute | solution.py:489
  85.6 7.3 %collective-permute-start.13 = (bf16[128,512]{1,0:T(8,128)(2,1)S(1)}, bf16[128,512]{1,0:T(8,128)(2,1)S(1)}, u32[]{:S(2)}, u32[]{:S(2)}) collective-permute-start(bf16[128,512]{1,0:T(8,128)(2,1)S(1)} %get-tuple-element.63), channel_id=1, source_target_pairs={{16,0},{20,4},{24,8},{28,12},{17,1},{21,5},{25,9},{29,13},{18,2},{... | collective-permute-start | bytes 393224 | tf_op jit(solution)/shard_map/ppermute | solution.py:489
  92.9 0.1 sum_chips.1
  93.2 4.3 %collective-permute-start.19 = (bf16[40,512]{1,0:T(8,128)(2,1)S(1)}, bf16[40,512]{1,0:T(8,128)(2,1)S(1)}, u32[]{:S(2)}, u32[]{:S(2)}) collective-permute-start(bf16[40,512]{1,0:T(8,128)(2,1)S(1)} %get-tuple-element.71), channel_id=1, source_target_pairs={{0,3},{1,2},{2,1},{3,0},{4,7},{5,6},{6,5},{7,4},{8,11},{9,10},{10,... | collective-permute-start | bytes 122888 | tf_op jit(solution)/shard_map/ppermute | solution.py:473
  97.5 0.6 collective-permute-done.18.refs_6_
  98.1 1.8 %collective-permute-done.19.refs_7_ = bf16[40,512]{1,0:T(8,128)(2,1)S(1)} collective-permute-done((bf16[40,512]{1,0:T(8,128)(2,1)S(1)}, bf16[40,512]{1,0:T(8,128)(2,1)S(1)}, u32[]{:S(2)}, u32[]{:S(2)}) %collective-permute-start.19) | collective-permute-done | bytes 40992 | tf_op jit(solution)/shard_map/ppermute | solution.py:473
  99.9 0.8 finish.1
  (32 shorter events, 0.4 us)
Async XLA Ops:
  2.5 24.9 %copy-start.1 = (bf16[256,512]{1,0:T(8,128)(2,1)S(1)}, bf16[256,512]{1,0:T(8,128)(2,1)}, u32[]{:S(2)}) copy-start(bf16[256,512]{1,0:T(8,128)(2,1)} %get-tuple-element.45.own_ref) | copy-start | bytes 786436
  2.5 13.0 %collective-permute-start.4 = (bf16[256,512]{1,0:T(8,128)(2,1)}, bf16[256,512]{1,0:T(8,128)(2,1)S(1)}, u32[]{:S(2)}, u32[]{:S(2)}) collective-permute-start(bf16[256,512]{1,0:T(8,128)(2,1)} %get-tuple-element.45.own_ref), channel_id=1, source_target_pairs={{0,16},{4,20},{8,24},{12,28},{1,17},{5,21},{9,25},{13,29},{2,18},{... | collective-permute-start | bytes 786440 | tf_op jit(solution)/shard_map/ppermute | solution.py:489
  3.9 11.5 %collective-permute-start.3 = (bf16[256,512]{1,0:T(8,128)(2,1)}, bf16[256,512]{1,0:T(8,128)(2,1)S(1)}, u32[]{:S(2)}, u32[]{:S(2)}) collective-permute-start(bf16[256,512]{1,0:T(8,128)(2,1)} %get-tuple-element.45.own_ref), channel_id=1, source_target_pairs={{0,8},{4,12},{8,16},{12,20},{16,24},{20,28},{1,9},{5,13},{9,17},{1... | collective-permute-start | bytes 786440 | tf_op jit(solution)/shard_map/ppermute | solution.py:489
  5.2 5.2 %collective-permute-start = (bf16[40,512]{1,0:T(8,128)(2,1)}, bf16[40,512]{1,0:T(8,128)(2,1)S(1)}, u32[]{:S(2)}, u32[]{:S(2)}) collective-permute-start(bf16[40,512]{1,0:T(8,128)(2,1)} %get-tuple-element.42), channel_id=1, source_target_pairs={{0,1},{1,0},{2,3},{3,2},{4,5},{5,4},{6,7},{7,6},{8,9},{9,8},{10,11... | collective-permute-start | bytes 122888 | tf_op jit(solution)/shard_map/ppermute | solution.py:473
  6.9 5.9 %collective-permute-start.1 = (bf16[40,512]{1,0:T(8,128)(2,1)}, bf16[40,512]{1,0:T(8,128)(2,1)S(1)}, u32[]{:S(2)}, u32[]{:S(2)}) collective-permute-start(bf16[40,512]{1,0:T(8,128)(2,1)} %get-tuple-element.43), channel_id=1, source_target_pairs={{0,2},{1,3},{2,0},{3,1},{4,6},{5,7},{6,4},{7,5},{8,10},{9,11},{10,... | collective-permute-start | bytes 122888 | tf_op jit(solution)/shard_map/ppermute | solution.py:473
  9.5 6.0 %collective-permute-start.2 = (bf16[40,512]{1,0:T(8,128)(2,1)}, bf16[40,512]{1,0:T(8,128)(2,1)S(1)}, u32[]{:S(2)}, u32[]{:S(2)}) collective-permute-start(bf16[40,512]{1,0:T(8,128)(2,1)} %get-tuple-element.44), channel_id=1, source_target_pairs={{0,3},{1,2},{2,1},{3,0},{4,7},{5,6},{6,5},{7,4},{8,11},{9,10},{10,... | collective-permute-start | bytes 122888 | tf_op jit(solution)/shard_map/ppermute | solution.py:473
  15.5 12.1 %copy-start = (bf16[256,2048]{1,0:T(8,128)(2,1)S(1)}, bf16[256,2048]{1,0:T(8,128)(2,1)}, u32[]{:S(2)}) copy-start(bf16[256,2048]{1,0:T(8,128)(2,1)} %q_ref.3) | copy-start | bytes 3145732
  15.5 12.1 %copy-start.2 = (s32[8]{0:T(128)S(1)}, s32[8]{0:T(128)}, u32[]{:S(2)}) copy-start(s32[8]{0:T(128)} %lengths.1) | copy-start | bytes 100
  15.6 7.9 %collective-permute-start.5 = (bf16[160,512]{1,0:T(8,128)(2,1)S(1)}, bf16[160,512]{1,0:T(8,128)(2,1)S(1)}, u32[]{:S(2)}, u32[]{:S(2)}) collective-permute-start(bf16[160,512]{1,0:T(8,128)(2,1)S(1)} %get-tuple-element.76), channel_id=1, source_target_pairs={{0,8},{4,12},{8,0},{12,4},{16,24},{20,28},{24,16},{28,20},{1,9},{5... | collective-permute-start | bytes 491528 | tf_op jit(solution)/shard_map/ppermute | solution.py:478
  19.1 8.3 %collective-permute-start.6 = (bf16[160,512]{1,0:T(8,128)(2,1)S(1)}, bf16[160,512]{1,0:T(8,128)(2,1)S(1)}, u32[]{:S(2)}, u32[]{:S(2)}) collective-permute-start(bf16[160,512]{1,0:T(8,128)(2,1)S(1)} %get-tuple-element.76), channel_id=1, source_target_pairs={{0,16},{4,20},{8,24},{12,28},{16,0},{20,4},{24,8},{28,12},{1,17},{... | collective-permute-start | bytes 491528 | tf_op jit(solution)/shard_map/ppermute | solution.py:478
  20.9 6.5 %collective-permute-start.7 = (bf16[160,512]{1,0:T(8,128)(2,1)S(1)}, bf16[160,512]{1,0:T(8,128)(2,1)S(1)}, u32[]{:S(2)}, u32[]{:S(2)}) collective-permute-start(bf16[160,512]{1,0:T(8,128)(2,1)S(1)} %get-tuple-element.76), channel_id=1, source_target_pairs={{0,24},{4,28},{8,16},{12,20},{16,8},{20,12},{24,0},{28,4},{1,25},{... | collective-permute-start | bytes 491528 | tf_op jit(solution)/shard_map/ppermute | solution.py:478
  27.5 2.9 %copy-start.3 = (bf16[256,2048]{1,0:T(8,128)(2,1)S(1)}, bf16[256,2048]{1,0:T(8,128)(2,1)}, u32[]{:S(2)}) copy-start(bf16[256,2048]{1,0:T(8,128)(2,1)} %do_ref.1) | copy-start | bytes 3145732
  27.5 2.9 %collective-permute-start.8 = (bf16[1152,512]{1,0:T(8,128)(2,1)S(1)}, bf16[1152,512]{1,0:T(8,128)(2,1)S(1)}, u32[]{:S(2)}, u32[]{:S(2)}) collective-permute-start(bf16[1152,512]{1,0:T(8,128)(2,1)S(1)} %select_dynamic-update-slice_fusion.sent_ref), channel_id=1, source_target_pairs={{0,4},{4,0},{8,12},{12,8},{16,20},{20,16},{24,28},{28,24},{1,5},{5... | collective-permute-start | bytes 3538952 | tf_op jit(solution)/shard_map/ppermute | solution.py:483
  70.6 2.8 %collective-permute-start.9 = (bf16[1152,512]{1,0:T(8,128)(2,1)S(1)}, bf16[1152,512]{1,0:T(8,128)(2,1)S(1)}, u32[]{:S(2)}, u32[]{:S(2)}) collective-permute-start(bf16[1152,512]{1,0:T(8,128)(2,1)S(1)} %get-tuple-element.58), channel_id=1, source_target_pairs={{0,4},{4,0},{8,12},{12,8},{16,20},{20,16},{24,28},{28,24},{1,5},{5... | collective-permute-start | bytes 3538952 | tf_op jit(solution)/shard_map/ppermute | solution.py:483
  73.8 10.5 %collective-permute-start.14 = (bf16[160,512]{1,0:T(8,128)(2,1)S(1)}, bf16[160,512]{1,0:T(8,128)(2,1)S(1)}, u32[]{:S(2)}, u32[]{:S(2)}) collective-permute-start(bf16[160,512]{1,0:T(8,128)(2,1)S(1)} %get-tuple-element.65), channel_id=1, source_target_pairs={{0,8},{4,12},{8,0},{12,4},{16,24},{20,28},{24,16},{28,20},{1,9},{5... | collective-permute-start | bytes 491528 | tf_op jit(solution)/shard_map/ppermute | solution.py:478
  74.2 11.4 %collective-permute-start.15 = (bf16[160,512]{1,0:T(8,128)(2,1)S(1)}, bf16[160,512]{1,0:T(8,128)(2,1)S(1)}, u32[]{:S(2)}, u32[]{:S(2)}) collective-permute-start(bf16[160,512]{1,0:T(8,128)(2,1)S(1)} %get-tuple-element.66), channel_id=1, source_target_pairs={{0,16},{4,20},{8,24},{12,28},{16,0},{20,4},{24,8},{28,12},{1,17},{... | collective-permute-start | bytes 491528 | tf_op jit(solution)/shard_map/ppermute | solution.py:478
  75.8 17.1 %collective-permute-start.16 = (bf16[160,512]{1,0:T(8,128)(2,1)S(1)}, bf16[160,512]{1,0:T(8,128)(2,1)S(1)}, u32[]{:S(2)}, u32[]{:S(2)}) collective-permute-start(bf16[160,512]{1,0:T(8,128)(2,1)S(1)} %get-tuple-element.67), channel_id=1, source_target_pairs={{0,24},{4,28},{8,16},{12,20},{16,8},{20,12},{24,0},{28,4},{1,25},{... | collective-permute-start | bytes 491528 | tf_op jit(solution)/shard_map/ppermute | solution.py:478
  77.3 15.7 %collective-permute-start.10 = (bf16[128,512]{1,0:T(8,128)(2,1)S(1)}, bf16[128,512]{1,0:T(8,128)(2,1)S(1)}, u32[]{:S(2)}, u32[]{:S(2)}) collective-permute-start(bf16[128,512]{1,0:T(8,128)(2,1)S(1)} %get-tuple-element.60), channel_id=1, source_target_pairs={{8,0},{12,4},{16,8},{20,12},{24,16},{28,20},{9,1},{13,5},{17,9},{2... | collective-permute-start | bytes 393224 | tf_op jit(solution)/shard_map/ppermute | solution.py:489
  79.6 13.6 %collective-permute-start.11 = (bf16[128,512]{1,0:T(8,128)(2,1)S(1)}, bf16[128,512]{1,0:T(8,128)(2,1)S(1)}, u32[]{:S(2)}, u32[]{:S(2)}) collective-permute-start(bf16[128,512]{1,0:T(8,128)(2,1)S(1)} %get-tuple-element.61), channel_id=1, source_target_pairs={{8,0},{12,4},{16,8},{20,12},{24,16},{28,20},{9,1},{13,5},{17,9},{2... | collective-permute-start | bytes 393224 | tf_op jit(solution)/shard_map/ppermute | solution.py:489
  84.3 13.2 %collective-permute-start.12 = (bf16[128,512]{1,0:T(8,128)(2,1)S(1)}, bf16[128,512]{1,0:T(8,128)(2,1)S(1)}, u32[]{:S(2)}, u32[]{:S(2)}) collective-permute-start(bf16[128,512]{1,0:T(8,128)(2,1)S(1)} %get-tuple-element.62), channel_id=1, source_target_pairs={{16,0},{20,4},{24,8},{28,12},{17,1},{21,5},{25,9},{29,13},{18,2},{... | collective-permute-start | bytes 393224 | tf_op jit(solution)/shard_map/ppermute | solution.py:489
  85.6 11.9 %collective-permute-start.13 = (bf16[128,512]{1,0:T(8,128)(2,1)S(1)}, bf16[128,512]{1,0:T(8,128)(2,1)S(1)}, u32[]{:S(2)}, u32[]{:S(2)}) collective-permute-start(bf16[128,512]{1,0:T(8,128)(2,1)S(1)} %get-tuple-element.63), channel_id=1, source_target_pairs={{16,0},{20,4},{24,8},{28,12},{17,1},{21,5},{25,9},{29,13},{18,2},{... | collective-permute-start | bytes 393224 | tf_op jit(solution)/shard_map/ppermute | solution.py:489
  93.0 4.5 %collective-permute-start.17 = (bf16[40,512]{1,0:T(8,128)(2,1)S(1)}, bf16[40,512]{1,0:T(8,128)(2,1)S(1)}, u32[]{:S(2)}, u32[]{:S(2)}) collective-permute-start(bf16[40,512]{1,0:T(8,128)(2,1)S(1)} %get-tuple-element.69), channel_id=1, source_target_pairs={{0,1},{1,0},{2,3},{3,2},{4,5},{5,4},{6,7},{7,6},{8,9},{9,8},{10,11... | collective-permute-start | bytes 122888 | tf_op jit(solution)/shard_map/ppermute | solution.py:473
  93.1 5.0 %collective-permute-start.18 = (bf16[40,512]{1,0:T(8,128)(2,1)S(1)}, bf16[40,512]{1,0:T(8,128)(2,1)S(1)}, u32[]{:S(2)}, u32[]{:S(2)}) collective-permute-start(bf16[40,512]{1,0:T(8,128)(2,1)S(1)} %get-tuple-element.70), channel_id=1, source_target_pairs={{0,2},{1,3},{2,0},{3,1},{4,6},{5,7},{6,4},{7,5},{8,10},{9,11},{10,... | collective-permute-start | bytes 122888 | tf_op jit(solution)/shard_map/ppermute | solution.py:473
  93.2 6.7 %collective-permute-start.19 = (bf16[40,512]{1,0:T(8,128)(2,1)S(1)}, bf16[40,512]{1,0:T(8,128)(2,1)S(1)}, u32[]{:S(2)}, u32[]{:S(2)}) collective-permute-start(bf16[40,512]{1,0:T(8,128)(2,1)S(1)} %get-tuple-element.71), channel_id=1, source_target_pairs={{0,3},{1,2},{2,1},{3,0},{4,7},{5,6},{6,5},{7,4},{8,11},{9,10},{10,... | collective-permute-start | bytes 122888 | tf_op jit(solution)/shard_map/ppermute | solution.py:473

commit v14 on v11

--- a/solution.py
+++ b/solution.py
@@ -328,16 +328,14 @@
         state = {}
         work, finish = weigh(which, step, fast)
         started = not isinstance(step, int)
-        late = key_grads(which, step - 1) if started else []
-        first = query_grads(which, step - 1) if started else []
+        first = key_grads(which, step - 1) if started else []
+        second = query_grads(which, step - 1) if started else []
         if started or which == 1:
             first = settled(before, before_step, state) + first
-        together(work, first + late[: len(late) // 2])
+            second = second + value_grads(before, before_step)
+        together(work, first)
         if started or which == 1:
-            together(
-                slopes(before, before_step, state),
-                late[len(late) // 2 :] + value_grads(before, before_step),
-            )
+            together(slopes(before, before_step, state), second)
         finish()
 
     def together(vector, matrix):
@@ -391,10 +389,10 @@
     pl.when(small)(functools.partial(run, True))
     pl.when(jnp.logical_not(small))(functools.partial(run, False))
     state = {}
-    for work in settled(1, steps - 1, state) + query_grads(0, steps - 1):
+    for work in settled(1, steps - 1, state) + key_grads(0, steps - 1):
         work()
     together(
-        slopes(1, steps - 1, state), key_grads(0, steps - 1) + value_grads(1, steps - 1)
+        slopes(1, steps - 1, state), query_grads(0, steps - 1) + value_grads(1, steps - 1)
     )
     for work in key_grads(1, steps - 1) + query_grads(1, steps - 1):
         work()

time: 101 us -> 100 us (0.990)
  no operation moved by 1% of the time
where the time goes in v14:
time: 100 us
  Pallas kernels  44.9 us (45%)
  starting transfers between devices  36.2 us (36%)
  waiting for transfers between devices  17.2 us (17%)
    pallas_call x1, Pallas kernels, attention(): pl.pallas_call(functools.partial(attention_kernel, halves), in_specs=whol...  39.6 us
    ppermute x6, starting transfers between devices, shift_chips(): lax.ppermute(array, 'seq', [(i, i + by) for i in range(devices) if 0 <= i...  18.2 us
    ppermute x6, starting transfers between devices, swap_chips(): lax.ppermute(array, 'seq', [(i, i ^ by * CORES) for i in range(devices)])  8.93 us
    ppermute x6, starting transfers between devices, swap_heads(): return lax.ppermute(array, 'head', [(i, i ^ by) for i in range(devices)])  8.88 us
    ppermute x6, waiting for transfers between devices, swap_heads(): return lax.ppermute(array, 'head', [(i, i ^ by) for i in range(devices)])  7.4 us
    ppermute x6, waiting for transfers between devices, swap_chips(): lax.ppermute(array, 'seq', [(i, i ^ by * CORES) for i in range(devices)])  6.44 us
    pallas_call x5, Pallas kernels, local_call(): pl.pallas_call(kernel, in_specs=[pl.BlockSpec(memory_space=pltpu.SMEM)] *...  3.4 us
    ppermute x2, waiting for transfers between devices, swap_cores(): return lax.ppermute(array, 'seq', [(i, i ^ 1) for i in range(devices)])  3.34 us
  transfers between devices with their start and end apart: 20, of which 8 were waited for; matrix products, arithmetic and copies ran while one was open for 1% of the time, Pallas kernels for 2%

profile of v14, /device:TPU:6, one launch (start us, length us, event | category | flops | bytes accessed | tf_op | source)
XLA Modules:
  0.0 100.2 jit_solution(4829741440855049368)
XLA Ops:
  0.6 1.9 %pack.1 = (bf16[40,512]{1,0:T(8,128)(2,1)}, bf16[40,512]{1,0:T(8,128)(2,1)}, bf16[40,512]{1,0:T(8,128)(2,1)}, bf16[40,512]{1,0:T(8,128)(2,1)}, bf16[256,512]{1,0:T(8,128)(2,1)}) custom-call(bf16[40,1024]{1,0:T(8,128)(2,1)} %pk_ref.1, bf16[40,1024]{1,0:T(8,128)(2,1)} %pv_ref.1, bf16[256,256]{1,0:T(8,128)(2,1)} %rk_ref.1, bf16[256,256]{1,0:T(8,128)(2,1)} %rv_ref.1), custom_call_target="tpu_custom_call" | custom-call | tf_op jit(solution)/shard_map/pack/pallas_call | solution.py:66
  2.5 1.4 %collective-permute-start.4 = (bf16[256,512]{1,0:T(8,128)(2,1)}, bf16[256,512]{1,0:T(8,128)(2,1)S(1)}, u32[]{:S(2)}, u32[]{:S(2)}) collective-permute-start(bf16[256,512]{1,0:T(8,128)(2,1)} %get-tuple-element.45.own_ref), channel_id=1, source_target_pairs={{0,16},{4,20},{8,24},{12,28},{1,17},{5,21},{9,25},{13,29},{2,18},{... | collective-permute-start | bytes 786440 | tf_op jit(solution)/shard_map/ppermute | solution.py:487
  3.9 1.3 %collective-permute-start.3 = (bf16[256,512]{1,0:T(8,128)(2,1)}, bf16[256,512]{1,0:T(8,128)(2,1)S(1)}, u32[]{:S(2)}, u32[]{:S(2)}) collective-permute-start(bf16[256,512]{1,0:T(8,128)(2,1)} %get-tuple-element.45.own_ref), channel_id=1, source_target_pairs={{0,8},{4,12},{8,16},{12,20},{16,24},{20,28},{1,9},{5,13},{9,17},{1... | collective-permute-start | bytes 786440 | tf_op jit(solution)/shard_map/ppermute | solution.py:487
  5.2 1.6 %collective-permute-start = (bf16[40,512]{1,0:T(8,128)(2,1)}, bf16[40,512]{1,0:T(8,128)(2,1)S(1)}, u32[]{:S(2)}, u32[]{:S(2)}) collective-permute-start(bf16[40,512]{1,0:T(8,128)(2,1)} %get-tuple-element.42), channel_id=1, source_target_pairs={{0,1},{1,0},{2,3},{3,2},{4,5},{5,4},{6,7},{7,6},{8,9},{9,8},{10,11... | collective-permute-start | bytes 122888 | tf_op jit(solution)/shard_map/ppermute | solution.py:471
  6.9 2.6 %collective-permute-start.1 = (bf16[40,512]{1,0:T(8,128)(2,1)}, bf16[40,512]{1,0:T(8,128)(2,1)S(1)}, u32[]{:S(2)}, u32[]{:S(2)}) collective-permute-start(bf16[40,512]{1,0:T(8,128)(2,1)} %get-tuple-element.43), channel_id=1, source_target_pairs={{0,2},{1,3},{2,0},{3,1},{4,6},{5,7},{6,4},{7,5},{8,10},{9,11},{10,... | collective-permute-start | bytes 122888 | tf_op jit(solution)/shard_map/ppermute | solution.py:471
  9.5 0.2 collective-permute-start.2
  9.7 0.8 constant_dynamic-update-slice_fusion.3
  10.5 2.3 %collective-permute-done.1 = bf16[40,512]{1,0:T(8,128)(2,1)S(1)} collective-permute-done((bf16[40,512]{1,0:T(8,128)(2,1)}, bf16[40,512]{1,0:T(8,128)(2,1)S(1)}, u32[]{:S(2)}, u32[]{:S(2)}) %collective-permute-start.1) | collective-permute-done | bytes 40992 | tf_op jit(solution)/shard_map/ppermute | solution.py:471
  12.8 2.7 %collective-permute-done.2 = bf16[40,512]{1,0:T(8,128)(2,1)S(1)} collective-permute-done((bf16[40,512]{1,0:T(8,128)(2,1)}, bf16[40,512]{1,0:T(8,128)(2,1)S(1)}, u32[]{:S(2)}, u32[]{:S(2)}) %collective-permute-start.2) | collective-permute-done | bytes 40992 | tf_op jit(solution)/shard_map/ppermute | solution.py:471
  15.6 3.5 %collective-permute-start.5 = (bf16[160,512]{1,0:T(8,128)(2,1)S(1)}, bf16[160,512]{1,0:T(8,128)(2,1)S(1)}, u32[]{:S(2)}, u32[]{:S(2)}) collective-permute-start(bf16[160,512]{1,0:T(8,128)(2,1)S(1)} %get-tuple-element.76), channel_id=1, source_target_pairs={{0,8},{4,12},{8,0},{12,4},{16,24},{20,28},{24,16},{28,20},{1,9},{5... | collective-permute-start | bytes 491528 | tf_op jit(solution)/shard_map/ppermute | solution.py:476
  19.1 1.9 %collective-permute-start.6 = (bf16[160,512]{1,0:T(8,128)(2,1)S(1)}, bf16[160,512]{1,0:T(8,128)(2,1)S(1)}, u32[]{:S(2)}, u32[]{:S(2)}) collective-permute-start(bf16[160,512]{1,0:T(8,128)(2,1)S(1)} %get-tuple-element.76), channel_id=1, source_target_pairs={{0,16},{4,20},{8,24},{12,28},{16,0},{20,4},{24,8},{28,12},{1,17},{... | collective-permute-start | bytes 491528 | tf_op jit(solution)/shard_map/ppermute | solution.py:476
  20.9 2.5 %collective-permute-done.5 = bf16[160,512]{1,0:T(8,128)(2,1)S(1)} collective-permute-done((bf16[160,512]{1,0:T(8,128)(2,1)S(1)}, bf16[160,512]{1,0:T(8,128)(2,1)S(1)}, u32[]{:S(2)}, u32[]{:S(2)}) %collective-permute-start.5) | collective-permute-done | bytes 163872 | tf_op jit(solution)/shard_map/ppermute | solution.py:476
  23.4 3.9 %collective-permute-done.6 = bf16[160,512]{1,0:T(8,128)(2,1)S(1)} collective-permute-done((bf16[160,512]{1,0:T(8,128)(2,1)S(1)}, bf16[160,512]{1,0:T(8,128)(2,1)S(1)}, u32[]{:S(2)}, u32[]{:S(2)}) %collective-permute-start.6) | collective-permute-done | bytes 163872 | tf_op jit(solution)/shard_map/ppermute | solution.py:476
  27.6 1.3 %mask.1 = (f32[1280,256]{1,0:T(8,128)S(1)}, f32[8,128]{1,0:T(8,128)S(1)}) custom-call(s32[8]{0:T(128)S(1)} %copy-done.2, bf16[256,2048]{1,0:T(8,128)(2,1)S(1)} %copy-done), custom_call_target="tpu_custom_call" | custom-call | tf_op jit(solution)/shard_map/mask/pallas_call | solution.py:33
  28.9 0.9 turn.1
  29.8 0.6 collective-permute-done.8.got_ref
  30.5 39.6 %attention.1 = (bf16[256,2048]{1,0:T(8,128)(2,1)}, bf16[256,2048]{1,0:T(8,128)(2,1)}, f32[1408,512]{1,0:T(8,128)S(1)}, bf16[1152,512]{1,0:T(8,128)(2,1)S(1)}) custom-call(bf16[256,2048]{1,0:T(8,128)(2,1)S(1)} %copy-done, bf16[256,2048]{1,0:T(8,128)(2,1)S(1)} %copy-done.3, bf16[1152,512]{1,0:T(8,128)(2,1)S(1)} %select_dynamic-update-slice_fusion.sent_ref, ...), custom_call_target="tpu_custom_call" | custom-call | flops 16106127360 | bytes 4194304 | tf_op jit(solution)/shard_map/attention/pallas_call | solution.py:435
  70.1 0.1 collective-permute-start.9
  70.2 2.7 %collective-permute-done.9.got_ref = bf16[1152,512]{1,0:T(8,128)(2,1)S(1)} collective-permute-done((bf16[1152,512]{1,0:T(8,128)(2,1)S(1)}, bf16[1152,512]{1,0:T(8,128)(2,1)S(1)}, u32[]{:S(2)}, u32[]{:S(2)}) %collective-permute-start.9) | collective-permute-done | bytes 1179680 | tf_op jit(solution)/shard_map/ppermute | solution.py:481
  73.0 0.3 merge.1
  73.3 0.4 collective-permute-start.14
  73.7 1.6 %collective-permute-start.15 = (bf16[160,512]{1,0:T(8,128)(2,1)S(1)}, bf16[160,512]{1,0:T(8,128)(2,1)S(1)}, u32[]{:S(2)}, u32[]{:S(2)}) collective-permute-start(bf16[160,512]{1,0:T(8,128)(2,1)S(1)} %get-tuple-element.66), channel_id=1, source_target_pairs={{0,16},{4,20},{8,24},{12,28},{16,0},{20,4},{24,8},{28,12},{1,17},{... | collective-permute-start | bytes 491528 | tf_op jit(solution)/shard_map/ppermute | solution.py:476
  75.3 1.6 %collective-permute-start.16 = (bf16[160,512]{1,0:T(8,128)(2,1)S(1)}, bf16[160,512]{1,0:T(8,128)(2,1)S(1)}, u32[]{:S(2)}, u32[]{:S(2)}) collective-permute-start(bf16[160,512]{1,0:T(8,128)(2,1)S(1)} %get-tuple-element.67), channel_id=1, source_target_pairs={{0,24},{4,28},{8,16},{12,20},{16,8},{20,12},{24,0},{28,4},{1,25},{... | collective-permute-start | bytes 491528 | tf_op jit(solution)/shard_map/ppermute | solution.py:476
  76.8 2.3 %collective-permute-start.10 = (bf16[128,512]{1,0:T(8,128)(2,1)S(1)}, bf16[128,512]{1,0:T(8,128)(2,1)S(1)}, u32[]{:S(2)}, u32[]{:S(2)}) collective-permute-start(bf16[128,512]{1,0:T(8,128)(2,1)S(1)} %get-tuple-element.60), channel_id=1, source_target_pairs={{8,0},{12,4},{16,8},{20,12},{24,16},{28,20},{9,1},{13,5},{17,9},{2... | collective-permute-start | bytes 393224 | tf_op jit(solution)/shard_map/ppermute | solution.py:487
  79.1 4.6 %collective-permute-start.11 = (bf16[128,512]{1,0:T(8,128)(2,1)S(1)}, bf16[128,512]{1,0:T(8,128)(2,1)S(1)}, u32[]{:S(2)}, u32[]{:S(2)}) collective-permute-start(bf16[128,512]{1,0:T(8,128)(2,1)S(1)} %get-tuple-element.61), channel_id=1, source_target_pairs={{8,0},{12,4},{16,8},{20,12},{24,16},{28,20},{9,1},{13,5},{17,9},{2... | collective-permute-start | bytes 393224 | tf_op jit(solution)/shard_map/ppermute | solution.py:487
  83.7 1.3 %collective-permute-start.12 = (bf16[128,512]{1,0:T(8,128)(2,1)S(1)}, bf16[128,512]{1,0:T(8,128)(2,1)S(1)}, u32[]{:S(2)}, u32[]{:S(2)}) collective-permute-start(bf16[128,512]{1,0:T(8,128)(2,1)S(1)} %get-tuple-element.62), channel_id=1, source_target_pairs={{16,0},{20,4},{24,8},{28,12},{17,1},{21,5},{25,9},{29,13},{18,2},{... | collective-permute-start | bytes 393224 | tf_op jit(solution)/shard_map/ppermute | solution.py:487
  85.1 7.3 %collective-permute-start.13 = (bf16[128,512]{1,0:T(8,128)(2,1)S(1)}, bf16[128,512]{1,0:T(8,128)(2,1)S(1)}, u32[]{:S(2)}, u32[]{:S(2)}) collective-permute-start(bf16[128,512]{1,0:T(8,128)(2,1)S(1)} %get-tuple-element.63), channel_id=1, source_target_pairs={{16,0},{20,4},{24,8},{28,12},{17,1},{21,5},{25,9},{29,13},{18,2},{... | collective-permute-start | bytes 393224 | tf_op jit(solution)/shard_map/ppermute | solution.py:487
  92.4 0.1 sum_chips.1
  92.7 4.3 %collective-permute-start.19 = (bf16[40,512]{1,0:T(8,128)(2,1)S(1)}, bf16[40,512]{1,0:T(8,128)(2,1)S(1)}, u32[]{:S(2)}, u32[]{:S(2)}) collective-permute-start(bf16[40,512]{1,0:T(8,128)(2,1)S(1)} %get-tuple-element.71), channel_id=1, source_target_pairs={{0,3},{1,2},{2,1},{3,0},{4,7},{5,6},{6,5},{7,4},{8,11},{9,10},{10,... | collective-permute-start | bytes 122888 | tf_op jit(solution)/shard_map/ppermute | solution.py:471
  97.0 0.6 collective-permute-done.18.refs_6_
  97.5 1.8 %collective-permute-done.19.refs_7_ = bf16[40,512]{1,0:T(8,128)(2,1)S(1)} collective-permute-done((bf16[40,512]{1,0:T(8,128)(2,1)S(1)}, bf16[40,512]{1,0:T(8,128)(2,1)S(1)}, u32[]{:S(2)}, u32[]{:S(2)}) %collective-permute-start.19) | collective-permute-done | bytes 40992 | tf_op jit(solution)/shard_map/ppermute | solution.py:471
  99.4 0.8 finish.1
  (32 shorter events, 0.4 us)
Async XLA Ops:
  2.5 24.9 %copy-start.1 = (bf16[256,512]{1,0:T(8,128)(2,1)S(1)}, bf16[256,512]{1,0:T(8,128)(2,1)}, u32[]{:S(2)}) copy-start(bf16[256,512]{1,0:T(8,128)(2,1)} %get-tuple-element.45.own_ref) | copy-start | bytes 786436
  2.5 13.0 %collective-permute-start.4 = (bf16[256,512]{1,0:T(8,128)(2,1)}, bf16[256,512]{1,0:T(8,128)(2,1)S(1)}, u32[]{:S(2)}, u32[]{:S(2)}) collective-permute-start(bf16[256,512]{1,0:T(8,128)(2,1)} %get-tuple-element.45.own_ref), channel_id=1, source_target_pairs={{0,16},{4,20},{8,24},{12,28},{1,17},{5,21},{9,25},{13,29},{2,18},{... | collective-permute-start | bytes 786440 | tf_op jit(solution)/shard_map/ppermute | solution.py:487
  3.9 11.5 %collective-permute-start.3 = (bf16[256,512]{1,0:T(8,128)(2,1)}, bf16[256,512]{1,0:T(8,128)(2,1)S(1)}, u32[]{:S(2)}, u32[]{:S(2)}) collective-permute-start(bf16[256,512]{1,0:T(8,128)(2,1)} %get-tuple-element.45.own_ref), channel_id=1, source_target_pairs={{0,8},{4,12},{8,16},{12,20},{16,24},{20,28},{1,9},{5,13},{9,17},{1... | collective-permute-start | bytes 786440 | tf_op jit(solution)/shard_map/ppermute | solution.py:487
  5.2 5.2 %collective-permute-start = (bf16[40,512]{1,0:T(8,128)(2,1)}, bf16[40,512]{1,0:T(8,128)(2,1)S(1)}, u32[]{:S(2)}, u32[]{:S(2)}) collective-permute-start(bf16[40,512]{1,0:T(8,128)(2,1)} %get-tuple-element.42), channel_id=1, source_target_pairs={{0,1},{1,0},{2,3},{3,2},{4,5},{5,4},{6,7},{7,6},{8,9},{9,8},{10,11... | collective-permute-start | bytes 122888 | tf_op jit(solution)/shard_map/ppermute | solution.py:471
  6.9 5.9 %collective-permute-start.1 = (bf16[40,512]{1,0:T(8,128)(2,1)}, bf16[40,512]{1,0:T(8,128)(2,1)S(1)}, u32[]{:S(2)}, u32[]{:S(2)}) collective-permute-start(bf16[40,512]{1,0:T(8,128)(2,1)} %get-tuple-element.43), channel_id=1, source_target_pairs={{0,2},{1,3},{2,0},{3,1},{4,6},{5,7},{6,4},{7,5},{8,10},{9,11},{10,... | collective-permute-start | bytes 122888 | tf_op jit(solution)/shard_map/ppermute | solution.py:471
  9.5 6.0 %collective-permute-start.2 = (bf16[40,512]{1,0:T(8,128)(2,1)}, bf16[40,512]{1,0:T(8,128)(2,1)S(1)}, u32[]{:S(2)}, u32[]{:S(2)}) collective-permute-start(bf16[40,512]{1,0:T(8,128)(2,1)} %get-tuple-element.44), channel_id=1, source_target_pairs={{0,3},{1,2},{2,1},{3,0},{4,7},{5,6},{6,5},{7,4},{8,11},{9,10},{10,... | collective-permute-start | bytes 122888 | tf_op jit(solution)/shard_map/ppermute | solution.py:471
  15.5 12.1 %copy-start = (bf16[256,2048]{1,0:T(8,128)(2,1)S(1)}, bf16[256,2048]{1,0:T(8,128)(2,1)}, u32[]{:S(2)}) copy-start(bf16[256,2048]{1,0:T(8,128)(2,1)} %q_ref.3) | copy-start | bytes 3145732
  15.5 12.1 %copy-start.2 = (s32[8]{0:T(128)S(1)}, s32[8]{0:T(128)}, u32[]{:S(2)}) copy-start(s32[8]{0:T(128)} %lengths.1) | copy-start | bytes 100
  15.6 7.9 %collective-permute-start.5 = (bf16[160,512]{1,0:T(8,128)(2,1)S(1)}, bf16[160,512]{1,0:T(8,128)(2,1)S(1)}, u32[]{:S(2)}, u32[]{:S(2)}) collective-permute-start(bf16[160,512]{1,0:T(8,128)(2,1)S(1)} %get-tuple-element.76), channel_id=1, source_target_pairs={{0,8},{4,12},{8,0},{12,4},{16,24},{20,28},{24,16},{28,20},{1,9},{5... | collective-permute-start | bytes 491528 | tf_op jit(solution)/shard_map/ppermute | solution.py:476
  19.1 8.3 %collective-permute-start.6 = (bf16[160,512]{1,0:T(8,128)(2,1)S(1)}, bf16[160,512]{1,0:T(8,128)(2,1)S(1)}, u32[]{:S(2)}, u32[]{:S(2)}) collective-permute-start(bf16[160,512]{1,0:T(8,128)(2,1)S(1)} %get-tuple-element.76), channel_id=1, source_target_pairs={{0,16},{4,20},{8,24},{12,28},{16,0},{20,4},{24,8},{28,12},{1,17},{... | collective-permute-start | bytes 491528 | tf_op jit(solution)/shard_map/ppermute | solution.py:476
  20.9 6.5 %collective-permute-start.7 = (bf16[160,512]{1,0:T(8,128)(2,1)S(1)}, bf16[160,512]{1,0:T(8,128)(2,1)S(1)}, u32[]{:S(2)}, u32[]{:S(2)}) collective-permute-start(bf16[160,512]{1,0:T(8,128)(2,1)S(1)} %get-tuple-element.76), channel_id=1, source_target_pairs={{0,24},{4,28},{8,16},{12,20},{16,8},{20,12},{24,0},{28,4},{1,25},{... | collective-permute-start | bytes 491528 | tf_op jit(solution)/shard_map/ppermute | solution.py:476
  27.5 2.9 %copy-start.3 = (bf16[256,2048]{1,0:T(8,128)(2,1)S(1)}, bf16[256,2048]{1,0:T(8,128)(2,1)}, u32[]{:S(2)}) copy-start(bf16[256,2048]{1,0:T(8,128)(2,1)} %do_ref.1) | copy-start | bytes 3145732
  27.5 2.9 %collective-permute-start.8 = (bf16[1152,512]{1,0:T(8,128)(2,1)S(1)}, bf16[1152,512]{1,0:T(8,128)(2,1)S(1)}, u32[]{:S(2)}, u32[]{:S(2)}) collective-permute-start(bf16[1152,512]{1,0:T(8,128)(2,1)S(1)} %select_dynamic-update-slice_fusion.sent_ref), channel_id=1, source_target_pairs={{0,4},{4,0},{8,12},{12,8},{16,20},{20,16},{24,28},{28,24},{1,5},{5... | collective-permute-start | bytes 3538952 | tf_op jit(solution)/shard_map/ppermute | solution.py:481
  70.1 2.8 %collective-permute-start.9 = (bf16[1152,512]{1,0:T(8,128)(2,1)S(1)}, bf16[1152,512]{1,0:T(8,128)(2,1)S(1)}, u32[]{:S(2)}, u32[]{:S(2)}) collective-permute-start(bf16[1152,512]{1,0:T(8,128)(2,1)S(1)} %get-tuple-element.58), channel_id=1, source_target_pairs={{0,4},{4,0},{8,12},{12,8},{16,20},{20,16},{24,28},{28,24},{1,5},{5... | collective-permute-start | bytes 3538952 | tf_op jit(solution)/shard_map/ppermute | solution.py:481
  73.3 10.5 %collective-permute-start.14 = (bf16[160,512]{1,0:T(8,128)(2,1)S(1)}, bf16[160,512]{1,0:T(8,128)(2,1)S(1)}, u32[]{:S(2)}, u32[]{:S(2)}) collective-permute-start(bf16[160,512]{1,0:T(8,128)(2,1)S(1)} %get-tuple-element.65), channel_id=1, source_target_pairs={{0,8},{4,12},{8,0},{12,4},{16,24},{20,28},{24,16},{28,20},{1,9},{5... | collective-permute-start | bytes 491528 | tf_op jit(solution)/shard_map/ppermute | solution.py:476
  73.7 11.4 %collective-permute-start.15 = (bf16[160,512]{1,0:T(8,128)(2,1)S(1)}, bf16[160,512]{1,0:T(8,128)(2,1)S(1)}, u32[]{:S(2)}, u32[]{:S(2)}) collective-permute-start(bf16[160,512]{1,0:T(8,128)(2,1)S(1)} %get-tuple-element.66), channel_id=1, source_target_pairs={{0,16},{4,20},{8,24},{12,28},{16,0},{20,4},{24,8},{28,12},{1,17},{... | collective-permute-start | bytes 491528 | tf_op jit(solution)/shard_map/ppermute | solution.py:476
  75.3 17.1 %collective-permute-start.16 = (bf16[160,512]{1,0:T(8,128)(2,1)S(1)}, bf16[160,512]{1,0:T(8,128)(2,1)S(1)}, u32[]{:S(2)}, u32[]{:S(2)}) collective-permute-start(bf16[160,512]{1,0:T(8,128)(2,1)S(1)} %get-tuple-element.67), channel_id=1, source_target_pairs={{0,24},{4,28},{8,16},{12,20},{16,8},{20,12},{24,0},{28,4},{1,25},{... | collective-permute-start | bytes 491528 | tf_op jit(solution)/shard_map/ppermute | solution.py:476
  76.8 15.7 %collective-permute-start.10 = (bf16[128,512]{1,0:T(8,128)(2,1)S(1)}, bf16[128,512]{1,0:T(8,128)(2,1)S(1)}, u32[]{:S(2)}, u32[]{:S(2)}) collective-permute-start(bf16[128,512]{1,0:T(8,128)(2,1)S(1)} %get-tuple-element.60), channel_id=1, source_target_pairs={{8,0},{12,4},{16,8},{20,12},{24,16},{28,20},{9,1},{13,5},{17,9},{2... | collective-permute-start | bytes 393224 | tf_op jit(solution)/shard_map/ppermute | solution.py:487
  79.1 13.6 %collective-permute-start.11 = (bf16[128,512]{1,0:T(8,128)(2,1)S(1)}, bf16[128,512]{1,0:T(8,128)(2,1)S(1)}, u32[]{:S(2)}, u32[]{:S(2)}) collective-permute-start(bf16[128,512]{1,0:T(8,128)(2,1)S(1)} %get-tuple-element.61), channel_id=1, source_target_pairs={{8,0},{12,4},{16,8},{20,12},{24,16},{28,20},{9,1},{13,5},{17,9},{2... | collective-permute-start | bytes 393224 | tf_op jit(solution)/shard_map/ppermute | solution.py:487
  83.7 13.2 %collective-permute-start.12 = (bf16[128,512]{1,0:T(8,128)(2,1)S(1)}, bf16[128,512]{1,0:T(8,128)(2,1)S(1)}, u32[]{:S(2)}, u32[]{:S(2)}) collective-permute-start(bf16[128,512]{1,0:T(8,128)(2,1)S(1)} %get-tuple-element.62), channel_id=1, source_target_pairs={{16,0},{20,4},{24,8},{28,12},{17,1},{21,5},{25,9},{29,13},{18,2},{... | collective-permute-start | bytes 393224 | tf_op jit(solution)/shard_map/ppermute | solution.py:487
  85.1 11.9 %collective-permute-start.13 = (bf16[128,512]{1,0:T(8,128)(2,1)S(1)}, bf16[128,512]{1,0:T(8,128)(2,1)S(1)}, u32[]{:S(2)}, u32[]{:S(2)}) collective-permute-start(bf16[128,512]{1,0:T(8,128)(2,1)S(1)} %get-tuple-element.63), channel_id=1, source_target_pairs={{16,0},{20,4},{24,8},{28,12},{17,1},{21,5},{25,9},{29,13},{18,2},{... | collective-permute-start | bytes 393224 | tf_op jit(solution)/shard_map/ppermute | solution.py:487
  92.5 4.5 %collective-permute-start.17 = (bf16[40,512]{1,0:T(8,128)(2,1)S(1)}, bf16[40,512]{1,0:T(8,128)(2,1)S(1)}, u32[]{:S(2)}, u32[]{:S(2)}) collective-permute-start(bf16[40,512]{1,0:T(8,128)(2,1)S(1)} %get-tuple-element.69), channel_id=1, source_target_pairs={{0,1},{1,0},{2,3},{3,2},{4,5},{5,4},{6,7},{7,6},{8,9},{9,8},{10,11... | collective-permute-start | bytes 122888 | tf_op jit(solution)/shard_map/ppermute | solution.py:471
  92.6 5.0 %collective-permute-start.18 = (bf16[40,512]{1,0:T(8,128)(2,1)S(1)}, bf16[40,512]{1,0:T(8,128)(2,1)S(1)}, u32[]{:S(2)}, u32[]{:S(2)}) collective-permute-start(bf16[40,512]{1,0:T(8,128)(2,1)S(1)} %get-tuple-element.70), channel_id=1, source_target_pairs={{0,2},{1,3},{2,0},{3,1},{4,6},{5,7},{6,4},{7,5},{8,10},{9,11},{10,... | collective-permute-start | bytes 122888 | tf_op jit(solution)/shard_map/ppermute | solution.py:471
  92.7 6.7 %collective-permute-start.19 = (bf16[40,512]{1,0:T(8,128)(2,1)S(1)}, bf16[40,512]{1,0:T(8,128)(2,1)S(1)}, u32[]{:S(2)}, u32[]{:S(2)}) collective-permute-start(bf16[40,512]{1,0:T(8,128)(2,1)S(1)} %get-tuple-element.71), channel_id=1, source_target_pairs={{0,3},{1,2},{2,1},{3,0},{4,7},{5,6},{6,5},{7,4},{8,11},{9,10},{10,... | collective-permute-start | bytes 122888 | tf_op jit(solution)/shard_map/ppermute | solution.py:471

commit v15 on v14

--- a/solution.py
+++ b/solution.py
@@ -14,7 +14,7 @@
 CHUNK = 256
 LONGER = 640
 SAFE_SCORE = 40.0
-TILE = 64
+TILE = 32
 MOST_SCORES = 2560 * 256
 NEG = -1e30
 BF16 = jnp.bfloat16

time: 100 us -> 101 us (1.010)
  no operation moved by 1% of the time
where the time goes in v15:
time: 101 us; the launch traced here: 100 us
  Pallas kernels  45 us (45%)
  starting transfers between devices  36.2 us (36%)
  waiting for transfers between devices  17.2 us (17%)
    pallas_call x1, Pallas kernels, attention(): pl.pallas_call(functools.partial(attention_kernel, halves), in_specs=whol...  39.7 us
    ppermute x6, starting transfers between devices, shift_chips(): lax.ppermute(array, 'seq', [(i, i + by) for i in range(devices) if 0 <= i...  18.2 us
    ppermute x6, starting transfers between devices, swap_chips(): lax.ppermute(array, 'seq', [(i, i ^ by * CORES) for i in range(devices)])  8.93 us
    ppermute x6, starting transfers between devices, swap_heads(): return lax.ppermute(array, 'head', [(i, i ^ by) for i in range(devices)])  8.88 us
    ppermute x6, waiting for transfers between devices, swap_heads(): return lax.ppermute(array, 'head', [(i, i ^ by) for i in range(devices)])  7.4 us
    ppermute x6, waiting for transfers between devices, swap_chips(): lax.ppermute(array, 'seq', [(i, i ^ by * CORES) for i in range(devices)])  6.44 us
    pallas_call x5, Pallas kernels, local_call(): pl.pallas_call(kernel, in_specs=[pl.BlockSpec(memory_space=pltpu.SMEM)] *...  3.4 us
    ppermute x2, waiting for transfers between devices, swap_cores(): return lax.ppermute(array, 'seq', [(i, i ^ 1) for i in range(devices)])  3.33 us
  transfers between devices with their start and end apart: 20, of which 8 were waited for; matrix products, arithmetic and copies ran while one was open for 1% of the time, Pallas kernels for 2%

profile of v15, /device:TPU:6, one launch (start us, length us, event | category | flops | bytes accessed | tf_op | source)
XLA Modules:
  0.0 100.2 jit_solution(4504734090544168884)
XLA Ops:
  0.6 1.9 %pack.1 = (bf16[40,512]{1,0:T(8,128)(2,1)}, bf16[40,512]{1,0:T(8,128)(2,1)}, bf16[40,512]{1,0:T(8,128)(2,1)}, bf16[40,512]{1,0:T(8,128)(2,1)}, bf16[256,512]{1,0:T(8,128)(2,1)}) custom-call(bf16[40,1024]{1,0:T(8,128)(2,1)} %pk_ref.1, bf16[40,1024]{1,0:T(8,128)(2,1)} %pv_ref.1, bf16[256,256]{1,0:T(8,128)(2,1)} %rk_ref.1, bf16[256,256]{1,0:T(8,128)(2,1)} %rv_ref.1), custom_call_target="tpu_custom_call" | custom-call | tf_op jit(solution)/shard_map/pack/pallas_call | solution.py:66
  2.5 1.4 %collective-permute-start.4 = (bf16[256,512]{1,0:T(8,128)(2,1)}, bf16[256,512]{1,0:T(8,128)(2,1)S(1)}, u32[]{:S(2)}, u32[]{:S(2)}) collective-permute-start(bf16[256,512]{1,0:T(8,128)(2,1)} %get-tuple-element.45.own_ref), channel_id=1, source_target_pairs={{0,16},{4,20},{8,24},{12,28},{1,17},{5,21},{9,25},{13,29},{2,18},{... | collective-permute-start | bytes 786440 | tf_op jit(solution)/shard_map/ppermute | solution.py:487
  3.9 1.3 %collective-permute-start.3 = (bf16[256,512]{1,0:T(8,128)(2,1)}, bf16[256,512]{1,0:T(8,128)(2,1)S(1)}, u32[]{:S(2)}, u32[]{:S(2)}) collective-permute-start(bf16[256,512]{1,0:T(8,128)(2,1)} %get-tuple-element.45.own_ref), channel_id=1, source_target_pairs={{0,8},{4,12},{8,16},{12,20},{16,24},{20,28},{1,9},{5,13},{9,17},{1... | collective-permute-start | bytes 786440 | tf_op jit(solution)/shard_map/ppermute | solution.py:487
  5.2 1.6 %collective-permute-start = (bf16[40,512]{1,0:T(8,128)(2,1)}, bf16[40,512]{1,0:T(8,128)(2,1)S(1)}, u32[]{:S(2)}, u32[]{:S(2)}) collective-permute-start(bf16[40,512]{1,0:T(8,128)(2,1)} %get-tuple-element.42), channel_id=1, source_target_pairs={{0,1},{1,0},{2,3},{3,2},{4,5},{5,4},{6,7},{7,6},{8,9},{9,8},{10,11... | collective-permute-start | bytes 122888 | tf_op jit(solution)/shard_map/ppermute | solution.py:471
  6.9 2.6 %collective-permute-start.1 = (bf16[40,512]{1,0:T(8,128)(2,1)}, bf16[40,512]{1,0:T(8,128)(2,1)S(1)}, u32[]{:S(2)}, u32[]{:S(2)}) collective-permute-start(bf16[40,512]{1,0:T(8,128)(2,1)} %get-tuple-element.43), channel_id=1, source_target_pairs={{0,2},{1,3},{2,0},{3,1},{4,6},{5,7},{6,4},{7,5},{8,10},{9,11},{10,... | collective-permute-start | bytes 122888 | tf_op jit(solution)/shard_map/ppermute | solution.py:471
  9.5 0.2 collective-permute-start.2
  9.7 0.8 constant_dynamic-update-slice_fusion.3
  10.5 2.3 %collective-permute-done.1 = bf16[40,512]{1,0:T(8,128)(2,1)S(1)} collective-permute-done((bf16[40,512]{1,0:T(8,128)(2,1)}, bf16[40,512]{1,0:T(8,128)(2,1)S(1)}, u32[]{:S(2)}, u32[]{:S(2)}) %collective-permute-start.1) | collective-permute-done | bytes 40992 | tf_op jit(solution)/shard_map/ppermute | solution.py:471
  12.8 2.7 %collective-permute-done.2 = bf16[40,512]{1,0:T(8,128)(2,1)S(1)} collective-permute-done((bf16[40,512]{1,0:T(8,128)(2,1)}, bf16[40,512]{1,0:T(8,128)(2,1)S(1)}, u32[]{:S(2)}, u32[]{:S(2)}) %collective-permute-start.2) | collective-permute-done | bytes 40992 | tf_op jit(solution)/shard_map/ppermute | solution.py:471
  15.6 3.5 %collective-permute-start.5 = (bf16[160,512]{1,0:T(8,128)(2,1)S(1)}, bf16[160,512]{1,0:T(8,128)(2,1)S(1)}, u32[]{:S(2)}, u32[]{:S(2)}) collective-permute-start(bf16[160,512]{1,0:T(8,128)(2,1)S(1)} %get-tuple-element.76), channel_id=1, source_target_pairs={{0,8},{4,12},{8,0},{12,4},{16,24},{20,28},{24,16},{28,20},{1,9},{5... | collective-permute-start | bytes 491528 | tf_op jit(solution)/shard_map/ppermute | solution.py:476
  19.1 1.9 %collective-permute-start.6 = (bf16[160,512]{1,0:T(8,128)(2,1)S(1)}, bf16[160,512]{1,0:T(8,128)(2,1)S(1)}, u32[]{:S(2)}, u32[]{:S(2)}) collective-permute-start(bf16[160,512]{1,0:T(8,128)(2,1)S(1)} %get-tuple-element.76), channel_id=1, source_target_pairs={{0,16},{4,20},{8,24},{12,28},{16,0},{20,4},{24,8},{28,12},{1,17},{... | collective-permute-start | bytes 491528 | tf_op jit(solution)/shard_map/ppermute | solution.py:476
  20.9 2.5 %collective-permute-done.5 = bf16[160,512]{1,0:T(8,128)(2,1)S(1)} collective-permute-done((bf16[160,512]{1,0:T(8,128)(2,1)S(1)}, bf16[160,512]{1,0:T(8,128)(2,1)S(1)}, u32[]{:S(2)}, u32[]{:S(2)}) %collective-permute-start.5) | collective-permute-done | bytes 163872 | tf_op jit(solution)/shard_map/ppermute | solution.py:476
  23.4 3.9 %collective-permute-done.6 = bf16[160,512]{1,0:T(8,128)(2,1)S(1)} collective-permute-done((bf16[160,512]{1,0:T(8,128)(2,1)S(1)}, bf16[160,512]{1,0:T(8,128)(2,1)S(1)}, u32[]{:S(2)}, u32[]{:S(2)}) %collective-permute-start.6) | collective-permute-done | bytes 163872 | tf_op jit(solution)/shard_map/ppermute | solution.py:476
  27.6 1.3 %mask.1 = (f32[1280,256]{1,0:T(8,128)S(1)}, f32[8,128]{1,0:T(8,128)S(1)}) custom-call(s32[8]{0:T(128)S(1)} %copy-done.2, bf16[256,2048]{1,0:T(8,128)(2,1)S(1)} %copy-done), custom_call_target="tpu_custom_call" | custom-call | tf_op jit(solution)/shard_map/mask/pallas_call | solution.py:33
  28.9 0.9 turn.1
  29.8 0.6 collective-permute-done.8.got_ref
  30.5 39.7 %attention.1 = (bf16[256,2048]{1,0:T(8,128)(2,1)}, bf16[256,2048]{1,0:T(8,128)(2,1)}, f32[1408,512]{1,0:T(8,128)S(1)}, bf16[1152,512]{1,0:T(8,128)(2,1)S(1)}) custom-call(bf16[256,2048]{1,0:T(8,128)(2,1)S(1)} %copy-done, bf16[256,2048]{1,0:T(8,128)(2,1)S(1)} %copy-done.3, bf16[1152,512]{1,0:T(8,128)(2,1)S(1)} %select_dynamic-update-slice_fusion.sent_ref, ...), custom_call_target="tpu_custom_call" | custom-call | flops 16106127360 | bytes 4194304 | tf_op jit(solution)/shard_map/attention/pallas_call | solution.py:435
  70.2 0.1 collective-permute-start.9
  70.3 2.7 %collective-permute-done.9.got_ref = bf16[1152,512]{1,0:T(8,128)(2,1)S(1)} collective-permute-done((bf16[1152,512]{1,0:T(8,128)(2,1)S(1)}, bf16[1152,512]{1,0:T(8,128)(2,1)S(1)}, u32[]{:S(2)}, u32[]{:S(2)}) %collective-permute-start.9) | collective-permute-done | bytes 1179680 | tf_op jit(solution)/shard_map/ppermute | solution.py:481
  73.0 0.3 merge.1
  73.3 0.4 collective-permute-start.14
  73.7 1.6 %collective-permute-start.15 = (bf16[160,512]{1,0:T(8,128)(2,1)S(1)}, bf16[160,512]{1,0:T(8,128)(2,1)S(1)}, u32[]{:S(2)}, u32[]{:S(2)}) collective-permute-start(bf16[160,512]{1,0:T(8,128)(2,1)S(1)} %get-tuple-element.66), channel_id=1, source_target_pairs={{0,16},{4,20},{8,24},{12,28},{16,0},{20,4},{24,8},{28,12},{1,17},{... | collective-permute-start | bytes 491528 | tf_op jit(solution)/shard_map/ppermute | solution.py:476
  75.3 1.5 %collective-permute-start.16 = (bf16[160,512]{1,0:T(8,128)(2,1)S(1)}, bf16[160,512]{1,0:T(8,128)(2,1)S(1)}, u32[]{:S(2)}, u32[]{:S(2)}) collective-permute-start(bf16[160,512]{1,0:T(8,128)(2,1)S(1)} %get-tuple-element.67), channel_id=1, source_target_pairs={{0,24},{4,28},{8,16},{12,20},{16,8},{20,12},{24,0},{28,4},{1,25},{... | collective-permute-start | bytes 491528 | tf_op jit(solution)/shard_map/ppermute | solution.py:476
  76.9 2.3 %collective-permute-start.10 = (bf16[128,512]{1,0:T(8,128)(2,1)S(1)}, bf16[128,512]{1,0:T(8,128)(2,1)S(1)}, u32[]{:S(2)}, u32[]{:S(2)}) collective-permute-start(bf16[128,512]{1,0:T(8,128)(2,1)S(1)} %get-tuple-element.60), channel_id=1, source_target_pairs={{8,0},{12,4},{16,8},{20,12},{24,16},{28,20},{9,1},{13,5},{17,9},{2... | collective-permute-start | bytes 393224 | tf_op jit(solution)/shard_map/ppermute | solution.py:487
  79.1 4.6 %collective-permute-start.11 = (bf16[128,512]{1,0:T(8,128)(2,1)S(1)}, bf16[128,512]{1,0:T(8,128)(2,1)S(1)}, u32[]{:S(2)}, u32[]{:S(2)}) collective-permute-start(bf16[128,512]{1,0:T(8,128)(2,1)S(1)} %get-tuple-element.61), channel_id=1, source_target_pairs={{8,0},{12,4},{16,8},{20,12},{24,16},{28,20},{9,1},{13,5},{17,9},{2... | collective-permute-start | bytes 393224 | tf_op jit(solution)/shard_map/ppermute | solution.py:487
  83.8 1.3 %collective-permute-start.12 = (bf16[128,512]{1,0:T(8,128)(2,1)S(1)}, bf16[128,512]{1,0:T(8,128)(2,1)S(1)}, u32[]{:S(2)}, u32[]{:S(2)}) collective-permute-start(bf16[128,512]{1,0:T(8,128)(2,1)S(1)} %get-tuple-element.62), channel_id=1, source_target_pairs={{16,0},{20,4},{24,8},{28,12},{17,1},{21,5},{25,9},{29,13},{18,2},{... | collective-permute-start | bytes 393224 | tf_op jit(solution)/shard_map/ppermute | solution.py:487
  85.1 7.3 %collective-permute-start.13 = (bf16[128,512]{1,0:T(8,128)(2,1)S(1)}, bf16[128,512]{1,0:T(8,128)(2,1)S(1)}, u32[]{:S(2)}, u32[]{:S(2)}) collective-permute-start(bf16[128,512]{1,0:T(8,128)(2,1)S(1)} %get-tuple-element.63), channel_id=1, source_target_pairs={{16,0},{20,4},{24,8},{28,12},{17,1},{21,5},{25,9},{29,13},{18,2},{... | collective-permute-start | bytes 393224 | tf_op jit(solution)/shard_map/ppermute | solution.py:487
  92.5 0.1 sum_chips.1
  92.7 4.3 %collective-permute-start.19 = (bf16[40,512]{1,0:T(8,128)(2,1)S(1)}, bf16[40,512]{1,0:T(8,128)(2,1)S(1)}, u32[]{:S(2)}, u32[]{:S(2)}) collective-permute-start(bf16[40,512]{1,0:T(8,128)(2,1)S(1)} %get-tuple-element.71), channel_id=1, source_target_pairs={{0,3},{1,2},{2,1},{3,0},{4,7},{5,6},{6,5},{7,4},{8,11},{9,10},{10,... | collective-permute-start | bytes 122888 | tf_op jit(solution)/shard_map/ppermute | solution.py:471
  97.0 0.6 collective-permute-done.18.refs_6_
  97.6 1.8 %collective-permute-done.19.refs_7_ = bf16[40,512]{1,0:T(8,128)(2,1)S(1)} collective-permute-done((bf16[40,512]{1,0:T(8,128)(2,1)S(1)}, bf16[40,512]{1,0:T(8,128)(2,1)S(1)}, u32[]{:S(2)}, u32[]{:S(2)}) %collective-permute-start.19) | collective-permute-done | bytes 40992 | tf_op jit(solution)/shard_map/ppermute | solution.py:471
  99.4 0.8 finish.1
  (32 shorter events, 0.4 us)
Async XLA Ops:
  2.5 24.9 %copy-start.1 = (bf16[256,512]{1,0:T(8,128)(2,1)S(1)}, bf16[256,512]{1,0:T(8,128)(2,1)}, u32[]{:S(2)}) copy-start(bf16[256,512]{1,0:T(8,128)(2,1)} %get-tuple-element.45.own_ref) | copy-start | bytes 786436
  2.5 13.0 %collective-permute-start.4 = (bf16[256,512]{1,0:T(8,128)(2,1)}, bf16[256,512]{1,0:T(8,128)(2,1)S(1)}, u32[]{:S(2)}, u32[]{:S(2)}) collective-permute-start(bf16[256,512]{1,0:T(8,128)(2,1)} %get-tuple-element.45.own_ref), channel_id=1, source_target_pairs={{0,16},{4,20},{8,24},{12,28},{1,17},{5,21},{9,25},{13,29},{2,18},{... | collective-permute-start | bytes 786440 | tf_op jit(solution)/shard_map/ppermute | solution.py:487
  3.9 11.5 %collective-permute-start.3 = (bf16[256,512]{1,0:T(8,128)(2,1)}, bf16[256,512]{1,0:T(8,128)(2,1)S(1)}, u32[]{:S(2)}, u32[]{:S(2)}) collective-permute-start(bf16[256,512]{1,0:T(8,128)(2,1)} %get-tuple-element.45.own_ref), channel_id=1, source_target_pairs={{0,8},{4,12},{8,16},{12,20},{16,24},{20,28},{1,9},{5,13},{9,17},{1... | collective-permute-start | bytes 786440 | tf_op jit(solution)/shard_map/ppermute | solution.py:487
  5.2 5.2 %collective-permute-start = (bf16[40,512]{1,0:T(8,128)(2,1)}, bf16[40,512]{1,0:T(8,128)(2,1)S(1)}, u32[]{:S(2)}, u32[]{:S(2)}) collective-permute-start(bf16[40,512]{1,0:T(8,128)(2,1)} %get-tuple-element.42), channel_id=1, source_target_pairs={{0,1},{1,0},{2,3},{3,2},{4,5},{5,4},{6,7},{7,6},{8,9},{9,8},{10,11... | collective-permute-start | bytes 122888 | tf_op jit(solution)/shard_map/ppermute | solution.py:471
  6.9 5.9 %collective-permute-start.1 = (bf16[40,512]{1,0:T(8,128)(2,1)}, bf16[40,512]{1,0:T(8,128)(2,1)S(1)}, u32[]{:S(2)}, u32[]{:S(2)}) collective-permute-start(bf16[40,512]{1,0:T(8,128)(2,1)} %get-tuple-element.43), channel_id=1, source_target_pairs={{0,2},{1,3},{2,0},{3,1},{4,6},{5,7},{6,4},{7,5},{8,10},{9,11},{10,... | collective-permute-start | bytes 122888 | tf_op jit(solution)/shard_map/ppermute | solution.py:471
  9.5 6.0 %collective-permute-start.2 = (bf16[40,512]{1,0:T(8,128)(2,1)}, bf16[40,512]{1,0:T(8,128)(2,1)S(1)}, u32[]{:S(2)}, u32[]{:S(2)}) collective-permute-start(bf16[40,512]{1,0:T(8,128)(2,1)} %get-tuple-element.44), channel_id=1, source_target_pairs={{0,3},{1,2},{2,1},{3,0},{4,7},{5,6},{6,5},{7,4},{8,11},{9,10},{10,... | collective-permute-start | bytes 122888 | tf_op jit(solution)/shard_map/ppermute | solution.py:471
  15.5 12.1 %copy-start = (bf16[256,2048]{1,0:T(8,128)(2,1)S(1)}, bf16[256,2048]{1,0:T(8,128)(2,1)}, u32[]{:S(2)}) copy-start(bf16[256,2048]{1,0:T(8,128)(2,1)} %q_ref.3) | copy-start | bytes 3145732
  15.5 12.1 %copy-start.2 = (s32[8]{0:T(128)S(1)}, s32[8]{0:T(128)}, u32[]{:S(2)}) copy-start(s32[8]{0:T(128)} %lengths.1) | copy-start | bytes 100
  15.6 7.9 %collective-permute-start.5 = (bf16[160,512]{1,0:T(8,128)(2,1)S(1)}, bf16[160,512]{1,0:T(8,128)(2,1)S(1)}, u32[]{:S(2)}, u32[]{:S(2)}) collective-permute-start(bf16[160,512]{1,0:T(8,128)(2,1)S(1)} %get-tuple-element.76), channel_id=1, source_target_pairs={{0,8},{4,12},{8,0},{12,4},{16,24},{20,28},{24,16},{28,20},{1,9},{5... | collective-permute-start | bytes 491528 | tf_op jit(solution)/shard_map/ppermute | solution.py:476
  19.1 8.3 %collective-permute-start.6 = (bf16[160,512]{1,0:T(8,128)(2,1)S(1)}, bf16[160,512]{1,0:T(8,128)(2,1)S(1)}, u32[]{:S(2)}, u32[]{:S(2)}) collective-permute-start(bf16[160,512]{1,0:T(8,128)(2,1)S(1)} %get-tuple-element.76), channel_id=1, source_target_pairs={{0,16},{4,20},{8,24},{12,28},{16,0},{20,4},{24,8},{28,12},{1,17},{... | collective-permute-start | bytes 491528 | tf_op jit(solution)/shard_map/ppermute | solution.py:476
  20.9 6.5 %collective-permute-start.7 = (bf16[160,512]{1,0:T(8,128)(2,1)S(1)}, bf16[160,512]{1,0:T(8,128)(2,1)S(1)}, u32[]{:S(2)}, u32[]{:S(2)}) collective-permute-start(bf16[160,512]{1,0:T(8,128)(2,1)S(1)} %get-tuple-element.76), channel_id=1, source_target_pairs={{0,24},{4,28},{8,16},{12,20},{16,8},{20,12},{24,0},{28,4},{1,25},{... | collective-permute-start | bytes 491528 | tf_op jit(solution)/shard_map/ppermute | solution.py:476
  27.5 2.9 %copy-start.3 = (bf16[256,2048]{1,0:T(8,128)(2,1)S(1)}, bf16[256,2048]{1,0:T(8,128)(2,1)}, u32[]{:S(2)}) copy-start(bf16[256,2048]{1,0:T(8,128)(2,1)} %do_ref.1) | copy-start | bytes 3145732
  27.5 2.9 %collective-permute-start.8 = (bf16[1152,512]{1,0:T(8,128)(2,1)S(1)}, bf16[1152,512]{1,0:T(8,128)(2,1)S(1)}, u32[]{:S(2)}, u32[]{:S(2)}) collective-permute-start(bf16[1152,512]{1,0:T(8,128)(2,1)S(1)} %select_dynamic-update-slice_fusion.sent_ref), channel_id=1, source_target_pairs={{0,4},{4,0},{8,12},{12,8},{16,20},{20,16},{24,28},{28,24},{1,5},{5... | collective-permute-start | bytes 3538952 | tf_op jit(solution)/shard_map/ppermute | solution.py:481
  70.2 2.8 %collective-permute-start.9 = (bf16[1152,512]{1,0:T(8,128)(2,1)S(1)}, bf16[1152,512]{1,0:T(8,128)(2,1)S(1)}, u32[]{:S(2)}, u32[]{:S(2)}) collective-permute-start(bf16[1152,512]{1,0:T(8,128)(2,1)S(1)} %get-tuple-element.58), channel_id=1, source_target_pairs={{0,4},{4,0},{8,12},{12,8},{16,20},{20,16},{24,28},{28,24},{1,5},{5... | collective-permute-start | bytes 3538952 | tf_op jit(solution)/shard_map/ppermute | solution.py:481
  73.3 10.5 %collective-permute-start.14 = (bf16[160,512]{1,0:T(8,128)(2,1)S(1)}, bf16[160,512]{1,0:T(8,128)(2,1)S(1)}, u32[]{:S(2)}, u32[]{:S(2)}) collective-permute-start(bf16[160,512]{1,0:T(8,128)(2,1)S(1)} %get-tuple-element.65), channel_id=1, source_target_pairs={{0,8},{4,12},{8,0},{12,4},{16,24},{20,28},{24,16},{28,20},{1,9},{5... | collective-permute-start | bytes 491528 | tf_op jit(solution)/shard_map/ppermute | solution.py:476
  73.7 11.4 %collective-permute-start.15 = (bf16[160,512]{1,0:T(8,128)(2,1)S(1)}, bf16[160,512]{1,0:T(8,128)(2,1)S(1)}, u32[]{:S(2)}, u32[]{:S(2)}) collective-permute-start(bf16[160,512]{1,0:T(8,128)(2,1)S(1)} %get-tuple-element.66), channel_id=1, source_target_pairs={{0,16},{4,20},{8,24},{12,28},{16,0},{20,4},{24,8},{28,12},{1,17},{... | collective-permute-start | bytes 491528 | tf_op jit(solution)/shard_map/ppermute | solution.py:476
  75.3 17.1 %collective-permute-start.16 = (bf16[160,512]{1,0:T(8,128)(2,1)S(1)}, bf16[160,512]{1,0:T(8,128)(2,1)S(1)}, u32[]{:S(2)}, u32[]{:S(2)}) collective-permute-start(bf16[160,512]{1,0:T(8,128)(2,1)S(1)} %get-tuple-element.67), channel_id=1, source_target_pairs={{0,24},{4,28},{8,16},{12,20},{16,8},{20,12},{24,0},{28,4},{1,25},{... | collective-permute-start | bytes 491528 | tf_op jit(solution)/shard_map/ppermute | solution.py:476
  76.9 15.7 %collective-permute-start.10 = (bf16[128,512]{1,0:T(8,128)(2,1)S(1)}, bf16[128,512]{1,0:T(8,128)(2,1)S(1)}, u32[]{:S(2)}, u32[]{:S(2)}) collective-permute-start(bf16[128,512]{1,0:T(8,128)(2,1)S(1)} %get-tuple-element.60), channel_id=1, source_target_pairs={{8,0},{12,4},{16,8},{20,12},{24,16},{28,20},{9,1},{13,5},{17,9},{2... | collective-permute-start | bytes 393224 | tf_op jit(solution)/shard_map/ppermute | solution.py:487
  79.1 13.6 %collective-permute-start.11 = (bf16[128,512]{1,0:T(8,128)(2,1)S(1)}, bf16[128,512]{1,0:T(8,128)(2,1)S(1)}, u32[]{:S(2)}, u32[]{:S(2)}) collective-permute-start(bf16[128,512]{1,0:T(8,128)(2,1)S(1)} %get-tuple-element.61), channel_id=1, source_target_pairs={{8,0},{12,4},{16,8},{20,12},{24,16},{28,20},{9,1},{13,5},{17,9},{2... | collective-permute-start | bytes 393224 | tf_op jit(solution)/shard_map/ppermute | solution.py:487
  83.8 13.2 %collective-permute-start.12 = (bf16[128,512]{1,0:T(8,128)(2,1)S(1)}, bf16[128,512]{1,0:T(8,128)(2,1)S(1)}, u32[]{:S(2)}, u32[]{:S(2)}) collective-permute-start(bf16[128,512]{1,0:T(8,128)(2,1)S(1)} %get-tuple-element.62), channel_id=1, source_target_pairs={{16,0},{20,4},{24,8},{28,12},{17,1},{21,5},{25,9},{29,13},{18,2},{... | collective-permute-start | bytes 393224 | tf_op jit(solution)/shard_map/ppermute | solution.py:487
  85.1 11.9 %collective-permute-start.13 = (bf16[128,512]{1,0:T(8,128)(2,1)S(1)}, bf16[128,512]{1,0:T(8,128)(2,1)S(1)}, u32[]{:S(2)}, u32[]{:S(2)}) collective-permute-start(bf16[128,512]{1,0:T(8,128)(2,1)S(1)} %get-tuple-element.63), channel_id=1, source_target_pairs={{16,0},{20,4},{24,8},{28,12},{17,1},{21,5},{25,9},{29,13},{18,2},{... | collective-permute-start | bytes 393224 | tf_op jit(solution)/shard_map/ppermute | solution.py:487
  92.5 4.5 %collective-permute-start.17 = (bf16[40,512]{1,0:T(8,128)(2,1)S(1)}, bf16[40,512]{1,0:T(8,128)(2,1)S(1)}, u32[]{:S(2)}, u32[]{:S(2)}) collective-permute-start(bf16[40,512]{1,0:T(8,128)(2,1)S(1)} %get-tuple-element.69), channel_id=1, source_target_pairs={{0,1},{1,0},{2,3},{3,2},{4,5},{5,4},{6,7},{7,6},{8,9},{9,8},{10,11... | collective-permute-start | bytes 122888 | tf_op jit(solution)/shard_map/ppermute | solution.py:471
  92.6 5.0 %collective-permute-start.18 = (bf16[40,512]{1,0:T(8,128)(2,1)S(1)}, bf16[40,512]{1,0:T(8,128)(2,1)S(1)}, u32[]{:S(2)}, u32[]{:S(2)}) collective-permute-start(bf16[40,512]{1,0:T(8,128)(2,1)S(1)} %get-tuple-element.70), channel_id=1, source_target_pairs={{0,2},{1,3},{2,0},{3,1},{4,6},{5,7},{6,4},{7,5},{8,10},{9,11},{10,... | collective-permute-start | bytes 122888 | tf_op jit(solution)/shard_map/ppermute | solution.py:471
  92.7 6.7 %collective-permute-start.19 = (bf16[40,512]{1,0:T(8,128)(2,1)S(1)}, bf16[40,512]{1,0:T(8,128)(2,1)S(1)}, u32[]{:S(2)}, u32[]{:S(2)}) collective-permute-start(bf16[40,512]{1,0:T(8,128)(2,1)S(1)} %get-tuple-element.71), channel_id=1, source_target_pairs={{0,3},{1,2},{2,1},{3,0},{4,7},{5,6},{6,5},{7,4},{8,11},{9,10},{10,... | collective-permute-start | bytes 122888 | tf_op jit(solution)/shard_map/ppermute | solution.py:471
